TPU v7x, 32 devices: a whole 2x2x4 slice. The times are simulated.
32 devices in a mesh: groups: 2 (over x), grid: 8 (over z, y), band: 2 (over core).
Axes of the slice: x: 2, y: 2, z: 4, core: 2. Of those that a mesh axis runs over, the one named last changes fastest.
Arguments:
- wavefunctions: bfloat16 [1024, 32768], P(('groups', 'grid', 'band')), parts along dimension 0, may hold values from -6 to 6
- tile_segment: int32 [3072], P('grid'), may hold values from 0 to 63
- tile_block: int32 [3072], P('grid'), may hold values from 0 to 31
- tile_count: int32 [8], P('grid'), may hold values from 48 to 384, as said below
- projectors: bfloat16 [3072, 64, 128], P('grid'), may hold values from -0.75 to 0.75
- coupling: float32 [32, 16, 8, 8], replicated, may hold values from -0.1875 to 0.1875
Outputs:
- applied_field: bfloat16 [1024, 32768], P(('groups', 'grid', 'band')), parts along dimension 0
There are 2 independent parts, one for each index of `groups`. A program takes and returns all parts, laid end to end along the dimension named above; an argument that names none is the same for every part. Nothing has to cross between parts.
Inputs may be any that keep to these rules, and one draw needn't show every extreme that they name: `tile_count`: some grid index has exactly 384 live slots; every other has 48 to 192.
All inputs are finite; a program needn't handle non-finite values.
Results may differ from a plain program's by a relative error of at most 0.0063.
Values may be sent and summed in bfloat16 or wider, within the bound.
No kernel may reach another device: no remote copies, remote signals or barrier semaphores. Data moves between devices by JAX's collectives and lax.ppermute only.
A program may use at most 128 MiB of HBM per device.

v0:
```python
import math

import jax
import jax.numpy as jnp
from jax import lax
from jax.sharding import PartitionSpec as P

TILE = 64


def tile_window(index, step, tile_segment, tile_block, projectors):
    start = index * step
    segment_row = lax.dynamic_slice_in_dim(tile_segment, start, step)
    block_row = lax.dynamic_slice_in_dim(tile_block, start, step)
    values = lax.dynamic_slice_in_dim(projectors, start, step, 0)
    return (start, segment_row, block_row, values)


def apply_coupling(totals, coupling):
    rows, nblocks, proj = totals.shape
    natoms, width = (coupling.shape[1], coupling.shape[2])
    per_atom = totals.reshape(rows, nblocks, natoms, width)
    result = jnp.einsum(
        "bamj,amjk->bamk",
        per_atom,
        coupling,
        precision=lax.Precision.HIGHEST,
        preferred_element_type=jnp.float32,
    )
    return result.reshape(rows, nblocks, proj).astype(jnp.bfloat16)


def nonlocal_part(local, tile_segment, tile_block, count, projectors, coupling):
    rows, seg_dev, width = local.shape
    tiles = projectors.shape[0]
    proj = projectors.shape[2]
    nblocks = coupling.shape[0]
    step = math.gcd(tiles, 64)
    rounds = (count + step - 1) // step
    block_range = jnp.arange(nblocks, dtype=jnp.int32)
    segment_range = jnp.arange(seg_dev, dtype=jnp.int32)
    lane_range = jnp.arange(step, dtype=jnp.int32)

    def forward(index, totals):
        start, segment_row, block_row, values = tile_window(
            index, step, tile_segment, tile_block, projectors
        )
        alive = start + lane_range < count
        gathered = jnp.take(local, segment_row, axis=1)
        contrib = jnp.einsum(
            "btr,trp->btp", gathered, values, preferred_element_type=jnp.float32
        ).astype(jnp.bfloat16)
        select = ((block_row[:, None] == block_range[None, :]) & alive[:, None]).astype(
            jnp.bfloat16
        )
        return totals + jnp.einsum(
            "btp,ta->bap", contrib, select, preferred_element_type=jnp.float32
        )

    totals = lax.fori_loop(0, rounds, forward, jnp.zeros((rows, nblocks, proj), jnp.float32))
    applied = apply_coupling(lax.psum(totals, "grid"), coupling)

    def backward(index, output):
        start, segment_row, block_row, values = tile_window(
            index, step, tile_segment, tile_block, projectors
        )
        alive = start + lane_range < count
        choose = (block_row[:, None] == block_range[None, :]).astype(jnp.bfloat16)
        picked = jnp.einsum(
            "bap,ta->btp", applied, choose, preferred_element_type=jnp.float32
        ).astype(jnp.bfloat16)
        spread = jnp.einsum(
            "btp,trp->btr", picked, values, preferred_element_type=jnp.float32
        ).astype(jnp.bfloat16)
        place = ((segment_row[:, None] == segment_range[None, :]) & alive[:, None]).astype(
            jnp.bfloat16
        )
        return output + jnp.einsum("btr,ts->bsr", spread, place, preferred_element_type=jnp.float32)

    output = lax.fori_loop(0, rounds, backward, jnp.zeros((rows, seg_dev, width), jnp.float32))
    return output.reshape(rows, seg_dev * width).astype(jnp.bfloat16)


def body(wavefunctions, tile_segment, tile_block, tile_count, projectors, coupling):
    bricks = lax.all_to_all(wavefunctions, "grid", split_axis=1, concat_axis=0, tiled=True)
    rows, points = bricks.shape
    local = bricks.reshape(rows, points // TILE, TILE)
    count = tile_count[0]
    result = nonlocal_part(local, tile_segment, tile_block, count, projectors, coupling)
    return lax.all_to_all(result, "grid", split_axis=0, concat_axis=1, tiled=True)


def solution(mesh):
    in_specs = (
        P(("groups", "grid", "band"), None),
        P("grid"),
        P("grid"),
        P("grid"),
        P("grid", None, None),
        P(),
    )
    out_specs = P(("groups", "grid", "band"), None)
    return jax.shard_map(body, mesh=mesh, in_specs=in_specs, out_specs=out_specs, check_vma=False)
```

profile of v0, /device:TPU:0, one launch (start us, length us, event | category | flops | bytes accessed | tf_op | source)
XLA Modules:
  0.0 531.2 jit_solution(7463870258696169731)
XLA Ops:
  6.5 3.1 copy.36
  9.7 7.3 %all-to-all-start = ((bf16[32,8,4096]{2,0,1:T(8,128)(2,1)}), bf16[32,8,4096]{2,0,1:T(8,128)(2,1)S(1)}, u32[]{:S(2)}, u32[]{:S(2)}) async-start(bf16[32,8,4096]{2,0,1:T(8,128)(2,1)} %bitcast.65), calls=%async_computation | async-start | bytes 4194304 | tf_op jit(solution)/shard_map/all_to_all | solution.py:85
  17.7 47.5 %all-to-all-done = bf16[32,8,4096]{2,0,1:T(8,128)(2,1)S(1)} async-done(((bf16[32,8,4096]{2,0,1:T(8,128)(2,1)}), bf16[32,8,4096]{2,0,1:T(8,128)(2,1)S(1)}, u32[]{:S(2)}, u32[]{:S(2)}) %all-to-all-start) | async-done | bytes 2097184 | tf_op jit(solution)/shard_map/all_to_all | solution.py:85
  65.2 5.5 %reshape.37 = bf16[256,64,64]{2,1,0:T(8,128)(2,1)} reshape(bf16[8,32,4096]{2,1,0:T(8,128)(2,1)S(1)} %bitcast.64) | data formatting | bytes 4194304 | tf_op jit(solution)/shard_map/reshape | solution.py:87
  70.7 5.9 %copy.21 = bf16[256,64,64]{0,2,1:T(8,128)(2,1)} copy(bf16[256,64,64]{2,1,0:T(8,128)(2,1)} %reshape.37) | data formatting | bytes 4194304
  76.6 2.5 broadcast_in_dim.32
  79.1 40.9 %while.24 = (s32[]{:T(128)}, f32[256,32,128]{2,1,0:T(8,128)}, s32[]{:T(128)}, s32[384]{0:T(512)S(1)}, s32[]{:T(128)}, /*index=5*/bf16[384,64,128]{2,1,0:T(8,128)...) while((s32[]{:T(128)}, f32[256,32,128]{2,1,0:T(8,128)}, ...), condition=%wide.region_1.2_spmd.clone, body=%wide.region_0.1_spmd.clone.sunk | while | flops 406853120 | bytes 32512184 | solution.py:60
  79.9 2.3 gather_fusion
  82.1 4.5 convert_bitcast_fusion.7
  86.6 6.6 %copy.40 = bf16[256,64,128]{2,1,0:T(8,128)(2,1)} copy(bf16[256,64,128]{0,2,1:T(8,128)(2,1)} %convert_bitcast_fusion.7) | data formatting | bytes 8388608 | tf_op jit(solution)/shard_map/while/body/convert_element_type | solution.py:52
  93.3 6.3 %bitcast_add_fusion.4 = f32[256,32,128]{2,1,0:T(8,128)} fusion(f32[256,32,128]{2,1,0:T(8,128)} %get-tuple-element.402, bf16[256,64,128]{2,1,0:T(8,128)(2,1)} %copy.40, s32[64]{0:T(128)S(1)} %dynamic_slice.42, pred[64]{0:T(512)(128)(4,1)S(1)} %get-tuple-element.380), kind=kOutput, calls=%fused_computation.5.clone.1 | convolution fusion | flops 135270400 | bytes 12583232 | tf_op jit(solution)/shard_map/while/body/btp,ta->bap/dot_general | solution.py:56
  100.3 2.3 gather_fusion
  102.6 4.5 convert_bitcast_fusion.7
  107.1 6.6 %copy.40 = bf16[256,64,128]{2,1,0:T(8,128)(2,1)} copy(bf16[256,64,128]{0,2,1:T(8,128)(2,1)} %convert_bitcast_fusion.7) | data formatting | bytes 8388608 | tf_op jit(solution)/shard_map/while/body/convert_element_type | solution.py:52
  113.7 6.3 %bitcast_add_fusion.4 = f32[256,32,128]{2,1,0:T(8,128)} fusion(f32[256,32,128]{2,1,0:T(8,128)} %get-tuple-element.402, bf16[256,64,128]{2,1,0:T(8,128)(2,1)} %copy.40, s32[64]{0:T(128)S(1)} %dynamic_slice.42, pred[64]{0:T(512)(128)(4,1)S(1)} %get-tuple-element.380), kind=kOutput, calls=%fused_computation.5.clone.1 | convolution fusion | flops 135270400 | bytes 12583232 | tf_op jit(solution)/shard_map/while/body/btp,ta->bap/dot_general | solution.py:56
  120.0 5.2 copy.22
  126.3 1.8 copy.23
  128.1 231.7 %all-reduce.2.cloned.1.call-done = f32[256,32,16,8]{0,3,2,1:T(8,128)} async-done(((f32[256,32,16,8]{0,3,2,1:T(8,128)}), f32[256,32,16,8]{0,3,2,1:T(8,128)}) %all-reduce.2.cloned.1.call-update) | async-done | bytes 4194320 | tf_op jit(solution)/shard_map/psum | solution.py:61
  359.8 7.4 %convert_bitcast_fusion.3 = bf16[256,32,128]{0,2,1:T(8,128)(2,1)} fusion(f32[256,32,16,8]{0,3,2,1:T(8,128)} %all-reduce.2.cloned.1.call-done, f32[32,16,8,8]{2,3,1,0:T(8,128)S(1)} %copy.23), kind=kOutput, calls=%fused_computation.43 | convolution fusion | flops 101711872 | bytes 6422528 | tf_op jit(solution)/shard_map/bamj,amjk->bamk/dot_general | solution.py:23
  367.2 3.4 copy.24
  370.6 2.5 broadcast_in_dim.31
  373.1 27.6 %while.25 = (s32[]{:T(128)}, f32[256,64,64]{0,1,2:T(8,128)}, s32[]{:T(128)}, s32[384]{0:T(512)S(1)}, s32[]{:T(128)}, /*index=5*/bf16[384,64,128]{2,1,0:T(8,128)(...) while((s32[]{:T(128)}, f32[256,64,64]{0,1,2:T(8,128)}, ...), condition=%wide.region_4.5_spmd.clone.clone, body=%wide.region_3.4_spmd.clone.clone.sunk | while | flops 541075584 | bytes 24119096 | solution.py:80
  373.1 1.3 convert_bitcast_fusion.8
  374.4 5.7 %convert_bitcast_fusion.9 = bf16[256,64,64]{0,2,1:T(8,128)(2,1)S(1)} fusion(bf16[256,64,128]{2,1,0:T(8,128)(2,1)S(1)} %convert_bitcast_fusion.8, bf16[384,64,128]{2,1,0:T(8,128)(2,1)} %get-tuple-element.454, s32[]{:T(128)S(6)} %select_n.43), kind=kOutput, calls=%fused_computation.29.clone.1 | convolution fusion | flops 269484032 | bytes 7340036 | tf_op jit(solution)/shard_map/while/body/btp,trp->btr/dot_general | solution.py:72
  380.8 6.0 %bitcast_add_fusion.5 = f32[256,64,64]{0,1,2:T(8,128)} fusion(f32[256,64,64]{0,1,2:T(8,128)} %get-tuple-element.438, bf16[256,64,64]{0,2,1:T(8,128)(2,1)S(1)} %convert_bitcast_fusion.9, s32[64]{0:T(128)S(1)} %dynamic_slice.45, pred[64]{0:T(512)(128)(4,1)S(1)} %fusion.62), kind=kOutput, calls=%fused_computation.24.clone.1 | convolution fusion | flops 135274496 | bytes 10486080 | tf_op jit(solution)/shard_map/while/body/btr,ts->bsr/dot_general | solution.py:78
  388.2 5.7 %convert_bitcast_fusion.9 = bf16[256,64,64]{0,2,1:T(8,128)(2,1)S(1)} fusion(bf16[256,64,128]{2,1,0:T(8,128)(2,1)S(1)} %convert_bitcast_fusion.8, bf16[384,64,128]{2,1,0:T(8,128)(2,1)} %get-tuple-element.454, s32[]{:T(128)S(6)} %select_n.43), kind=kOutput, calls=%fused_computation.29.clone.1 | convolution fusion | flops 269484032 | bytes 7340036 | tf_op jit(solution)/shard_map/while/body/btp,trp->btr/dot_general | solution.py:72
  394.6 6.0 %bitcast_add_fusion.5 = f32[256,64,64]{0,1,2:T(8,128)} fusion(f32[256,64,64]{0,1,2:T(8,128)} %get-tuple-element.438, bf16[256,64,64]{0,2,1:T(8,128)(2,1)S(1)} %convert_bitcast_fusion.9, s32[64]{0:T(128)S(1)} %dynamic_slice.45, pred[64]{0:T(512)(128)(4,1)S(1)} %fusion.62), kind=kOutput, calls=%fused_computation.24.clone.1 | convolution fusion | flops 135274496 | bytes 10486080 | tf_op jit(solution)/shard_map/while/body/btr,ts->bsr/dot_general | solution.py:78
  400.7 2.5 convert_element_type.44
  403.2 8.1 %copy.25 = bf16[256,64,64]{2,1,0:T(8,128)(2,1)} copy(bf16[256,64,64]{0,1,2:T(8,128)(2,1)S(1)} %convert_element_type.44) | data formatting | bytes 4194304 | tf_op jit(solution)/shard_map/convert_element_type | solution.py:81
  411.3 5.7 %convert_element_type.45 = bf16[8,32,4096]{2,1,0:T(8,128)(2,1)S(1)} reshape(bf16[256,64,64]{2,1,0:T(8,128)(2,1)} %copy.25) | data formatting | bytes 4194304 | tf_op jit(solution)/shard_map/convert_element_type | solution.py:81
  416.9 106.0 %all_to_all.32 = bf16[8,32,4096]{2,1,0:T(8,128)(2,1)S(1)} all-to-all(bf16[8,32,4096]{2,1,0:T(8,128)(2,1)S(1)} %convert_element_type.45), channel_id=1, replica_groups=mesh['groups'=2,'grid'=8,'band'=2] {'grid'}, dimensions={0} | all-to-all | bytes 4194304 | tf_op jit(solution)/shard_map/all_to_all | solution.py:90
  522.9 1.5 copy.28
  (21 shorter events, 5.6 us)
Async XLA Ops:
  9.7 55.5 %all-to-all-start = ((bf16[32,8,4096]{2,0,1:T(8,128)(2,1)}), bf16[32,8,4096]{2,0,1:T(8,128)(2,1)S(1)}, u32[]{:S(2)}, u32[]{:S(2)}) async-start(bf16[32,8,4096]{2,0,1:T(8,128)(2,1)} %bitcast.65), calls=%async_computation | async-start | bytes 4194304 | tf_op jit(solution)/shard_map/all_to_all | solution.py:85
  16.9 342.8 %all-reduce.2.cloned.1.call-start = ((), (), s32[]{:S(2)}) async-start(), calls=%async_computation.2 | async-start | bytes 8388608 | tf_op jit(solution)/shard_map/psum | solution.py:61
  70.7 8.4 %copy-start.1 = (s32[384]{0:T(512)S(1)}, s32[384]{0:T(512)}, u32[]{:S(2)}) copy-start(s32[384]{0:T(512)} %param.11) | copy-start | bytes 4612
  70.7 8.4 %copy-start.2 = (s32[384]{0:T(512)S(1)}, s32[384]{0:T(512)}, u32[]{:S(2)}) copy-start(s32[384]{0:T(512)} %param.12) | copy-start | bytes 4612
  125.2 1.0 copy-start
Sparse Core Ops, SparseCore 0:
  125.4 234.3 all-reduce.1
where the time goes:
time: 533 us; the launch traced here: 531 us
  waiting for transfers between devices  279 us (52%)
  blocking collectives  106 us (20%)
  local copies, waits for them, and re-layouts  64.3 us (12%)
  matrix products  54.9 us (10%)
  between operations  14.1 us (3%)
  starting transfers between devices  7.32 us (1%)
    psum x1, waiting for transfers between devices, nonlocal_part(): applied = apply_coupling(lax.psum(totals, 'grid'), coupling)  232 us
    all_to_all x1, blocking collectives, body(): lax.all_to_all(result, 'grid', split_axis=0, concat_axis=1, tiled=True)  106 us
    all_to_all x1, waiting for transfers between devices, body(): lax.all_to_all(wavefunctions, 'grid', split_axis=1, concat_axis=0, tiled=...  47.5 us
    convert_element_type x2, local copies, waits for them, and re-layouts, nonlocal_part(): return output.reshape(rows, seg_dev * width).astype(jnp.bfloat16)  13.8 us
    convert_element_type x2, local copies, waits for them, and re-layouts, forward(): contrib = jnp.einsum('btr,trp->btp', gathered, values, preferred_element_...  13.1 us
    dot_general x2, matrix products, forward(): jnp.einsum('btp,ta->bap', contrib, select, preferred_element_type=jnp.flo...  12.6 us
    unnamed x9, local copies, waits for them, and re-layouts  12.2 us
    dot_general x2, matrix products, backward(): jnp.einsum('btr,ts->bsr', spread, place, preferred_element_type=jnp.float32)  12 us
  transfers between devices with their start and end apart: 2, of which 2 were waited for; matrix products, arithmetic and copies ran while one was open for 0% of the time, Pallas kernels for 0%

commit v1 on v0

v1 whole, which is shorter than its diff:
```python
import functools

import jax
import jax.numpy as jnp
from jax import lax
from jax.experimental import pallas as pl
from jax.experimental.pallas import tpu as pltpu
from jax.sharding import PartitionSpec as P

TILE = 64
PAIR = 2 * TILE
UNROLL = 8
VMEM_LIMIT = 56 * 1024 * 1024


def padded_tile(values, half):
    zero = jnp.zeros_like(values)
    return jnp.concatenate(
        [jnp.where(half == 0, values, zero), jnp.where(half == 1, values, zero)], axis=0
    )


def tile_loop(meta, proj_ref, chunk, tiles, step):
    base = pl.program_id(1) * chunk
    live = jnp.clip(meta[2 * tiles] - base, 0, chunk)

    def group(index, carry):
        for lane in range(UNROLL):
            local = index * UNROLL + lane
            slot = base + local
            segment = meta[slot]
            block = meta[tiles + slot]
            half = jnp.where(local < live, segment % 2, 2)
            points = pl.ds(pl.multiple_of((segment // 2) * PAIR, PAIR), PAIR)
            step(block, points, padded_tile(proj_ref[local], half))
        return carry

    lax.fori_loop(0, (live + UNROLL - 1) // UNROLL, group, 0)


def project_kernel(chunk, tiles, meta, wave_ref, proj_ref, *rest):
    out_ref = rest[-1]
    proj = proj_ref.shape[2]

    @pl.when(pl.program_id(1) == 0)
    def start():
        if len(rest) == 2:
            out_ref[...] = rest[0][...]
        else:
            out_ref[...] = jnp.zeros_like(out_ref)

    def step(block, points, tile):
        lanes = pl.ds(pl.multiple_of(block * proj, proj), proj)
        term = jnp.dot(wave_ref[:, points], tile, preferred_element_type=jnp.float32)
        out_ref[:, lanes] += term

    tile_loop(meta, proj_ref, chunk, tiles, step)


def spread_kernel(chunk, tiles, meta, applied_ref, proj_ref, out_ref, field):
    proj = proj_ref.shape[2]

    @pl.when(pl.program_id(1) == 0)
    def start():
        field[...] = jnp.zeros_like(field)

    def step(block, points, tile):
        lanes = pl.ds(pl.multiple_of(block * proj, proj), proj)
        term = lax.dot_general(
            applied_ref[:, lanes],
            tile,
            (((1,), (1,)), ((), ())),
            preferred_element_type=jnp.float32,
        )
        field[:, points] += term

    tile_loop(meta, proj_ref, chunk, tiles, step)

    @pl.when(pl.program_id(1) == pl.num_programs(1) - 1)
    def finish():
        out_ref[...] = field[...].astype(out_ref.dtype)


def row_block(rows):
    return rows if rows <= 256 else 256


def tile_chunk(tiles):
    for chunk in (96, 64, 48, 32, 16, 8):
        if tiles % chunk == 0:
            return chunk
    return tiles


def chunk_index(chunk, tiles):
    def index(row, step, meta):
        last = (meta[2 * tiles] + chunk - 1) // chunk - 1
        return (jnp.clip(step, 0, jnp.maximum(last, 0)), 0, 0)

    return index


def whole_rows(row, step, meta):
    return (row, 0)


def project(meta, wave, projectors, width, total=None):
    rows, points = wave.shape
    tiles, tile, proj = projectors.shape
    chunk, block = tile_chunk(tiles), row_block(rows)
    in_specs = [
        pl.BlockSpec((block, points), whole_rows),
        pl.BlockSpec((chunk, tile, proj), chunk_index(chunk, tiles)),
    ]
    operands = [meta, wave, projectors]
    if total is not None:
        in_specs.append(pl.BlockSpec((block, width), whole_rows))
        operands.append(total)
    return pl.pallas_call(
        functools.partial(project_kernel, chunk, tiles),
        grid_spec=pltpu.PrefetchScalarGridSpec(
            num_scalar_prefetch=1,
            grid=(rows // block, tiles // chunk),
            in_specs=in_specs,
            out_specs=pl.BlockSpec((block, width), whole_rows),
        ),
        out_shape=jax.ShapeDtypeStruct((rows, width), jnp.float32),
        compiler_params=pltpu.CompilerParams(vmem_limit_bytes=VMEM_LIMIT),
        cost_estimate=pl.CostEstimate(
            flops=2 * rows * tiles * tile * proj,
            bytes_accessed=projectors.size * 2 + wave.size * 2 + rows * width * 4,
            transcendentals=0,
        ),
    )(*operands)


def spread(meta, applied, projectors, points):
    rows, width = applied.shape
    tiles, tile, proj = projectors.shape
    chunk, block = tile_chunk(tiles), row_block(rows)
    return pl.pallas_call(
        functools.partial(spread_kernel, chunk, tiles),
        grid_spec=pltpu.PrefetchScalarGridSpec(
            num_scalar_prefetch=1,
            grid=(rows // block, tiles // chunk),
            in_specs=[
                pl.BlockSpec((block, width), whole_rows),
                pl.BlockSpec((chunk, tile, proj), chunk_index(chunk, tiles)),
            ],
            out_specs=pl.BlockSpec((block, points), whole_rows),
            scratch_shapes=[pltpu.VMEM((block, points), jnp.float32)],
        ),
        out_shape=jax.ShapeDtypeStruct((rows, points), jnp.bfloat16),
        compiler_params=pltpu.CompilerParams(vmem_limit_bytes=VMEM_LIMIT),
        cost_estimate=pl.CostEstimate(
            flops=2 * rows * tiles * tile * proj,
            bytes_accessed=projectors.size * 2 + applied.size * 2 + rows * points * 2,
            transcendentals=0,
        ),
    )(meta, applied, projectors)


def couple_kernel(parts_ref, matrix_ref, out_ref):
    blocks, proj, unused = matrix_ref.shape
    for block in range(blocks):
        lanes = slice(block * proj, (block + 1) * proj)
        total = jnp.sum(parts_ref[:, :, lanes].astype(jnp.float32), axis=0)
        out_ref[:, lanes] = jnp.dot(
            total,
            matrix_ref[block],
            precision=lax.Precision.HIGHEST,
            preferred_element_type=jnp.float32,
        ).astype(out_ref.dtype)


def couple(parts, matrix):
    count, rows, width = parts.shape
    return pl.pallas_call(
        couple_kernel,
        out_shape=jax.ShapeDtypeStruct((rows, width), jnp.bfloat16),
        compiler_params=pltpu.CompilerParams(vmem_limit_bytes=VMEM_LIMIT),
        cost_estimate=pl.CostEstimate(
            flops=12 * rows * width * matrix.shape[1],
            bytes_accessed=parts.size * 2 + matrix.size * 4,
            transcendentals=0,
        ),
    )(parts, matrix)


def coupling_matrix(coupling):
    blocks, atoms, width, unused = coupling.shape
    proj = atoms * width
    wide = jnp.tile(coupling.reshape(blocks, proj, width), (1, 1, atoms))
    same = jnp.arange(proj)[:, None] // width == jnp.arange(proj)[None, :] // width
    return jnp.where(same[None], wide, 0.0)


def body(n_grid, n_copies, wavefunctions, tile_segment, tile_block, tile_count, projectors, coupling):
    half = n_grid // 2
    bands, npts = wavefunctions.shape
    points = npts // n_grid
    tiles = projectors.shape[0]
    width = coupling.shape[0] * projectors.shape[2]
    side = lax.axis_index("grid") // half
    pools = [list(range(half)), list(range(half, n_grid))]
    partners = [(index, (index + half) % n_grid) for index in range(n_grid)]

    meta = jnp.concatenate([tile_segment, tile_block, tile_count])
    other_meta = lax.ppermute(meta, "grid", partners)

    share = tiles // n_copies
    mine = lax.dynamic_slice_in_dim(
        projectors, lax.axis_index(("groups", "band")) * share, share, 0
    )
    arrived = lax.ppermute(mine, "grid", partners)
    other_projectors = lax.all_gather(arrived, ("groups", "band"), axis=0, tiled=True)

    def to_bricks(which):
        part = lax.dynamic_slice_in_dim(wavefunctions, which * half * points, half * points, 1)
        return lax.all_to_all(
            part, "grid", split_axis=1, concat_axis=0, tiled=True, axis_index_groups=pools
        )

    own_wave = to_bricks(side)
    other_wave = to_bricks(1 - side)
    matrix = coupling_matrix(coupling)

    total = project(meta, own_wave, projectors, width)
    total = project(other_meta, other_wave, other_projectors, width, total)

    partial = total.astype(jnp.bfloat16).reshape(half, bands, width)
    parts = lax.all_to_all(
        partial, "grid", split_axis=0, concat_axis=0, tiled=True, axis_index_groups=pools
    )
    applied = lax.all_gather(
        couple(parts, matrix), "grid", axis=0, tiled=True, axis_index_groups=pools
    )

    def to_bands(field):
        return lax.all_to_all(
            field, "grid", split_axis=0, concat_axis=1, tiled=True, axis_index_groups=pools
        )

    other_field = to_bands(spread(other_meta, applied, other_projectors, points))
    own_field = to_bands(spread(meta, applied, projectors, points))
    return jnp.where(
        side == 0,
        jnp.concatenate([own_field, other_field], axis=1),
        jnp.concatenate([other_field, own_field], axis=1),
    )


def solution(mesh):
    in_specs = (
        P(("groups", "grid", "band"), None),
        P("grid"),
        P("grid"),
        P("grid"),
        P("grid", None, None),
        P(),
    )
    out_specs = P(("groups", "grid", "band"), None)
    n_copies = mesh.shape["groups"] * mesh.shape["band"]
    return jax.shard_map(
        functools.partial(body, mesh.shape["grid"], n_copies),
        mesh=mesh,
        in_specs=in_specs,
        out_specs=out_specs,
        check_vma=False,
    )
```

time: 533 us -> 258 us (0.48)
  waiting for transfers between devices: 279 us -> 147 us
  blocking collectives: 106 us -> 0 us
  matrix products: 54.9 us -> 0 us
  local copies, waits for them, and re-layouts: 64.3 us -> 11.3 us
  Pallas kernels: 0 us -> 38.1 us
  starting transfers between devices: 7.32 us -> 39.1 us
    psum x1 -> x0, waiting for transfers between devices: 232 us -> none  [nonlocal_part(): applied = apply_coupling(lax.psum(totals, 'grid'), coupling)]
    all_to_all x1 -> x0, blocking collectives: 106 us -> none  [body(): lax.all_to_all(result, 'grid', split_axis=0, concat_axis=1, tiled=True)]
    ppermute x0 -> x2, waiting for transfers between devices: none -> 69.2 us  [the longest x1 68.1 us: body(): arrived = lax.ppermute(mine, 'grid', partners)]
    dot_general x11 -> x0, matrix products: 54.9 us -> none  [the longest x2 12.6 us: forward(): jnp.einsum('btp,ta->bap', contrib, select, preferred_element_type=jnp.flo...]
    pallas_call x0 -> x5, Pallas kernels: none -> 38.1 us  [the longest x2 17.1 us: spread(): pl.pallas_call(functools.partial(spread_kernel, chunk, tiles), grid_spec=...]
    all_gather x0 -> x2, waiting for transfers between devices: none -> 35.1 us  [the longest x1 24.4 us: body(): lax.all_gather(couple(parts, matrix), 'grid', axis=0, tiled=True, axis_in...]
    convert_element_type x4 -> x0, local copies, waits for them, and re-layouts: 26.9 us -> none  [the longest x2 13.8 us: nonlocal_part(): return output.reshape(rows, seg_dev * width).astype(jnp.bfloat16)]
    all_to_all x1 -> x5, starting transfers between devices: 7.28 us -> 31.6 us  [the longest x2 15 us: to_bands(): lax.all_to_all(field, 'grid', split_axis=0, concat_axis=1, tiled=True, ax...]
  transfers between devices with their start and end apart: 2 -> 9, of which waited for: 2 -> 9; matrix products, arithmetic and copies ran while one was open for 0% -> 4% of each run, Pallas kernels for 0% -> 7%
where the time goes in v1:
time: 258 us; the launch traced here: 255 us
  waiting for transfers between devices  147 us (57%)
  starting transfers between devices  39.1 us (15%)
  Pallas kernels  38.1 us (15%)
  between operations  14.2 us (6%)
  local copies, waits for them, and re-layouts  11.3 us (4%)
  other arithmetic  6.25 us (2%)
    ppermute x1, waiting for transfers between devices, body(): arrived = lax.ppermute(mine, 'grid', partners)  68.1 us
    all_gather x1, waiting for transfers between devices, body(): lax.all_gather(couple(parts, matrix), 'grid', axis=0, tiled=True, axis_in...  24.4 us
    all_to_all x2, waiting for transfers between devices, to_bands(): lax.all_to_all(field, 'grid', split_axis=0, concat_axis=1, tiled=True, ax...  17.6 us
    pallas_call x2, Pallas kernels, spread(): pl.pallas_call(functools.partial(spread_kernel, chunk, tiles), grid_spec=...  17.1 us
    pallas_call x2, Pallas kernels, project(): pl.pallas_call(functools.partial(project_kernel, chunk, tiles), grid_spec...  16.6 us
    all_to_all x2, starting transfers between devices, to_bands(): lax.all_to_all(field, 'grid', split_axis=0, concat_axis=1, tiled=True, ax...  15 us
    all_to_all x2, waiting for transfers between devices, to_bricks(): lax.all_to_all(part, 'grid', split_axis=1, concat_axis=0, tiled=True, axi...  15 us
    all_gather x1, waiting for transfers between devices, body(): lax.all_gather(arrived, ('groups', 'band'), axis=0, tiled=True)  10.6 us
  transfers between devices with their start and end apart: 9, of which 9 were waited for; matrix products, arithmetic and copies ran while one was open for 4% of the time, Pallas kernels for 7%

profile of v1, /device:TPU:0, one launch (start us, length us, event | category | flops | bytes accessed | tf_op | source)
XLA Modules:
  0.0 255.4 jit_solution(9102238784518004833)
XLA Ops:
  6.5 1.5 constant_dynamic-slice_fusion.1
  8.1 4.1 %collective-permute-start.1 = (bf16[96,64,128]{2,1,0:T(8,128)(2,1)S(1)}, bf16[96,64,128]{2,1,0:T(8,128)(2,1)S(1)}, u32[]{:S(2)}, u32[]{:S(2)}) collective-permute-start(bf16[96,64,128]{2,1,0:T(8,128)(2,1)S(1)} %constant_dynamic-slice_fusion.1), channel_id=1, source_target_pairs={{0,8},{2,10},{4,12},{6,14},{8,0},{10,2},{12,4},{14,6},{1,9},{3,11}... | collective-permute-start | bytes 4718600 | tf_op jit(solution)/shard_map/ppermute | solution.py:215
  12.2 68.1 %collective-permute-done.1 = bf16[96,64,128]{2,1,0:T(8,128)(2,1)S(1)} collective-permute-done((bf16[96,64,128]{2,1,0:T(8,128)(2,1)S(1)}, bf16[96,64,128]{2,1,0:T(8,128)(2,1)S(1)}, u32[]{:S(2)}, u32[]{:S(2)}) %collective-permute-start.1) | collective-permute-done | bytes 1572896 | tf_op jit(solution)/shard_map/ppermute | solution.py:215
  80.3 1.1 copy-done.3
  81.5 1.7 constant_dynamic-slice_fusion
  83.2 1.0 copy.28
  84.2 3.5 %all-to-all-start.1 = ((bf16[32,4,4096]{2,0,1:T(8,128)(2,1)}), bf16[32,4,4096]{2,0,1:T(8,128)(2,1)S(1)}, u32[]{:S(2)}, u32[]{:S(2)}) async-start(bf16[32,4,4096]{2,0,1:T(8,128)(2,1)} %bitcast.24), calls=%async_computation.1 | async-start | bytes 2097152 | tf_op jit(solution)/shard_map/all_to_all | solution.py:220
  87.7 1.1 copy.29
  88.9 12.2 %all-to-all-done.1 = bf16[32,4,4096]{2,0,1:T(8,128)(2,1)S(1)} async-done(((bf16[32,4,4096]{2,0,1:T(8,128)(2,1)}), bf16[32,4,4096]{2,0,1:T(8,128)(2,1)S(1)}, u32[]{:S(2)}, u32[]{:S(2)}) %all-to-all-start.1) | async-done | bytes 1048608 | tf_op jit(solution)/shard_map/all_to_all | solution.py:220
  101.1 3.5 %all-to-all-start = ((bf16[32,4,4096]{2,0,1:T(8,128)(2,1)}), bf16[32,4,4096]{2,0,1:T(8,128)(2,1)S(1)}, u32[]{:S(2)}, u32[]{:S(2)}) async-start(bf16[32,4,4096]{2,0,1:T(8,128)(2,1)} %bitcast.25), calls=%async_computation | async-start | bytes 2097152 | tf_op jit(solution)/shard_map/all_to_all | solution.py:220
  105.3 3.3 %collective-permute-start = (s32[769]{0:T(1024)S(1)}, s32[769]{0:T(1024)S(1)}, u32[]{:S(2)}, u32[]{:S(2)}) collective-permute-start(s32[769]{0:T(1024)S(1)} %constant_dynamic-update-slice_fusion.meta), channel_id=1, source_target_pairs={{0,8},{2,10},{4,12},{6,14},{8,0},{10,2},{12,4},{14,6},{1,9},{3,11}... | collective-permute-start | bytes 9236 | tf_op jit(solution)/shard_map/ppermute | solution.py:209
  108.7 5.9 %shard_map.64.rest_0_ = f32[128,4096]{1,0:T(8,128)} custom-call(s32[769]{0:T(1024)} %copy-done.6, bf16[128,4096]{1,0:T(8,128)(2,1)} %bitcast.26, bf16[384,64,128]{2,1,0:T(8,128)(2,1)} %proj_ref.3), custom_call_target="tpu_custom_call" | custom-call | flops 805306368 | bytes 9437184 | tf_op jit(solution)/shard_map/pallas_call | solution.py:119
  114.6 1.1 collective-permute-done.meta
  115.7 2.8 %all-to-all-done = bf16[32,4,4096]{2,0,1:T(8,128)(2,1)S(1)} async-done(((bf16[32,4,4096]{2,0,1:T(8,128)(2,1)}), bf16[32,4,4096]{2,0,1:T(8,128)(2,1)S(1)}, u32[]{:S(2)}, u32[]{:S(2)}) %all-to-all-start) | async-done | bytes 1048608 | tf_op jit(solution)/shard_map/all_to_all | solution.py:220
  118.5 10.6 %all-gather.3.cloned.1.call-done.proj_ref = bf16[384,64,128]{2,1,0:T(8,128)(2,1)} async-done(((bf16[96,64,128]{2,1,0:T(8,128)(2,1)}), bf16[384,64,128]{2,1,0:T(8,128)(2,1)}) %all-gather.3.cloned.1.call-update) | async-done | bytes 6291472 | tf_op jit(solution)/shard_map/all_gather | solution.py:216
  129.2 10.7 %shard_map.65 = f32[128,4096]{1,0:T(8,128)} custom-call(s32[769]{0:T(1024)} %copy-done.5, bf16[128,4096]{1,0:T(8,128)(2,1)} %bitcast.33, bf16[384,64,128]{2,1,0:T(8,128)(2,1)} %all-gather.3.cloned.1.call-done.proj_ref, f32[128,4096]{1,0:T(8,128)} %shard_map.64.rest_0_), custom_call_target="tpu_custom_call" | custom-call | flops 805306368 | bytes 9437184 | tf_op jit(solution)/shard_map/pallas_call | solution.py:119
  139.8 2.8 %convert_element_type.3 = bf16[128,4096]{1,0:T(8,128)(2,1)} convert(f32[128,4096]{1,0:T(8,128)} %shard_map.65) | non-fusion elementwise | flops 524288 | bytes 3145728 | tf_op jit(solution)/shard_map/convert_element_type | solution.py:231
  142.7 9.6 %all-to-all-start.2 = ((bf16[4,32,4096]{2,1,0:T(8,128)(2,1)}), bf16[4,32,4096]{2,1,0:T(8,128)(2,1)S(1)}, u32[]{:S(2)}, u32[]{:S(2)}) async-start(bf16[4,32,4096]{2,1,0:T(8,128)(2,1)} %bitcast.4), calls=%async_computation.2 | async-start | bytes 2097152 | tf_op jit(solution)/shard_map/all_to_all | solution.py:232
  152.5 1.5 broadcast_bitcast_fusion
  153.9 1.9 copy.19
  156.0 1.5 broadcast_select_fusion.matrix_ref
  157.5 9.6 %all-to-all-done.2.parts_ref = bf16[4,32,4096]{2,1,0:T(8,128)(2,1)S(1)} async-done(((bf16[4,32,4096]{2,1,0:T(8,128)(2,1)}), bf16[4,32,4096]{2,1,0:T(8,128)(2,1)S(1)}, u32[]{:S(2)}, u32[]{:S(2)}) %all-to-all-start.2) | async-done | bytes 1048608 | tf_op jit(solution)/shard_map/all_to_all | solution.py:232
  167.0 1.0 copy-done.1
  168.0 4.4 %shard_map.66 = bf16[32,4096]{1,0:T(8,128)(2,1)} custom-call(bf16[4,32,4096]{2,1,0:T(8,128)(2,1)} %copy-done.1, f32[32,128,128]{2,1,0:T(8,128)} %broadcast_select_fusion.matrix_ref), custom_call_target="tpu_custom_call" | custom-call | flops 201326592 | bytes 3145728 | tf_op jit(solution)/shard_map/pallas_call | solution.py:178
  172.4 24.4 %all-gather.5.cloned.1.call-done.applied_ref = bf16[128,4096]{1,0:T(8,128)(2,1)} async-done(((bf16[32,4096]{1,0:T(8,128)(2,1)}), bf16[128,4096]{1,0:T(8,128)(2,1)}) %all-gather.5.cloned.1.call-update) | async-done | bytes 1048592 | tf_op jit(solution)/shard_map/all_gather | solution.py:235
  196.9 6.2 %shard_map.67 = bf16[128,4096]{1,0:T(8,128)(2,1)} custom-call(s32[769]{0:T(1024)} %copy-done.6, bf16[128,4096]{1,0:T(8,128)(2,1)} %all-gather.5.cloned.1.call-done.applied_ref, bf16[384,64,128]{2,1,0:T(8,128)(2,1)} %proj_ref.3), custom_call_target="tpu_custom_call" | custom-call | flops 805306368 | bytes 8388608 | tf_op jit(solution)/shard_map/pallas_call | solution.py:141
  203.1 7.1 %all-to-all-start.3 = ((bf16[4,32,4096]{2,1,0:T(8,128)(2,1)}), bf16[4,32,4096]{2,1,0:T(8,128)(2,1)S(1)}, u32[]{:S(2)}, u32[]{:S(2)}) async-start(bf16[4,32,4096]{2,1,0:T(8,128)(2,1)} %bitcast.35), calls=%async_computation.3 | async-start | bytes 2097152 | tf_op jit(solution)/shard_map/all_to_all | solution.py:240
  210.1 10.9 %shard_map.68 = bf16[128,4096]{1,0:T(8,128)(2,1)} custom-call(s32[769]{0:T(1024)} %copy-done.5, bf16[128,4096]{1,0:T(8,128)(2,1)} %all-gather.5.cloned.1.call-done.applied_ref, bf16[384,64,128]{2,1,0:T(8,128)(2,1)} %all-gather.3.cloned.1.call-done.proj_ref), custom_call_target="tpu_custom_call" | custom-call | flops 805306368 | bytes 8388608 | tf_op jit(solution)/shard_map/pallas_call | solution.py:141
  221.0 3.7 %all-to-all-done.3 = bf16[4,32,4096]{2,1,0:T(8,128)(2,1)S(1)} async-done(((bf16[4,32,4096]{2,1,0:T(8,128)(2,1)}), bf16[4,32,4096]{2,1,0:T(8,128)(2,1)S(1)}, u32[]{:S(2)}, u32[]{:S(2)}) %all-to-all-start.3) | async-done | bytes 1048608 | tf_op jit(solution)/shard_map/all_to_all | solution.py:240
  224.8 7.9 %all-to-all-start.4 = ((bf16[4,32,4096]{2,1,0:T(8,128)(2,1)}), bf16[4,32,4096]{2,1,0:T(8,128)(2,1)S(1)}, u32[]{:S(2)}, u32[]{:S(2)}) async-start(bf16[4,32,4096]{2,1,0:T(8,128)(2,1)} %bitcast.34), calls=%async_computation.4 | async-start | bytes 2097152 | tf_op jit(solution)/shard_map/all_to_all | solution.py:240
  232.8 13.9 %all-to-all-done.4 = bf16[4,32,4096]{2,1,0:T(8,128)(2,1)S(1)} async-done(((bf16[4,32,4096]{2,1,0:T(8,128)(2,1)}), bf16[4,32,4096]{2,1,0:T(8,128)(2,1)S(1)}, u32[]{:S(2)}, u32[]{:S(2)}) %all-to-all-start.4) | async-done | bytes 1048608 | tf_op jit(solution)/shard_map/all_to_all | solution.py:240
  246.8 1.8 maximum_select_fusion
  (29 shorter events, 0.5 us)
Async XLA Ops:
  6.5 122.6 %all-gather.3.cloned.1.call-start = ((), (), s32[]{:S(2)}) async-start(), calls=%async_computation.5 | async-start | bytes 7864320 | tf_op jit(solution)/shard_map/all_gather | solution.py:216
  8.1 72.2 %collective-permute-start.1 = (bf16[96,64,128]{2,1,0:T(8,128)(2,1)S(1)}, bf16[96,64,128]{2,1,0:T(8,128)(2,1)S(1)}, u32[]{:S(2)}, u32[]{:S(2)}) collective-permute-start(bf16[96,64,128]{2,1,0:T(8,128)(2,1)S(1)} %constant_dynamic-slice_fusion.1), channel_id=1, source_target_pairs={{0,8},{2,10},{4,12},{6,14},{8,0},{10,2},{12,4},{14,6},{1,9},{3,11}... | collective-permute-start | bytes 4718600 | tf_op jit(solution)/shard_map/ppermute | solution.py:215
  80.3 1.1 copy-start.3
  84.2 16.9 %all-to-all-start.1 = ((bf16[32,4,4096]{2,0,1:T(8,128)(2,1)}), bf16[32,4,4096]{2,0,1:T(8,128)(2,1)S(1)}, u32[]{:S(2)}, u32[]{:S(2)}) async-start(bf16[32,4,4096]{2,0,1:T(8,128)(2,1)} %bitcast.24), calls=%async_computation.1 | async-start | bytes 2097152 | tf_op jit(solution)/shard_map/all_to_all | solution.py:220
  87.7 17.5 %copy-start.7 = (s32[384]{0:T(512)S(1)}, s32[384]{0:T(512)}, u32[]{:S(2)}) copy-start(s32[384]{0:T(512)} %param.7) | copy-start | bytes 4612
  87.7 17.5 %copy-start.8 = (s32[384]{0:T(512)S(1)}, s32[384]{0:T(512)}, u32[]{:S(2)}) copy-start(s32[384]{0:T(512)} %param.8) | copy-start | bytes 4612
  101.1 7.6 %copy-start = (bf16[32,4,4096]{2,0,1:T(8,128)(2,1)}, bf16[32,4,4096]{2,0,1:T(8,128)(2,1)S(1)}, u32[]{:S(2)}) copy-start(bf16[32,4,4096]{2,0,1:T(8,128)(2,1)S(1)} %all-to-all-done.1) | copy-start | bytes 3145732
  101.1 17.5 %all-to-all-start = ((bf16[32,4,4096]{2,0,1:T(8,128)(2,1)}), bf16[32,4,4096]{2,0,1:T(8,128)(2,1)S(1)}, u32[]{:S(2)}, u32[]{:S(2)}) async-start(bf16[32,4,4096]{2,0,1:T(8,128)(2,1)} %bitcast.25), calls=%async_computation | async-start | bytes 2097152 | tf_op jit(solution)/shard_map/all_to_all | solution.py:220
  105.3 3.4 %copy-start.6 = (s32[769]{0:T(1024)}, s32[769]{0:T(1024)S(1)}, u32[]{:S(2)}) copy-start(s32[769]{0:T(1024)S(1)} %constant_dynamic-update-slice_fusion.meta) | copy-start | bytes 9232
  105.3 10.4 %collective-permute-start = (s32[769]{0:T(1024)S(1)}, s32[769]{0:T(1024)S(1)}, u32[]{:S(2)}, u32[]{:S(2)}) collective-permute-start(s32[769]{0:T(1024)S(1)} %constant_dynamic-update-slice_fusion.meta), channel_id=1, source_target_pairs={{0,8},{2,10},{4,12},{6,14},{8,0},{10,2},{12,4},{14,6},{1,9},{3,11}... | collective-permute-start | bytes 9236 | tf_op jit(solution)/shard_map/ppermute | solution.py:209
  115.7 13.5 %copy-start.5 = (s32[769]{0:T(1024)}, s32[769]{0:T(1024)S(1)}, u32[]{:S(2)}) copy-start(s32[769]{0:T(1024)S(1)} %collective-permute-done.meta) | copy-start | bytes 9232
  118.5 10.7 %copy-start.2 = (bf16[32,4,4096]{2,0,1:T(8,128)(2,1)}, bf16[32,4,4096]{2,0,1:T(8,128)(2,1)S(1)}, u32[]{:S(2)}) copy-start(bf16[32,4,4096]{2,0,1:T(8,128)(2,1)S(1)} %all-to-all-done) | copy-start | bytes 3145732
  139.8 12.4 %copy-start.4 = (f32[32,16,8,8]{0,3,2,1:T(8,128)S(1)}, f32[32,16,8,8]{0,3,2,1:T(8,128)}, u32[]{:S(2)}) copy-start(f32[32,16,8,8]{0,3,2,1:T(8,128)} %param.11) | copy-start | bytes 393220
  142.7 24.3 %all-to-all-start.2 = ((bf16[4,32,4096]{2,1,0:T(8,128)(2,1)}), bf16[4,32,4096]{2,1,0:T(8,128)(2,1)S(1)}, u32[]{:S(2)}, u32[]{:S(2)}) async-start(bf16[4,32,4096]{2,1,0:T(8,128)(2,1)} %bitcast.4), calls=%async_computation.2 | async-start | bytes 2097152 | tf_op jit(solution)/shard_map/all_to_all | solution.py:232
  152.3 44.6 %all-gather.5.cloned.1.call-start = ((), (), s32[]{:S(2)}) async-start(), calls=%async_computation.6 | async-start | bytes 1310720 | tf_op jit(solution)/shard_map/all_gather | solution.py:235
  167.0 1.0 copy-start.1
  203.1 21.7 %all-to-all-start.3 = ((bf16[4,32,4096]{2,1,0:T(8,128)(2,1)}), bf16[4,32,4096]{2,1,0:T(8,128)(2,1)S(1)}, u32[]{:S(2)}, u32[]{:S(2)}) async-start(bf16[4,32,4096]{2,1,0:T(8,128)(2,1)} %bitcast.35), calls=%async_computation.3 | async-start | bytes 2097152 | tf_op jit(solution)/shard_map/all_to_all | solution.py:240
  224.8 21.9 %all-to-all-start.4 = ((bf16[4,32,4096]{2,1,0:T(8,128)(2,1)}), bf16[4,32,4096]{2,1,0:T(8,128)(2,1)S(1)}, u32[]{:S(2)}, u32[]{:S(2)}) async-start(bf16[4,32,4096]{2,1,0:T(8,128)(2,1)} %bitcast.34), calls=%async_computation.4 | async-start | bytes 2097152 | tf_op jit(solution)/shard_map/all_to_all | solution.py:240
Sparse Core Ops, SparseCore 0:
  81.6 47.5 all-gather.2
  172.6 24.2 all-gather.4

commit v2 on v1

v2 whole, which is shorter than its diff:
```python
import functools

import jax
import jax.numpy as jnp
from jax import lax
from jax.experimental import pallas as pl
from jax.experimental.pallas import tpu as pltpu
from jax.sharding import PartitionSpec as P

TILE = 64
PAIR = 2 * TILE
UNROLL = 8
VMEM_LIMIT = 56 * 1024 * 1024


def padded_tile(values, half):
    zero = jnp.zeros_like(values)
    return jnp.concatenate(
        [jnp.where(half == 0, values, zero), jnp.where(half == 1, values, zero)], axis=0
    )


def tile_loop(meta, tiles, ref, offset, base, size, step):
    live = jnp.clip(meta[2 * tiles] - base, 0, size)

    def group(index, carry):
        for lane in range(UNROLL):
            local = index * UNROLL + lane
            segment = meta[base + local]
            block = meta[tiles + base + local]
            half = jnp.where(local < live, segment % 2, 2)
            points = pl.ds(pl.multiple_of((segment // 2) * PAIR, PAIR), PAIR)
            step(block, points, padded_tile(ref[offset + local], half))
        return carry

    lax.fori_loop(0, (live + UNROLL - 1) // UNROLL, group, 0)


def all_tiles(meta, tiles, pieces, step):
    if len(pieces) == 1:
        size = pieces[0].shape[0]
        tile_loop(meta, tiles, pieces[0], 0, pl.program_id(1) * size, size, step)
        return
    for number, ref in enumerate(pieces):
        size = ref.shape[0] // 2

        def share(which, carry, number=number, ref=ref, size=size):
            base = meta[2 * tiles + 1 + 2 * number + which]
            tile_loop(meta, tiles, ref, which * size, base, size, step)
            return carry

        lax.fori_loop(0, 2, share, 0)


def project_kernel(tiles, count, last, meta, wave_ref, *rest):
    pieces, rest = rest[:count], rest[count:]
    total = rest[-1]
    out_ref = rest[-2] if last else None
    proj = pieces[0].shape[2]

    @pl.when(pl.program_id(1) == 0)
    def start():
        if len(rest) == (3 if last else 2):
            total[...] = rest[0][...]
        else:
            total[...] = jnp.zeros_like(total)

    def step(block, points, tile):
        lanes = pl.ds(pl.multiple_of(block * proj, proj), proj)
        term = jnp.dot(wave_ref[:, points], tile, preferred_element_type=jnp.float32)
        total[:, lanes] += term

    all_tiles(meta, tiles, pieces, step)
    if last:

        @pl.when(pl.program_id(1) == pl.num_programs(1) - 1)
        def finish():
            out_ref[...] = total[...].astype(out_ref.dtype)


def spread_kernel(tiles, count, meta, applied_ref, *rest):
    pieces, (out_ref, field) = rest[:count], rest[count:]
    proj = pieces[0].shape[2]

    @pl.when(pl.program_id(1) == 0)
    def start():
        field[...] = jnp.zeros_like(field)

    def step(block, points, tile):
        lanes = pl.ds(pl.multiple_of(block * proj, proj), proj)
        term = lax.dot_general(
            applied_ref[:, lanes],
            tile,
            (((1,), (1,)), ((), ())),
            preferred_element_type=jnp.float32,
        )
        field[:, points] += term

    all_tiles(meta, tiles, pieces, step)

    @pl.when(pl.program_id(1) == pl.num_programs(1) - 1)
    def finish():
        out_ref[...] = field[...].astype(out_ref.dtype)


def row_block(rows):
    return rows if rows <= 256 else 256


def tile_chunk(tiles):
    for chunk in (96, 64, 48, 32, 16, 8):
        if tiles % chunk == 0:
            return chunk
    return tiles


def whole_rows(row, step, meta):
    return (row, 0)


def piece_specs(tiles, pieces):
    if len(pieces) > 1:
        return 1, [pl.BlockSpec(piece.shape, lambda row, step, meta: (0, 0, 0)) for piece in pieces]
    chunk = tile_chunk(tiles)

    def index(row, step, meta):
        last = (meta[2 * tiles] + chunk - 1) // chunk - 1
        return (jnp.clip(step, 0, jnp.maximum(last, 0)), 0, 0)

    return tiles // chunk, [pl.BlockSpec((chunk,) + pieces[0].shape[1:], index)]


def cost(rows, pieces, data):
    size = sum(piece.size for piece in pieces)
    return pl.CostEstimate(flops=2 * rows * size, bytes_accessed=2 * size + data, transcendentals=0)


def project(tiles, meta, wave, pieces, width, total=None, last=False):
    rows, points = wave.shape
    block = row_block(rows)
    steps, specs = piece_specs(tiles, pieces)
    in_specs = [pl.BlockSpec((block, points), whole_rows)] + specs
    operands = [meta, wave] + pieces
    if total is not None:
        in_specs.append(pl.BlockSpec((block, width), whole_rows))
        operands.append(total)
    return pl.pallas_call(
        functools.partial(project_kernel, tiles, len(pieces), last),
        grid_spec=pltpu.PrefetchScalarGridSpec(
            num_scalar_prefetch=1,
            grid=(rows // block, steps),
            in_specs=in_specs,
            out_specs=pl.BlockSpec((block, width), whole_rows),
            scratch_shapes=[pltpu.VMEM((block, width), jnp.float32)] if last else [],
        ),
        out_shape=jax.ShapeDtypeStruct((rows, width), jnp.bfloat16 if last else jnp.float32),
        compiler_params=pltpu.CompilerParams(vmem_limit_bytes=VMEM_LIMIT),
        cost_estimate=cost(rows, pieces, wave.size * 2 + rows * width * 4),
    )(*operands)


def spread(tiles, meta, applied, pieces, points):
    rows, width = applied.shape
    block = row_block(rows)
    steps, specs = piece_specs(tiles, pieces)
    return pl.pallas_call(
        functools.partial(spread_kernel, tiles, len(pieces)),
        grid_spec=pltpu.PrefetchScalarGridSpec(
            num_scalar_prefetch=1,
            grid=(rows // block, steps),
            in_specs=[pl.BlockSpec((block, width), whole_rows)] + specs,
            out_specs=pl.BlockSpec((block, points), whole_rows),
            scratch_shapes=[pltpu.VMEM((block, points), jnp.float32)],
        ),
        out_shape=jax.ShapeDtypeStruct((rows, points), jnp.bfloat16),
        compiler_params=pltpu.CompilerParams(vmem_limit_bytes=VMEM_LIMIT),
        cost_estimate=cost(rows, pieces, applied.size * 2 + rows * points * 2),
    )(meta, applied, *pieces)


def two_parts(values):
    high = values.astype(jnp.bfloat16)
    return high, (values - high.astype(jnp.float32)).astype(jnp.bfloat16)


def couple_kernel(parts_ref, high_ref, low_ref, out_ref):
    blocks, proj, unused = high_ref.shape
    for block in range(blocks):
        lanes = slice(block * proj, (block + 1) * proj)
        total = jnp.sum(parts_ref[:, :, lanes].astype(jnp.float32), axis=0)
        high, low = two_parts(total)
        result = jnp.dot(high, high_ref[block], preferred_element_type=jnp.float32)
        result += jnp.dot(high, low_ref[block], preferred_element_type=jnp.float32)
        result += jnp.dot(low, high_ref[block], preferred_element_type=jnp.float32)
        out_ref[:, lanes] = result.astype(out_ref.dtype)


def couple(parts, matrix):
    count, rows, width = parts.shape
    high, low = two_parts(matrix)
    return pl.pallas_call(
        couple_kernel,
        out_shape=jax.ShapeDtypeStruct((rows, width), jnp.bfloat16),
        compiler_params=pltpu.CompilerParams(vmem_limit_bytes=VMEM_LIMIT),
        cost_estimate=pl.CostEstimate(
            flops=6 * rows * width * matrix.shape[1],
            bytes_accessed=parts.size * 2 + matrix.size * 4,
            transcendentals=0,
        ),
    )(parts, high, low)


def coupling_matrix(coupling):
    blocks, atoms, width, unused = coupling.shape
    proj = atoms * width
    wide = jnp.tile(coupling.reshape(blocks, proj, width), (1, 1, atoms))
    same = jnp.arange(proj)[:, None] // width == jnp.arange(proj)[None, :] // width
    return jnp.where(same[None], wide, 0.0)


def body(n_grid, wavefunctions, tile_segment, tile_block, tile_count, projectors, coupling):
    half = n_grid // 2
    bands, npts = wavefunctions.shape
    points = npts // n_grid
    tiles = projectors.shape[0]
    width = coupling.shape[0] * projectors.shape[2]
    side = lax.axis_index("grid") // half
    group, core = lax.axis_index("groups"), lax.axis_index("band")
    pools = [list(range(half)), list(range(half, n_grid))]
    partners = [(index, (index + half) % n_grid) for index in range(n_grid)]
    swap = [(0, 1), (1, 0)]

    meta = jnp.concatenate([tile_segment, tile_block, tile_count])

    def to_bricks(which):
        part = lax.dynamic_slice_in_dim(wavefunctions, which * half * points, half * points, 1)
        return lax.all_to_all(
            part, "grid", split_axis=1, concat_axis=0, tiled=True, axis_index_groups=pools
        )

    own_wave = to_bricks(side)
    other_wave = to_bricks(1 - side)

    pieces, bases = [], []
    start = 0
    for size in (tiles // 2, tiles // 4, tiles // 4):
        share = size // 4
        quarter = 2 * group + core
        mine = lax.dynamic_slice_in_dim(projectors, start + quarter * share, share, 0)
        mine = lax.ppermute(mine, "grid", partners)
        both = jnp.concatenate([mine, lax.ppermute(mine, "groups", swap)])
        pieces += [both, lax.ppermute(both, "band", swap)]
        for other_core in (core, 1 - core):
            for other_group in (group, 1 - group):
                bases.append(start + (2 * other_group + other_core) * share)
        start += size
    other_meta = lax.ppermute(meta, "grid", partners)
    metas = [jnp.concatenate([other_meta, jnp.stack(bases[i : i + 4])]) for i in (0, 4, 8)]
    other_meta = jnp.concatenate([other_meta, jnp.stack(bases)])

    matrix = coupling_matrix(coupling)

    total = project(tiles, meta, own_wave, [projectors], width)
    total = project(tiles, metas[0], other_wave, pieces[0:2], width, total)
    total = project(tiles, metas[1], other_wave, pieces[2:4], width, total)
    partial = project(tiles, metas[2], other_wave, pieces[4:6], width, total, last=True)

    parts = lax.all_to_all(
        partial.reshape(half, bands, width),
        "grid",
        split_axis=0,
        concat_axis=0,
        tiled=True,
        axis_index_groups=pools,
    )
    applied = couple(parts, matrix)
    applied = lax.all_to_all(
        jnp.broadcast_to(applied[None], (half, bands, width)),
        "grid",
        split_axis=0,
        concat_axis=0,
        tiled=True,
        axis_index_groups=pools,
    ).reshape(half * bands, width)

    def to_bands(field):
        return lax.all_to_all(
            field, "grid", split_axis=0, concat_axis=1, tiled=True, axis_index_groups=pools
        )

    other_field = to_bands(spread(tiles, other_meta, applied, pieces, points))
    own_field = to_bands(spread(tiles, meta, applied, [projectors], points))
    return jnp.where(
        side == 0,
        jnp.concatenate([own_field, other_field], axis=1),
        jnp.concatenate([other_field, own_field], axis=1),
    )


def solution(mesh):
    in_specs = (
        P(("groups", "grid", "band"), None),
        P("grid"),
        P("grid"),
        P("grid"),
        P("grid", None, None),
        P(),
    )
    out_specs = P(("groups", "grid", "band"), None)
    return jax.shard_map(
        functools.partial(body, mesh.shape["grid"]),
        mesh=mesh,
        in_specs=in_specs,
        out_specs=out_specs,
        check_vma=False,
    )
```

time: 258 us -> 238 us (0.922)
  waiting for transfers between devices: 147 us -> 110 us
  local copies, waits for them, and re-layouts: 11.3 us -> 25.3 us
  between operations: 14.2 us -> 0.94 us
  Pallas kernels: 38.1 us -> 49.2 us
  starting transfers between devices: 39.1 us -> 44.9 us
    all_gather x2 -> x0, waiting for transfers between devices: 35.1 us -> none  [the longest x1 24.4 us: body(): lax.all_gather(couple(parts, matrix), 'grid', axis=0, tiled=True, axis_in...]
    all_to_all x2, waiting for transfers between devices: 15 us -> 0.01 us  [to_bricks(): lax.all_to_all(part, 'grid', split_axis=1, concat_axis=0, tiled=True, axi...]
    pallas_call x4 -> x6, Pallas kernels: 33.7 us -> 45.8 us  [the longest x4 26.7 us: project(): pl.pallas_call(functools.partial(project_kernel, tiles, len(pieces), last...]
    all_to_all x1 -> x2, waiting for transfers between devices: 9.58 us -> 20.8 us  [the longest x1 13.2 us: body(): lax.all_to_all(jnp.broadcast_to(applied[None], (half, bands, width)), 'gr...]
    ppermute x1 -> x9, starting transfers between devices: 4.1 us -> 10.6 us  [the longest x3 6.96 us: body(): mine = lax.ppermute(mine, 'grid', partners)]
    concatenate x0 -> x7, local copies, waits for them, and re-layouts: none -> 4.73 us  [the longest x3 2.06 us: body(): both = jnp.concatenate([mine, lax.ppermute(mine, 'groups', swap)])]
    unnamed x20 -> x25, local copies, waits for them, and re-layouts: 2.15 us -> 6.86 us
    all_to_all x1 -> x2, starting transfers between devices: 9.57 us -> 14.2 us  [the longest x1 10.7 us: body(): lax.all_to_all(partial.reshape(half, bands, width), 'grid', split_axis=0,...]
  transfers between devices with their start and end apart: 9 -> 16, of which waited for: 9 -> 10; matrix products, arithmetic and copies ran while one was open for 4% -> 8% of each run, Pallas kernels for 7% -> 13%
where the time goes in v2:
time: 238 us; the launch traced here: 235 us
  waiting for transfers between devices  110 us (46%)
  Pallas kernels  49.2 us (21%)
  starting transfers between devices  44.9 us (19%)
  local copies, waits for them, and re-layouts  25.3 us (11%)
  other arithmetic  4.46 us (2%)
    ppermute x3, waiting for transfers between devices, body(): mine = lax.ppermute(mine, 'grid', partners)  43.3 us
    pallas_call x4, Pallas kernels, project(): pl.pallas_call(functools.partial(project_kernel, tiles, len(pieces), last...  26.7 us
    ppermute x3, waiting for transfers between devices, body(): both = jnp.concatenate([mine, lax.ppermute(mine, 'groups', swap)])  23.2 us
    pallas_call x2, Pallas kernels, spread(): pl.pallas_call(functools.partial(spread_kernel, tiles, len(pieces)), grid...  19.1 us
    all_to_all x2, waiting for transfers between devices, to_bands(): lax.all_to_all(field, 'grid', split_axis=0, concat_axis=1, tiled=True, ax...  18.7 us
    all_to_all x1, waiting for transfers between devices, body(): lax.all_to_all(jnp.broadcast_to(applied[None], (half, bands, width)), 'gr...  13.2 us
    all_to_all x2, starting transfers between devices, to_bands(): lax.all_to_all(field, 'grid', split_axis=0, concat_axis=1, tiled=True, ax...  12.5 us
    all_to_all x1, starting transfers between devices, body(): lax.all_to_all(partial.reshape(half, bands, width), 'grid', split_axis=0,...  10.7 us
  transfers between devices with their start and end apart: 16, of which 10 were waited for; matrix products, arithmetic and copies ran while one was open for 8% of the time, Pallas kernels for 13%

profile of v2, /device:TPU:0, one launch (start us, length us, event | category | flops | bytes accessed | tf_op | source)
XLA Modules:
  0.0 235.2 jit_solution(16568971137674614592)
XLA Ops:
  0.0 2.1 constant_dynamic-slice_fusion.1
  2.1 4.0 %collective-permute-start.7 = (bf16[48,64,128]{2,1,0:T(8,128)(2,1)}, bf16[48,64,128]{2,1,0:T(8,128)(2,1)S(1)}, u32[]{:S(2)}, u32[]{:S(2)}) collective-permute-start(bf16[48,64,128]{2,1,0:T(8,128)(2,1)} %constant_dynamic-slice_fusion.1), channel_id=1, source_target_pairs={{0,8},{2,10},{4,12},{6,14},{8,0},{10,2},{12,4},{14,6},{1,9},{3,11}... | collective-permute-start | bytes 2359304 | tf_op jit(solution)/shard_map/ppermute | solution.py:250
  6.1 1.7 constant_dynamic-slice_fusion
  8.9 3.8 %all-to-all-start.1 = ((bf16[32,4,4096]{2,0,1:T(8,128)(2,1)}), bf16[32,4,4096]{2,0,1:T(8,128)(2,1)S(1)}, u32[]{:S(2)}, u32[]{:S(2)}) async-start(bf16[32,4,4096]{2,0,1:T(8,128)(2,1)} %bitcast.51), calls=%async_computation.1 | async-start | bytes 2097152 | tf_op jit(solution)/shard_map/all_to_all | solution.py:237
  12.7 28.2 %collective-permute-done.7 = bf16[48,64,128]{2,1,0:T(8,128)(2,1)S(1)} collective-permute-done((bf16[48,64,128]{2,1,0:T(8,128)(2,1)}, bf16[48,64,128]{2,1,0:T(8,128)(2,1)S(1)}, u32[]{:S(2)}, u32[]{:S(2)}) %collective-permute-start.7) | collective-permute-done | bytes 786464 | tf_op jit(solution)/shard_map/ppermute | solution.py:250
  42.4 2.1 constant_dynamic-slice_fusion.2
  44.5 2.9 %collective-permute-start.4 = (bf16[24,64,128]{2,1,0:T(8,128)(2,1)}, bf16[24,64,128]{2,1,0:T(8,128)(2,1)}, u32[]{:S(2)}, u32[]{:S(2)}) collective-permute-start(bf16[24,64,128]{2,1,0:T(8,128)(2,1)} %get-tuple-element.5), channel_id=1, source_target_pairs={{0,8},{2,10},{4,12},{6,14},{8,0},{10,2},{12,4},{14,6},{1,9},{3,11}... | collective-permute-start | bytes 1179656 | tf_op jit(solution)/shard_map/ppermute | solution.py:250
  48.5 11.1 %collective-permute-done.8 = bf16[48,64,128]{2,1,0:T(8,128)(2,1)} collective-permute-done((bf16[48,64,128]{2,1,0:T(8,128)(2,1)S(1)}, bf16[48,64,128]{2,1,0:T(8,128)(2,1)}, u32[]{:S(2)}, u32[]{:S(2)}) %collective-permute-start.8) | collective-permute-done | bytes 786464 | tf_op jit(solution)/shard_map/ppermute | solution.py:251
  61.9 3.7 %all-to-all-start = ((bf16[32,4,4096]{2,0,1:T(8,128)(2,1)}), bf16[32,4,4096]{2,0,1:T(8,128)(2,1)S(1)}, u32[]{:S(2)}, u32[]{:S(2)}) async-start(bf16[32,4,4096]{2,0,1:T(8,128)(2,1)} %bitcast.50), calls=%async_computation | async-start | bytes 2097152 | tf_op jit(solution)/shard_map/all_to_all | solution.py:237
  65.6 15.1 %collective-permute-done.4 = bf16[24,64,128]{2,1,0:T(8,128)(2,1)} collective-permute-done((bf16[24,64,128]{2,1,0:T(8,128)(2,1)}, bf16[24,64,128]{2,1,0:T(8,128)(2,1)}, u32[]{:S(2)}, u32[]{:S(2)}) %collective-permute-start.4) | collective-permute-done | bytes 393248 | tf_op jit(solution)/shard_map/ppermute | solution.py:250
  83.8 1.8 constant_dynamic-update-slice_fusion.4
  85.6 7.4 %collective-permute-done.5 = bf16[24,64,128]{2,1,0:T(8,128)(2,1)S(1)} collective-permute-done((bf16[24,64,128]{2,1,0:T(8,128)(2,1)}, bf16[24,64,128]{2,1,0:T(8,128)(2,1)S(1)}, u32[]{:S(2)}, u32[]{:S(2)}) %collective-permute-start.5) | collective-permute-done | bytes 393248 | tf_op jit(solution)/shard_map/ppermute | solution.py:251
  93.7 4.7 %collective-permute-done.2 = bf16[24,64,128]{2,1,0:T(8,128)(2,1)S(1)} collective-permute-done((bf16[24,64,128]{2,1,0:T(8,128)(2,1)}, bf16[24,64,128]{2,1,0:T(8,128)(2,1)S(1)}, u32[]{:S(2)}, u32[]{:S(2)}) %collective-permute-start.2) | collective-permute-done | bytes 393248 | tf_op jit(solution)/shard_map/ppermute | solution.py:251
  99.4 4.5 %collective-permute-done = s32[769]{0:T(1024)S(1)} collective-permute-done((s32[769]{0:T(1024)S(1)}, s32[769]{0:T(1024)S(1)}, u32[]{:S(2)}, u32[]{:S(2)}) %collective-permute-start) | collective-permute-done | bytes 3108 | tf_op jit(solution)/shard_map/ppermute | solution.py:257
  105.9 7.3 %shard_map.64.rest_2_ = f32[128,4096]{1,0:T(8,128)} custom-call(s32[769]{0:T(1024)} %copy-done.7, bf16[128,4096]{1,0:T(8,128)(2,1)} %bitcast.44, bf16[384,64,128]{2,1,0:T(8,128)(2,1)} %rest_0_.3), custom_call_target="tpu_custom_call" | custom-call | flops 805306368 | bytes 9437184 | tf_op jit(solution)/shard_map/pallas_call | solution.py:147
  114.2 10.4 %shard_map.65.rest_2_ = f32[128,4096]{1,0:T(8,128)} custom-call(s32[773]{0:T(1024)} %concatenate.35.meta, bf16[128,4096]{1,0:T(8,128)(2,1)} %bitcast.39, bf16[96,64,128]{2,1,0:T(8,128)(2,1)} %copy-done.1, bf16[96,64,128]{2,1,0:T(8,128)(2,1)} %collective-permute-done.9.rest_1_, f32[128,4096]{1,0:T(8,128)} %shard_map.64.rest_2_), custom_call_target="tpu_custom_call" | custom-call | flops 402653184 | bytes 6291456 | tf_op jit(solution)/shard_map/pallas_call | solution.py:147
  124.6 4.6 %shard_map.66.rest_2_ = f32[128,4096]{1,0:T(8,128)} custom-call(s32[773]{0:T(1024)} %concatenate.33.meta, bf16[128,4096]{1,0:T(8,128)(2,1)} %bitcast.40, bf16[48,64,128]{2,1,0:T(8,128)(2,1)} %constant_dynamic-update-slice_fusion.3.rest_0_.rest_2_, bf16[48,64,128]{2,1,0:T(8,128)(2,1)} %collective-permute-done.6.rest_1_.rest_3_, f32[128,4096]{1,0:T(8,128)} %shard_map.65.rest_2_), custom_call_target="tpu_custom_call" | custom-call | flops 201326592 | bytes 4718592 | tf_op jit(solution)/shard_map/pallas_call | solution.py:147
  129.2 4.4 %shard_map.67 = bf16[128,4096]{1,0:T(8,128)(2,1)} custom-call(s32[773]{0:T(1024)} %concatenate.31.meta, bf16[128,4096]{1,0:T(8,128)(2,1)} %bitcast.41, bf16[48,64,128]{2,1,0:T(8,128)(2,1)} %copy-done.3, bf16[48,64,128]{2,1,0:T(8,128)(2,1)} %collective-permute-done.3.rest_1_.rest_5_, f32[128,4096]{1,0:T(8,128)} %shard_map.66.rest_2_), custom_call_target="tpu_custom_call" | custom-call | flops 201326592 | bytes 4718592 | tf_op jit(solution)/shard_map/pallas_call | solution.py:147
  133.6 10.7 %all-to-all-start.2 = ((bf16[4,32,4096]{2,1,0:T(8,128)(2,1)}), bf16[4,32,4096]{2,1,0:T(8,128)(2,1)S(1)}, u32[]{:S(2)}, u32[]{:S(2)}) async-start(bf16[4,32,4096]{2,1,0:T(8,128)(2,1)} %bitcast.46), calls=%async_computation.2 | async-start | bytes 2097152 | tf_op jit(solution)/shard_map/all_to_all | solution.py:268
  145.9 1.9 copy.19
  150.5 7.6 %all-to-all-done.2.parts_ref = bf16[4,32,4096]{2,1,0:T(8,128)(2,1)S(1)} async-done(((bf16[4,32,4096]{2,1,0:T(8,128)(2,1)}), bf16[4,32,4096]{2,1,0:T(8,128)(2,1)S(1)}, u32[]{:S(2)}, u32[]{:S(2)}) %all-to-all-start.2) | async-done | bytes 1048608 | tf_op jit(solution)/shard_map/all_to_all | solution.py:268
  159.1 3.5 %shard_map.68 = bf16[32,4096]{1,0:T(8,128)(2,1)} custom-call(bf16[4,32,4096]{2,1,0:T(8,128)(2,1)} %copy-done.5, bf16[32,128,128]{2,1,0:T(8,128)(2,1)} %select_convert_fusion.high_ref, bf16[32,128,128]{2,1,0:T(8,128)(2,1)} %subtract_convert_fusion.low_ref), custom_call_target="tpu_custom_call" | custom-call | flops 100663296 | bytes 3145728 | tf_op jit(solution)/shard_map/pallas_call | solution.py:201
  162.5 2.0 broadcast_in_dim.23
  164.6 3.5 %all-to-all-start.3 = ((bf16[4,32,4096]{2,1,0:T(8,128)(2,1)}), bf16[4,32,4096]{2,1,0:T(8,128)(2,1)S(1)}, u32[]{:S(2)}, u32[]{:S(2)}) async-start(bf16[4,32,4096]{2,1,0:T(8,128)(2,1)} %broadcast_in_dim.23), calls=%async_computation.3 | async-start | bytes 2097152 | tf_op jit(solution)/shard_map/all_to_all | solution.py:277
  168.8 13.2 %all-to-all-done.3 = bf16[4,32,4096]{2,1,0:T(8,128)(2,1)S(1)} async-done(((bf16[4,32,4096]{2,1,0:T(8,128)(2,1)}), bf16[4,32,4096]{2,1,0:T(8,128)(2,1)S(1)}, u32[]{:S(2)}, u32[]{:S(2)}) %all-to-all-start.3) | async-done | bytes 1048608 | tf_op jit(solution)/shard_map/all_to_all | solution.py:277
  183.0 11.5 %shard_map.70 = bf16[128,4096]{1,0:T(8,128)(2,1)} custom-call(s32[781]{0:T(1024)} %concatenate.37.meta, bf16[128,4096]{1,0:T(8,128)(2,1)} %bitcast.42, bf16[96,64,128]{2,1,0:T(8,128)(2,1)} %copy-done.1, bf16[96,64,128]{2,1,0:T(8,128)(2,1)} %collective-permute-done.9.rest_1_, bf16[48,64,128]{2,1,0:T(8,128)(2,1)} %constant_dynamic-update-slice_fusion.3.rest_0_.rest_2_, ...), custom_call_target="tpu_custom_call" | custom-call | flops 805306368 | bytes 8388608 | tf_op jit(solution)/shard_map/pallas_call | solution.py:166
  194.5 3.5 %all-to-all-start.5 = ((bf16[4,32,4096]{2,1,0:T(8,128)(2,1)}), bf16[4,32,4096]{2,1,0:T(8,128)(2,1)S(1)}, u32[]{:S(2)}, u32[]{:S(2)}) async-start(bf16[4,32,4096]{2,1,0:T(8,128)(2,1)} %bitcast.55), calls=%async_computation.5 | async-start | bytes 2097152 | tf_op jit(solution)/shard_map/all_to_all | solution.py:287
  198.0 7.6 %shard_map.69 = bf16[128,4096]{1,0:T(8,128)(2,1)} custom-call(s32[769]{0:T(1024)} %copy-done.7, bf16[128,4096]{1,0:T(8,128)(2,1)} %bitcast.43, bf16[384,64,128]{2,1,0:T(8,128)(2,1)} %rest_0_.3), custom_call_target="tpu_custom_call" | custom-call | flops 805306368 | bytes 8388608 | tf_op jit(solution)/shard_map/pallas_call | solution.py:166
  205.6 5.5 %all-to-all-done.5 = bf16[4,32,4096]{2,1,0:T(8,128)(2,1)S(1)} async-done(((bf16[4,32,4096]{2,1,0:T(8,128)(2,1)}), bf16[4,32,4096]{2,1,0:T(8,128)(2,1)S(1)}, u32[]{:S(2)}, u32[]{:S(2)}) %all-to-all-start.5) | async-done | bytes 1048608 | tf_op jit(solution)/shard_map/all_to_all | solution.py:287
  211.1 8.9 %all-to-all-start.4 = ((bf16[4,32,4096]{2,1,0:T(8,128)(2,1)}), bf16[4,32,4096]{2,1,0:T(8,128)(2,1)S(1)}, u32[]{:S(2)}, u32[]{:S(2)}) async-start(bf16[4,32,4096]{2,1,0:T(8,128)(2,1)} %bitcast.54), calls=%async_computation.4 | async-start | bytes 2097152 | tf_op jit(solution)/shard_map/all_to_all | solution.py:287
  220.1 13.2 %all-to-all-done.4 = bf16[4,32,4096]{2,1,0:T(8,128)(2,1)S(1)} async-done(((bf16[4,32,4096]{2,1,0:T(8,128)(2,1)}), bf16[4,32,4096]{2,1,0:T(8,128)(2,1)S(1)}, u32[]{:S(2)}, u32[]{:S(2)}) %all-to-all-start.4) | async-done | bytes 1048608 | tf_op jit(solution)/shard_map/all_to_all | solution.py:287
  233.4 1.8 maximum_select_fusion
  (57 shorter events, 20.1 us)
Async XLA Ops:
  2.1 38.7 %collective-permute-start.7 = (bf16[48,64,128]{2,1,0:T(8,128)(2,1)}, bf16[48,64,128]{2,1,0:T(8,128)(2,1)S(1)}, u32[]{:S(2)}, u32[]{:S(2)}) collective-permute-start(bf16[48,64,128]{2,1,0:T(8,128)(2,1)} %constant_dynamic-slice_fusion.1), channel_id=1, source_target_pairs={{0,8},{2,10},{4,12},{6,14},{8,0},{10,2},{12,4},{14,6},{1,9},{3,11}... | collective-permute-start | bytes 2359304 | tf_op jit(solution)/shard_map/ppermute | solution.py:250
  8.9 52.0 %all-to-all-start.1 = ((bf16[32,4,4096]{2,0,1:T(8,128)(2,1)}), bf16[32,4,4096]{2,0,1:T(8,128)(2,1)S(1)}, u32[]{:S(2)}, u32[]{:S(2)}) async-start(bf16[32,4,4096]{2,0,1:T(8,128)(2,1)} %bitcast.51), calls=%async_computation.1 | async-start | bytes 2097152 | tf_op jit(solution)/shard_map/all_to_all | solution.py:237
  40.8 18.8 %collective-permute-start.8 = (bf16[48,64,128]{2,1,0:T(8,128)(2,1)S(1)}, bf16[48,64,128]{2,1,0:T(8,128)(2,1)}, u32[]{:S(2)}, u32[]{:S(2)}) collective-permute-start(bf16[48,64,128]{2,1,0:T(8,128)(2,1)S(1)} %collective-permute-done.7), channel_id=1, source_target_pairs={{0,16},{16,0},{1,17},{17,1},{2,18},{18,2},{3,19},{19,3},{4,20},{20... | collective-permute-start | bytes 2359304 | tf_op jit(solution)/shard_map/ppermute | solution.py:251
  44.4 37.0 %collective-permute-start.1 = (bf16[24,64,128]{2,1,0:T(8,128)(2,1)}, bf16[24,64,128]{2,1,0:T(8,128)(2,1)}, u32[]{:S(2)}, u32[]{:S(2)}) collective-permute-start(bf16[24,64,128]{2,1,0:T(8,128)(2,1)} %get-tuple-element.6), channel_id=1, source_target_pairs={{0,8},{2,10},{4,12},{6,14},{8,0},{10,2},{12,4},{14,6},{1,9},{3,11}... | collective-permute-start | bytes 1179656 | tf_op jit(solution)/shard_map/ppermute | solution.py:250
  44.5 36.3 %collective-permute-start.4 = (bf16[24,64,128]{2,1,0:T(8,128)(2,1)}, bf16[24,64,128]{2,1,0:T(8,128)(2,1)}, u32[]{:S(2)}, u32[]{:S(2)}) collective-permute-start(bf16[24,64,128]{2,1,0:T(8,128)(2,1)} %get-tuple-element.5), channel_id=1, source_target_pairs={{0,8},{2,10},{4,12},{6,14},{8,0},{10,2},{12,4},{14,6},{1,9},{3,11}... | collective-permute-start | bytes 1179656 | tf_op jit(solution)/shard_map/ppermute | solution.py:250
  60.8 32.9 %copy-start.1 = (bf16[96,64,128]{2,1,0:T(8,128)(2,1)}, bf16[96,64,128]{2,1,0:T(8,128)(2,1)S(1)}, u32[]{:S(2)}) copy-start(bf16[96,64,128]{2,1,0:T(8,128)(2,1)S(1)} %constant_dynamic-update-slice_fusion.5.rest_0_) | copy-start | bytes 4718596
  60.9 1.0 copy-start.4
  61.9 51.3 %all-to-all-start = ((bf16[32,4,4096]{2,0,1:T(8,128)(2,1)}), bf16[32,4,4096]{2,0,1:T(8,128)(2,1)S(1)}, u32[]{:S(2)}, u32[]{:S(2)}) async-start(bf16[32,4,4096]{2,0,1:T(8,128)(2,1)} %bitcast.50), calls=%async_computation | async-start | bytes 2097152 | tf_op jit(solution)/shard_map/all_to_all | solution.py:237
  65.6 33.6 %copy-start.8 = (s32[384]{0:T(512)S(1)}, s32[384]{0:T(512)}, u32[]{:S(2)}) copy-start(s32[384]{0:T(512)} %param.7) | copy-start | bytes 4612
  65.6 33.7 %copy-start.9 = (s32[384]{0:T(512)S(1)}, s32[384]{0:T(512)}, u32[]{:S(2)}) copy-start(s32[384]{0:T(512)} %param.8) | copy-start | bytes 4612
  65.6 47.6 %collective-permute-start.9 = (bf16[96,64,128]{2,1,0:T(8,128)(2,1)S(1)}, bf16[96,64,128]{2,1,0:T(8,128)(2,1)}, u32[]{:S(2)}, u32[]{:S(2)}) collective-permute-start(bf16[96,64,128]{2,1,0:T(8,128)(2,1)S(1)} %constant_dynamic-update-slice_fusion.5.rest_0_), channel_id=1, source_target_pairs={{0,1},{1,0},{2,3},{3,2},{4,5},{5,4},{6,7},{7,6},{8,9},{9,8},{10,11... | collective-permute-start | bytes 4718600 | tf_op jit(solution)/shard_map/ppermute | solution.py:252
  80.7 12.3 %collective-permute-start.5 = (bf16[24,64,128]{2,1,0:T(8,128)(2,1)}, bf16[24,64,128]{2,1,0:T(8,128)(2,1)S(1)}, u32[]{:S(2)}, u32[]{:S(2)}) collective-permute-start(bf16[24,64,128]{2,1,0:T(8,128)(2,1)} %collective-permute-done.4), channel_id=1, source_target_pairs={{0,16},{16,0},{1,17},{17,1},{2,18},{18,2},{3,19},{19,3},{4,20},{20... | collective-permute-start | bytes 1179656 | tf_op jit(solution)/shard_map/ppermute | solution.py:251
  81.5 16.9 %collective-permute-start.2 = (bf16[24,64,128]{2,1,0:T(8,128)(2,1)}, bf16[24,64,128]{2,1,0:T(8,128)(2,1)S(1)}, u32[]{:S(2)}, u32[]{:S(2)}) collective-permute-start(bf16[24,64,128]{2,1,0:T(8,128)(2,1)} %collective-permute-done.1), channel_id=1, source_target_pairs={{0,16},{16,0},{1,17},{17,1},{2,18},{18,2},{3,19},{19,3},{4,20},{20... | collective-permute-start | bytes 1179656 | tf_op jit(solution)/shard_map/ppermute | solution.py:251
  93.7 30.8 %collective-permute-start.6 = (bf16[48,64,128]{2,1,0:T(8,128)(2,1)}, bf16[48,64,128]{2,1,0:T(8,128)(2,1)}, u32[]{:S(2)}, u32[]{:S(2)}) collective-permute-start(bf16[48,64,128]{2,1,0:T(8,128)(2,1)} %constant_dynamic-update-slice_fusion.3.rest_0_.rest_2_), channel_id=1, source_target_pairs={{0,1},{1,0},{2,3},{3,2},{4,5},{5,4},{6,7},{7,6},{8,9},{9,8},{10,11... | collective-permute-start | bytes 2359304 | tf_op jit(solution)/shard_map/ppermute | solution.py:252
  98.5 14.7 %copy-start.3 = (bf16[48,64,128]{2,1,0:T(8,128)(2,1)}, bf16[48,64,128]{2,1,0:T(8,128)(2,1)S(1)}, u32[]{:S(2)}) copy-start(bf16[48,64,128]{2,1,0:T(8,128)(2,1)S(1)} %constant_dynamic-update-slice_fusion.1.rest_0_.rest_4_) | copy-start | bytes 2359300
  98.5 30.7 %collective-permute-start.3 = (bf16[48,64,128]{2,1,0:T(8,128)(2,1)S(1)}, bf16[48,64,128]{2,1,0:T(8,128)(2,1)}, u32[]{:S(2)}, u32[]{:S(2)}) collective-permute-start(bf16[48,64,128]{2,1,0:T(8,128)(2,1)S(1)} %constant_dynamic-update-slice_fusion.1.rest_0_.rest_4_), channel_id=1, source_target_pairs={{0,1},{1,0},{2,3},{3,2},{4,5},{5,4},{6,7},{7,6},{8,9},{9,8},{10,11... | collective-permute-start | bytes 2359304 | tf_op jit(solution)/shard_map/ppermute | solution.py:252
  99.3 6.6 %copy-start.7 = (s32[769]{0:T(1024)}, s32[769]{0:T(1024)S(1)}, u32[]{:S(2)}) copy-start(s32[769]{0:T(1024)S(1)} %constant_dynamic-update-slice_fusion.7.meta) | copy-start | bytes 9232
  99.3 4.6 %collective-permute-start = (s32[769]{0:T(1024)S(1)}, s32[769]{0:T(1024)S(1)}, u32[]{:S(2)}, u32[]{:S(2)}) collective-permute-start(s32[769]{0:T(1024)S(1)} %constant_dynamic-update-slice_fusion.7.meta), channel_id=1, source_target_pairs={{0,8},{2,10},{4,12},{6,14},{8,0},{10,2},{12,4},{14,6},{1,9},{3,11}... | collective-permute-start | bytes 9236 | tf_op jit(solution)/shard_map/ppermute | solution.py:257
  113.2 1.0 copy-start
  133.6 10.7 %copy-start.6 = (f32[32,16,8,8]{0,3,2,1:T(8,128)S(1)}, f32[32,16,8,8]{0,3,2,1:T(8,128)}, u32[]{:S(2)}) copy-start(f32[32,16,8,8]{0,3,2,1:T(8,128)} %param.11) | copy-start | bytes 393220
  133.6 24.5 %all-to-all-start.2 = ((bf16[4,32,4096]{2,1,0:T(8,128)(2,1)}), bf16[4,32,4096]{2,1,0:T(8,128)(2,1)S(1)}, u32[]{:S(2)}, u32[]{:S(2)}) async-start(bf16[4,32,4096]{2,1,0:T(8,128)(2,1)} %bitcast.46), calls=%async_computation.2 | async-start | bytes 2097152 | tf_op jit(solution)/shard_map/all_to_all | solution.py:268
  158.1 1.0 copy-start.5
  164.6 17.4 %all-to-all-start.3 = ((bf16[4,32,4096]{2,1,0:T(8,128)(2,1)}), bf16[4,32,4096]{2,1,0:T(8,128)(2,1)S(1)}, u32[]{:S(2)}, u32[]{:S(2)}) async-start(bf16[4,32,4096]{2,1,0:T(8,128)(2,1)} %broadcast_in_dim.23), calls=%async_computation.3 | async-start | bytes 2097152 | tf_op jit(solution)/shard_map/all_to_all | solution.py:277
  182.0 1.0 copy-start.2
  194.5 16.6 %all-to-all-start.5 = ((bf16[4,32,4096]{2,1,0:T(8,128)(2,1)}), bf16[4,32,4096]{2,1,0:T(8,128)(2,1)S(1)}, u32[]{:S(2)}, u32[]{:S(2)}) async-start(bf16[4,32,4096]{2,1,0:T(8,128)(2,1)} %bitcast.55), calls=%async_computation.5 | async-start | bytes 2097152 | tf_op jit(solution)/shard_map/all_to_all | solution.py:287
  211.1 22.2 %all-to-all-start.4 = ((bf16[4,32,4096]{2,1,0:T(8,128)(2,1)}), bf16[4,32,4096]{2,1,0:T(8,128)(2,1)S(1)}, u32[]{:S(2)}, u32[]{:S(2)}) async-start(bf16[4,32,4096]{2,1,0:T(8,128)(2,1)} %bitcast.54), calls=%async_computation.4 | async-start | bytes 2097152 | tf_op jit(solution)/shard_map/all_to_all | solution.py:287

commit v3 on v2

--- a/solution.py
+++ b/solution.py
@@ -10,7 +10,7 @@
 TILE = 64
 PAIR = 2 * TILE
 UNROLL = 8
-VMEM_LIMIT = 56 * 1024 * 1024
+VMEM_LIMIT = 24 * 1024 * 1024
 
 
 def padded_tile(values, half):
@@ -20,17 +20,27 @@
     )
 
 
+def diagonal(first, second):
+    zero = jnp.zeros_like(first)
+    return jnp.concatenate(
+        [jnp.concatenate([first, zero], axis=1), jnp.concatenate([zero, second], axis=1)], axis=0
+    )
+
+
 def tile_loop(meta, tiles, ref, offset, base, size, step):
     live = jnp.clip(meta[2 * tiles] - base, 0, size)
 
     def group(index, carry):
-        for lane in range(UNROLL):
-            local = index * UNROLL + lane
-            segment = meta[base + local]
-            block = meta[tiles + base + local]
-            half = jnp.where(local < live, segment % 2, 2)
-            points = pl.ds(pl.multiple_of((segment // 2) * PAIR, PAIR), PAIR)
-            step(block, points, padded_tile(ref[offset + local], half))
+        for pair in range(0, UNROLL, 2):
+            places = []
+            for lane in (pair, pair + 1):
+                local = index * UNROLL + lane
+                segment = meta[base + local]
+                block = meta[tiles + base + local]
+                half = jnp.where(local < live, segment % 2, 2)
+                points = pl.ds(pl.multiple_of((segment // 2) * PAIR, PAIR), PAIR)
+                places.append((block, points, padded_tile(ref[offset + local], half)))
+            step(*places)
         return carry
 
     lax.fori_loop(0, (live + UNROLL - 1) // UNROLL, group, 0)
@@ -39,7 +49,7 @@
 def all_tiles(meta, tiles, pieces, step):
     if len(pieces) == 1:
         size = pieces[0].shape[0]
-        tile_loop(meta, tiles, pieces[0], 0, pl.program_id(1) * size, size, step)
+        tile_loop(meta, tiles, pieces[0], 0, pl.program_id(0) * size, size, step)
         return
     for number, ref in enumerate(pieces):
         size = ref.shape[0] // 2
@@ -58,22 +68,24 @@
     out_ref = rest[-2] if last else None
     proj = pieces[0].shape[2]
 
-    @pl.when(pl.program_id(1) == 0)
+    @pl.when(pl.program_id(0) == 0)
     def start():
         if len(rest) == (3 if last else 2):
             total[...] = rest[0][...]
         else:
             total[...] = jnp.zeros_like(total)
 
-    def step(block, points, tile):
-        lanes = pl.ds(pl.multiple_of(block * proj, proj), proj)
-        term = jnp.dot(wave_ref[:, points], tile, preferred_element_type=jnp.float32)
-        total[:, lanes] += term
+    def step(first, second):
+        waves = jnp.concatenate([wave_ref[:, first[1]], wave_ref[:, second[1]]], axis=1)
+        terms = jnp.dot(waves, diagonal(first[2], second[2]), preferred_element_type=jnp.float32)
+        for index, place in enumerate((first, second)):
+            lanes = pl.ds(pl.multiple_of(place[0] * proj, proj), proj)
+            total[:, lanes] += terms[:, index * proj : (index + 1) * proj]
 
     all_tiles(meta, tiles, pieces, step)
     if last:
 
-        @pl.when(pl.program_id(1) == pl.num_programs(1) - 1)
+        @pl.when(pl.program_id(0) == pl.num_programs(0) - 1)
         def finish():
             out_ref[...] = total[...].astype(out_ref.dtype)
 
@@ -82,29 +94,26 @@
     pieces, (out_ref, field) = rest[:count], rest[count:]
     proj = pieces[0].shape[2]
 
-    @pl.when(pl.program_id(1) == 0)
+    @pl.when(pl.program_id(0) == 0)
     def start():
         field[...] = jnp.zeros_like(field)
 
-    def step(block, points, tile):
-        lanes = pl.ds(pl.multiple_of(block * proj, proj), proj)
-        term = lax.dot_general(
-            applied_ref[:, lanes],
-            tile,
+    def step(first, second):
+        lanes = [pl.ds(pl.multiple_of(place[0] * proj, proj), proj) for place in (first, second)]
+        terms = lax.dot_general(
+            jnp.concatenate([applied_ref[:, lanes[0]], applied_ref[:, lanes[1]]], axis=1),
+            diagonal(first[2], second[2]),
             (((1,), (1,)), ((), ())),
             preferred_element_type=jnp.float32,
         )
-        field[:, points] += term
+        for index, place in enumerate((first, second)):
+            field[:, place[1]] += terms[:, index * PAIR : (index + 1) * PAIR]
 
     all_tiles(meta, tiles, pieces, step)
 
-    @pl.when(pl.program_id(1) == pl.num_programs(1) - 1)
+    @pl.when(pl.program_id(0) == pl.num_programs(0) - 1)
     def finish():
         out_ref[...] = field[...].astype(out_ref.dtype)
-
-
-def row_block(rows):
-    return rows if rows <= 256 else 256
 
 
 def tile_chunk(tiles):
@@ -114,67 +123,62 @@
     return tiles
 
 
-def whole_rows(row, step, meta):
-    return (row, 0)
+WHOLE = pl.BlockSpec(memory_space=pltpu.VMEM)
 
 
 def piece_specs(tiles, pieces):
     if len(pieces) > 1:
-        return 1, [pl.BlockSpec(piece.shape, lambda row, step, meta: (0, 0, 0)) for piece in pieces]
+        return 1, [WHOLE] * len(pieces)
     chunk = tile_chunk(tiles)
 
-    def index(row, step, meta):
+    def index(step, meta):
         last = (meta[2 * tiles] + chunk - 1) // chunk - 1
         return (jnp.clip(step, 0, jnp.maximum(last, 0)), 0, 0)
 
     return tiles // chunk, [pl.BlockSpec((chunk,) + pieces[0].shape[1:], index)]
 
 
-def cost(rows, pieces, data):
-    size = sum(piece.size for piece in pieces)
-    return pl.CostEstimate(flops=2 * rows * size, bytes_accessed=2 * size + data, transcendentals=0)
+COST = pl.CostEstimate(flops=1, bytes_accessed=1, transcendentals=0)
 
 
 def project(tiles, meta, wave, pieces, width, total=None, last=False):
     rows, points = wave.shape
-    block = row_block(rows)
     steps, specs = piece_specs(tiles, pieces)
-    in_specs = [pl.BlockSpec((block, points), whole_rows)] + specs
+    in_specs = [WHOLE] + specs
     operands = [meta, wave] + pieces
     if total is not None:
-        in_specs.append(pl.BlockSpec((block, width), whole_rows))
+        in_specs.append(WHOLE)
         operands.append(total)
     return pl.pallas_call(
         functools.partial(project_kernel, tiles, len(pieces), last),
         grid_spec=pltpu.PrefetchScalarGridSpec(
             num_scalar_prefetch=1,
-            grid=(rows // block, steps),
+            grid=(steps,),
             in_specs=in_specs,
-            out_specs=pl.BlockSpec((block, width), whole_rows),
-            scratch_shapes=[pltpu.VMEM((block, width), jnp.float32)] if last else [],
+            out_specs=WHOLE,
+            scratch_shapes=[pltpu.VMEM((rows, width), jnp.float32)] if last else [],
         ),
         out_shape=jax.ShapeDtypeStruct((rows, width), jnp.bfloat16 if last else jnp.float32),
         compiler_params=pltpu.CompilerParams(vmem_limit_bytes=VMEM_LIMIT),
-        cost_estimate=cost(rows, pieces, wave.size * 2 + rows * width * 4),
+        cost_estimate=COST,
     )(*operands)
 
 
 def spread(tiles, meta, applied, pieces, points):
     rows, width = applied.shape
-    block = row_block(rows)
     steps, specs = piece_specs(tiles, pieces)
     return pl.pallas_call(
         functools.partial(spread_kernel, tiles, len(pieces)),
         grid_spec=pltpu.PrefetchScalarGridSpec(
             num_scalar_prefetch=1,
-            grid=(rows // block, steps),
-            in_specs=[pl.BlockSpec((block, width), whole_rows)] + specs,
-            out_specs=pl.BlockSpec((block, points), whole_rows),
-            scratch_shapes=[pltpu.VMEM((block, points), jnp.float32)],
+            grid=(steps,),
+            in_specs=[WHOLE] + specs,
+            out_specs=WHOLE,
+            scratch_shapes=[pltpu.VMEM((rows, points), jnp.float32)],
         ),
         out_shape=jax.ShapeDtypeStruct((rows, points), jnp.bfloat16),
         compiler_params=pltpu.CompilerParams(vmem_limit_bytes=VMEM_LIMIT),
-        cost_estimate=cost(rows, pieces, applied.size * 2 + rows * points * 2),
+        cost_estimate=COST,
     )(meta, applied, *pieces)
 
 
@@ -200,13 +204,11 @@
     high, low = two_parts(matrix)
     return pl.pallas_call(
         couple_kernel,
+        in_specs=[WHOLE] * 3,
+        out_specs=WHOLE,
         out_shape=jax.ShapeDtypeStruct((rows, width), jnp.bfloat16),
         compiler_params=pltpu.CompilerParams(vmem_limit_bytes=VMEM_LIMIT),
-        cost_estimate=pl.CostEstimate(
-            flops=6 * rows * width * matrix.shape[1],
-            bytes_accessed=parts.size * 2 + matrix.size * 4,
-            transcendentals=0,
-        ),
+        cost_estimate=COST,
     )(parts, high, low)
 
 
@@ -241,6 +243,8 @@
     own_wave = to_bricks(side)
     other_wave = to_bricks(1 - side)
 
+    total = project(tiles, meta, own_wave, [projectors], width)
+
     pieces, bases = [], []
     start = 0
     for size in (tiles // 2, tiles // 4, tiles // 4):
@@ -248,6 +252,8 @@
         quarter = 2 * group + core
         mine = lax.dynamic_slice_in_dim(projectors, start + quarter * share, share, 0)
         mine = lax.ppermute(mine, "grid", partners)
+        if start == 0:
+            mine, total = lax.optimization_barrier((mine, total))
         both = jnp.concatenate([mine, lax.ppermute(mine, "groups", swap)])
         pieces += [both, lax.ppermute(both, "band", swap)]
         for other_core in (core, 1 - core):
@@ -260,7 +266,6 @@
 
     matrix = coupling_matrix(coupling)
 
-    total = project(tiles, meta, own_wave, [projectors], width)
     total = project(tiles, metas[0], other_wave, pieces[0:2], width, total)
     total = project(tiles, metas[1], other_wave, pieces[2:4], width, total)
     partial = project(tiles, metas[2], other_wave, pieces[4:6], width, total, last=True)

time: 238 us -> 230 us (0.966)
  Pallas kernels: 49.2 us -> 27.1 us
  starting transfers between devices: 44.9 us -> 56.8 us
  local copies, waits for them, and re-layouts: 25.3 us -> 31.2 us
  waiting for transfers between devices: 110 us -> 106 us
    all_to_all x2, waiting for transfers between devices: 0.01 us -> 18.6 us  [to_bricks(): lax.all_to_all(part, 'grid', split_axis=1, concat_axis=0, tiled=True, axi...]
    ppermute x3, waiting for transfers between devices: 43.3 us -> 29.1 us  [body(): mine = lax.ppermute(mine, 'grid', partners)]
    pallas_call x4, Pallas kernels: 26.7 us -> 13.5 us  [project(): pl.pallas_call(functools.partial(project_kernel, tiles, len(pieces), last...]
    all_to_all x2, starting transfers between devices: 12.5 us -> 20.4 us  [to_bands(): lax.all_to_all(field, 'grid', split_axis=0, concat_axis=1, tiled=True, ax...]
    unnamed x25 -> x27, local copies, waits for them, and re-layouts: 6.86 us -> 13.7 us
    pallas_call x2, Pallas kernels: 19.1 us -> 12.7 us  [spread(): pl.pallas_call(functools.partial(spread_kernel, tiles, len(pieces)), grid...]
    all_to_all x1, waiting for transfers between devices: 7.58 us -> 3.41 us  [body(): lax.all_to_all(partial.reshape(half, bands, width), 'grid', split_axis=0,...]
    all_to_all x1, starting transfers between devices: 10.7 us -> 14.5 us  [body(): lax.all_to_all(partial.reshape(half, bands, width), 'grid', split_axis=0,...]
  transfers between devices with their start and end apart: 16 -> 16, of which waited for: 10 -> 11; matrix products, arithmetic and copies ran while one was open for 8% -> 8% of each run, Pallas kernels for 13% -> 8%
where the time goes in v3:
time: 230 us; the launch traced here: 229 us
  waiting for transfers between devices  106 us (46%)
  starting transfers between devices  56.8 us (25%)
  local copies, waits for them, and re-layouts  31.2 us (14%)
  Pallas kernels  27.1 us (12%)
  other arithmetic  6.17 us (3%)
    ppermute x3, waiting for transfers between devices, body(): mine = lax.ppermute(mine, 'grid', partners)  29.1 us
    ppermute x3, waiting for transfers between devices, body(): both = jnp.concatenate([mine, lax.ppermute(mine, 'groups', swap)])  21.2 us
    all_to_all x2, starting transfers between devices, to_bands(): lax.all_to_all(field, 'grid', split_axis=0, concat_axis=1, tiled=True, ax...  20.4 us
    all_to_all x2, waiting for transfers between devices, to_bricks(): lax.all_to_all(part, 'grid', split_axis=1, concat_axis=0, tiled=True, axi...  18.6 us
    all_to_all x2, waiting for transfers between devices, to_bands(): lax.all_to_all(field, 'grid', split_axis=0, concat_axis=1, tiled=True, ax...  16 us
    all_to_all x1, starting transfers between devices, body(): lax.all_to_all(partial.reshape(half, bands, width), 'grid', split_axis=0,...  14.5 us
    unnamed x27, local copies, waits for them, and re-layouts  13.7 us
    all_to_all x1, waiting for transfers between devices, body(): lax.all_to_all(jnp.broadcast_to(applied[None], (half, bands, width)), 'gr...  13.6 us
  transfers between devices with their start and end apart: 16, of which 11 were waited for; matrix products, arithmetic and copies ran while one was open for 8% of the time, Pallas kernels for 8%

profile of v3, /device:TPU:0, one launch (start us, length us, event | category | flops | bytes accessed | tf_op | source)
XLA Modules:
  0.0 228.6 jit_solution(15229806183777516124)
XLA Ops:
  0.0 1.7 constant_dynamic-slice_fusion
  2.7 5.4 %all-to-all-start.1 = ((bf16[32,4,4096]{2,0,1:T(8,128)(2,1)}), bf16[32,4,4096]{2,0,1:T(8,128)(2,1)S(1)}, u32[]{:S(2)}, u32[]{:S(2)}) async-start(bf16[32,4,4096]{2,0,1:T(8,128)(2,1)} %bitcast.37), calls=%async_computation.1 | async-start | bytes 2097152 | tf_op jit(solution)/shard_map/all_to_all | solution.py:239
  8.1 2.1 constant_dynamic-slice_fusion.1
  10.2 2.6 %collective-permute-start.7 = (bf16[48,64,128]{2,1,0:T(8,128)(2,1)}, bf16[48,64,128]{2,1,0:T(8,128)(2,1)S(1)}, u32[]{:S(2)}, u32[]{:S(2)}) collective-permute-start(bf16[48,64,128]{2,1,0:T(8,128)(2,1)} %constant_dynamic-slice_fusion.1), channel_id=1, source_target_pairs={{0,8},{2,10},{4,12},{6,14},{8,0},{10,2},{12,4},{14,6},{1,9},{3,11}... | collective-permute-start | bytes 2359304 | tf_op jit(solution)/shard_map/ppermute | solution.py:254
  13.5 18.6 %all-to-all-done.1 = bf16[32,4,4096]{2,0,1:T(8,128)(2,1)S(1)} async-done(((bf16[32,4,4096]{2,0,1:T(8,128)(2,1)}), bf16[32,4,4096]{2,0,1:T(8,128)(2,1)S(1)}, u32[]{:S(2)}, u32[]{:S(2)}) %all-to-all-start.1) | async-done | bytes 1048608 | tf_op jit(solution)/shard_map/all_to_all | solution.py:239
  32.1 2.8 %copy-done = bf16[384,64,128]{2,1,0:T(8,128)(2,1)S(1)} copy-done((bf16[384,64,128]{2,1,0:T(8,128)(2,1)S(1)}, bf16[384,64,128]{2,1,0:T(8,128)(2,1)}, u32[]{:S(2)}) %copy-start) | copy-done | bytes 6291480
  34.9 5.3 %shard_map.64.rest_2_ = f32[128,4096]{1,0:T(8,128)S(1)} custom-call(s32[769]{0:T(1024)S(1)} %constant_dynamic-update-slice_fusion.7.meta, bf16[128,4096]{1,0:T(8,128)(2,1)S(1)} %bitcast.44, bf16[384,64,128]{2,1,0:T(8,128)(2,1)S(1)} %copy-done), custom_call_target="tpu_custom_call" | custom-call | flops 1 | bytes 1 | tf_op jit(solution)/shard_map/pallas_call | solution.py:152
  41.5 5.7 %collective-permute-done.7 = bf16[48,64,128]{2,1,0:T(8,128)(2,1)S(1)} collective-permute-done((bf16[48,64,128]{2,1,0:T(8,128)(2,1)}, bf16[48,64,128]{2,1,0:T(8,128)(2,1)S(1)}, u32[]{:S(2)}, u32[]{:S(2)}) %collective-permute-start.7) | collective-permute-done | bytes 786464 | tf_op jit(solution)/shard_map/ppermute | solution.py:254
  49.8 3.5 %all-to-all-start = ((bf16[32,4,4096]{2,0,1:T(8,128)(2,1)}), bf16[32,4,4096]{2,0,1:T(8,128)(2,1)S(1)}, u32[]{:S(2)}, u32[]{:S(2)}) async-start(bf16[32,4,4096]{2,0,1:T(8,128)(2,1)} %bitcast.38), calls=%async_computation | async-start | bytes 2097152 | tf_op jit(solution)/shard_map/all_to_all | solution.py:239
  54.5 3.0 %collective-permute-start.1 = (bf16[24,64,128]{2,1,0:T(8,128)(2,1)S(1)}, bf16[24,64,128]{2,1,0:T(8,128)(2,1)S(1)}, u32[]{:S(2)}, u32[]{:S(2)}) collective-permute-start(bf16[24,64,128]{2,1,0:T(8,128)(2,1)S(1)} %get-tuple-element.10), channel_id=1, source_target_pairs={{0,8},{2,10},{4,12},{6,14},{8,0},{10,2},{12,4},{14,6},{1,9},{3,11}... | collective-permute-start | bytes 1179656 | tf_op jit(solution)/shard_map/ppermute | solution.py:254
  57.6 7.8 %collective-permute-done.8 = bf16[48,64,128]{2,1,0:T(8,128)(2,1)} collective-permute-done((bf16[48,64,128]{2,1,0:T(8,128)(2,1)S(1)}, bf16[48,64,128]{2,1,0:T(8,128)(2,1)}, u32[]{:S(2)}, u32[]{:S(2)}) %collective-permute-start.8) | collective-permute-done | bytes 786464 | tf_op jit(solution)/shard_map/ppermute | solution.py:257
  66.8 23.4 %collective-permute-done.4 = bf16[24,64,128]{2,1,0:T(8,128)(2,1)S(1)} collective-permute-done((bf16[24,64,128]{2,1,0:T(8,128)(2,1)S(1)}, bf16[24,64,128]{2,1,0:T(8,128)(2,1)S(1)}, u32[]{:S(2)}, u32[]{:S(2)}) %collective-permute-start.4) | collective-permute-done | bytes 393248 | tf_op jit(solution)/shard_map/ppermute | solution.py:254
  93.1 9.2 %collective-permute-done.5 = bf16[24,64,128]{2,1,0:T(8,128)(2,1)S(1)} collective-permute-done((bf16[24,64,128]{2,1,0:T(8,128)(2,1)S(1)}, bf16[24,64,128]{2,1,0:T(8,128)(2,1)S(1)}, u32[]{:S(2)}, u32[]{:S(2)}) %collective-permute-start.5) | collective-permute-done | bytes 393248 | tf_op jit(solution)/shard_map/ppermute | solution.py:257
  103.0 4.1 %collective-permute-done.2 = bf16[24,64,128]{2,1,0:T(8,128)(2,1)S(1)} collective-permute-done((bf16[24,64,128]{2,1,0:T(8,128)(2,1)S(1)}, bf16[24,64,128]{2,1,0:T(8,128)(2,1)S(1)}, u32[]{:S(2)}, u32[]{:S(2)}) %collective-permute-start.2) | collective-permute-done | bytes 393248 | tf_op jit(solution)/shard_map/ppermute | solution.py:257
  107.4 4.5 %collective-permute-done = s32[769]{0:T(1024)S(1)} collective-permute-done((s32[769]{0:T(1024)S(1)}, s32[769]{0:T(1024)S(1)}, u32[]{:S(2)}, u32[]{:S(2)}) %collective-permute-start) | collective-permute-done | bytes 3108 | tf_op jit(solution)/shard_map/ppermute | solution.py:263
  113.7 3.9 %shard_map.65.rest_2_ = f32[128,4096]{1,0:T(8,128)S(1)} custom-call(s32[773]{0:T(1024)S(1)} %concatenate.35.meta, bf16[128,4096]{1,0:T(8,128)(2,1)S(1)} %bitcast.39, bf16[96,64,128]{2,1,0:T(8,128)(2,1)S(1)} %constant_dynamic-update-slice_fusion.5.rest_0_, bf16[96,64,128]{2,1,0:T(8,128)(2,1)} %collective-permute-done.9.rest_1_, f32[128,4096]{1,0:T(8,128)S(1)} %copy-done.3), custom_call_target="tpu_custom_call" | custom-call | flops 1 | bytes 1 | tf_op jit(solution)/shard_map/pallas_call | solution.py:152
  117.7 2.2 shard_map.66.rest_2_
  119.9 2.0 shard_map.67
  122.9 14.5 %all-to-all-start.2 = ((bf16[4,32,4096]{2,1,0:T(8,128)(2,1)}), bf16[4,32,4096]{2,1,0:T(8,128)(2,1)S(1)}, u32[]{:S(2)}, u32[]{:S(2)}) async-start(bf16[4,32,4096]{2,1,0:T(8,128)(2,1)} %bitcast.45), calls=%async_computation.2 | async-start | bytes 2097152 | tf_op jit(solution)/shard_map/all_to_all | solution.py:273
  140.1 2.9 %copy.19 = f32[32,128,128]{2,1,0:T(8,128)} copy(f32[32,128,128]{1,2,0:T(8,128)} %broadcast_bitcast_fusion) | data formatting | bytes 4194304 | tf_op jit(solution)/shard_map/tile | solution.py:218
  143.1 3.0 %select_convert_fusion.high_ref = bf16[32,128,128]{2,1,0:T(8,128)(2,1)} fusion(f32[32,128,128]{2,1,0:T(8,128)} %copy.19, pred[128,128]{1,0:T(8,128)(4,1)S(1)} %broadcast_compare_fusion), kind=kLoop, calls=%fused_computation.2 | loop fusion | flops 524288 | bytes 3162112 | tf_op jit(solution)/shard_map/convert_element_type | solution.py:186
  147.4 3.4 %all-to-all-done.2.parts_ref = bf16[4,32,4096]{2,1,0:T(8,128)(2,1)S(1)} async-done(((bf16[4,32,4096]{2,1,0:T(8,128)(2,1)}), bf16[4,32,4096]{2,1,0:T(8,128)(2,1)S(1)}, u32[]{:S(2)}, u32[]{:S(2)}) %all-to-all-start.2) | async-done | bytes 1048608 | tf_op jit(solution)/shard_map/all_to_all | solution.py:273
  155.3 3.5 %all-to-all-start.3 = ((bf16[4,32,4096]{2,1,0:T(8,128)(2,1)}), bf16[4,32,4096]{2,1,0:T(8,128)(2,1)S(1)}, u32[]{:S(2)}, u32[]{:S(2)}) async-start(bf16[4,32,4096]{2,1,0:T(8,128)(2,1)} %broadcast_in_dim.23), calls=%async_computation.3 | async-start | bytes 2097152 | tf_op jit(solution)/shard_map/all_to_all | solution.py:282
  158.9 13.6 %all-to-all-done.3 = bf16[4,32,4096]{2,1,0:T(8,128)(2,1)S(1)} async-done(((bf16[4,32,4096]{2,1,0:T(8,128)(2,1)}), bf16[4,32,4096]{2,1,0:T(8,128)(2,1)S(1)}, u32[]{:S(2)}, u32[]{:S(2)}) %all-to-all-start.3) | async-done | bytes 1048608 | tf_op jit(solution)/shard_map/all_to_all | solution.py:282
  172.5 5.3 %shard_map.70 = bf16[128,4096]{1,0:T(8,128)(2,1)S(1)} custom-call(s32[781]{0:T(1024)S(1)} %concatenate.37.meta, bf16[128,4096]{1,0:T(8,128)(2,1)S(1)} %bitcast.42, bf16[96,64,128]{2,1,0:T(8,128)(2,1)S(1)} %constant_dynamic-update-slice_fusion.5.rest_0_, bf16[96,64,128]{2,1,0:T(8,128)(2,1)} %collective-permute-done.9.rest_1_, ...), custom_call_target="tpu_custom_call" | custom-call | flops 1 | bytes 1 | tf_op jit(solution)/shard_map/pallas_call | solution.py:170
  178.9 16.9 %all-to-all-start.5 = ((bf16[4,32,4096]{2,1,0:T(8,128)(2,1)}), bf16[4,32,4096]{2,1,0:T(8,128)(2,1)}, u32[]{:S(2)}, u32[]{:S(2)}) async-start(bf16[4,32,4096]{2,1,0:T(8,128)(2,1)} %bitcast.46), calls=%async_computation.5 | async-start | bytes 2097152 | tf_op jit(solution)/shard_map/all_to_all | solution.py:292
  195.8 2.8 %copy-done.1 = bf16[384,64,128]{2,1,0:T(8,128)(2,1)S(1)} copy-done((bf16[384,64,128]{2,1,0:T(8,128)(2,1)S(1)}, bf16[384,64,128]{2,1,0:T(8,128)(2,1)}, u32[]{:S(2)}) %copy-start.1) | copy-done | bytes 6291480
  198.6 7.3 %shard_map.69 = bf16[128,4096]{1,0:T(8,128)(2,1)} custom-call(s32[769]{0:T(1024)S(1)} %constant_dynamic-update-slice_fusion.7.meta, bf16[128,4096]{1,0:T(8,128)(2,1)S(1)} %bitcast.43, bf16[384,64,128]{2,1,0:T(8,128)(2,1)S(1)} %copy-done.1), custom_call_target="tpu_custom_call" | custom-call | flops 1 | bytes 1 | tf_op jit(solution)/shard_map/pallas_call | solution.py:170
  205.9 3.5 %all-to-all-done.5 = bf16[4,32,4096]{2,1,0:T(8,128)(2,1)} async-done(((bf16[4,32,4096]{2,1,0:T(8,128)(2,1)}), bf16[4,32,4096]{2,1,0:T(8,128)(2,1)}, u32[]{:S(2)}, u32[]{:S(2)}) %all-to-all-start.5) | async-done | bytes 1048608 | tf_op jit(solution)/shard_map/all_to_all | solution.py:292
  209.4 3.5 %all-to-all-start.4 = ((bf16[4,32,4096]{2,1,0:T(8,128)(2,1)}), bf16[4,32,4096]{2,1,0:T(8,128)(2,1)S(1)}, u32[]{:S(2)}, u32[]{:S(2)}) async-start(bf16[4,32,4096]{2,1,0:T(8,128)(2,1)} %bitcast.21), calls=%async_computation.4 | async-start | bytes 2097152 | tf_op jit(solution)/shard_map/all_to_all | solution.py:292
  214.3 12.4 %all-to-all-done.4 = bf16[4,32,4096]{2,1,0:T(8,128)(2,1)S(1)} async-done(((bf16[4,32,4096]{2,1,0:T(8,128)(2,1)}), bf16[4,32,4096]{2,1,0:T(8,128)(2,1)S(1)}, u32[]{:S(2)}, u32[]{:S(2)}) %all-to-all-start.4) | async-done | bytes 1048608 | tf_op jit(solution)/shard_map/all_to_all | solution.py:292
  226.8 1.8 maximum_select_fusion
  (59 shorter events, 25.1 us)
Async XLA Ops:
  2.7 10.7 %copy-start.9 = (s32[384]{0:T(512)S(1)}, s32[384]{0:T(512)}, u32[]{:S(2)}) copy-start(s32[384]{0:T(512)} %param.7) | copy-start | bytes 4612
  2.7 10.7 %copy-start.10 = (s32[384]{0:T(512)S(1)}, s32[384]{0:T(512)}, u32[]{:S(2)}) copy-start(s32[384]{0:T(512)} %param.8) | copy-start | bytes 4612
  2.7 29.4 %all-to-all-start.1 = ((bf16[32,4,4096]{2,0,1:T(8,128)(2,1)}), bf16[32,4,4096]{2,0,1:T(8,128)(2,1)S(1)}, u32[]{:S(2)}, u32[]{:S(2)}) async-start(bf16[32,4,4096]{2,0,1:T(8,128)(2,1)} %bitcast.37), calls=%async_computation.1 | async-start | bytes 2097152 | tf_op jit(solution)/shard_map/all_to_all | solution.py:239
  10.2 37.0 %collective-permute-start.7 = (bf16[48,64,128]{2,1,0:T(8,128)(2,1)}, bf16[48,64,128]{2,1,0:T(8,128)(2,1)S(1)}, u32[]{:S(2)}, u32[]{:S(2)}) collective-permute-start(bf16[48,64,128]{2,1,0:T(8,128)(2,1)} %constant_dynamic-slice_fusion.1), channel_id=1, source_target_pairs={{0,8},{2,10},{4,12},{6,14},{8,0},{10,2},{12,4},{14,6},{1,9},{3,11}... | collective-permute-start | bytes 2359304 | tf_op jit(solution)/shard_map/ppermute | solution.py:254
  32.1 2.8 %copy-start = (bf16[384,64,128]{2,1,0:T(8,128)(2,1)S(1)}, bf16[384,64,128]{2,1,0:T(8,128)(2,1)}, u32[]{:S(2)}) copy-start(bf16[384,64,128]{2,1,0:T(8,128)(2,1)} %rest_0_.3) | copy-start | bytes 18874372
  40.2 1.3 copy-start.2
  47.2 18.2 %collective-permute-start.8 = (bf16[48,64,128]{2,1,0:T(8,128)(2,1)S(1)}, bf16[48,64,128]{2,1,0:T(8,128)(2,1)}, u32[]{:S(2)}, u32[]{:S(2)}) collective-permute-start(bf16[48,64,128]{2,1,0:T(8,128)(2,1)S(1)} %collective-permute-done.7), channel_id=1, source_target_pairs={{0,16},{16,0},{1,17},{17,1},{2,18},{18,2},{3,19},{19,3},{4,20},{20... | collective-permute-start | bytes 2359304 | tf_op jit(solution)/shard_map/ppermute | solution.py:257
  49.8 62.4 %all-to-all-start = ((bf16[32,4,4096]{2,0,1:T(8,128)(2,1)}), bf16[32,4,4096]{2,0,1:T(8,128)(2,1)S(1)}, u32[]{:S(2)}, u32[]{:S(2)}) async-start(bf16[32,4,4096]{2,0,1:T(8,128)(2,1)} %bitcast.38), calls=%async_computation | async-start | bytes 2097152 | tf_op jit(solution)/shard_map/all_to_all | solution.py:239
  54.5 36.2 %collective-permute-start.1 = (bf16[24,64,128]{2,1,0:T(8,128)(2,1)S(1)}, bf16[24,64,128]{2,1,0:T(8,128)(2,1)S(1)}, u32[]{:S(2)}, u32[]{:S(2)}) collective-permute-start(bf16[24,64,128]{2,1,0:T(8,128)(2,1)S(1)} %get-tuple-element.10), channel_id=1, source_target_pairs={{0,8},{2,10},{4,12},{6,14},{8,0},{10,2},{12,4},{14,6},{1,9},{3,11}... | collective-permute-start | bytes 1179656 | tf_op jit(solution)/shard_map/ppermute | solution.py:254
  57.5 32.7 %collective-permute-start.4 = (bf16[24,64,128]{2,1,0:T(8,128)(2,1)S(1)}, bf16[24,64,128]{2,1,0:T(8,128)(2,1)S(1)}, u32[]{:S(2)}, u32[]{:S(2)}) collective-permute-start(bf16[24,64,128]{2,1,0:T(8,128)(2,1)S(1)} %get-tuple-element.9), channel_id=1, source_target_pairs={{0,8},{2,10},{4,12},{6,14},{8,0},{10,2},{12,4},{14,6},{1,9},{3,11}... | collective-permute-start | bytes 1179656 | tf_op jit(solution)/shard_map/ppermute | solution.py:254
  66.7 45.5 %collective-permute-start.9 = (bf16[96,64,128]{2,1,0:T(8,128)(2,1)S(1)}, bf16[96,64,128]{2,1,0:T(8,128)(2,1)}, u32[]{:S(2)}, u32[]{:S(2)}) collective-permute-start(bf16[96,64,128]{2,1,0:T(8,128)(2,1)S(1)} %constant_dynamic-update-slice_fusion.5.rest_0_), channel_id=1, source_target_pairs={{0,1},{1,0},{2,3},{3,2},{4,5},{5,4},{6,7},{7,6},{8,9},{9,8},{10,11... | collective-permute-start | bytes 4718600 | tf_op jit(solution)/shard_map/ppermute | solution.py:258
  90.2 12.1 %collective-permute-start.5 = (bf16[24,64,128]{2,1,0:T(8,128)(2,1)S(1)}, bf16[24,64,128]{2,1,0:T(8,128)(2,1)S(1)}, u32[]{:S(2)}, u32[]{:S(2)}) collective-permute-start(bf16[24,64,128]{2,1,0:T(8,128)(2,1)S(1)} %collective-permute-done.4), channel_id=1, source_target_pairs={{0,16},{16,0},{1,17},{17,1},{2,18},{18,2},{3,19},{19,3},{4,20},{20... | collective-permute-start | bytes 1179656 | tf_op jit(solution)/shard_map/ppermute | solution.py:257
  90.7 16.5 %collective-permute-start.2 = (bf16[24,64,128]{2,1,0:T(8,128)(2,1)S(1)}, bf16[24,64,128]{2,1,0:T(8,128)(2,1)S(1)}, u32[]{:S(2)}, u32[]{:S(2)}) collective-permute-start(bf16[24,64,128]{2,1,0:T(8,128)(2,1)S(1)} %collective-permute-done.1), channel_id=1, source_target_pairs={{0,16},{16,0},{1,17},{17,1},{2,18},{18,2},{3,19},{19,3},{4,20},{20... | collective-permute-start | bytes 1179656 | tf_op jit(solution)/shard_map/ppermute | solution.py:257
  103.0 14.7 %collective-permute-start.6 = (bf16[48,64,128]{2,1,0:T(8,128)(2,1)}, bf16[48,64,128]{2,1,0:T(8,128)(2,1)}, u32[]{:S(2)}, u32[]{:S(2)}) collective-permute-start(bf16[48,64,128]{2,1,0:T(8,128)(2,1)} %constant_dynamic-update-slice_fusion.3.rest_0_.rest_2_), channel_id=1, source_target_pairs={{0,1},{1,0},{2,3},{3,2},{4,5},{5,4},{6,7},{7,6},{8,9},{9,8},{10,11... | collective-permute-start | bytes 2359304 | tf_op jit(solution)/shard_map/ppermute | solution.py:258
  107.2 12.7 %collective-permute-start.3 = (bf16[48,64,128]{2,1,0:T(8,128)(2,1)S(1)}, bf16[48,64,128]{2,1,0:T(8,128)(2,1)}, u32[]{:S(2)}, u32[]{:S(2)}) collective-permute-start(bf16[48,64,128]{2,1,0:T(8,128)(2,1)S(1)} %constant_dynamic-update-slice_fusion.1.rest_0_.rest_4_), channel_id=1, source_target_pairs={{0,1},{1,0},{2,3},{3,2},{4,5},{5,4},{6,7},{7,6},{8,9},{9,8},{10,11... | collective-permute-start | bytes 2359304 | tf_op jit(solution)/shard_map/ppermute | solution.py:258
  107.3 4.6 %collective-permute-start = (s32[769]{0:T(1024)S(1)}, s32[769]{0:T(1024)S(1)}, u32[]{:S(2)}, u32[]{:S(2)}) collective-permute-start(s32[769]{0:T(1024)S(1)} %constant_dynamic-update-slice_fusion.7.meta), channel_id=1, source_target_pairs={{0,8},{2,10},{4,12},{6,14},{8,0},{10,2},{12,4},{14,6},{1,9},{3,11}... | collective-permute-start | bytes 9236 | tf_op jit(solution)/shard_map/ppermute | solution.py:263
  112.1 1.6 copy-start.3
  122.0 1.0 copy-start.4
  122.9 27.9 %all-to-all-start.2 = ((bf16[4,32,4096]{2,1,0:T(8,128)(2,1)}), bf16[4,32,4096]{2,1,0:T(8,128)(2,1)S(1)}, u32[]{:S(2)}, u32[]{:S(2)}) async-start(bf16[4,32,4096]{2,1,0:T(8,128)(2,1)} %bitcast.45), calls=%async_computation.2 | async-start | bytes 2097152 | tf_op jit(solution)/shard_map/all_to_all | solution.py:273
  143.0 3.1 %copy-start.8 = (f32[32,128,128]{2,1,0:T(8,128)S(1)}, f32[32,128,128]{2,1,0:T(8,128)}, u32[]{:S(2)}) copy-start(f32[32,128,128]{2,1,0:T(8,128)} %copy.19) | copy-start | bytes 6291460
  150.8 1.2 copy-start.5
  152.0 1.2 copy-start.6
  155.3 17.3 %all-to-all-start.3 = ((bf16[4,32,4096]{2,1,0:T(8,128)(2,1)}), bf16[4,32,4096]{2,1,0:T(8,128)(2,1)S(1)}, u32[]{:S(2)}, u32[]{:S(2)}) async-start(bf16[4,32,4096]{2,1,0:T(8,128)(2,1)} %broadcast_in_dim.23), calls=%async_computation.3 | async-start | bytes 2097152 | tf_op jit(solution)/shard_map/all_to_all | solution.py:282
  177.9 1.0 copy-start.7
  178.9 30.6 %all-to-all-start.5 = ((bf16[4,32,4096]{2,1,0:T(8,128)(2,1)}), bf16[4,32,4096]{2,1,0:T(8,128)(2,1)}, u32[]{:S(2)}, u32[]{:S(2)}) async-start(bf16[4,32,4096]{2,1,0:T(8,128)(2,1)} %bitcast.46), calls=%async_computation.5 | async-start | bytes 2097152 | tf_op jit(solution)/shard_map/all_to_all | solution.py:292
  195.8 2.8 %copy-start.1 = (bf16[384,64,128]{2,1,0:T(8,128)(2,1)S(1)}, bf16[384,64,128]{2,1,0:T(8,128)(2,1)}, u32[]{:S(2)}) copy-start(bf16[384,64,128]{2,1,0:T(8,128)(2,1)} %rest_0_.3) | copy-start | bytes 18874372
  209.4 17.3 %all-to-all-start.4 = ((bf16[4,32,4096]{2,1,0:T(8,128)(2,1)}), bf16[4,32,4096]{2,1,0:T(8,128)(2,1)S(1)}, u32[]{:S(2)}, u32[]{:S(2)}) async-start(bf16[4,32,4096]{2,1,0:T(8,128)(2,1)} %bitcast.21), calls=%async_computation.4 | async-start | bytes 2097152 | tf_op jit(solution)/shard_map/all_to_all | solution.py:292

commit v4 on v3

--- a/solution.py
+++ b/solution.py
@@ -245,30 +245,37 @@
 
     total = project(tiles, meta, own_wave, [projectors], width)
 
+    other_meta = lax.ppermute(meta, "grid", partners)
+
     pieces, bases = [], []
     start = 0
-    for size in (tiles // 2, tiles // 4, tiles // 4):
+    for size in [tiles // 4] * 4:
         share = size // 4
         quarter = 2 * group + core
         mine = lax.dynamic_slice_in_dim(projectors, start + quarter * share, share, 0)
         mine = lax.ppermute(mine, "grid", partners)
         if start == 0:
-            mine, total = lax.optimization_barrier((mine, total))
+            mine, total, other_meta = lax.optimization_barrier((mine, total, other_meta))
         both = jnp.concatenate([mine, lax.ppermute(mine, "groups", swap)])
         pieces += [both, lax.ppermute(both, "band", swap)]
         for other_core in (core, 1 - core):
             for other_group in (group, 1 - group):
                 bases.append(start + (2 * other_group + other_core) * share)
         start += size
-    other_meta = lax.ppermute(meta, "grid", partners)
-    metas = [jnp.concatenate([other_meta, jnp.stack(bases[i : i + 4])]) for i in (0, 4, 8)]
+    ranges = ((0, 2), (2, 3), (3, 4))
+    metas = [
+        jnp.concatenate([other_meta, jnp.stack(bases[4 * first : 4 * end])])
+        for first, end in ranges
+    ]
     other_meta = jnp.concatenate([other_meta, jnp.stack(bases)])
 
     matrix = coupling_matrix(coupling)
 
-    total = project(tiles, metas[0], other_wave, pieces[0:2], width, total)
-    total = project(tiles, metas[1], other_wave, pieces[2:4], width, total)
-    partial = project(tiles, metas[2], other_wave, pieces[4:6], width, total, last=True)
+    for (first, end), piece_meta in zip(ranges, metas):
+        total = project(
+            tiles, piece_meta, other_wave, pieces[2 * first : 2 * end], width, total, last=end == 4
+        )
+    partial = total
 
     parts = lax.all_to_all(
         partial.reshape(half, bands, width),

time: 230 us -> 218 us (0.948)
  Pallas kernels: 27.1 us -> 53.2 us
  waiting for transfers between devices: 106 us -> 86.7 us
  starting transfers between devices: 56.8 us -> 42.9 us
    ppermute x3 -> x4, waiting for transfers between devices: 21.2 us -> 0.08 us  [body(): both = jnp.concatenate([mine, lax.ppermute(mine, 'groups', swap)])]
    ppermute x3 -> x4, waiting for transfers between devices: 29.1 us -> 49.7 us  [body(): mine = lax.ppermute(mine, 'grid', partners)]
    all_to_all x2, waiting for transfers between devices: 18.6 us -> 0.01 us  [to_bricks(): lax.all_to_all(part, 'grid', split_axis=1, concat_axis=0, tiled=True, axi...]
    pallas_call x2, Pallas kernels: 12.7 us -> 26.9 us  [spread(): pl.pallas_call(functools.partial(spread_kernel, tiles, len(pieces)), grid...]
    pallas_call x4, Pallas kernels: 13.5 us -> 25.4 us  [project(): pl.pallas_call(functools.partial(project_kernel, tiles, len(pieces), last...]
    all_to_all x1, starting transfers between devices: 14.5 us -> 3.65 us  [body(): lax.all_to_all(partial.reshape(half, bands, width), 'grid', split_axis=0,...]
    all_to_all x2, starting transfers between devices: 20.4 us -> 11.5 us  [to_bands(): lax.all_to_all(field, 'grid', split_axis=0, concat_axis=1, tiled=True, ax...]
    all_to_all x1, waiting for transfers between devices: 3.41 us -> 9.46 us  [body(): lax.all_to_all(partial.reshape(half, bands, width), 'grid', split_axis=0,...]
  transfers between devices with their start and end apart: 16 -> 19, of which waited for: 11 -> 8; matrix products, arithmetic and copies ran while one was open for 8% -> 10% of each run, Pallas kernels for 8% -> 19%
where the time goes in v4:
time: 218 us; the launch traced here: 217 us
  waiting for transfers between devices  86.7 us (40%)
  Pallas kernels  53.2 us (24%)
  starting transfers between devices  42.9 us (20%)
  local copies, waits for them, and re-layouts  29.2 us (13%)
  other arithmetic  4.19 us (2%)
    ppermute x4, waiting for transfers between devices, body(): mine = lax.ppermute(mine, 'grid', partners)  49.7 us
    pallas_call x2, Pallas kernels, spread(): pl.pallas_call(functools.partial(spread_kernel, tiles, len(pieces)), grid...  26.9 us
    pallas_call x4, Pallas kernels, project(): pl.pallas_call(functools.partial(project_kernel, tiles, len(pieces), last...  25.4 us
    all_to_all x2, waiting for transfers between devices, to_bands(): lax.all_to_all(field, 'grid', split_axis=0, concat_axis=1, tiled=True, ax...  13.7 us
    all_to_all x1, waiting for transfers between devices, body(): lax.all_to_all(jnp.broadcast_to(applied[None], (half, bands, width)), 'gr...  13.7 us
    unnamed x22, local copies, waits for them, and re-layouts  13.1 us
    all_to_all x2, starting transfers between devices, to_bands(): lax.all_to_all(field, 'grid', split_axis=0, concat_axis=1, tiled=True, ax...  11.5 us
    all_to_all x1, waiting for transfers between devices, body(): lax.all_to_all(partial.reshape(half, bands, width), 'grid', split_axis=0,...  9.46 us
  transfers between devices with their start and end apart: 19, of which 8 were waited for; matrix products, arithmetic and copies ran while one was open for 10% of the time, Pallas kernels for 19%

profile of v4, /device:TPU:0, one launch (start us, length us, event | category | flops | bytes accessed | tf_op | source)
XLA Modules:
  0.0 217.0 jit_solution(4338711176112335540)
XLA Ops:
  2.7 5.2 %all-to-all-start = ((bf16[32,4,4096]{2,0,1:T(8,128)(2,1)}), bf16[32,4,4096]{2,0,1:T(8,128)(2,1)S(1)}, u32[]{:S(2)}, u32[]{:S(2)}) async-start(bf16[32,4,4096]{2,0,1:T(8,128)(2,1)} %bitcast.42), calls=%async_computation | async-start | bytes 2097152 | tf_op jit(solution)/shard_map/all_to_all | solution.py:239
  8.0 2.5 %constant_dynamic-slice_fusion = (bf16[24,64,128]{2,1,0:T(8,128)(2,1)S(1)}, bf16[24,64,128]{2,1,0:T(8,128)(2,1)}, bf16[24,64,128]{2,1,0:T(8,128)(2,1)S(1)}, bf16[24,64,128]{2,1,0:T(8,128)(2,1)}) fusion(bf16[384,64,128]{2,1,0:T(8,128)(2,1)} %rest_0_.3, s32[]{:T(128)S(6)} %select_n.60, s32[]{:T(128)S(6)} %select_n.59, s32[]{:T(128)S(6)} %select_n.58, ...), kind=kLoop, calls=%fused_computation.19 | loop fusion | bytes 3145744 | tf_op jit(solution)/shard_map/dynamic_slice | solution.py:255
  10.5 2.6 %collective-permute-start.5 = (bf16[24,64,128]{2,1,0:T(8,128)(2,1)}, bf16[24,64,128]{2,1,0:T(8,128)(2,1)}, u32[]{:S(2)}, u32[]{:S(2)}) collective-permute-start(bf16[24,64,128]{2,1,0:T(8,128)(2,1)} %get-tuple-element.12), channel_id=1, source_target_pairs={{0,8},{2,10},{4,12},{6,14},{8,0},{10,2},{12,4},{14,6},{1,9},{3,11}... | collective-permute-start | bytes 1179656 | tf_op jit(solution)/shard_map/ppermute | solution.py:256
  13.4 2.6 %collective-permute-start.2 = (bf16[24,64,128]{2,1,0:T(8,128)(2,1)S(1)}, bf16[24,64,128]{2,1,0:T(8,128)(2,1)S(1)}, u32[]{:S(2)}, u32[]{:S(2)}) collective-permute-start(bf16[24,64,128]{2,1,0:T(8,128)(2,1)S(1)} %get-tuple-element.13), channel_id=1, source_target_pairs={{0,8},{2,10},{4,12},{6,14},{8,0},{10,2},{12,4},{14,6},{1,9},{3,11}... | collective-permute-start | bytes 1179656 | tf_op jit(solution)/shard_map/ppermute | solution.py:256
  16.3 12.8 %collective-permute-done.5 = bf16[24,64,128]{2,1,0:T(8,128)(2,1)} collective-permute-done((bf16[24,64,128]{2,1,0:T(8,128)(2,1)}, bf16[24,64,128]{2,1,0:T(8,128)(2,1)}, u32[]{:S(2)}, u32[]{:S(2)}) %collective-permute-start.5) | collective-permute-done | bytes 393248 | tf_op jit(solution)/shard_map/ppermute | solution.py:256
  31.3 3.5 %collective-permute-start.1 = (s32[769]{0:T(1024)S(1)}, s32[769]{0:T(1024)S(1)}, u32[]{:S(2)}, u32[]{:S(2)}) collective-permute-start(s32[769]{0:T(1024)S(1)} %constant_dynamic-update-slice_fusion.9.meta), channel_id=1, source_target_pairs={{0,8},{2,10},{4,12},{6,14},{8,0},{10,2},{12,4},{14,6},{1,9},{3,11}... | collective-permute-start | bytes 9236 | tf_op jit(solution)/shard_map/ppermute | solution.py:248
  35.9 30.1 %collective-permute-done.10 = bf16[24,64,128]{2,1,0:T(8,128)(2,1)} collective-permute-done((bf16[24,64,128]{2,1,0:T(8,128)(2,1)S(1)}, bf16[24,64,128]{2,1,0:T(8,128)(2,1)}, u32[]{:S(2)}, u32[]{:S(2)}) %collective-permute-start.10) | collective-permute-done | bytes 393248 | tf_op jit(solution)/shard_map/ppermute | solution.py:256
  67.4 6.8 %collective-permute-done.2 = bf16[24,64,128]{2,1,0:T(8,128)(2,1)S(1)} collective-permute-done((bf16[24,64,128]{2,1,0:T(8,128)(2,1)S(1)}, bf16[24,64,128]{2,1,0:T(8,128)(2,1)S(1)}, u32[]{:S(2)}, u32[]{:S(2)}) %collective-permute-start.2) | collective-permute-done | bytes 393248 | tf_op jit(solution)/shard_map/ppermute | solution.py:256
  76.5 3.5 %all-to-all-start.1 = ((bf16[32,4,4096]{2,0,1:T(8,128)(2,1)}), bf16[32,4,4096]{2,0,1:T(8,128)(2,1)S(1)}, u32[]{:S(2)}, u32[]{:S(2)}) async-start(bf16[32,4,4096]{2,0,1:T(8,128)(2,1)} %bitcast.41), calls=%async_computation.1 | async-start | bytes 2097152 | tf_op jit(solution)/shard_map/all_to_all | solution.py:239
  81.8 2.8 %copy-done = bf16[384,64,128]{2,1,0:T(8,128)(2,1)S(1)} copy-done((bf16[384,64,128]{2,1,0:T(8,128)(2,1)S(1)}, bf16[384,64,128]{2,1,0:T(8,128)(2,1)}, u32[]{:S(2)}) %copy-start) | copy-done | bytes 6291480
  85.8 14.9 %shard_map.64.rest_4_ = f32[128,4096]{1,0:T(8,128)S(1)} custom-call(s32[769]{0:T(1024)S(1)} %constant_dynamic-update-slice_fusion.9.meta, bf16[128,4096]{1,0:T(8,128)(2,1)S(1)} %bitcast.48, bf16[384,64,128]{2,1,0:T(8,128)(2,1)S(1)} %copy-done), custom_call_target="tpu_custom_call" | custom-call | flops 1 | bytes 1 | tf_op jit(solution)/shard_map/pallas_call | solution.py:152
  101.4 1.8 constant_dynamic-update-slice_fusion.8
  103.2 1.8 constant_dynamic-update-slice_fusion.3.rest_0_.rest_4_
  105.0 1.8 constant_dynamic-update-slice_fusion.7.rest_2_
  107.3 1.8 constant_dynamic-update-slice_fusion.6
  109.9 1.8 constant_dynamic-update-slice_fusion.1.rest_0_.rest_6_
  112.5 5.0 %shard_map.65.rest_2_ = f32[128,4096]{1,0:T(8,128)S(1)} custom-call(s32[777]{0:T(1024)S(1)} %concatenate.38.meta, bf16[128,4096]{1,0:T(8,128)(2,1)S(1)} %bitcast.43, bf16[48,64,128]{2,1,0:T(8,128)(2,1)} %constant_dynamic-update-slice_fusion.5.rest_0_, bf16[48,64,128]{2,1,0:T(8,128)(2,1)} %collective-permute-done.9.rest_1_, ...), custom_call_target="tpu_custom_call" | custom-call | flops 1 | bytes 1 | tf_op jit(solution)/shard_map/pallas_call | solution.py:152
  117.6 2.2 %shard_map.66.rest_2_ = f32[128,4096]{1,0:T(8,128)S(1)} custom-call(s32[773]{0:T(1024)S(1)} %concatenate.36.meta, bf16[128,4096]{1,0:T(8,128)(2,1)S(1)} %bitcast.44, bf16[48,64,128]{2,1,0:T(8,128)(2,1)} %constant_dynamic-update-slice_fusion.3.rest_0_.rest_4_, bf16[48,64,128]{2,1,0:T(8,128)(2,1)} %collective-permute-done.7.rest_1_.rest_5_, ...), custom_call_target="tpu_custom_call" | custom-call | flops 1 | bytes 1 | tf_op jit(solution)/shard_map/pallas_call | solution.py:152
  119.8 3.3 %shard_map.67 = bf16[128,4096]{1,0:T(8,128)(2,1)} custom-call(s32[773]{0:T(1024)S(1)} %concatenate.34.meta, bf16[128,4096]{1,0:T(8,128)(2,1)S(1)} %bitcast.45, bf16[48,64,128]{2,1,0:T(8,128)(2,1)} %constant_dynamic-update-slice_fusion.1.rest_0_.rest_6_, bf16[48,64,128]{2,1,0:T(8,128)(2,1)} %collective-permute-done.4.rest_1_.rest_7_, ...), custom_call_target="tpu_custom_call" | custom-call | flops 1 | bytes 1 | tf_op jit(solution)/shard_map/pallas_call | solution.py:152
  123.0 3.6 %all-to-all-start.2 = ((bf16[4,32,4096]{2,1,0:T(8,128)(2,1)}), bf16[4,32,4096]{2,1,0:T(8,128)(2,1)S(1)}, u32[]{:S(2)}, u32[]{:S(2)}) async-start(bf16[4,32,4096]{2,1,0:T(8,128)(2,1)} %bitcast.21), calls=%async_computation.2 | async-start | bytes 2097152 | tf_op jit(solution)/shard_map/all_to_all | solution.py:280
  127.1 1.8 copy.19
  129.0 2.0 select_convert_fusion.high_ref
  131.4 9.5 %all-to-all-done.2.parts_ref = bf16[4,32,4096]{2,1,0:T(8,128)(2,1)S(1)} async-done(((bf16[4,32,4096]{2,1,0:T(8,128)(2,1)}), bf16[4,32,4096]{2,1,0:T(8,128)(2,1)S(1)}, u32[]{:S(2)}, u32[]{:S(2)}) %all-to-all-start.2) | async-done | bytes 1048608 | tf_op jit(solution)/shard_map/all_to_all | solution.py:280
  142.9 3.5 %all-to-all-start.3 = ((bf16[4,32,4096]{2,1,0:T(8,128)(2,1)}), bf16[4,32,4096]{2,1,0:T(8,128)(2,1)S(1)}, u32[]{:S(2)}, u32[]{:S(2)}) async-start(bf16[4,32,4096]{2,1,0:T(8,128)(2,1)} %broadcast_in_dim.23), calls=%async_computation.3 | async-start | bytes 2097152 | tf_op jit(solution)/shard_map/all_to_all | solution.py:289
  146.5 13.7 %all-to-all-done.3 = bf16[4,32,4096]{2,1,0:T(8,128)(2,1)S(1)} async-done(((bf16[4,32,4096]{2,1,0:T(8,128)(2,1)}), bf16[4,32,4096]{2,1,0:T(8,128)(2,1)S(1)}, u32[]{:S(2)}, u32[]{:S(2)}) %all-to-all-start.3) | async-done | bytes 1048608 | tf_op jit(solution)/shard_map/all_to_all | solution.py:289
  160.2 7.8 %shard_map.70 = bf16[128,4096]{1,0:T(8,128)(2,1)} custom-call(s32[785]{0:T(1024)S(1)} %concatenate.41.meta, bf16[128,4096]{1,0:T(8,128)(2,1)S(1)} %bitcast.46, bf16[48,64,128]{2,1,0:T(8,128)(2,1)} %constant_dynamic-update-slice_fusion.5.rest_0_, bf16[48,64,128]{2,1,0:T(8,128)(2,1)} %collective-permute-done.9.rest_1_, ...), custom_call_target="tpu_custom_call" | custom-call | flops 1 | bytes 1 | tf_op jit(solution)/shard_map/pallas_call | solution.py:170
  168.0 8.0 %all-to-all-start.5 = ((bf16[4,32,4096]{2,1,0:T(8,128)(2,1)}), bf16[4,32,4096]{2,1,0:T(8,128)(2,1)S(1)}, u32[]{:S(2)}, u32[]{:S(2)}) async-start(bf16[4,32,4096]{2,1,0:T(8,128)(2,1)} %bitcast.27), calls=%async_computation.5 | async-start | bytes 2097152 | tf_op jit(solution)/shard_map/all_to_all | solution.py:299
  176.0 2.8 %copy-done.1 = bf16[384,64,128]{2,1,0:T(8,128)(2,1)S(1)} copy-done((bf16[384,64,128]{2,1,0:T(8,128)(2,1)S(1)}, bf16[384,64,128]{2,1,0:T(8,128)(2,1)}, u32[]{:S(2)}) %copy-start.1) | copy-done | bytes 6291480
  178.8 19.1 %shard_map.69 = bf16[128,4096]{1,0:T(8,128)(2,1)} custom-call(s32[769]{0:T(1024)S(1)} %constant_dynamic-update-slice_fusion.9.meta, bf16[128,4096]{1,0:T(8,128)(2,1)S(1)} %bitcast.47, bf16[384,64,128]{2,1,0:T(8,128)(2,1)S(1)} %copy-done.1), custom_call_target="tpu_custom_call" | custom-call | flops 1 | bytes 1 | tf_op jit(solution)/shard_map/pallas_call | solution.py:170
  197.8 3.5 %all-to-all-start.4 = ((bf16[4,32,4096]{2,1,0:T(8,128)(2,1)}), bf16[4,32,4096]{2,1,0:T(8,128)(2,1)S(1)}, u32[]{:S(2)}, u32[]{:S(2)}) async-start(bf16[4,32,4096]{2,1,0:T(8,128)(2,1)} %bitcast.25), calls=%async_computation.4 | async-start | bytes 2097152 | tf_op jit(solution)/shard_map/all_to_all | solution.py:299
  201.5 13.7 %all-to-all-done.4 = bf16[4,32,4096]{2,1,0:T(8,128)(2,1)S(1)} async-done(((bf16[4,32,4096]{2,1,0:T(8,128)(2,1)}), bf16[4,32,4096]{2,1,0:T(8,128)(2,1)S(1)}, u32[]{:S(2)}, u32[]{:S(2)}) %all-to-all-start.4) | async-done | bytes 1048608 | tf_op jit(solution)/shard_map/all_to_all | solution.py:299
  215.2 1.8 maximum_select_fusion
  (60 shorter events, 18.7 us)
Async XLA Ops:
  2.7 73.8 %all-to-all-start = ((bf16[32,4,4096]{2,0,1:T(8,128)(2,1)}), bf16[32,4,4096]{2,0,1:T(8,128)(2,1)S(1)}, u32[]{:S(2)}, u32[]{:S(2)}) async-start(bf16[32,4,4096]{2,0,1:T(8,128)(2,1)} %bitcast.42), calls=%async_computation | async-start | bytes 2097152 | tf_op jit(solution)/shard_map/all_to_all | solution.py:239
  8.0 8.3 %copy-start.6 = (s32[384]{0:T(512)S(1)}, s32[384]{0:T(512)}, u32[]{:S(2)}) copy-start(s32[384]{0:T(512)} %param.7) | copy-start | bytes 4612
  8.0 22.7 %copy-start.7 = (s32[384]{0:T(512)S(1)}, s32[384]{0:T(512)}, u32[]{:S(2)}) copy-start(s32[384]{0:T(512)} %param.8) | copy-start | bytes 4612
  10.5 18.7 %collective-permute-start.5 = (bf16[24,64,128]{2,1,0:T(8,128)(2,1)}, bf16[24,64,128]{2,1,0:T(8,128)(2,1)}, u32[]{:S(2)}, u32[]{:S(2)}) collective-permute-start(bf16[24,64,128]{2,1,0:T(8,128)(2,1)} %get-tuple-element.12), channel_id=1, source_target_pairs={{0,8},{2,10},{4,12},{6,14},{8,0},{10,2},{12,4},{14,6},{1,9},{3,11}... | collective-permute-start | bytes 1179656 | tf_op jit(solution)/shard_map/ppermute | solution.py:256
  13.0 52.9 %collective-permute-start.10 = (bf16[24,64,128]{2,1,0:T(8,128)(2,1)S(1)}, bf16[24,64,128]{2,1,0:T(8,128)(2,1)}, u32[]{:S(2)}, u32[]{:S(2)}) collective-permute-start(bf16[24,64,128]{2,1,0:T(8,128)(2,1)S(1)} %get-tuple-element.11), channel_id=1, source_target_pairs={{0,8},{2,10},{4,12},{6,14},{8,0},{10,2},{12,4},{14,6},{1,9},{3,11}... | collective-permute-start | bytes 1179656 | tf_op jit(solution)/shard_map/ppermute | solution.py:256
  13.4 60.9 %collective-permute-start.2 = (bf16[24,64,128]{2,1,0:T(8,128)(2,1)S(1)}, bf16[24,64,128]{2,1,0:T(8,128)(2,1)S(1)}, u32[]{:S(2)}, u32[]{:S(2)}) collective-permute-start(bf16[24,64,128]{2,1,0:T(8,128)(2,1)S(1)} %get-tuple-element.13), channel_id=1, source_target_pairs={{0,8},{2,10},{4,12},{6,14},{8,0},{10,2},{12,4},{14,6},{1,9},{3,11}... | collective-permute-start | bytes 1179656 | tf_op jit(solution)/shard_map/ppermute | solution.py:256
  16.0 84.8 %collective-permute-start = (bf16[24,64,128]{2,1,0:T(8,128)(2,1)}, bf16[24,64,128]{2,1,0:T(8,128)(2,1)}, u32[]{:S(2)}, u32[]{:S(2)}) collective-permute-start(bf16[24,64,128]{2,1,0:T(8,128)(2,1)} %get-tuple-element.14), channel_id=1, source_target_pairs={{0,8},{2,10},{4,12},{6,14},{8,0},{10,2},{12,4},{14,6},{1,9},{3,11}... | collective-permute-start | bytes 1179656 | tf_op jit(solution)/shard_map/ppermute | solution.py:256
  29.1 74.1 %collective-permute-start.6 = (bf16[24,64,128]{2,1,0:T(8,128)(2,1)}, bf16[24,64,128]{2,1,0:T(8,128)(2,1)}, u32[]{:S(2)}, u32[]{:S(2)}) collective-permute-start(bf16[24,64,128]{2,1,0:T(8,128)(2,1)} %collective-permute-done.5), channel_id=1, source_target_pairs={{0,16},{16,0},{1,17},{17,1},{2,18},{18,2},{3,19},{19,3},{4,20},{20... | collective-permute-start | bytes 1179656 | tf_op jit(solution)/shard_map/ppermute | solution.py:259
  31.3 69.5 %collective-permute-start.1 = (s32[769]{0:T(1024)S(1)}, s32[769]{0:T(1024)S(1)}, u32[]{:S(2)}, u32[]{:S(2)}) collective-permute-start(s32[769]{0:T(1024)S(1)} %constant_dynamic-update-slice_fusion.9.meta), channel_id=1, source_target_pairs={{0,8},{2,10},{4,12},{6,14},{8,0},{10,2},{12,4},{14,6},{1,9},{3,11}... | collective-permute-start | bytes 9236 | tf_op jit(solution)/shard_map/ppermute | solution.py:248
  65.9 39.1 %collective-permute-start.11 = (bf16[24,64,128]{2,1,0:T(8,128)(2,1)}, bf16[24,64,128]{2,1,0:T(8,128)(2,1)}, u32[]{:S(2)}, u32[]{:S(2)}) collective-permute-start(bf16[24,64,128]{2,1,0:T(8,128)(2,1)} %collective-permute-done.10), channel_id=1, source_target_pairs={{0,16},{16,0},{1,17},{17,1},{2,18},{18,2},{3,19},{19,3},{4,20},{20... | collective-permute-start | bytes 1179656 | tf_op jit(solution)/shard_map/ppermute | solution.py:259
  75.0 34.9 %collective-permute-start.3 = (bf16[24,64,128]{2,1,0:T(8,128)(2,1)S(1)}, bf16[24,64,128]{2,1,0:T(8,128)(2,1)}, u32[]{:S(2)}, u32[]{:S(2)}) collective-permute-start(bf16[24,64,128]{2,1,0:T(8,128)(2,1)S(1)} %collective-permute-done.2), channel_id=1, source_target_pairs={{0,16},{16,0},{1,17},{17,1},{2,18},{18,2},{3,19},{19,3},{4,20},{20... | collective-permute-start | bytes 1179656 | tf_op jit(solution)/shard_map/ppermute | solution.py:259
  76.5 5.3 %copy-start.2 = (bf16[32,4,4096]{2,0,1:T(8,128)(2,1)}, bf16[32,4,4096]{2,0,1:T(8,128)(2,1)S(1)}, u32[]{:S(2)}) copy-start(bf16[32,4,4096]{2,0,1:T(8,128)(2,1)S(1)} %all-to-all-done) | copy-start | bytes 3145732
  76.5 35.9 %all-to-all-start.1 = ((bf16[32,4,4096]{2,0,1:T(8,128)(2,1)}), bf16[32,4,4096]{2,0,1:T(8,128)(2,1)S(1)}, u32[]{:S(2)}, u32[]{:S(2)}) async-start(bf16[32,4,4096]{2,0,1:T(8,128)(2,1)} %bitcast.41), calls=%async_computation.1 | async-start | bytes 2097152 | tf_op jit(solution)/shard_map/all_to_all | solution.py:239
  81.8 2.8 %copy-start = (bf16[384,64,128]{2,1,0:T(8,128)(2,1)S(1)}, bf16[384,64,128]{2,1,0:T(8,128)(2,1)}, u32[]{:S(2)}) copy-start(bf16[384,64,128]{2,1,0:T(8,128)(2,1)} %rest_0_.3) | copy-start | bytes 18874372
  84.6 1.2 copy-start.3
  100.8 8.3 %collective-permute-start.8 = (bf16[24,64,128]{2,1,0:T(8,128)(2,1)}, bf16[24,64,128]{2,1,0:T(8,128)(2,1)S(1)}, u32[]{:S(2)}, u32[]{:S(2)}) collective-permute-start(bf16[24,64,128]{2,1,0:T(8,128)(2,1)} %collective-permute-done), channel_id=1, source_target_pairs={{0,16},{16,0},{1,17},{17,1},{2,18},{18,2},{3,19},{19,3},{4,20},{20... | collective-permute-start | bytes 1179656 | tf_op jit(solution)/shard_map/ppermute | solution.py:259
  105.0 12.6 %collective-permute-start.7 = (bf16[48,64,128]{2,1,0:T(8,128)(2,1)}, bf16[48,64,128]{2,1,0:T(8,128)(2,1)}, u32[]{:S(2)}, u32[]{:S(2)}) collective-permute-start(bf16[48,64,128]{2,1,0:T(8,128)(2,1)} %constant_dynamic-update-slice_fusion.3.rest_0_.rest_4_), channel_id=1, source_target_pairs={{0,1},{1,0},{2,3},{3,2},{4,5},{5,4},{6,7},{7,6},{8,9},{9,8},{10,11... | collective-permute-start | bytes 2359304 | tf_op jit(solution)/shard_map/ppermute | solution.py:260
  106.8 5.7 %collective-permute-start.12 = (bf16[48,64,128]{2,1,0:T(8,128)(2,1)}, bf16[48,64,128]{2,1,0:T(8,128)(2,1)}, u32[]{:S(2)}, u32[]{:S(2)}) collective-permute-start(bf16[48,64,128]{2,1,0:T(8,128)(2,1)} %constant_dynamic-update-slice_fusion.7.rest_2_), channel_id=1, source_target_pairs={{0,1},{1,0},{2,3},{3,2},{4,5},{5,4},{6,7},{7,6},{8,9},{9,8},{10,11... | collective-permute-start | bytes 2359304 | tf_op jit(solution)/shard_map/ppermute | solution.py:260
  109.9 2.6 %collective-permute-start.9 = (bf16[48,64,128]{2,1,0:T(8,128)(2,1)}, bf16[48,64,128]{2,1,0:T(8,128)(2,1)}, u32[]{:S(2)}, u32[]{:S(2)}) collective-permute-start(bf16[48,64,128]{2,1,0:T(8,128)(2,1)} %constant_dynamic-update-slice_fusion.5.rest_0_), channel_id=1, source_target_pairs={{0,1},{1,0},{2,3},{3,2},{4,5},{5,4},{6,7},{7,6},{8,9},{9,8},{10,11... | collective-permute-start | bytes 2359304 | tf_op jit(solution)/shard_map/ppermute | solution.py:260
  111.7 8.1 %collective-permute-start.4 = (bf16[48,64,128]{2,1,0:T(8,128)(2,1)}, bf16[48,64,128]{2,1,0:T(8,128)(2,1)}, u32[]{:S(2)}, u32[]{:S(2)}) collective-permute-start(bf16[48,64,128]{2,1,0:T(8,128)(2,1)} %constant_dynamic-update-slice_fusion.1.rest_0_.rest_6_), channel_id=1, source_target_pairs={{0,1},{1,0},{2,3},{3,2},{4,5},{5,4},{6,7},{7,6},{8,9},{9,8},{10,11... | collective-permute-start | bytes 2359304 | tf_op jit(solution)/shard_map/ppermute | solution.py:260
  123.0 3.7 %copy-start.5 = (f32[32,16,8,8]{0,3,2,1:T(8,128)S(1)}, f32[32,16,8,8]{0,3,2,1:T(8,128)}, u32[]{:S(2)}) copy-start(f32[32,16,8,8]{0,3,2,1:T(8,128)} %param.11) | copy-start | bytes 393220
  123.0 17.8 %all-to-all-start.2 = ((bf16[4,32,4096]{2,1,0:T(8,128)(2,1)}), bf16[4,32,4096]{2,1,0:T(8,128)(2,1)S(1)}, u32[]{:S(2)}, u32[]{:S(2)}) async-start(bf16[4,32,4096]{2,1,0:T(8,128)(2,1)} %bitcast.21), calls=%async_computation.2 | async-start | bytes 2097152 | tf_op jit(solution)/shard_map/all_to_all | solution.py:280
  128.9 2.2 %copy-start.4 = (f32[32,128,128]{2,1,0:T(8,128)S(1)}, f32[32,128,128]{2,1,0:T(8,128)}, u32[]{:S(2)}) copy-start(f32[32,128,128]{2,1,0:T(8,128)} %copy.19) | copy-start | bytes 6291460
  142.9 17.3 %all-to-all-start.3 = ((bf16[4,32,4096]{2,1,0:T(8,128)(2,1)}), bf16[4,32,4096]{2,1,0:T(8,128)(2,1)S(1)}, u32[]{:S(2)}, u32[]{:S(2)}) async-start(bf16[4,32,4096]{2,1,0:T(8,128)(2,1)} %broadcast_in_dim.23), calls=%async_computation.3 | async-start | bytes 2097152 | tf_op jit(solution)/shard_map/all_to_all | solution.py:289
  168.0 29.8 %all-to-all-start.5 = ((bf16[4,32,4096]{2,1,0:T(8,128)(2,1)}), bf16[4,32,4096]{2,1,0:T(8,128)(2,1)S(1)}, u32[]{:S(2)}, u32[]{:S(2)}) async-start(bf16[4,32,4096]{2,1,0:T(8,128)(2,1)} %bitcast.27), calls=%async_computation.5 | async-start | bytes 2097152 | tf_op jit(solution)/shard_map/all_to_all | solution.py:299
  176.0 2.8 %copy-start.1 = (bf16[384,64,128]{2,1,0:T(8,128)(2,1)S(1)}, bf16[384,64,128]{2,1,0:T(8,128)(2,1)}, u32[]{:S(2)}) copy-start(bf16[384,64,128]{2,1,0:T(8,128)(2,1)} %rest_0_.3) | copy-start | bytes 18874372
  197.8 17.3 %all-to-all-start.4 = ((bf16[4,32,4096]{2,1,0:T(8,128)(2,1)}), bf16[4,32,4096]{2,1,0:T(8,128)(2,1)S(1)}, u32[]{:S(2)}, u32[]{:S(2)}) async-start(bf16[4,32,4096]{2,1,0:T(8,128)(2,1)} %bitcast.25), calls=%async_computation.4 | async-start | bytes 2097152 | tf_op jit(solution)/shard_map/all_to_all | solution.py:299

commit v5 on v3

v5 whole, which is shorter than its diff:
```python
import functools

import jax
import jax.numpy as jnp
from jax import lax
from jax.experimental import pallas as pl
from jax.experimental.pallas import tpu as pltpu
from jax.sharding import PartitionSpec as P

TILE = 64
PAIR = 2 * TILE
UNROLL = 8
HEAD = 3
VMEM_LIMIT = 24 * 1024 * 1024


def padded_tile(values, half):
    zero = jnp.zeros_like(values)
    return jnp.concatenate(
        [jnp.where(half == 0, values, zero), jnp.where(half == 1, values, zero)], axis=0
    )


def diagonal(first, second):
    zero = jnp.zeros_like(first)
    return jnp.concatenate(
        [jnp.concatenate([first, zero], axis=1), jnp.concatenate([zero, second], axis=1)], axis=0
    )


def tile_loop(meta, tiles, ref, base, size, step):
    live = jnp.clip(meta[2 * tiles] - base, 0, size)

    def group(index, carry):
        for pair in range(0, UNROLL, 2):
            places = []
            for lane in (pair, pair + 1):
                local = index * UNROLL + lane
                segment = meta[base + local]
                block = meta[tiles + base + local]
                half = jnp.where(local < live, segment % 2, 2)
                places.append((block, segment // 2, padded_tile(ref[local], half)))
            step(*places)
        return carry

    lax.fori_loop(0, (live + UNROLL - 1) // UNROLL, group, 0)


def tile_points(place, column):
    return pl.ds(pl.multiple_of(column + place[1] * PAIR, PAIR), PAIR)


def all_tiles(meta, tiles, pieces, step):
    if len(pieces) == 1:
        size = pieces[0].shape[0]
        tile_loop(meta, tiles, pieces[0], pl.program_id(0) * size, size, step)
        return
    for number, ref in enumerate(pieces):
        tile_loop(meta, tiles, ref, meta[2 * tiles + HEAD + number], ref.shape[0], step)


def rows_of(refs, lanes):
    return jnp.concatenate([ref[:, lanes] for ref in refs], axis=0)


def store_rows(refs, values):
    start = 0
    for ref in refs:
        rows = ref.shape[0]
        ref[...] = values[start : start + rows].astype(ref.dtype)
        start += rows


def project_kernel(tiles, n_pieces, first, last, meta, wave, *refs):
    pieces, refs = refs[:n_pieces], refs[n_pieces:]
    total = refs[-1]
    proj = pieces[0].shape[2]
    side, place = meta[2 * tiles + 1], meta[2 * tiles + 2]
    column = side * (wave.shape[1] // 2)

    @pl.when(pl.program_id(0) == 0)
    def start():
        total[...] = jnp.zeros_like(total) if first else refs[0][...]

    def step(first, second):
        values = jnp.concatenate([wave[:, tile_points(place, column)] for place in (first, second)], axis=1)
        terms = jnp.dot(values, diagonal(first[2], second[2]), preferred_element_type=jnp.float32)
        for index, place in enumerate((first, second)):
            lanes = pl.ds(pl.multiple_of(place[0] * proj, proj), proj)
            total[:, lanes] += terms[:, index * proj : (index + 1) * proj]

    all_tiles(meta, tiles, pieces, step)
    if last:
        outs = refs[1:-1]
        rows = outs[0].shape[0]
        for d, out in enumerate(outs):
            start = 0 if len(outs) == 1 else pl.multiple_of((place ^ d) * rows, rows)
            out[...] = total[pl.ds(start, rows), :].astype(out.dtype)


def spread_kernel(tiles, n_rows, n_pieces, meta, *refs):
    applied, refs = refs[:n_rows], refs[n_rows:]
    pieces, refs = refs[:n_pieces], refs[n_pieces:]
    outs, field = refs[:-1], refs[-1]
    proj = pieces[0].shape[2]

    @pl.when(pl.program_id(0) == 0)
    def start():
        field[...] = jnp.zeros_like(field)

    def step(first, second):
        lanes = [pl.ds(pl.multiple_of(place[0] * proj, proj), proj) for place in (first, second)]
        terms = lax.dot_general(
            jnp.concatenate([rows_of(applied, lanes[0]), rows_of(applied, lanes[1])], axis=1),
            diagonal(first[2], second[2]),
            (((1,), (1,)), ((), ())),
            preferred_element_type=jnp.float32,
        )
        for index, place in enumerate((first, second)):
            field[:, tile_points(place, 0)] += terms[:, index * PAIR : (index + 1) * PAIR]

    all_tiles(meta, tiles, pieces, step)

    @pl.when(pl.program_id(0) == pl.num_programs(0) - 1)
    def finish():
        store_rows(outs, field)


def tile_chunk(tiles):
    for chunk in (96, 64, 48, 32, 16, 8):
        if tiles % chunk == 0:
            return chunk
    return tiles


WHOLE = pl.BlockSpec(memory_space=pltpu.VMEM)


def piece_specs(tiles, pieces):
    if len(pieces) > 1:
        return 1, [WHOLE] * len(pieces)
    chunk = tile_chunk(tiles)

    def index(step, meta):
        last = (meta[2 * tiles] + chunk - 1) // chunk - 1
        return (jnp.clip(step, 0, jnp.maximum(last, 0)), 0, 0)

    return tiles // chunk, [pl.BlockSpec((chunk,) + pieces[0].shape[1:], index)]


COST = pl.CostEstimate(flops=1, bytes_accessed=1, transcendentals=0)


def join_small(blocks):
    return blocks if blocks[0].shape[0] % 16 == 0 else [jnp.concatenate(blocks)]


def split_small(blocks, count):
    return blocks if len(blocks) == count else jnp.split(blocks[0], count)


def project(tiles, meta, wave, pieces, count, width, total=None, last=False):
    rows = wave.shape[0]
    bands = rows // count
    split = bands % 16 == 0
    steps, specs = piece_specs(tiles, pieces)
    operands = [wave, *pieces] + ([] if total is None else [total])
    in_specs = [WHOLE] + specs + [WHOLE] * (total is not None)
    outs = count if split else 1
    out_shape = [jax.ShapeDtypeStruct((rows // outs, width), jnp.bfloat16)] * outs
    return pl.pallas_call(
        functools.partial(project_kernel, tiles, len(pieces), total is None, last),
        grid_spec=pltpu.PrefetchScalarGridSpec(
            num_scalar_prefetch=1,
            grid=(steps,),
            in_specs=in_specs,
            out_specs=[WHOLE] * outs if last else WHOLE,
            scratch_shapes=[pltpu.VMEM((rows, width), jnp.float32)] if last else [],
        ),
        out_shape=out_shape if last else jax.ShapeDtypeStruct((rows, width), jnp.float32),
        compiler_params=pltpu.CompilerParams(vmem_limit_bytes=VMEM_LIMIT),
        cost_estimate=COST,
    )(meta, *operands)


def spread(tiles, meta, applied, pieces, points):
    count = len(applied)
    applied = join_small(applied)
    rows = sum(block.shape[0] for block in applied)
    steps, specs = piece_specs(tiles, pieces)
    result = pl.pallas_call(
        functools.partial(spread_kernel, tiles, len(applied), len(pieces)),
        grid_spec=pltpu.PrefetchScalarGridSpec(
            num_scalar_prefetch=1,
            grid=(steps,),
            in_specs=[WHOLE] * len(applied) + specs,
            out_specs=[WHOLE] * len(applied),
            scratch_shapes=[pltpu.VMEM((rows, points), jnp.float32)],
        ),
        out_shape=[
            jax.ShapeDtypeStruct((block.shape[0], points), jnp.bfloat16) for block in applied
        ],
        compiler_params=pltpu.CompilerParams(vmem_limit_bytes=VMEM_LIMIT),
        cost_estimate=COST,
    )(meta, *applied, *pieces)
    return split_small(result, count)


def two_parts(values):
    high = values.astype(jnp.bfloat16)
    return high, (values - high.astype(jnp.float32)).astype(jnp.bfloat16)


def couple_kernel(high_ref, low_ref, *refs):
    parts, out_ref = refs[:-1], refs[-1]
    blocks, proj, unused = high_ref.shape
    for block in range(blocks):
        lanes = slice(block * proj, (block + 1) * proj)
        total = parts[0][:, lanes].astype(jnp.float32)
        for part in parts[1:]:
            total += part[:, lanes].astype(jnp.float32)
        high, low = two_parts(total)
        result = jnp.dot(high, high_ref[block], preferred_element_type=jnp.float32)
        result += jnp.dot(high, low_ref[block], preferred_element_type=jnp.float32)
        result += jnp.dot(low, high_ref[block], preferred_element_type=jnp.float32)
        out_ref[:, lanes] = result.astype(out_ref.dtype)


def couple(parts, high, low):
    return pl.pallas_call(
        couple_kernel,
        in_specs=[WHOLE] * (2 + len(parts)),
        out_specs=WHOLE,
        out_shape=jax.ShapeDtypeStruct(parts[0].shape, jnp.bfloat16),
        compiler_params=pltpu.CompilerParams(vmem_limit_bytes=VMEM_LIMIT),
        cost_estimate=COST,
    )(high, low, *parts)


def coupling_matrix(coupling):
    blocks, atoms, width, unused = coupling.shape
    proj = atoms * width
    wide = jnp.tile(coupling.reshape(blocks, proj, width), (1, 1, atoms))
    same = jnp.arange(proj)[:, None] // width == jnp.arange(proj)[None, :] // width
    return jnp.where(same[None], wide, 0.0)


def body(n_grid, wavefunctions, tile_segment, tile_block, tile_count, projectors, coupling):
    half = n_grid // 2
    bands, npts = wavefunctions.shape
    points = npts // n_grid
    tiles = projectors.shape[0]
    width = coupling.shape[0] * projectors.shape[2]
    index = lax.axis_index("grid")
    side, place = index // half, index % half
    group, core = lax.axis_index("groups"), lax.axis_index("band")
    partners = [(i, (i + half) % n_grid) for i in range(n_grid)]
    swap = [(0, 1), (1, 0)]

    def exchange(blocks):
        return [blocks[0]] + [
            lax.ppermute(
                blocks[d], "grid", [(i, i // half * half + (i % half ^ d)) for i in range(n_grid)]
            )
            for d in range(1, half)
        ]

    waves = wavefunctions.reshape(bands, 2, half, points).transpose(2, 0, 1, 3)
    waves = lax.all_to_all(
        waves.reshape(half, bands, 2 * points),
        "grid",
        split_axis=0,
        concat_axis=0,
        tiled=True,
        axis_index_groups=[list(range(half)), list(range(half, n_grid))],
    ).reshape(half * bands, 2 * points)

    lists = jnp.concatenate([tile_segment, tile_block, tile_count])
    other_lists = lax.ppermute(lists, "grid", partners)
    meta = jnp.concatenate([lists, jnp.stack([side, place])])
    total = project(tiles, meta, waves, [projectors], half, width)

    pieces, bases = [], []
    parts = 4
    size = tiles // parts
    share = size // 4
    for part in range(parts):
        mine = lax.dynamic_slice_in_dim(
            projectors, part * size + (2 * group + core) * share, share, 0
        )
        mine = lax.ppermute(mine, "grid", partners)
        if part > 0:
            mine, total, other_lists = lax.optimization_barrier((mine, total, other_lists))
        across = lax.ppermute(mine, "groups", swap)
        pieces += [mine, across, lax.ppermute(mine, "band", swap), lax.ppermute(across, "band", swap)]
        for other_core in (core, 1 - core):
            for other_group in (group, 1 - group):
                bases.append(part * size + (2 * other_group + other_core) * share)

    matrix = two_parts(coupling_matrix(coupling))
    other_meta = jnp.concatenate([other_lists, jnp.stack([1 - side, place] + bases)])
    for first, end in ((0, 2), (2, 3), (3, 4)):
        skip = 2 * tiles + HEAD
        piece_meta = jnp.concatenate(
            [other_meta[:skip], other_meta[skip + 4 * first : skip + 4 * end]]
        )
        total = project(
            tiles,
            piece_meta,
            waves,
            pieces[4 * first : 4 * end],
            half,
            width,
            total,
            last=end == parts,
        )
    if len(total) < half:
        total = [lax.dynamic_slice_in_dim(total[0], (place ^ d) * bands, bands, 0) for d in range(half)]

    applied = couple(exchange(total), *matrix)
    applied = exchange([applied] * half)

    result = jnp.zeros((bands, npts), jnp.bfloat16)
    for which, field in (
        (1 - side, spread(tiles, other_meta, applied, pieces, points)),
        (side, spread(tiles, meta, applied, [projectors], points)),
    ):
        for d, block in enumerate(exchange(field)):
            start = (which * half + (place ^ d)) * points
            result = lax.dynamic_update_slice_in_dim(result, block, start, 1)
    return result


def solution(mesh):
    in_specs = (
        P(("groups", "grid", "band"), None),
        P("grid"),
        P("grid"),
        P("grid"),
        P("grid", None, None),
        P(),
    )
    out_specs = P(("groups", "grid", "band"), None)
    return jax.shard_map(
        functools.partial(body, mesh.shape["grid"]),
        mesh=mesh,
        in_specs=in_specs,
        out_specs=out_specs,
        check_vma=False,
    )
```

time: 230 us -> 229 us (level)
  the two profiles are of different devices: /device:TPU:0 before, /device:TPU:18 now
where the time goes in v5:
time: 229 us; the launch traced here: 227 us
  waiting for transfers between devices  106 us (46%)
  starting transfers between devices  54.3 us (24%)
  local copies, waits for them, and re-layouts  33.7 us (15%)
  Pallas kernels  28.8 us (13%)
  other arithmetic  2.85 us (1%)
    ppermute x4, waiting for transfers between devices, body(): mine = lax.ppermute(mine, 'grid', partners)  61.4 us
    ppermute x12, starting transfers between devices, exchange(): lax.ppermute(blocks[d], 'grid', [(i, i // half * half + (i % half ^ d)) f...  39.4 us
    ppermute x12, waiting for transfers between devices, exchange(): lax.ppermute(blocks[d], 'grid', [(i, i // half * half + (i % half ^ d)) f...  31.8 us
    pallas_call x4, Pallas kernels, project(): pl.pallas_call(functools.partial(project_kernel, tiles, len(pieces), tota...  14.8 us
    ppermute x4, waiting for transfers between devices, body(): across = lax.ppermute(mine, 'groups', swap)  13.2 us
    pallas_call x2, Pallas kernels, spread(): pl.pallas_call(functools.partial(spread_kernel, tiles, len(applied), len(...  13.1 us
    unnamed x38, local copies, waits for them, and re-layouts  12.5 us
    another operation x3, local copies, waits for them, and re-layouts, coupling_matrix(): wide = jnp.tile(coupling.reshape(blocks, proj, width), (1, 1, atoms))  5.59 us
  transfers between devices with their start and end apart: 30, of which 14 were waited for; matrix products, arithmetic and copies ran while one was open for 5% of the time, Pallas kernels for 9%

profile of v5, /device:TPU:18, one launch (start us, length us, event | category | flops | bytes accessed | tf_op | source)
XLA Modules:
  0.0 227.0 jit_solution(4771960367733309408)
XLA Ops:
  0.0 4.5 %reshape.114 = bf16[32,2,4,4096]{3,2,1,0:T(4,128)(2,1)} reshape(bf16[32,32768]{1,0:T(8,128)(2,1)} %param.6) | data formatting | bytes 4194304 | tf_op jit(solution)/shard_map/reshape | solution.py:268
  4.5 3.8 %copy.9 = bf16[4,32,2,4096]{3,2,1,0:T(2,128)(2,1)S(1)} copy(bf16[4,32,2,4096]{3,0,2,1:T(4,128)(2,1)} %bitcast.28) | data formatting | bytes 4194304 | tf_op jit(solution)/shard_map/transpose | solution.py:268
  8.3 2.8 %reshape.115 = bf16[4,32,8192]{2,1,0:T(8,128)(2,1)} reshape(bf16[4,32,2,4096]{3,2,1,0:T(2,128)(2,1)S(1)} %copy.9) | data formatting | bytes 4194304 | tf_op jit(solution)/shard_map/reshape | solution.py:270
  11.1 3.8 %all-to-all-start = ((bf16[4,32,8192]{2,1,0:T(8,128)(2,1)}), bf16[4,32,8192]{2,1,0:T(8,128)(2,1)S(1)}, u32[]{:S(2)}, u32[]{:S(2)}) async-start(bf16[4,32,8192]{2,1,0:T(8,128)(2,1)} %reshape.115), calls=%async_computation | async-start | bytes 4194304 | tf_op jit(solution)/shard_map/all_to_all | solution.py:269
  14.9 2.4 %constant_dynamic-slice_fusion = (bf16[24,64,128]{2,1,0:T(8,128)(2,1)S(1)}, bf16[24,64,128]{2,1,0:T(8,128)(2,1)}, bf16[24,64,128]{2,1,0:T(8,128)(2,1)}, bf16[24,64,128]{2,1,0:T(8,128)(2,1)}) fusion(bf16[384,64,128]{2,1,0:T(8,128)(2,1)} %refs_4_.1, s32[]{:T(128)S(6)} %select_n.76, s32[]{:T(128)S(6)} %select_n.71, s32[]{:T(128)S(6)} %select_n.70, s32[]{:T(128)S(6)} %select_n.69), kind=kLoop, calls=%fused_computation.13 | loop fusion | bytes 3145744 | tf_op jit(solution)/shard_map/dynamic_slice | solution.py:288
  18.3 2.7 %collective-permute-start.3 = (s32[769]{0:T(1024)S(1)}, s32[769]{0:T(1024)S(1)}, u32[]{:S(2)}, u32[]{:S(2)}) collective-permute-start(s32[769]{0:T(1024)S(1)} %pad_add_fusion), channel_id=1, source_target_pairs={{0,8},{2,10},{4,12},{6,14},{8,0},{10,2},{12,4},{14,6},{1,9},{3,11}... | collective-permute-start | bytes 9236 | tf_op jit(solution)/shard_map/ppermute | solution.py:279
  21.0 25.9 %collective-permute-done.10.refs_0_.refs_4_ = bf16[24,64,128]{2,1,0:T(8,128)(2,1)S(1)} collective-permute-done((bf16[24,64,128]{2,1,0:T(8,128)(2,1)S(1)}, bf16[24,64,128]{2,1,0:T(8,128)(2,1)S(1)}, u32[]{:S(2)}, u32[]{:S(2)}) %collective-permute-start.10) | collective-permute-done | bytes 393248 | tf_op jit(solution)/shard_map/ppermute | solution.py:291
  47.4 2.9 %collective-permute-start.1 = (bf16[24,64,128]{2,1,0:T(8,128)(2,1)}, bf16[24,64,128]{2,1,0:T(8,128)(2,1)}, u32[]{:S(2)}, u32[]{:S(2)}) collective-permute-start(bf16[24,64,128]{2,1,0:T(8,128)(2,1)} %get-tuple-element.49), channel_id=1, source_target_pairs={{0,8},{2,10},{4,12},{6,14},{8,0},{10,2},{12,4},{14,6},{1,9},{3,11}... | collective-permute-start | bytes 1179656 | tf_op jit(solution)/shard_map/ppermute | solution.py:291
  50.5 2.8 %copy-done = bf16[384,64,128]{2,1,0:T(8,128)(2,1)S(1)} copy-done((bf16[384,64,128]{2,1,0:T(8,128)(2,1)S(1)}, bf16[384,64,128]{2,1,0:T(8,128)(2,1)}, u32[]{:S(2)}) %copy-start) | copy-done | bytes 6291480
  53.3 5.9 %shard_map.64.refs_8_ = f32[128,4096]{1,0:T(8,128)S(1)} custom-call(s32[771]{0:T(1024)S(1)} %concatenate.30.meta, bf16[128,8192]{1,0:T(8,128)(2,1)S(1)} %bitcast.24, bf16[384,64,128]{2,1,0:T(8,128)(2,1)S(1)} %copy-done), custom_call_target="tpu_custom_call" | custom-call | flops 1 | bytes 1 | tf_op jit(solution)/shard_map/pallas_call | solution.py:171
  60.9 21.6 %collective-permute-done.2.refs_4_.refs_8_ = bf16[24,64,128]{2,1,0:T(8,128)(2,1)S(1)} collective-permute-done((bf16[24,64,128]{2,1,0:T(8,128)(2,1)}, bf16[24,64,128]{2,1,0:T(8,128)(2,1)S(1)}, u32[]{:S(2)}, u32[]{:S(2)}) %collective-permute-start.2) | collective-permute-done | bytes 393248 | tf_op jit(solution)/shard_map/ppermute | solution.py:291
  84.1 6.9 %collective-permute-done.1.refs_0_.refs_12_ = bf16[24,64,128]{2,1,0:T(8,128)(2,1)} collective-permute-done((bf16[24,64,128]{2,1,0:T(8,128)(2,1)}, bf16[24,64,128]{2,1,0:T(8,128)(2,1)}, u32[]{:S(2)}, u32[]{:S(2)}) %collective-permute-start.1) | collective-permute-done | bytes 393248 | tf_op jit(solution)/shard_map/ppermute | solution.py:291
  91.0 7.0 %collective-permute-done.refs_0_.refs_16_ = bf16[24,64,128]{2,1,0:T(8,128)(2,1)} collective-permute-done((bf16[24,64,128]{2,1,0:T(8,128)(2,1)}, bf16[24,64,128]{2,1,0:T(8,128)(2,1)}, u32[]{:S(2)}, u32[]{:S(2)}) %collective-permute-start) | collective-permute-done | bytes 393248 | tf_op jit(solution)/shard_map/ppermute | solution.py:291
  103.3 7.0 %collective-permute-done.7.refs_1_.refs_13_ = bf16[24,64,128]{2,1,0:T(8,128)(2,1)} collective-permute-done((bf16[24,64,128]{2,1,0:T(8,128)(2,1)}, bf16[24,64,128]{2,1,0:T(8,128)(2,1)}, u32[]{:S(2)}, u32[]{:S(2)}) %collective-permute-start.7) | collective-permute-done | bytes 393248 | tf_op jit(solution)/shard_map/ppermute | solution.py:294
  110.3 6.1 %collective-permute-done.4.refs_1_.refs_17_ = bf16[24,64,128]{2,1,0:T(8,128)(2,1)} collective-permute-done((bf16[24,64,128]{2,1,0:T(8,128)(2,1)}, bf16[24,64,128]{2,1,0:T(8,128)(2,1)}, u32[]{:S(2)}, u32[]{:S(2)}) %collective-permute-start.4) | collective-permute-done | bytes 393248 | tf_op jit(solution)/shard_map/ppermute | solution.py:294
  117.1 2.9 %copy.11 = f32[32,128,128]{2,1,0:T(8,128)} copy(f32[32,128,128]{1,2,0:T(8,128)} %broadcast_bitcast_fusion) | data formatting | bytes 4194304 | tf_op jit(solution)/shard_map/tile | solution.py:243
  126.4 4.4 %shard_map.65.refs_4_ = f32[128,4096]{1,0:T(8,128)S(1)} custom-call(s32[779]{0:T(1024)S(1)} %concatenate.35.meta, bf16[128,8192]{1,0:T(8,128)(2,1)S(1)} %bitcast.25, bf16[24,64,128]{2,1,0:T(8,128)(2,1)S(1)} %collective-permute-done.10.refs_0_.refs_4_, bf16[24,64,128]{2,1,0:T(8,128)(2,1)S(1)} %copy-done.7, ...), custom_call_target="tpu_custom_call" | custom-call | flops 1 | bytes 1 | tf_op jit(solution)/shard_map/pallas_call | solution.py:171
  130.8 2.1 shard_map.66.refs_4_
  133.0 2.4 %shard_map.67 = (bf16[32,4096]{1,0:T(8,128)(2,1)S(1)}, bf16[32,4096]{1,0:T(8,128)(2,1)S(1)}, bf16[32,4096]{1,0:T(8,128)(2,1)S(1)}, bf16[32,4096]{1,0:T(8,128)(2,1)S(1)}) custom-call(s32[775]{0:T(1024)S(1)} %concatenate.33.meta, bf16[128,8192]{1,0:T(8,128)(2,1)S(1)} %bitcast.27, bf16[24,64,128]{2,1,0:T(8,128)(2,1)} %collective-permute-done.refs_0_.refs_16_, ...), custom_call_target="tpu_custom_call" | custom-call | flops 1 | bytes 1 | tf_op jit(solution)/shard_map/pallas_call | solution.py:171
  135.4 13.2 %collective-permute-start.17 = (bf16[32,4096]{1,0:T(8,128)(2,1)S(1)}, bf16[32,4096]{1,0:T(8,128)(2,1)S(1)}, u32[]{:S(2)}, u32[]{:S(2)}) collective-permute-start(bf16[32,4096]{1,0:T(8,128)(2,1)S(1)} %get-tuple-element.36), channel_id=1, source_target_pairs={{0,2},{2,0},{4,6},{6,4},{8,10},{10,8},{12,14},{14,12},{1,3},{3,1},... | collective-permute-start | bytes 786440 | tf_op jit(solution)/shard_map/ppermute | solution.py:262
  150.5 5.1 %collective-permute-done.17.refs_1_ = bf16[32,4096]{1,0:T(8,128)(2,1)S(1)} collective-permute-done((bf16[32,4096]{1,0:T(8,128)(2,1)S(1)}, bf16[32,4096]{1,0:T(8,128)(2,1)S(1)}, u32[]{:S(2)}, u32[]{:S(2)}) %collective-permute-start.17) | collective-permute-done | bytes 262176 | tf_op jit(solution)/shard_map/ppermute | solution.py:262
  155.6 2.2 collective-permute-done.18.refs_2_
  157.8 4.7 %collective-permute-done.19.refs_3_ = bf16[32,4096]{1,0:T(8,128)(2,1)S(1)} collective-permute-done((bf16[32,4096]{1,0:T(8,128)(2,1)S(1)}, bf16[32,4096]{1,0:T(8,128)(2,1)S(1)}, u32[]{:S(2)}, u32[]{:S(2)}) %collective-permute-start.19) | collective-permute-done | bytes 262176 | tf_op jit(solution)/shard_map/ppermute | solution.py:262
  167.0 4.7 %collective-permute-done.20.refs_1_ = bf16[32,4096]{1,0:T(8,128)(2,1)S(1)} collective-permute-done((bf16[32,4096]{1,0:T(8,128)(2,1)S(1)}, bf16[32,4096]{1,0:T(8,128)(2,1)S(1)}, u32[]{:S(2)}, u32[]{:S(2)}) %collective-permute-start.20) | collective-permute-done | bytes 262176 | tf_op jit(solution)/shard_map/ppermute | solution.py:262
  171.8 2.6 %collective-permute-done.21.refs_2_ = bf16[32,4096]{1,0:T(8,128)(2,1)S(1)} collective-permute-done((bf16[32,4096]{1,0:T(8,128)(2,1)S(1)}, bf16[32,4096]{1,0:T(8,128)(2,1)S(1)}, u32[]{:S(2)}, u32[]{:S(2)}) %collective-permute-start.21) | collective-permute-done | bytes 262176 | tf_op jit(solution)/shard_map/ppermute | solution.py:262
  174.4 3.8 %collective-permute-done.22.refs_3_ = bf16[32,4096]{1,0:T(8,128)(2,1)S(1)} collective-permute-done((bf16[32,4096]{1,0:T(8,128)(2,1)S(1)}, bf16[32,4096]{1,0:T(8,128)(2,1)S(1)}, u32[]{:S(2)}, u32[]{:S(2)}) %collective-permute-start.22) | collective-permute-done | bytes 262176 | tf_op jit(solution)/shard_map/ppermute | solution.py:262
  180.2 6.0 %shard_map.69 = (bf16[32,4096]{1,0:T(8,128)(2,1)S(1)}, bf16[32,4096]{1,0:T(8,128)(2,1)S(1)}, bf16[32,4096]{1,0:T(8,128)(2,1)S(1)}, bf16[32,4096]{1,0:T(8,128)(2,1)S(1)}) custom-call(s32[787]{0:T(1024)S(1)} %concatenate.32.meta, bf16[32,4096]{1,0:T(8,128)(2,1)S(1)} %shard_map.68.refs_0_, bf16[32,4096]{1,0:T(8,128)(2,1)S(1)} %collective-permute-done.20.refs_1_, ...), custom_call_target="tpu_custom_call" | custom-call | flops 1 | bytes 1 | tf_op jit(solution)/shard_map/pallas_call | solution.py:191
  186.2 16.0 %collective-permute-start.23 = (bf16[32,4096]{1,0:T(8,128)(2,1)S(1)}, bf16[32,4096]{1,0:T(8,128)(2,1)S(1)}, u32[]{:S(2)}, u32[]{:S(2)}) collective-permute-start(bf16[32,4096]{1,0:T(8,128)(2,1)S(1)} %get-tuple-element.40), channel_id=1, source_target_pairs={{0,2},{2,0},{4,6},{6,4},{8,10},{10,8},{12,14},{14,12},{1,3},{3,1},... | collective-permute-start | bytes 786440 | tf_op jit(solution)/shard_map/ppermute | solution.py:262
  203.7 2.8 %copy-done.1 = bf16[384,64,128]{2,1,0:T(8,128)(2,1)S(1)} copy-done((bf16[384,64,128]{2,1,0:T(8,128)(2,1)S(1)}, bf16[384,64,128]{2,1,0:T(8,128)(2,1)}, u32[]{:S(2)}) %copy-start.1) | copy-done | bytes 6291480
  206.5 7.1 %shard_map.70 = (bf16[32,4096]{1,0:T(8,128)(2,1)S(1)}, bf16[32,4096]{1,0:T(8,128)(2,1)S(1)}, bf16[32,4096]{1,0:T(8,128)(2,1)S(1)}, bf16[32,4096]{1,0:T(8,128)(2,1)S(1)}) custom-call(s32[771]{0:T(1024)S(1)} %concatenate.30.meta, bf16[32,4096]{1,0:T(8,128)(2,1)S(1)} %shard_map.68.refs_0_, bf16[32,4096]{1,0:T(8,128)(2,1)S(1)} %collective-permute-done.20.refs_1_, ...), custom_call_target="tpu_custom_call" | custom-call | flops 1 | bytes 1 | tf_op jit(solution)/shard_map/pallas_call | solution.py:191
  217.5 5.3 %collective-permute-done.26 = bf16[32,4096]{1,0:T(8,128)(2,1)S(1)} collective-permute-done((bf16[32,4096]{1,0:T(8,128)(2,1)S(1)}, bf16[32,4096]{1,0:T(8,128)(2,1)S(1)}, u32[]{:S(2)}, u32[]{:S(2)}) %collective-permute-start.26) | collective-permute-done | bytes 262176 | tf_op jit(solution)/shard_map/ppermute | solution.py:262
  222.9 3.4 %collective-permute-done.28 = bf16[32,4096]{1,0:T(8,128)(2,1)S(1)} collective-permute-done((bf16[32,4096]{1,0:T(8,128)(2,1)S(1)}, bf16[32,4096]{1,0:T(8,128)(2,1)S(1)}, u32[]{:S(2)}, u32[]{:S(2)}) %collective-permute-start.28) | collective-permute-done | bytes 262176 | tf_op jit(solution)/shard_map/ppermute | solution.py:262
  (99 shorter events, 31.3 us)
Async XLA Ops:
  11.1 39.4 %all-to-all-start = ((bf16[4,32,8192]{2,1,0:T(8,128)(2,1)}), bf16[4,32,8192]{2,1,0:T(8,128)(2,1)S(1)}, u32[]{:S(2)}, u32[]{:S(2)}) async-start(bf16[4,32,8192]{2,1,0:T(8,128)(2,1)} %reshape.115), calls=%async_computation | async-start | bytes 4194304 | tf_op jit(solution)/shard_map/all_to_all | solution.py:269
  17.3 29.6 %collective-permute-start.10 = (bf16[24,64,128]{2,1,0:T(8,128)(2,1)S(1)}, bf16[24,64,128]{2,1,0:T(8,128)(2,1)S(1)}, u32[]{:S(2)}, u32[]{:S(2)}) collective-permute-start(bf16[24,64,128]{2,1,0:T(8,128)(2,1)S(1)} %get-tuple-element.47), channel_id=1, source_target_pairs={{0,8},{2,10},{4,12},{6,14},{8,0},{10,2},{12,4},{14,6},{1,9},{3,11}... | collective-permute-start | bytes 1179656 | tf_op jit(solution)/shard_map/ppermute | solution.py:291
  18.3 32.0 %collective-permute-start.3 = (s32[769]{0:T(1024)S(1)}, s32[769]{0:T(1024)S(1)}, u32[]{:S(2)}, u32[]{:S(2)}) collective-permute-start(s32[769]{0:T(1024)S(1)} %pad_add_fusion), channel_id=1, source_target_pairs={{0,8},{2,10},{4,12},{6,14},{8,0},{10,2},{12,4},{14,6},{1,9},{3,11}... | collective-permute-start | bytes 9236 | tf_op jit(solution)/shard_map/ppermute | solution.py:279
  46.9 76.0 %copy-start.4 = (bf16[24,64,128]{2,1,0:T(8,128)(2,1)}, bf16[24,64,128]{2,1,0:T(8,128)(2,1)S(1)}, u32[]{:S(2)}) copy-start(bf16[24,64,128]{2,1,0:T(8,128)(2,1)S(1)} %collective-permute-done.10.refs_0_.refs_4_) | copy-start | bytes 1179652
  46.9 13.6 %collective-permute-start.11 = (bf16[24,64,128]{2,1,0:T(8,128)(2,1)S(1)}, bf16[24,64,128]{2,1,0:T(8,128)(2,1)S(1)}, u32[]{:S(2)}, u32[]{:S(2)}) collective-permute-start(bf16[24,64,128]{2,1,0:T(8,128)(2,1)S(1)} %collective-permute-done.10.refs_0_.refs_4_), channel_id=1, source_target_pairs={{0,16},{16,0},{1,17},{17,1},{2,18},{18,2},{3,19},{19,3},{4,20},{20... | collective-permute-start | bytes 1179656 | tf_op jit(solution)/shard_map/ppermute | solution.py:294
  47.4 35.2 %collective-permute-start.2 = (bf16[24,64,128]{2,1,0:T(8,128)(2,1)}, bf16[24,64,128]{2,1,0:T(8,128)(2,1)S(1)}, u32[]{:S(2)}, u32[]{:S(2)}) collective-permute-start(bf16[24,64,128]{2,1,0:T(8,128)(2,1)} %get-tuple-element.48), channel_id=1, source_target_pairs={{0,8},{2,10},{4,12},{6,14},{8,0},{10,2},{12,4},{14,6},{1,9},{3,11}... | collective-permute-start | bytes 1179656 | tf_op jit(solution)/shard_map/ppermute | solution.py:291
  47.4 43.6 %collective-permute-start.1 = (bf16[24,64,128]{2,1,0:T(8,128)(2,1)}, bf16[24,64,128]{2,1,0:T(8,128)(2,1)}, u32[]{:S(2)}, u32[]{:S(2)}) collective-permute-start(bf16[24,64,128]{2,1,0:T(8,128)(2,1)} %get-tuple-element.49), channel_id=1, source_target_pairs={{0,8},{2,10},{4,12},{6,14},{8,0},{10,2},{12,4},{14,6},{1,9},{3,11}... | collective-permute-start | bytes 1179656 | tf_op jit(solution)/shard_map/ppermute | solution.py:291
  50.3 47.7 %collective-permute-start = (bf16[24,64,128]{2,1,0:T(8,128)(2,1)}, bf16[24,64,128]{2,1,0:T(8,128)(2,1)}, u32[]{:S(2)}, u32[]{:S(2)}) collective-permute-start(bf16[24,64,128]{2,1,0:T(8,128)(2,1)} %get-tuple-element.50), channel_id=1, source_target_pairs={{0,8},{2,10},{4,12},{6,14},{8,0},{10,2},{12,4},{14,6},{1,9},{3,11}... | collective-permute-start | bytes 1179656 | tf_op jit(solution)/shard_map/ppermute | solution.py:291
  50.3 71.7 %copy-start.15 = (s32[769]{0:T(1024)}, s32[769]{0:T(1024)S(1)}, u32[]{:S(2)}) copy-start(s32[769]{0:T(1024)S(1)} %collective-permute-done.3) | copy-start | bytes 9232
  50.3 48.6 %collective-permute-start.12 = (bf16[24,64,128]{2,1,0:T(8,128)(2,1)S(1)}, bf16[24,64,128]{2,1,0:T(8,128)(2,1)}, u32[]{:S(2)}, u32[]{:S(2)}) collective-permute-start(bf16[24,64,128]{2,1,0:T(8,128)(2,1)S(1)} %collective-permute-done.10.refs_0_.refs_4_), channel_id=1, source_target_pairs={{0,1},{1,0},{2,3},{3,2},{4,5},{5,4},{6,7},{7,6},{8,9},{9,8},{10,11... | collective-permute-start | bytes 1179656 | tf_op jit(solution)/shard_map/ppermute | solution.py:295
  60.5 42.2 %collective-permute-start.13 = (bf16[24,64,128]{2,1,0:T(8,128)(2,1)S(1)}, bf16[24,64,128]{2,1,0:T(8,128)(2,1)}, u32[]{:S(2)}, u32[]{:S(2)}) collective-permute-start(bf16[24,64,128]{2,1,0:T(8,128)(2,1)S(1)} %collective-permute-done.11.refs_1_.refs_5_), channel_id=1, source_target_pairs={{0,1},{1,0},{2,3},{3,2},{4,5},{5,4},{6,7},{7,6},{8,9},{9,8},{10,11... | collective-permute-start | bytes 1179656 | tf_op jit(solution)/shard_map/ppermute | solution.py:295
  82.5 20.2 %collective-permute-start.14 = (bf16[24,64,128]{2,1,0:T(8,128)(2,1)S(1)}, bf16[24,64,128]{2,1,0:T(8,128)(2,1)}, u32[]{:S(2)}, u32[]{:S(2)}) collective-permute-start(bf16[24,64,128]{2,1,0:T(8,128)(2,1)S(1)} %collective-permute-done.2.refs_4_.refs_8_), channel_id=1, source_target_pairs={{0,16},{16,0},{1,17},{17,1},{2,18},{18,2},{3,19},{19,3},{4,20},{20... | collective-permute-start | bytes 1179656 | tf_op jit(solution)/shard_map/ppermute | solution.py:294
  90.9 12.3 %collective-permute-start.15 = (bf16[24,64,128]{2,1,0:T(8,128)(2,1)S(1)}, bf16[24,64,128]{2,1,0:T(8,128)(2,1)}, u32[]{:S(2)}, u32[]{:S(2)}) collective-permute-start(bf16[24,64,128]{2,1,0:T(8,128)(2,1)S(1)} %collective-permute-done.2.refs_4_.refs_8_), channel_id=1, source_target_pairs={{0,1},{1,0},{2,3},{3,2},{4,5},{5,4},{6,7},{7,6},{8,9},{9,8},{10,11... | collective-permute-start | bytes 1179656 | tf_op jit(solution)/shard_map/ppermute | solution.py:295
  98.0 12.4 %collective-permute-start.7 = (bf16[24,64,128]{2,1,0:T(8,128)(2,1)}, bf16[24,64,128]{2,1,0:T(8,128)(2,1)}, u32[]{:S(2)}, u32[]{:S(2)}) collective-permute-start(bf16[24,64,128]{2,1,0:T(8,128)(2,1)} %collective-permute-done.1.refs_0_.refs_12_), channel_id=1, source_target_pairs={{0,16},{16,0},{1,17},{17,1},{2,18},{18,2},{3,19},{19,3},{4,20},{20... | collective-permute-start | bytes 1179656 | tf_op jit(solution)/shard_map/ppermute | solution.py:294
  98.9 17.5 %collective-permute-start.4 = (bf16[24,64,128]{2,1,0:T(8,128)(2,1)}, bf16[24,64,128]{2,1,0:T(8,128)(2,1)}, u32[]{:S(2)}, u32[]{:S(2)}) collective-permute-start(bf16[24,64,128]{2,1,0:T(8,128)(2,1)} %collective-permute-done.refs_0_.refs_16_), channel_id=1, source_target_pairs={{0,16},{16,0},{1,17},{17,1},{2,18},{18,2},{3,19},{19,3},{4,20},{20... | collective-permute-start | bytes 1179656 | tf_op jit(solution)/shard_map/ppermute | solution.py:294
  102.7 28.1 %collective-permute-start.8 = (bf16[24,64,128]{2,1,0:T(8,128)(2,1)}, bf16[24,64,128]{2,1,0:T(8,128)(2,1)}, u32[]{:S(2)}, u32[]{:S(2)}) collective-permute-start(bf16[24,64,128]{2,1,0:T(8,128)(2,1)} %collective-permute-done.1.refs_0_.refs_12_), channel_id=1, source_target_pairs={{0,1},{1,0},{2,3},{3,2},{4,5},{5,4},{6,7},{7,6},{8,9},{9,8},{10,11... | collective-permute-start | bytes 1179656 | tf_op jit(solution)/shard_map/ppermute | solution.py:295
  102.7 30.3 %collective-permute-start.5 = (bf16[24,64,128]{2,1,0:T(8,128)(2,1)}, bf16[24,64,128]{2,1,0:T(8,128)(2,1)}, u32[]{:S(2)}, u32[]{:S(2)}) collective-permute-start(bf16[24,64,128]{2,1,0:T(8,128)(2,1)} %collective-permute-done.refs_0_.refs_16_), channel_id=1, source_target_pairs={{0,1},{1,0},{2,3},{3,2},{4,5},{5,4},{6,7},{7,6},{8,9},{9,8},{10,11... | collective-permute-start | bytes 1179656 | tf_op jit(solution)/shard_map/ppermute | solution.py:295
  103.2 19.6 %collective-permute-start.16 = (bf16[24,64,128]{2,1,0:T(8,128)(2,1)}, bf16[24,64,128]{2,1,0:T(8,128)(2,1)}, u32[]{:S(2)}, u32[]{:S(2)}) collective-permute-start(bf16[24,64,128]{2,1,0:T(8,128)(2,1)} %collective-permute-done.14.refs_5_.refs_9_), channel_id=1, source_target_pairs={{0,1},{1,0},{2,3},{3,2},{4,5},{5,4},{6,7},{7,6},{8,9},{9,8},{10,11... | collective-permute-start | bytes 1179656 | tf_op jit(solution)/shard_map/ppermute | solution.py:295
  110.3 20.5 %collective-permute-start.9 = (bf16[24,64,128]{2,1,0:T(8,128)(2,1)}, bf16[24,64,128]{2,1,0:T(8,128)(2,1)}, u32[]{:S(2)}, u32[]{:S(2)}) collective-permute-start(bf16[24,64,128]{2,1,0:T(8,128)(2,1)} %collective-permute-done.7.refs_1_.refs_13_), channel_id=1, source_target_pairs={{0,1},{1,0},{2,3},{3,2},{4,5},{5,4},{6,7},{7,6},{8,9},{9,8},{10,11... | collective-permute-start | bytes 1179656 | tf_op jit(solution)/shard_map/ppermute | solution.py:295
  116.4 16.6 %collective-permute-start.6 = (bf16[24,64,128]{2,1,0:T(8,128)(2,1)}, bf16[24,64,128]{2,1,0:T(8,128)(2,1)}, u32[]{:S(2)}, u32[]{:S(2)}) collective-permute-start(bf16[24,64,128]{2,1,0:T(8,128)(2,1)} %collective-permute-done.4.refs_1_.refs_17_), channel_id=1, source_target_pairs={{0,1},{1,0},{2,3},{3,2},{4,5},{5,4},{6,7},{7,6},{8,9},{9,8},{10,11... | collective-permute-start | bytes 1179656 | tf_op jit(solution)/shard_map/ppermute | solution.py:295
  135.4 20.2 %collective-permute-start.17 = (bf16[32,4096]{1,0:T(8,128)(2,1)S(1)}, bf16[32,4096]{1,0:T(8,128)(2,1)S(1)}, u32[]{:S(2)}, u32[]{:S(2)}) collective-permute-start(bf16[32,4096]{1,0:T(8,128)(2,1)S(1)} %get-tuple-element.36), channel_id=1, source_target_pairs={{0,2},{2,0},{4,6},{6,4},{8,10},{10,8},{12,14},{14,12},{1,3},{3,1},... | collective-permute-start | bytes 786440 | tf_op jit(solution)/shard_map/ppermute | solution.py:262
  148.7 9.1 %collective-permute-start.18 = (bf16[32,4096]{1,0:T(8,128)(2,1)S(1)}, bf16[32,4096]{1,0:T(8,128)(2,1)S(1)}, u32[]{:S(2)}, u32[]{:S(2)}) collective-permute-start(bf16[32,4096]{1,0:T(8,128)(2,1)S(1)} %get-tuple-element.37), channel_id=1, source_target_pairs={{0,4},{2,6},{4,0},{6,2},{8,12},{10,14},{12,8},{14,10},{1,5},{3,7},... | collective-permute-start | bytes 786440 | tf_op jit(solution)/shard_map/ppermute | solution.py:262
  148.7 13.8 %collective-permute-start.19 = (bf16[32,4096]{1,0:T(8,128)(2,1)S(1)}, bf16[32,4096]{1,0:T(8,128)(2,1)S(1)}, u32[]{:S(2)}, u32[]{:S(2)}) collective-permute-start(bf16[32,4096]{1,0:T(8,128)(2,1)S(1)} %get-tuple-element.38), channel_id=1, source_target_pairs={{0,6},{2,4},{4,2},{6,0},{8,14},{10,12},{12,10},{14,8},{1,7},{3,5},... | collective-permute-start | bytes 786440 | tf_op jit(solution)/shard_map/ppermute | solution.py:262
  163.4 8.3 %collective-permute-start.20 = (bf16[32,4096]{1,0:T(8,128)(2,1)S(1)}, bf16[32,4096]{1,0:T(8,128)(2,1)S(1)}, u32[]{:S(2)}, u32[]{:S(2)}) collective-permute-start(bf16[32,4096]{1,0:T(8,128)(2,1)S(1)} %shard_map.68.refs_0_), channel_id=1, source_target_pairs={{0,2},{2,0},{4,6},{6,4},{8,10},{10,8},{12,14},{14,12},{1,3},{3,1},... | collective-permute-start | bytes 786440 | tf_op jit(solution)/shard_map/ppermute | solution.py:262
  165.1 9.2 %collective-permute-start.21 = (bf16[32,4096]{1,0:T(8,128)(2,1)S(1)}, bf16[32,4096]{1,0:T(8,128)(2,1)S(1)}, u32[]{:S(2)}, u32[]{:S(2)}) collective-permute-start(bf16[32,4096]{1,0:T(8,128)(2,1)S(1)} %shard_map.68.refs_0_), channel_id=1, source_target_pairs={{0,4},{2,6},{4,0},{6,2},{8,12},{10,14},{12,8},{14,10},{1,5},{3,7},... | collective-permute-start | bytes 786440 | tf_op jit(solution)/shard_map/ppermute | solution.py:262
  165.4 12.8 %collective-permute-start.22 = (bf16[32,4096]{1,0:T(8,128)(2,1)S(1)}, bf16[32,4096]{1,0:T(8,128)(2,1)S(1)}, u32[]{:S(2)}, u32[]{:S(2)}) collective-permute-start(bf16[32,4096]{1,0:T(8,128)(2,1)S(1)} %shard_map.68.refs_0_), channel_id=1, source_target_pairs={{0,6},{2,4},{4,2},{6,0},{8,14},{10,12},{12,10},{14,8},{1,7},{3,5},... | collective-permute-start | bytes 786440 | tf_op jit(solution)/shard_map/ppermute | solution.py:262
  186.2 29.6 %collective-permute-start.23 = (bf16[32,4096]{1,0:T(8,128)(2,1)S(1)}, bf16[32,4096]{1,0:T(8,128)(2,1)S(1)}, u32[]{:S(2)}, u32[]{:S(2)}) collective-permute-start(bf16[32,4096]{1,0:T(8,128)(2,1)S(1)} %get-tuple-element.40), channel_id=1, source_target_pairs={{0,2},{2,0},{4,6},{6,4},{8,10},{10,8},{12,14},{14,12},{1,3},{3,1},... | collective-permute-start | bytes 786440 | tf_op jit(solution)/shard_map/ppermute | solution.py:262
  202.1 15.3 %collective-permute-start.24 = (bf16[32,4096]{1,0:T(8,128)(2,1)S(1)}, bf16[32,4096]{1,0:T(8,128)(2,1)S(1)}, u32[]{:S(2)}, u32[]{:S(2)}) collective-permute-start(bf16[32,4096]{1,0:T(8,128)(2,1)S(1)} %get-tuple-element.41), channel_id=1, source_target_pairs={{0,4},{2,6},{4,0},{6,2},{8,12},{10,14},{12,8},{14,10},{1,5},{3,7},... | collective-permute-start | bytes 786440 | tf_op jit(solution)/shard_map/ppermute | solution.py:262
  202.1 15.3 %collective-permute-start.25 = (bf16[32,4096]{1,0:T(8,128)(2,1)S(1)}, bf16[32,4096]{1,0:T(8,128)(2,1)S(1)}, u32[]{:S(2)}, u32[]{:S(2)}) collective-permute-start(bf16[32,4096]{1,0:T(8,128)(2,1)S(1)} %get-tuple-element.42), channel_id=1, source_target_pairs={{0,6},{2,4},{4,2},{6,0},{8,14},{10,12},{12,10},{14,8},{1,7},{3,5},... | collective-permute-start | bytes 786440 | tf_op jit(solution)/shard_map/ppermute | solution.py:262
  213.6 9.2 %collective-permute-start.26 = (bf16[32,4096]{1,0:T(8,128)(2,1)S(1)}, bf16[32,4096]{1,0:T(8,128)(2,1)S(1)}, u32[]{:S(2)}, u32[]{:S(2)}) collective-permute-start(bf16[32,4096]{1,0:T(8,128)(2,1)S(1)} %get-tuple-element.44), channel_id=1, source_target_pairs={{0,2},{2,0},{4,6},{6,4},{8,10},{10,8},{12,14},{14,12},{1,3},{3,1},... | collective-permute-start | bytes 786440 | tf_op jit(solution)/shard_map/ppermute | solution.py:262
  213.7 9.2 %collective-permute-start.27 = (bf16[32,4096]{1,0:T(8,128)(2,1)S(1)}, bf16[32,4096]{1,0:T(8,128)(2,1)S(1)}, u32[]{:S(2)}, u32[]{:S(2)}) collective-permute-start(bf16[32,4096]{1,0:T(8,128)(2,1)S(1)} %get-tuple-element.45), channel_id=1, source_target_pairs={{0,4},{2,6},{4,0},{6,2},{8,12},{10,14},{12,8},{14,10},{1,5},{3,7},... | collective-permute-start | bytes 786440 | tf_op jit(solution)/shard_map/ppermute | solution.py:262
  215.8 10.5 %collective-permute-start.28 = (bf16[32,4096]{1,0:T(8,128)(2,1)S(1)}, bf16[32,4096]{1,0:T(8,128)(2,1)S(1)}, u32[]{:S(2)}, u32[]{:S(2)}) collective-permute-start(bf16[32,4096]{1,0:T(8,128)(2,1)S(1)} %get-tuple-element.46), channel_id=1, source_target_pairs={{0,6},{2,4},{4,2},{6,0},{8,14},{10,12},{12,10},{14,8},{1,7},{3,5},... | collective-permute-start | bytes 786440 | tf_op jit(solution)/shard_map/ppermute | solution.py:262
  (17 other events, 192.5 us)

commit v6 on v5

--- a/solution.py
+++ b/solution.py
@@ -10,8 +10,8 @@
 TILE = 64
 PAIR = 2 * TILE
 UNROLL = 8
-HEAD = 3
-VMEM_LIMIT = 24 * 1024 * 1024
+HEAD = 2
+VMEM_LIMIT = 12 * 1024 * 1024
 
 
 def padded_tile(values, half):
@@ -46,17 +46,23 @@
     lax.fori_loop(0, (live + UNROLL - 1) // UNROLL, group, 0)
 
 
-def tile_points(place, column):
-    return pl.ds(pl.multiple_of(column + place[1] * PAIR, PAIR), PAIR)
+def tile_points(place):
+    return pl.ds(pl.multiple_of(place[1] * PAIR, PAIR), PAIR)
 
 
 def all_tiles(meta, tiles, pieces, step):
     if len(pieces) == 1:
-        size = pieces[0].shape[0]
-        tile_loop(meta, tiles, pieces[0], pl.program_id(0) * size, size, step)
+        tile_loop(meta, tiles, pieces[0], 0, tiles, step)
         return
     for number, ref in enumerate(pieces):
-        tile_loop(meta, tiles, ref, meta[2 * tiles + HEAD + number], ref.shape[0], step)
+        size = ref.shape[0] // 2
+
+        def share(which, carry, number=number, ref=ref, size=size):
+            base = meta[2 * tiles + HEAD + 2 * number + which]
+            tile_loop(meta, tiles, ref.at[pl.ds(which * size, size)], base, size, step)
+            return carry
+
+        lax.fori_loop(0, 2, share, 0)
 
 
 def rows_of(refs, lanes):
@@ -75,15 +81,12 @@
     pieces, refs = refs[:n_pieces], refs[n_pieces:]
     total = refs[-1]
     proj = pieces[0].shape[2]
-    side, place = meta[2 * tiles + 1], meta[2 * tiles + 2]
-    column = side * (wave.shape[1] // 2)
-
-    @pl.when(pl.program_id(0) == 0)
-    def start():
-        total[...] = jnp.zeros_like(total) if first else refs[0][...]
+    place = meta[2 * tiles + 1]
+
+    total[...] = jnp.zeros_like(total) if first else refs[0][...]
 
     def step(first, second):
-        values = jnp.concatenate([wave[:, tile_points(place, column)] for place in (first, second)], axis=1)
+        values = jnp.concatenate([wave[:, tile_points(at)] for at in (first, second)], axis=1)
         terms = jnp.dot(values, diagonal(first[2], second[2]), preferred_element_type=jnp.float32)
         for index, place in enumerate((first, second)):
             lanes = pl.ds(pl.multiple_of(place[0] * proj, proj), proj)
@@ -104,9 +107,7 @@
     outs, field = refs[:-1], refs[-1]
     proj = pieces[0].shape[2]
 
-    @pl.when(pl.program_id(0) == 0)
-    def start():
-        field[...] = jnp.zeros_like(field)
+    field[...] = jnp.zeros_like(field)
 
     def step(first, second):
         lanes = [pl.ds(pl.multiple_of(place[0] * proj, proj), proj) for place in (first, second)]
@@ -117,35 +118,14 @@
             preferred_element_type=jnp.float32,
         )
         for index, place in enumerate((first, second)):
-            field[:, tile_points(place, 0)] += terms[:, index * PAIR : (index + 1) * PAIR]
+            field[:, tile_points(place)] += terms[:, index * PAIR : (index + 1) * PAIR]
 
     all_tiles(meta, tiles, pieces, step)
 
-    @pl.when(pl.program_id(0) == pl.num_programs(0) - 1)
-    def finish():
-        store_rows(outs, field)
-
-
-def tile_chunk(tiles):
-    for chunk in (96, 64, 48, 32, 16, 8):
-        if tiles % chunk == 0:
-            return chunk
-    return tiles
+    store_rows(outs, field)
 
 
 WHOLE = pl.BlockSpec(memory_space=pltpu.VMEM)
-
-
-def piece_specs(tiles, pieces):
-    if len(pieces) > 1:
-        return 1, [WHOLE] * len(pieces)
-    chunk = tile_chunk(tiles)
-
-    def index(step, meta):
-        last = (meta[2 * tiles] + chunk - 1) // chunk - 1
-        return (jnp.clip(step, 0, jnp.maximum(last, 0)), 0, 0)
-
-    return tiles // chunk, [pl.BlockSpec((chunk,) + pieces[0].shape[1:], index)]
 
 
 COST = pl.CostEstimate(flops=1, bytes_accessed=1, transcendentals=0)
@@ -163,17 +143,15 @@
     rows = wave.shape[0]
     bands = rows // count
     split = bands % 16 == 0
-    steps, specs = piece_specs(tiles, pieces)
     operands = [wave, *pieces] + ([] if total is None else [total])
-    in_specs = [WHOLE] + specs + [WHOLE] * (total is not None)
     outs = count if split else 1
     out_shape = [jax.ShapeDtypeStruct((rows // outs, width), jnp.bfloat16)] * outs
     return pl.pallas_call(
         functools.partial(project_kernel, tiles, len(pieces), total is None, last),
         grid_spec=pltpu.PrefetchScalarGridSpec(
             num_scalar_prefetch=1,
-            grid=(steps,),
-            in_specs=in_specs,
+            grid=(1,),
+            in_specs=[WHOLE] * len(operands),
             out_specs=[WHOLE] * outs if last else WHOLE,
             scratch_shapes=[pltpu.VMEM((rows, width), jnp.float32)] if last else [],
         ),
@@ -187,13 +165,12 @@
     count = len(applied)
     applied = join_small(applied)
     rows = sum(block.shape[0] for block in applied)
-    steps, specs = piece_specs(tiles, pieces)
     result = pl.pallas_call(
         functools.partial(spread_kernel, tiles, len(applied), len(pieces)),
         grid_spec=pltpu.PrefetchScalarGridSpec(
             num_scalar_prefetch=1,
-            grid=(steps,),
-            in_specs=[WHOLE] * len(applied) + specs,
+            grid=(1,),
+            in_specs=[WHOLE] * (len(applied) + len(pieces)),
             out_specs=[WHOLE] * len(applied),
             scratch_shapes=[pltpu.VMEM((rows, points), jnp.float32)],
         ),
@@ -255,6 +232,7 @@
     side, place = index // half, index % half
     group, core = lax.axis_index("groups"), lax.axis_index("band")
     partners = [(i, (i + half) % n_grid) for i in range(n_grid)]
+    pools = [list(range(half)), list(range(half, n_grid))]
     swap = [(0, 1), (1, 0)]
 
     def exchange(blocks):
@@ -265,20 +243,19 @@
             for d in range(1, half)
         ]
 
-    waves = wavefunctions.reshape(bands, 2, half, points).transpose(2, 0, 1, 3)
-    waves = lax.all_to_all(
-        waves.reshape(half, bands, 2 * points),
-        "grid",
-        split_axis=0,
-        concat_axis=0,
-        tiled=True,
-        axis_index_groups=[list(range(half)), list(range(half, n_grid))],
-    ).reshape(half * bands, 2 * points)
+    def to_bricks(which):
+        part = lax.dynamic_slice_in_dim(wavefunctions, which * half * points, half * points, 1)
+        return lax.all_to_all(
+            part, "grid", split_axis=1, concat_axis=0, tiled=True, axis_index_groups=pools
+        )
 
     lists = jnp.concatenate([tile_segment, tile_block, tile_count])
     other_lists = lax.ppermute(lists, "grid", partners)
-    meta = jnp.concatenate([lists, jnp.stack([side, place])])
-    total = project(tiles, meta, waves, [projectors], half, width)
+    own_wave = to_bricks(side)
+    other_wave = to_bricks(1 - side)
+    meta = jnp.concatenate([lists, jnp.stack([place])])
+    total = project(tiles, meta, own_wave, [projectors], half, width)
+    matrix = two_parts(coupling_matrix(coupling))
 
     pieces, bases = [], []
     parts = 4
@@ -289,16 +266,17 @@
             projectors, part * size + (2 * group + core) * share, share, 0
         )
         mine = lax.ppermute(mine, "grid", partners)
-        if part > 0:
-            mine, total, other_lists = lax.optimization_barrier((mine, total, other_lists))
-        across = lax.ppermute(mine, "groups", swap)
-        pieces += [mine, across, lax.ppermute(mine, "band", swap), lax.ppermute(across, "band", swap)]
+        if part == 0:
+            mine, matrix, other_lists = lax.optimization_barrier((mine, matrix, other_lists))
+        both = jnp.concatenate([mine, lax.ppermute(mine, "groups", swap)])
+        if part == 0:
+            both, total, other_wave = lax.optimization_barrier((both, total, other_wave))
+        pieces += [both, lax.ppermute(both, "band", swap)]
         for other_core in (core, 1 - core):
             for other_group in (group, 1 - group):
                 bases.append(part * size + (2 * other_group + other_core) * share)
 
-    matrix = two_parts(coupling_matrix(coupling))
-    other_meta = jnp.concatenate([other_lists, jnp.stack([1 - side, place] + bases)])
+    other_meta = jnp.concatenate([other_lists, jnp.stack([place] + bases)])
     for first, end in ((0, 2), (2, 3), (3, 4)):
         skip = 2 * tiles + HEAD
         piece_meta = jnp.concatenate(
@@ -307,8 +285,8 @@
         total = project(
             tiles,
             piece_meta,
-            waves,
-            pieces[4 * first : 4 * end],
+            other_wave,
+            pieces[2 * first : 2 * end],
             half,
             width,
             total,

time: 229 us -> 211 us (0.921)
  the two profiles are of different devices: /device:TPU:18 before, /device:TPU:0 now
where the time goes in v6:
time: 211 us; the launch traced here: 209 us
  waiting for transfers between devices  83.7 us (40%)
  Pallas kernels  54.2 us (26%)
  starting transfers between devices  37.3 us (18%)
  local copies, waits for them, and re-layouts  25.8 us (12%)
  other arithmetic  7 us (3%)
    ppermute x4, waiting for transfers between devices, body(): mine = lax.ppermute(mine, 'grid', partners)  33 us
    ppermute x12, waiting for transfers between devices, exchange(): lax.ppermute(blocks[d], 'grid', [(i, i // half * half + (i % half ^ d)) f...  31.4 us
    pallas_call x2, Pallas kernels, spread(): pl.pallas_call(functools.partial(spread_kernel, tiles, len(applied), len(...  27.4 us
    pallas_call x4, Pallas kernels, project(): pl.pallas_call(functools.partial(project_kernel, tiles, len(pieces), tota...  25.9 us
    ppermute x12, starting transfers between devices, exchange(): lax.ppermute(blocks[d], 'grid', [(i, i // half * half + (i % half ^ d)) f...  14.4 us
    ppermute x4, waiting for transfers between devices, body(): both = jnp.concatenate([mine, lax.ppermute(mine, 'groups', swap)])  10.7 us
    unnamed x31, local copies, waits for them, and re-layouts  10.1 us
    all_to_all x2, starting transfers between devices, to_bricks(): lax.all_to_all(part, 'grid', split_axis=1, concat_axis=0, tiled=True, axi...  8.76 us
  transfers between devices with their start and end apart: 27, of which 14 were waited for; matrix products, arithmetic and copies ran while one was open for 11% of the time, Pallas kernels for 20%

profile of v6, /device:TPU:0, one launch (start us, length us, event | category | flops | bytes accessed | tf_op | source)
XLA Modules:
  0.0 209.1 jit_solution(1190766640068669058)
XLA Ops:
  2.8 5.2 %all-to-all-start = ((bf16[32,4,4096]{2,0,1:T(8,128)(2,1)}), bf16[32,4,4096]{2,0,1:T(8,128)(2,1)S(1)}, u32[]{:S(2)}, u32[]{:S(2)}) async-start(bf16[32,4,4096]{2,0,1:T(8,128)(2,1)} %bitcast.33), calls=%async_computation | async-start | bytes 2097152 | tf_op jit(solution)/shard_map/all_to_all | solution.py:248
  8.0 2.6 %constant_dynamic-slice_fusion = (bf16[24,64,128]{2,1,0:T(8,128)(2,1)}, bf16[24,64,128]{2,1,0:T(8,128)(2,1)}, bf16[24,64,128]{2,1,0:T(8,128)(2,1)}, bf16[24,64,128]{2,1,0:T(8,128)(2,1)}) fusion(bf16[384,64,128]{2,1,0:T(8,128)(2,1)} %refs_4_.1, s32[]{:T(128)S(6)} %select_n.84, s32[]{:T(128)S(6)} %select_n.83, s32[]{:T(128)S(6)} %select_n.82, s32[]{:T(128)S(6)} %select_n.75), kind=kLoop, calls=%fused_computation.23 | loop fusion | bytes 3145744 | tf_op jit(solution)/shard_map/dynamic_slice | solution.py:265
  10.6 2.6 %collective-permute-start = (bf16[24,64,128]{2,1,0:T(8,128)(2,1)}, bf16[24,64,128]{2,1,0:T(8,128)(2,1)}, u32[]{:S(2)}, u32[]{:S(2)}) collective-permute-start(bf16[24,64,128]{2,1,0:T(8,128)(2,1)} %get-tuple-element.46), channel_id=1, source_target_pairs={{0,8},{2,10},{4,12},{6,14},{8,0},{10,2},{12,4},{14,6},{1,9},{3,11}... | collective-permute-start | bytes 1179656 | tf_op jit(solution)/shard_map/ppermute | solution.py:268
  14.8 2.6 %collective-permute-start.10 = (bf16[24,64,128]{2,1,0:T(8,128)(2,1)}, bf16[24,64,128]{2,1,0:T(8,128)(2,1)}, u32[]{:S(2)}, u32[]{:S(2)}) collective-permute-start(bf16[24,64,128]{2,1,0:T(8,128)(2,1)} %get-tuple-element.43), channel_id=1, source_target_pairs={{0,8},{2,10},{4,12},{6,14},{8,0},{10,2},{12,4},{14,6},{1,9},{3,11}... | collective-permute-start | bytes 1179656 | tf_op jit(solution)/shard_map/ppermute | solution.py:268
  17.8 2.6 %collective-permute-start.3 = (bf16[24,64,128]{2,1,0:T(8,128)(2,1)}, bf16[24,64,128]{2,1,0:T(8,128)(2,1)S(1)}, u32[]{:S(2)}, u32[]{:S(2)}) collective-permute-start(bf16[24,64,128]{2,1,0:T(8,128)(2,1)} %get-tuple-element.45), channel_id=1, source_target_pairs={{0,8},{2,10},{4,12},{6,14},{8,0},{10,2},{12,4},{14,6},{1,9},{3,11}... | collective-permute-start | bytes 1179656 | tf_op jit(solution)/shard_map/ppermute | solution.py:268
  23.1 8.4 %all-to-all-done = bf16[32,4,4096]{2,0,1:T(8,128)(2,1)S(1)} async-done(((bf16[32,4,4096]{2,0,1:T(8,128)(2,1)}), bf16[32,4,4096]{2,0,1:T(8,128)(2,1)S(1)}, u32[]{:S(2)}, u32[]{:S(2)}) %all-to-all-start) | async-done | bytes 1048608 | tf_op jit(solution)/shard_map/all_to_all | solution.py:248
  31.5 3.5 %all-to-all-start.1 = ((bf16[32,4,4096]{2,0,1:T(8,128)(2,1)}), bf16[32,4,4096]{2,0,1:T(8,128)(2,1)S(1)}, u32[]{:S(2)}, u32[]{:S(2)}) async-start(bf16[32,4,4096]{2,0,1:T(8,128)(2,1)} %bitcast.32), calls=%async_computation.1 | async-start | bytes 2097152 | tf_op jit(solution)/shard_map/all_to_all | solution.py:248
  35.1 2.9 %copy.13 = f32[32,128,128]{2,1,0:T(8,128)} copy(f32[32,128,128]{1,2,0:T(8,128)} %broadcast_bitcast_fusion) | data formatting | bytes 4194304 | tf_op jit(solution)/shard_map/tile | solution.py:220
  38.0 3.0 %select_convert_fusion.high_ref = bf16[32,128,128]{2,1,0:T(8,128)(2,1)} fusion(f32[32,128,128]{2,1,0:T(8,128)} %copy.13, pred[128,128]{1,0:T(8,128)(4,1)S(1)} %broadcast_compare_fusion), kind=kLoop, calls=%fused_computation.1 | loop fusion | flops 524288 | bytes 3162112 | tf_op jit(solution)/shard_map/convert_element_type | solution.py:187
  42.3 23.9 %collective-permute-done.10 = bf16[24,64,128]{2,1,0:T(8,128)(2,1)} collective-permute-done((bf16[24,64,128]{2,1,0:T(8,128)(2,1)}, bf16[24,64,128]{2,1,0:T(8,128)(2,1)}, u32[]{:S(2)}, u32[]{:S(2)}) %collective-permute-start.10) | collective-permute-done | bytes 393248 | tf_op jit(solution)/shard_map/ppermute | solution.py:268
  68.3 6.2 %collective-permute-done.6 = bf16[24,64,128]{2,1,0:T(8,128)(2,1)S(1)} collective-permute-done((bf16[24,64,128]{2,1,0:T(8,128)(2,1)}, bf16[24,64,128]{2,1,0:T(8,128)(2,1)S(1)}, u32[]{:S(2)}, u32[]{:S(2)}) %collective-permute-start.6) | collective-permute-done | bytes 393248 | tf_op jit(solution)/shard_map/ppermute | solution.py:268
  78.6 2.9 %collective-permute-done.3 = bf16[24,64,128]{2,1,0:T(8,128)(2,1)S(1)} collective-permute-done((bf16[24,64,128]{2,1,0:T(8,128)(2,1)}, bf16[24,64,128]{2,1,0:T(8,128)(2,1)S(1)}, u32[]{:S(2)}, u32[]{:S(2)}) %collective-permute-start.3) | collective-permute-done | bytes 393248 | tf_op jit(solution)/shard_map/ppermute | solution.py:268
  84.6 10.7 %collective-permute-done.7 = bf16[24,64,128]{2,1,0:T(8,128)(2,1)S(1)} collective-permute-done((bf16[24,64,128]{2,1,0:T(8,128)(2,1)S(1)}, bf16[24,64,128]{2,1,0:T(8,128)(2,1)S(1)}, u32[]{:S(2)}, u32[]{:S(2)}) %collective-permute-start.7) | collective-permute-done | bytes 393248 | tf_op jit(solution)/shard_map/ppermute | solution.py:271
  96.1 1.9 pad_maximum_fusion.refs_0_.refs_4_
  98.0 2.8 %copy-done = bf16[384,64,128]{2,1,0:T(8,128)(2,1)S(1)} copy-done((bf16[384,64,128]{2,1,0:T(8,128)(2,1)S(1)}, bf16[384,64,128]{2,1,0:T(8,128)(2,1)}, u32[]{:S(2)}) %copy-start) | copy-done | bytes 6291480
  100.8 14.3 %shard_map.64.refs_4_ = f32[128,4096]{1,0:T(8,128)S(1)} custom-call(s32[770]{0:T(1024)S(1)} %pad_add_fusion.1.meta, bf16[128,4096]{1,0:T(8,128)(2,1)S(1)} %bitcast.37, bf16[384,64,128]{2,1,0:T(8,128)(2,1)S(1)} %copy-done), custom_call_target="tpu_custom_call" | custom-call | flops 1 | bytes 1 | tf_op jit(solution)/shard_map/pallas_call | solution.py:149
  119.1 7.3 %shard_map.65.refs_2_ = f32[128,4096]{1,0:T(8,128)S(1)} custom-call(s32[778]{0:T(1024)S(1)} %concatenate.50.meta, bf16[128,4096]{1,0:T(8,128)(2,1)S(1)} %bitcast.34, bf16[48,64,128]{2,1,0:T(8,128)(2,1)S(1)} %copy-done.2, bf16[48,64,128]{2,1,0:T(8,128)(2,1)} %collective-permute-done.9.refs_1_.refs_5_, ...), custom_call_target="tpu_custom_call" | custom-call | flops 1 | bytes 1 | tf_op jit(solution)/shard_map/pallas_call | solution.py:149
  126.5 2.2 %shard_map.66.refs_2_ = f32[128,4096]{1,0:T(8,128)S(1)} custom-call(s32[774]{0:T(1024)S(1)} %concatenate.48.meta, bf16[128,4096]{1,0:T(8,128)(2,1)S(1)} %bitcast.35, bf16[48,64,128]{2,1,0:T(8,128)(2,1)} %constant_dynamic-update-slice_fusion.2.refs_0_.refs_8_, bf16[48,64,128]{2,1,0:T(8,128)(2,1)} %collective-permute-done.8.refs_1_.refs_9_, ...), custom_call_target="tpu_custom_call" | custom-call | flops 1 | bytes 1 | tf_op jit(solution)/shard_map/pallas_call | solution.py:149
  128.7 2.1 shard_map.67
  130.9 3.4 %collective-permute-start.15 = (bf16[32,4096]{1,0:T(8,128)(2,1)S(1)}, bf16[32,4096]{1,0:T(8,128)(2,1)S(1)}, u32[]{:S(2)}, u32[]{:S(2)}) collective-permute-start(bf16[32,4096]{1,0:T(8,128)(2,1)S(1)} %get-tuple-element.34), channel_id=1, source_target_pairs={{0,6},{2,4},{4,2},{6,0},{8,14},{10,12},{12,10},{14,8},{1,7},{3,5},... | collective-permute-start | bytes 786440 | tf_op jit(solution)/shard_map/ppermute | solution.py:240
  134.4 5.1 %collective-permute-done.13.refs_1_ = bf16[32,4096]{1,0:T(8,128)(2,1)S(1)} collective-permute-done((bf16[32,4096]{1,0:T(8,128)(2,1)S(1)}, bf16[32,4096]{1,0:T(8,128)(2,1)S(1)}, u32[]{:S(2)}, u32[]{:S(2)}) %collective-permute-start.13) | collective-permute-done | bytes 262176 | tf_op jit(solution)/shard_map/ppermute | solution.py:240
  140.1 6.2 %collective-permute-done.15.refs_3_ = bf16[32,4096]{1,0:T(8,128)(2,1)S(1)} collective-permute-done((bf16[32,4096]{1,0:T(8,128)(2,1)S(1)}, bf16[32,4096]{1,0:T(8,128)(2,1)S(1)}, u32[]{:S(2)}, u32[]{:S(2)}) %collective-permute-start.15) | collective-permute-done | bytes 262176 | tf_op jit(solution)/shard_map/ppermute | solution.py:240
  147.9 2.8 %collective-permute-start.18 = (bf16[32,4096]{1,0:T(8,128)(2,1)S(1)}, bf16[32,4096]{1,0:T(8,128)(2,1)S(1)}, u32[]{:S(2)}, u32[]{:S(2)}) collective-permute-start(bf16[32,4096]{1,0:T(8,128)(2,1)S(1)} %shard_map.68.refs_0_), channel_id=1, source_target_pairs={{0,6},{2,4},{4,2},{6,0},{8,14},{10,12},{12,10},{14,8},{1,7},{3,5},... | collective-permute-start | bytes 786440 | tf_op jit(solution)/shard_map/ppermute | solution.py:240
  150.8 4.8 %collective-permute-done.16.refs_1_ = bf16[32,4096]{1,0:T(8,128)(2,1)S(1)} collective-permute-done((bf16[32,4096]{1,0:T(8,128)(2,1)S(1)}, bf16[32,4096]{1,0:T(8,128)(2,1)S(1)}, u32[]{:S(2)}, u32[]{:S(2)}) %collective-permute-start.16) | collective-permute-done | bytes 262176 | tf_op jit(solution)/shard_map/ppermute | solution.py:240
  156.8 4.7 %collective-permute-done.18.refs_3_ = bf16[32,4096]{1,0:T(8,128)(2,1)S(1)} collective-permute-done((bf16[32,4096]{1,0:T(8,128)(2,1)S(1)}, bf16[32,4096]{1,0:T(8,128)(2,1)S(1)}, u32[]{:S(2)}, u32[]{:S(2)}) %collective-permute-start.18) | collective-permute-done | bytes 262176 | tf_op jit(solution)/shard_map/ppermute | solution.py:240
  161.5 9.6 %shard_map.69 = (bf16[32,4096]{1,0:T(8,128)(2,1)S(1)}, bf16[32,4096]{1,0:T(8,128)(2,1)S(1)}, bf16[32,4096]{1,0:T(8,128)(2,1)S(1)}, bf16[32,4096]{1,0:T(8,128)(2,1)S(1)}) custom-call(s32[786]{0:T(1024)S(1)} %concatenate.43.meta, bf16[32,4096]{1,0:T(8,128)(2,1)S(1)} %shard_map.68.refs_0_, bf16[32,4096]{1,0:T(8,128)(2,1)S(1)} %collective-permute-done.16.refs_1_, ...), custom_call_target="tpu_custom_call" | custom-call | flops 1 | bytes 1 | tf_op jit(solution)/shard_map/pallas_call | solution.py:168
  171.0 2.2 %collective-permute-start.19 = (bf16[32,4096]{1,0:T(8,128)(2,1)S(1)}, bf16[32,4096]{1,0:T(8,128)(2,1)S(1)}, u32[]{:S(2)}, u32[]{:S(2)}) collective-permute-start(bf16[32,4096]{1,0:T(8,128)(2,1)S(1)} %get-tuple-element.36), channel_id=1, source_target_pairs={{0,2},{2,0},{4,6},{6,4},{8,10},{10,8},{12,14},{14,12},{1,3},{3,1},... | collective-permute-start | bytes 786440 | tf_op jit(solution)/shard_map/ppermute | solution.py:240
  174.8 2.8 %copy-done.1 = bf16[384,64,128]{2,1,0:T(8,128)(2,1)S(1)} copy-done((bf16[384,64,128]{2,1,0:T(8,128)(2,1)S(1)}, bf16[384,64,128]{2,1,0:T(8,128)(2,1)}, u32[]{:S(2)}) %copy-start.1) | copy-done | bytes 6291480
  177.6 17.9 %shard_map.70 = (bf16[32,4096]{1,0:T(8,128)(2,1)S(1)}, bf16[32,4096]{1,0:T(8,128)(2,1)S(1)}, bf16[32,4096]{1,0:T(8,128)(2,1)S(1)}, bf16[32,4096]{1,0:T(8,128)(2,1)S(1)}) custom-call(s32[770]{0:T(1024)S(1)} %pad_add_fusion.1.meta, bf16[32,4096]{1,0:T(8,128)(2,1)S(1)} %shard_map.68.refs_0_, bf16[32,4096]{1,0:T(8,128)(2,1)S(1)} %collective-permute-done.16.refs_1_, ...), custom_call_target="tpu_custom_call" | custom-call | flops 1 | bytes 1 | tf_op jit(solution)/shard_map/pallas_call | solution.py:168
  195.8 3.5 %collective-permute-start.24 = (bf16[32,4096]{1,0:T(8,128)(2,1)S(1)}, bf16[32,4096]{1,0:T(8,128)(2,1)S(1)}, u32[]{:S(2)}, u32[]{:S(2)}) collective-permute-start(bf16[32,4096]{1,0:T(8,128)(2,1)S(1)} %get-tuple-element.42), channel_id=1, source_target_pairs={{0,6},{2,4},{4,2},{6,0},{8,14},{10,12},{12,10},{14,8},{1,7},{3,5},... | collective-permute-start | bytes 786440 | tf_op jit(solution)/shard_map/ppermute | solution.py:240
  199.4 5.2 %collective-permute-done.22 = bf16[32,4096]{1,0:T(8,128)(2,1)S(1)} collective-permute-done((bf16[32,4096]{1,0:T(8,128)(2,1)S(1)}, bf16[32,4096]{1,0:T(8,128)(2,1)S(1)}, u32[]{:S(2)}, u32[]{:S(2)}) %collective-permute-start.22) | collective-permute-done | bytes 262176 | tf_op jit(solution)/shard_map/ppermute | solution.py:240
  204.7 3.7 %collective-permute-done.24 = bf16[32,4096]{1,0:T(8,128)(2,1)S(1)} collective-permute-done((bf16[32,4096]{1,0:T(8,128)(2,1)S(1)}, bf16[32,4096]{1,0:T(8,128)(2,1)S(1)}, u32[]{:S(2)}, u32[]{:S(2)}) %collective-permute-start.24) | collective-permute-done | bytes 262176 | tf_op jit(solution)/shard_map/ppermute | solution.py:240
  (90 shorter events, 28.7 us)
Async XLA Ops:
  2.8 28.7 %all-to-all-start = ((bf16[32,4,4096]{2,0,1:T(8,128)(2,1)}), bf16[32,4,4096]{2,0,1:T(8,128)(2,1)S(1)}, u32[]{:S(2)}, u32[]{:S(2)}) async-start(bf16[32,4,4096]{2,0,1:T(8,128)(2,1)} %bitcast.33), calls=%async_computation | async-start | bytes 2097152 | tf_op jit(solution)/shard_map/all_to_all | solution.py:248
  8.0 12.3 %copy-start.11 = (f32[32,16,8,8]{0,3,2,1:T(8,128)S(1)}, f32[32,16,8,8]{0,3,2,1:T(8,128)}, u32[]{:S(2)}) copy-start(f32[32,16,8,8]{0,3,2,1:T(8,128)} %param.11) | copy-start | bytes 393220
  10.6 57.1 %collective-permute-start = (bf16[24,64,128]{2,1,0:T(8,128)(2,1)}, bf16[24,64,128]{2,1,0:T(8,128)(2,1)}, u32[]{:S(2)}, u32[]{:S(2)}) collective-permute-start(bf16[24,64,128]{2,1,0:T(8,128)(2,1)} %get-tuple-element.46), channel_id=1, source_target_pairs={{0,8},{2,10},{4,12},{6,14},{8,0},{10,2},{12,4},{14,6},{1,9},{3,11}... | collective-permute-start | bytes 1179656 | tf_op jit(solution)/shard_map/ppermute | solution.py:268
  14.5 53.3 %collective-permute-start.1 = (s32[769]{0:T(1024)}, s32[769]{0:T(1024)S(1)}, u32[]{:S(2)}, u32[]{:S(2)}) collective-permute-start(s32[769]{0:T(1024)} %pad_add_fusion), channel_id=1, source_target_pairs={{0,8},{2,10},{4,12},{6,14},{8,0},{10,2},{12,4},{14,6},{1,9},{3,11}... | collective-permute-start | bytes 9236 | tf_op jit(solution)/shard_map/ppermute | solution.py:253
  14.8 51.4 %collective-permute-start.10 = (bf16[24,64,128]{2,1,0:T(8,128)(2,1)}, bf16[24,64,128]{2,1,0:T(8,128)(2,1)}, u32[]{:S(2)}, u32[]{:S(2)}) collective-permute-start(bf16[24,64,128]{2,1,0:T(8,128)(2,1)} %get-tuple-element.43), channel_id=1, source_target_pairs={{0,8},{2,10},{4,12},{6,14},{8,0},{10,2},{12,4},{14,6},{1,9},{3,11}... | collective-permute-start | bytes 1179656 | tf_op jit(solution)/shard_map/ppermute | solution.py:268
  17.4 57.1 %collective-permute-start.6 = (bf16[24,64,128]{2,1,0:T(8,128)(2,1)}, bf16[24,64,128]{2,1,0:T(8,128)(2,1)S(1)}, u32[]{:S(2)}, u32[]{:S(2)}) collective-permute-start(bf16[24,64,128]{2,1,0:T(8,128)(2,1)} %get-tuple-element.44), channel_id=1, source_target_pairs={{0,8},{2,10},{4,12},{6,14},{8,0},{10,2},{12,4},{14,6},{1,9},{3,11}... | collective-permute-start | bytes 1179656 | tf_op jit(solution)/shard_map/ppermute | solution.py:268
  17.8 63.8 %collective-permute-start.3 = (bf16[24,64,128]{2,1,0:T(8,128)(2,1)}, bf16[24,64,128]{2,1,0:T(8,128)(2,1)S(1)}, u32[]{:S(2)}, u32[]{:S(2)}) collective-permute-start(bf16[24,64,128]{2,1,0:T(8,128)(2,1)} %get-tuple-element.45), channel_id=1, source_target_pairs={{0,8},{2,10},{4,12},{6,14},{8,0},{10,2},{12,4},{14,6},{1,9},{3,11}... | collective-permute-start | bytes 1179656 | tf_op jit(solution)/shard_map/ppermute | solution.py:268
  31.5 83.7 %all-to-all-start.1 = ((bf16[32,4,4096]{2,0,1:T(8,128)(2,1)}), bf16[32,4,4096]{2,0,1:T(8,128)(2,1)S(1)}, u32[]{:S(2)}, u32[]{:S(2)}) async-start(bf16[32,4,4096]{2,0,1:T(8,128)(2,1)} %bitcast.32), calls=%async_computation.1 | async-start | bytes 2097152 | tf_op jit(solution)/shard_map/all_to_all | solution.py:248
  66.2 17.6 %collective-permute-start.11 = (bf16[24,64,128]{2,1,0:T(8,128)(2,1)}, bf16[24,64,128]{2,1,0:T(8,128)(2,1)S(1)}, u32[]{:S(2)}, u32[]{:S(2)}) collective-permute-start(bf16[24,64,128]{2,1,0:T(8,128)(2,1)} %collective-permute-done.10), channel_id=1, source_target_pairs={{0,16},{16,0},{1,17},{17,1},{2,18},{18,2},{3,19},{19,3},{4,20},{20... | collective-permute-start | bytes 1179656 | tf_op jit(solution)/shard_map/ppermute | solution.py:271
  67.8 28.3 %collective-permute-start.2 = (bf16[24,64,128]{2,1,0:T(8,128)(2,1)}, bf16[24,64,128]{2,1,0:T(8,128)(2,1)S(1)}, u32[]{:S(2)}, u32[]{:S(2)}) collective-permute-start(bf16[24,64,128]{2,1,0:T(8,128)(2,1)} %collective-permute-done), channel_id=1, source_target_pairs={{0,16},{16,0},{1,17},{17,1},{2,18},{18,2},{3,19},{19,3},{4,20},{20... | collective-permute-start | bytes 1179656 | tf_op jit(solution)/shard_map/ppermute | solution.py:271
  74.5 20.8 %collective-permute-start.7 = (bf16[24,64,128]{2,1,0:T(8,128)(2,1)S(1)}, bf16[24,64,128]{2,1,0:T(8,128)(2,1)S(1)}, u32[]{:S(2)}, u32[]{:S(2)}) collective-permute-start(bf16[24,64,128]{2,1,0:T(8,128)(2,1)S(1)} %collective-permute-done.6), channel_id=1, source_target_pairs={{0,16},{16,0},{1,17},{17,1},{2,18},{18,2},{3,19},{19,3},{4,20},{20... | collective-permute-start | bytes 1179656 | tf_op jit(solution)/shard_map/ppermute | solution.py:271
  78.6 19.5 %copy-start.8 = (bf16[32,4,4096]{2,0,1:T(8,128)(2,1)S(1)}, bf16[32,4,4096]{2,0,1:T(8,128)(2,1)}, u32[]{:S(2)}) copy-start(bf16[32,4,4096]{2,0,1:T(8,128)(2,1)} %copy-done.7) | copy-start | bytes 3145732
  81.5 34.2 %collective-permute-start.4 = (bf16[24,64,128]{2,1,0:T(8,128)(2,1)S(1)}, bf16[24,64,128]{2,1,0:T(8,128)(2,1)}, u32[]{:S(2)}, u32[]{:S(2)}) collective-permute-start(bf16[24,64,128]{2,1,0:T(8,128)(2,1)S(1)} %collective-permute-done.3), channel_id=1, source_target_pairs={{0,16},{16,0},{1,17},{17,1},{2,18},{18,2},{3,19},{19,3},{4,20},{20... | collective-permute-start | bytes 1179656 | tf_op jit(solution)/shard_map/ppermute | solution.py:271
  84.6 33.2 %collective-permute-start.12 = (bf16[48,64,128]{2,1,0:T(8,128)(2,1)}, bf16[48,64,128]{2,1,0:T(8,128)(2,1)}, u32[]{:S(2)}, u32[]{:S(2)}) collective-permute-start(bf16[48,64,128]{2,1,0:T(8,128)(2,1)} %constant_dynamic-update-slice_fusion.4.refs_2_.refs_6_), channel_id=1, source_target_pairs={{0,1},{1,0},{2,3},{3,2},{4,5},{5,4},{6,7},{7,6},{8,9},{9,8},{10,11... | collective-permute-start | bytes 2359304 | tf_op jit(solution)/shard_map/ppermute | solution.py:274
  96.1 30.4 %collective-permute-start.8 = (bf16[48,64,128]{2,1,0:T(8,128)(2,1)}, bf16[48,64,128]{2,1,0:T(8,128)(2,1)}, u32[]{:S(2)}, u32[]{:S(2)}) collective-permute-start(bf16[48,64,128]{2,1,0:T(8,128)(2,1)} %constant_dynamic-update-slice_fusion.2.refs_0_.refs_8_), channel_id=1, source_target_pairs={{0,1},{1,0},{2,3},{3,2},{4,5},{5,4},{6,7},{7,6},{8,9},{9,8},{10,11... | collective-permute-start | bytes 2359304 | tf_op jit(solution)/shard_map/ppermute | solution.py:274
  115.2 2.8 %collective-permute-start.9 = (bf16[48,64,128]{2,1,0:T(8,128)(2,1)}, bf16[48,64,128]{2,1,0:T(8,128)(2,1)}, u32[]{:S(2)}, u32[]{:S(2)}) collective-permute-start(bf16[48,64,128]{2,1,0:T(8,128)(2,1)} %pad_maximum_fusion.refs_0_.refs_4_), channel_id=1, source_target_pairs={{0,1},{1,0},{2,3},{3,2},{4,5},{5,4},{6,7},{7,6},{8,9},{9,8},{10,11... | collective-permute-start | bytes 2359304 | tf_op jit(solution)/shard_map/ppermute | solution.py:274
  117.5 11.2 %collective-permute-start.5 = (bf16[48,64,128]{2,1,0:T(8,128)(2,1)}, bf16[48,64,128]{2,1,0:T(8,128)(2,1)}, u32[]{:S(2)}, u32[]{:S(2)}) collective-permute-start(bf16[48,64,128]{2,1,0:T(8,128)(2,1)} %constant_dynamic-update-slice_fusion.refs_0_.refs_10_), channel_id=1, source_target_pairs={{0,1},{1,0},{2,3},{3,2},{4,5},{5,4},{6,7},{7,6},{8,9},{9,8},{10,11... | collective-permute-start | bytes 2359304 | tf_op jit(solution)/shard_map/ppermute | solution.py:274
  128.7 17.6 %copy-start.5 = (bf16[32,128,128]{2,1,0:T(8,128)(2,1)S(1)}, bf16[32,128,128]{2,1,0:T(8,128)(2,1)}, u32[]{:S(2)}) copy-start(bf16[32,128,128]{2,1,0:T(8,128)(2,1)} %select_convert_fusion.high_ref) | copy-start | bytes 3145732
  128.7 17.6 %copy-start.6 = (bf16[32,128,128]{2,1,0:T(8,128)(2,1)S(1)}, bf16[32,128,128]{2,1,0:T(8,128)(2,1)}, u32[]{:S(2)}) copy-start(bf16[32,128,128]{2,1,0:T(8,128)(2,1)} %subtract_convert_fusion.low_ref) | copy-start | bytes 3145732
  130.8 30.7 %copy-start.3 = (bf16[48,64,128]{2,1,0:T(8,128)(2,1)S(1)}, bf16[48,64,128]{2,1,0:T(8,128)(2,1)}, u32[]{:S(2)}) copy-start(bf16[48,64,128]{2,1,0:T(8,128)(2,1)} %pad_maximum_fusion.refs_0_.refs_4_) | copy-start | bytes 2359300
  130.8 8.7 %collective-permute-start.13 = (bf16[32,4096]{1,0:T(8,128)(2,1)S(1)}, bf16[32,4096]{1,0:T(8,128)(2,1)S(1)}, u32[]{:S(2)}, u32[]{:S(2)}) collective-permute-start(bf16[32,4096]{1,0:T(8,128)(2,1)S(1)} %get-tuple-element.32), channel_id=1, source_target_pairs={{0,2},{2,0},{4,6},{6,4},{8,10},{10,8},{12,14},{14,12},{1,3},{3,1},... | collective-permute-start | bytes 786440 | tf_op jit(solution)/shard_map/ppermute | solution.py:240
  130.9 9.2 %collective-permute-start.14 = (bf16[32,4096]{1,0:T(8,128)(2,1)S(1)}, bf16[32,4096]{1,0:T(8,128)(2,1)S(1)}, u32[]{:S(2)}, u32[]{:S(2)}) collective-permute-start(bf16[32,4096]{1,0:T(8,128)(2,1)S(1)} %get-tuple-element.33), channel_id=1, source_target_pairs={{0,4},{2,6},{4,0},{6,2},{8,12},{10,14},{12,8},{14,10},{1,5},{3,7},... | collective-permute-start | bytes 786440 | tf_op jit(solution)/shard_map/ppermute | solution.py:240
  130.9 15.3 %collective-permute-start.15 = (bf16[32,4096]{1,0:T(8,128)(2,1)S(1)}, bf16[32,4096]{1,0:T(8,128)(2,1)S(1)}, u32[]{:S(2)}, u32[]{:S(2)}) collective-permute-start(bf16[32,4096]{1,0:T(8,128)(2,1)S(1)} %get-tuple-element.34), channel_id=1, source_target_pairs={{0,6},{2,4},{4,2},{6,0},{8,14},{10,12},{12,10},{14,8},{1,7},{3,5},... | collective-permute-start | bytes 786440 | tf_op jit(solution)/shard_map/ppermute | solution.py:240
  147.2 8.4 %collective-permute-start.16 = (bf16[32,4096]{1,0:T(8,128)(2,1)S(1)}, bf16[32,4096]{1,0:T(8,128)(2,1)S(1)}, u32[]{:S(2)}, u32[]{:S(2)}) collective-permute-start(bf16[32,4096]{1,0:T(8,128)(2,1)S(1)} %shard_map.68.refs_0_), channel_id=1, source_target_pairs={{0,2},{2,0},{4,6},{6,4},{8,10},{10,8},{12,14},{14,12},{1,3},{3,1},... | collective-permute-start | bytes 786440 | tf_op jit(solution)/shard_map/ppermute | solution.py:240
  147.6 9.2 %collective-permute-start.17 = (bf16[32,4096]{1,0:T(8,128)(2,1)S(1)}, bf16[32,4096]{1,0:T(8,128)(2,1)S(1)}, u32[]{:S(2)}, u32[]{:S(2)}) collective-permute-start(bf16[32,4096]{1,0:T(8,128)(2,1)S(1)} %shard_map.68.refs_0_), channel_id=1, source_target_pairs={{0,4},{2,6},{4,0},{6,2},{8,12},{10,14},{12,8},{14,10},{1,5},{3,7},... | collective-permute-start | bytes 786440 | tf_op jit(solution)/shard_map/ppermute | solution.py:240
  147.9 13.6 %collective-permute-start.18 = (bf16[32,4096]{1,0:T(8,128)(2,1)S(1)}, bf16[32,4096]{1,0:T(8,128)(2,1)S(1)}, u32[]{:S(2)}, u32[]{:S(2)}) collective-permute-start(bf16[32,4096]{1,0:T(8,128)(2,1)S(1)} %shard_map.68.refs_0_), channel_id=1, source_target_pairs={{0,6},{2,4},{4,2},{6,0},{8,14},{10,12},{12,10},{14,8},{1,7},{3,5},... | collective-permute-start | bytes 786440 | tf_op jit(solution)/shard_map/ppermute | solution.py:240
  171.0 24.7 %collective-permute-start.19 = (bf16[32,4096]{1,0:T(8,128)(2,1)S(1)}, bf16[32,4096]{1,0:T(8,128)(2,1)S(1)}, u32[]{:S(2)}, u32[]{:S(2)}) collective-permute-start(bf16[32,4096]{1,0:T(8,128)(2,1)S(1)} %get-tuple-element.36), channel_id=1, source_target_pairs={{0,2},{2,0},{4,6},{6,4},{8,10},{10,8},{12,14},{14,12},{1,3},{3,1},... | collective-permute-start | bytes 786440 | tf_op jit(solution)/shard_map/ppermute | solution.py:240
  173.3 26.0 %collective-permute-start.20 = (bf16[32,4096]{1,0:T(8,128)(2,1)S(1)}, bf16[32,4096]{1,0:T(8,128)(2,1)S(1)}, u32[]{:S(2)}, u32[]{:S(2)}) collective-permute-start(bf16[32,4096]{1,0:T(8,128)(2,1)S(1)} %get-tuple-element.37), channel_id=1, source_target_pairs={{0,4},{2,6},{4,0},{6,2},{8,12},{10,14},{12,8},{14,10},{1,5},{3,7},... | collective-permute-start | bytes 786440 | tf_op jit(solution)/shard_map/ppermute | solution.py:240
  173.3 26.1 %collective-permute-start.21 = (bf16[32,4096]{1,0:T(8,128)(2,1)S(1)}, bf16[32,4096]{1,0:T(8,128)(2,1)S(1)}, u32[]{:S(2)}, u32[]{:S(2)}) collective-permute-start(bf16[32,4096]{1,0:T(8,128)(2,1)S(1)} %get-tuple-element.38), channel_id=1, source_target_pairs={{0,6},{2,4},{4,2},{6,0},{8,14},{10,12},{12,10},{14,8},{1,7},{3,5},... | collective-permute-start | bytes 786440 | tf_op jit(solution)/shard_map/ppermute | solution.py:240
  195.5 9.1 %collective-permute-start.22 = (bf16[32,4096]{1,0:T(8,128)(2,1)S(1)}, bf16[32,4096]{1,0:T(8,128)(2,1)S(1)}, u32[]{:S(2)}, u32[]{:S(2)}) collective-permute-start(bf16[32,4096]{1,0:T(8,128)(2,1)S(1)} %get-tuple-element.40), channel_id=1, source_target_pairs={{0,2},{2,0},{4,6},{6,4},{8,10},{10,8},{12,14},{14,12},{1,3},{3,1},... | collective-permute-start | bytes 786440 | tf_op jit(solution)/shard_map/ppermute | solution.py:240
  195.5 9.1 %collective-permute-start.23 = (bf16[32,4096]{1,0:T(8,128)(2,1)S(1)}, bf16[32,4096]{1,0:T(8,128)(2,1)S(1)}, u32[]{:S(2)}, u32[]{:S(2)}) collective-permute-start(bf16[32,4096]{1,0:T(8,128)(2,1)S(1)} %get-tuple-element.41), channel_id=1, source_target_pairs={{0,4},{2,6},{4,0},{6,2},{8,12},{10,14},{12,8},{14,10},{1,5},{3,7},... | collective-permute-start | bytes 786440 | tf_op jit(solution)/shard_map/ppermute | solution.py:240
  195.8 12.5 %collective-permute-start.24 = (bf16[32,4096]{1,0:T(8,128)(2,1)S(1)}, bf16[32,4096]{1,0:T(8,128)(2,1)S(1)}, u32[]{:S(2)}, u32[]{:S(2)}) collective-permute-start(bf16[32,4096]{1,0:T(8,128)(2,1)S(1)} %get-tuple-element.42), channel_id=1, source_target_pairs={{0,6},{2,4},{4,2},{6,0},{8,14},{10,12},{12,10},{14,8},{1,7},{3,5},... | collective-permute-start | bytes 786440 | tf_op jit(solution)/shard_map/ppermute | solution.py:240
  (9 other events, 33.9 us)

commit v7 on v6

v7 whole, which is shorter than its diff:
```python
import functools

import jax
import jax.numpy as jnp
from jax import lax
from jax.experimental import pallas as pl
from jax.experimental.pallas import tpu as pltpu
from jax.sharding import PartitionSpec as P

TILE = 64
PAIR = 2 * TILE
UNROLL = 4
VMEM_LIMIT = 16 * 1024 * 1024
PARTS = 4
RANGES = ((0, 2), (2, 3), (3, 4))
OWN_FORWARD, OWN_BACKWARD, OTHER_FORWARD, OTHER_BACKWARD = range(4)
BOUNDS = 3
STEPS = len(RANGES) + 1
LISTS = BOUNDS + 4 * STEPS


def bits(count):
    return max(1, (count - 1).bit_length())


def pair_lists(codes, keys, live, blocks, absent):
    n_lists, tiles = codes.shape
    n_keys = len(RANGES) * blocks
    order = jnp.arange(tiles, dtype=jnp.int32)
    key_range = jnp.arange(n_keys, dtype=jnp.int32)
    mine = (keys[:, None, :] == key_range[None, :, None]) & live[:, None, :]
    pairs = (jnp.sum(mine, axis=2, dtype=jnp.int32) + 1) // 2
    lower = key_range[None, :, None] < key_range[None, None, :]
    starts = jnp.sum(jnp.where(lower, pairs[:, :, None], 0), axis=1, dtype=jnp.int32)
    before = (
        (keys[:, :, None] == keys[:, None, :]) & live[:, :, None] & (order[:, None] < order[None, :])
    )
    entry = jnp.sum(before, axis=1, dtype=jnp.int32) + 2 * jnp.sum(
        jnp.where(mine, starts[:, :, None], 0), axis=1, dtype=jnp.int32
    )
    entry = jnp.where(live, entry, -1)
    found = entry[:, :, None] == jnp.arange(tiles + n_keys, dtype=jnp.int32)
    entries = absent + jnp.sum(
        jnp.where(found, codes[:, :, None] - absent, 0), axis=1, dtype=jnp.int32
    )
    ends = jnp.arange(STEPS, dtype=jnp.int32) * blocks
    bounds = jnp.sum(
        jnp.where(key_range[None, :, None] < ends, pairs[:, :, None], 0), axis=1, dtype=jnp.int32
    )
    return jnp.concatenate([bounds.reshape(-1), entries.reshape(-1)])


def padded_tile(values, half):
    zero = jnp.zeros_like(values)
    return jnp.concatenate(
        [jnp.where(half == 0, values, zero), jnp.where(half == 1, values, zero)], axis=0
    )


def pair_loop(sizes, meta, ref, proj, which, first, last, origin, step):
    tiles, segments, blocks = sizes
    begin, end = (meta[BOUNDS + STEPS * which + number] for number in (first, last))
    base = LISTS + which * (tiles + len(RANGES) * blocks)

    def tile(entry, live):
        code = meta[base + entry]
        index = jnp.where(live, (code & ((1 << bits(tiles)) - 1)) - origin, 0)
        code = code >> bits(tiles)
        segment = code & ((1 << bits(segments)) - 1)
        code = code >> bits(segments)
        block = code & ((1 << bits(blocks)) - 1)
        half = jnp.where(live, (segment & 1) + 2 * (code >> bits(blocks)), 2)
        points = pl.ds(pl.multiple_of((segment >> 1) * PAIR, PAIR), PAIR)
        lanes = pl.ds(pl.multiple_of(block * proj, proj), proj)
        return points, lanes, padded_tile(ref[jnp.maximum(index, 0)], half)

    def group(index, carry):
        for lane in range(UNROLL):
            pair = begin + index * UNROLL + lane
            live = pair < end
            pair = jnp.minimum(pair, end - 1)
            step(tile(2 * pair, live), tile(2 * pair + 1, live))
        return carry

    lax.fori_loop(0, (end - begin + UNROLL - 1) // UNROLL, group, 0)


def join_pieces(meta, pieces, joined, first):
    size = pieces[0].shape[0]
    for number, ref in enumerate(pieces):

        @pl.when(meta[2] > first + number // 2 * 2 * size)
        def copy(number=number, ref=ref):
            joined[number * size : (number + 1) * size] = ref[...]


def rows_of(refs, lanes):
    return jnp.concatenate([ref[:, lanes] for ref in refs], axis=0)


def store_rows(refs, values):
    start = 0
    for ref in refs:
        rows = ref.shape[0]
        ref[...] = values[start : start + rows].astype(ref.dtype)
        start += rows


def project_kernel(sizes, n_pieces, spot, first, last, meta, wave, *refs):
    pieces, refs = refs[:n_pieces], refs[n_pieces:]
    proj = pieces[0].shape[2]
    values = pieces[0]
    if n_pieces > 1:
        values, refs = refs[-1], refs[:-1]
        join_pieces(meta, pieces, values, spot[-1])
    total = refs[-1]
    total[...] = jnp.zeros_like(total) if first else refs[0][...]

    def step(one, two):
        waves = jnp.concatenate([wave[:, one[0]], wave[:, two[0]]], axis=1)
        tiles = jnp.concatenate([one[2], two[2]], axis=0)
        total[:, one[1]] += jnp.dot(waves, tiles, preferred_element_type=jnp.float32)

    pair_loop(sizes, meta, values, proj, *spot, step)
    if last:
        outs = refs[1:-1]
        rows = outs[0].shape[0]
        for d, out in enumerate(outs):
            start = 0 if len(outs) == 1 else pl.multiple_of((meta[0] ^ d) * rows, rows)
            out[...] = total[pl.ds(start, rows), :].astype(out.dtype)


def spread_kernel(sizes, n_rows, n_pieces, which, meta, *refs):
    applied, refs = refs[:n_rows], refs[n_rows:]
    pieces, refs = refs[:n_pieces], refs[n_pieces:]
    proj = pieces[0].shape[2]
    values = pieces[0]
    if n_pieces > 1:
        values, refs = refs[-1], refs[:-1]
        join_pieces(meta, pieces, values, 0)
    outs, field = refs[:-1], refs[-1]
    field[...] = jnp.zeros_like(field)

    def step(one, two):
        rows = jnp.concatenate([rows_of(applied, one[1]), rows_of(applied, two[1])], axis=1)
        tiles = jnp.concatenate([one[2], two[2]], axis=1)
        field[:, one[0]] += lax.dot_general(
            rows, tiles, (((1,), (1,)), ((), ())), preferred_element_type=jnp.float32
        )

    pair_loop(sizes, meta, values, proj, which, 0, len(RANGES), 0, step)
    store_rows(outs, field)


WHOLE = pl.BlockSpec(memory_space=pltpu.VMEM)


COST = pl.CostEstimate(flops=1, bytes_accessed=1, transcendentals=0)


def join_small(blocks):
    return blocks if blocks[0].shape[0] % 16 == 0 else [jnp.concatenate(blocks)]


def split_small(blocks, count):
    return blocks if len(blocks) == count else jnp.split(blocks[0], count)


def joined_shape(pieces):
    if len(pieces) == 1:
        return []
    shape = pieces[0].shape
    return [pltpu.VMEM((len(pieces) * shape[0],) + shape[1:], jnp.bfloat16)]


def project(sizes, meta, wave, pieces, count, width, spot, total=None, last=False):
    rows = wave.shape[0]
    bands = rows // count
    split = bands % 16 == 0
    operands = [wave, *pieces] + ([] if total is None else [total])
    outs = count if split else 1
    out_shape = [jax.ShapeDtypeStruct((rows // outs, width), jnp.bfloat16)] * outs
    return pl.pallas_call(
        functools.partial(
            project_kernel, sizes, len(pieces), spot, total is None, last
        ),
        grid_spec=pltpu.PrefetchScalarGridSpec(
            num_scalar_prefetch=1,
            grid=(1,),
            in_specs=[WHOLE] * len(operands),
            out_specs=[WHOLE] * outs if last else WHOLE,
            scratch_shapes=([pltpu.VMEM((rows, width), jnp.float32)] if last else [])
            + joined_shape(pieces),
        ),
        out_shape=out_shape if last else jax.ShapeDtypeStruct((rows, width), jnp.float32),
        compiler_params=pltpu.CompilerParams(vmem_limit_bytes=VMEM_LIMIT),
        cost_estimate=COST,
    )(meta, *operands)


def spread(sizes, meta, applied, pieces, points, which):
    count = len(applied)
    applied = join_small(applied)
    rows = sum(block.shape[0] for block in applied)
    result = pl.pallas_call(
        functools.partial(spread_kernel, sizes, len(applied), len(pieces), which),
        grid_spec=pltpu.PrefetchScalarGridSpec(
            num_scalar_prefetch=1,
            grid=(1,),
            in_specs=[WHOLE] * (len(applied) + len(pieces)),
            out_specs=[WHOLE] * len(applied),
            scratch_shapes=[pltpu.VMEM((rows, points), jnp.float32)] + joined_shape(pieces),
        ),
        out_shape=[
            jax.ShapeDtypeStruct((block.shape[0], points), jnp.bfloat16) for block in applied
        ],
        compiler_params=pltpu.CompilerParams(vmem_limit_bytes=VMEM_LIMIT),
        cost_estimate=COST,
    )(meta, *applied, *pieces)
    return split_small(result, count)


def two_parts(values):
    high = values.astype(jnp.bfloat16)
    return high, (values - high.astype(jnp.float32)).astype(jnp.bfloat16)


def couple_kernel(high_ref, low_ref, *refs):
    parts, out_ref = refs[:-1], refs[-1]
    blocks, proj, unused = high_ref.shape
    for block in range(blocks):
        lanes = slice(block * proj, (block + 1) * proj)
        total = parts[0][:, lanes].astype(jnp.float32)
        for part in parts[1:]:
            total += part[:, lanes].astype(jnp.float32)
        high, low = two_parts(total)
        result = jnp.dot(high, high_ref[block], preferred_element_type=jnp.float32)
        result += jnp.dot(high, low_ref[block], preferred_element_type=jnp.float32)
        result += jnp.dot(low, high_ref[block], preferred_element_type=jnp.float32)
        out_ref[:, lanes] = result.astype(out_ref.dtype)


def couple(parts, high, low):
    return pl.pallas_call(
        couple_kernel,
        in_specs=[WHOLE] * (2 + len(parts)),
        out_specs=WHOLE,
        out_shape=jax.ShapeDtypeStruct(parts[0].shape, jnp.bfloat16),
        compiler_params=pltpu.CompilerParams(vmem_limit_bytes=VMEM_LIMIT),
        cost_estimate=COST,
    )(high, low, *parts)


def coupling_matrix(coupling):
    blocks, atoms, width, unused = coupling.shape
    proj = atoms * width
    wide = jnp.tile(coupling.reshape(blocks, proj, width), (1, 1, atoms))
    same = jnp.arange(proj)[:, None] // width == jnp.arange(proj)[None, :] // width
    return jnp.where(same[None], wide, 0.0)


def body(n_grid, wavefunctions, tile_segment, tile_block, tile_count, projectors, coupling):
    half = n_grid // 2
    bands, npts = wavefunctions.shape
    points = npts // n_grid
    tiles = projectors.shape[0]
    width = coupling.shape[0] * projectors.shape[2]
    index = lax.axis_index("grid")
    side, place = index // half, index % half
    group, core = lax.axis_index("groups"), lax.axis_index("band")
    partners = [(i, (i + half) % n_grid) for i in range(n_grid)]
    pools = [list(range(half)), list(range(half, n_grid))]
    swap = [(0, 1), (1, 0)]

    def exchange(blocks):
        return [blocks[0]] + [
            lax.ppermute(
                blocks[d], "grid", [(i, i // half * half + (i % half ^ d)) for i in range(n_grid)]
            )
            for d in range(1, half)
        ]

    def to_bricks(which):
        part = lax.dynamic_slice_in_dim(wavefunctions, which * half * points, half * points, 1)
        return lax.all_to_all(
            part, "grid", split_axis=1, concat_axis=0, tiled=True, axis_index_groups=pools
        )

    segments, blocks = points // TILE, coupling.shape[0]
    sizes = (tiles, segments, blocks)
    size = tiles // PARTS
    share = size // 4
    slots = jnp.arange(tiles, dtype=jnp.int32)
    part, quarter = slots // size, slots % size // share
    held = part * size + slots % share
    held += share * ((quarter // 2 ^ group) + 2 * (quarter % 2 ^ core))

    numbers = jnp.stack([tile_segment, tile_block, jnp.broadcast_to(tile_count, (tiles,))])
    others = lax.ppermute(numbers, "grid", partners)
    absent = 1 << (bits(tiles) + bits(segments) + bits(blocks))
    segment, block = (jnp.stack([numbers[i], others[i]]) for i in (0, 1))
    codes = jnp.stack([slots, held]) + ((segment + (block << bits(segments))) << bits(tiles))
    live = slots < jnp.stack([numbers[2], others[2]])
    group_of = sum(jnp.where(part >= first, 1, 0) for first, end in RANGES[1:])
    keys = jnp.stack([block + blocks * jnp.stack([0 * part, group_of]), segment // 2], axis=1)
    codes, live = (jnp.stack([values] * 2, axis=1) for values in (codes, live))
    meta = jnp.concatenate(
        [
            jnp.stack([place, numbers[2, 0], others[2, 0]]),
            pair_lists(*(v.reshape(4, tiles) for v in (codes, keys, live)), blocks, absent),
        ]
    )

    own_wave = to_bricks(side)
    other_wave = to_bricks(1 - side)
    spot = (OWN_FORWARD, 0, len(RANGES), 0)
    own_total = project(sizes, meta, own_wave, [projectors], half, width, spot)
    matrix = two_parts(coupling_matrix(coupling))

    pieces = []
    for part in range(PARTS):
        mine = lax.dynamic_slice_in_dim(
            projectors, part * size + (2 * group + core) * share, share, 0
        )
        mine = lax.ppermute(mine, "grid", partners)
        if part == 0:
            mine, total, matrix = lax.optimization_barrier((mine, own_total, matrix))
        else:
            mine = lax.optimization_barrier((mine, own_total))[0]
        both = jnp.concatenate([mine, lax.ppermute(mine, "groups", swap)])
        if part == 0:
            both, other_wave = lax.optimization_barrier((both, other_wave))
        pieces += [both, lax.ppermute(both, "band", swap)]

    for number, (first, end) in enumerate(RANGES):
        total = project(
            sizes,
            meta,
            other_wave,
            pieces[2 * first : 2 * end],
            half,
            width,
            (OTHER_FORWARD, number, number + 1, first * size),
            total,
            last=end == PARTS,
        )
    if len(total) < half:
        total = [lax.dynamic_slice_in_dim(total[0], (place ^ d) * bands, bands, 0) for d in range(half)]

    applied = couple(exchange(total), *matrix)
    applied = exchange([applied] * half)

    result = jnp.zeros((bands, npts), jnp.bfloat16)
    for which, field in (
        (1 - side, spread(sizes, meta, applied, pieces, points, OTHER_BACKWARD)),
        (side, spread(sizes, meta, applied, [projectors], points, OWN_BACKWARD)),
    ):
        for d, block in enumerate(exchange(field)):
            start = (which * half + (place ^ d)) * points
            result = lax.dynamic_update_slice_in_dim(result, block, start, 1)
    return result


def solution(mesh):
    in_specs = (
        P(("groups", "grid", "band"), None),
        P("grid"),
        P("grid"),
        P("grid"),
        P("grid", None, None),
        P(),
    )
    out_specs = P(("groups", "grid", "band"), None)
    return jax.shard_map(
        functools.partial(body, mesh.shape["grid"]),
        mesh=mesh,
        in_specs=in_specs,
        out_specs=out_specs,
        check_vma=False,
    )
```

time: 211 us -> 215 us (1.019)
  Pallas kernels: 54.2 us -> 41.4 us
  local copies, waits for them, and re-layouts: 25.8 us -> 35.6 us
  waiting for transfers between devices: 83.7 us -> 90.8 us
    ppermute x4, waiting for transfers between devices: 33 us -> 10.5 us  [body(): mine = lax.ppermute(mine, 'grid', partners)]
    all_to_all x2, waiting for transfers between devices: 8.43 us -> 23.5 us  [to_bricks(): lax.all_to_all(part, 'grid', split_axis=1, concat_axis=0, tiled=True, axi...]
    pallas_call x6, Pallas kernels: 53.3 us -> 40.5 us  [the longest x2 20.4 us: spread(): pl.pallas_call(functools.partial(spread_kernel, sizes, len(applied), len(...]
    ppermute x4, waiting for transfers between devices: 10.7 us -> 22.4 us  [body(): both = jnp.concatenate([mine, lax.ppermute(mine, 'groups', swap)])]
    unnamed x31 -> x57, local copies, waits for them, and re-layouts: 10.1 us -> 16.7 us
    ppermute x1, starting transfers between devices: 0.34 us -> 4.04 us  [body(): others = lax.ppermute(numbers, 'grid', partners)]
    ppermute x4, starting transfers between devices: 8.1 us -> 5.85 us  [body(): mine = lax.ppermute(mine, 'grid', partners)]
  transfers between devices with their start and end apart: 27 -> 27, of which waited for: 14 -> 15; matrix products, arithmetic and copies ran while one was open for 11% -> 14% of each run, Pallas kernels for 20% -> 10%
where the time goes in v7:
time: 215 us
  waiting for transfers between devices  90.8 us (42%)
  Pallas kernels  41.4 us (19%)
  starting transfers between devices  37.1 us (17%)
  local copies, waits for them, and re-layouts  35.6 us (17%)
  other arithmetic  8.32 us (4%)
    ppermute x12, waiting for transfers between devices, exchange(): lax.ppermute(blocks[d], 'grid', [(i, i // half * half + (i % half ^ d)) f...  33.1 us
    all_to_all x2, waiting for transfers between devices, to_bricks(): lax.all_to_all(part, 'grid', split_axis=1, concat_axis=0, tiled=True, axi...  23.5 us
    ppermute x4, waiting for transfers between devices, body(): both = jnp.concatenate([mine, lax.ppermute(mine, 'groups', swap)])  22.4 us
    pallas_call x2, Pallas kernels, spread(): pl.pallas_call(functools.partial(spread_kernel, sizes, len(applied), len(...  20.4 us
    pallas_call x4, Pallas kernels, project(): pl.pallas_call(functools.partial(project_kernel, sizes, len(pieces), spot...  20 us
    unnamed x57, local copies, waits for them, and re-layouts  16.7 us
    ppermute x12, starting transfers between devices, exchange(): lax.ppermute(blocks[d], 'grid', [(i, i // half * half + (i % half ^ d)) f...  14.2 us
    ppermute x4, waiting for transfers between devices, body(): mine = lax.ppermute(mine, 'grid', partners)  10.5 us
  transfers between devices with their start and end apart: 27, of which 15 were waited for; matrix products, arithmetic and copies ran while one was open for 14% of the time, Pallas kernels for 10%

profile of v7, /device:TPU:0, one launch (start us, length us, event | category | flops | bytes accessed | tf_op | source)
XLA Modules:
  0.0 214.6 jit_solution(7791545844873378965)
XLA Ops:
  2.3 4.0 %collective-permute-start = (s32[3,384]{1,0:T(4,128)S(1)}, s32[3,384]{1,0:T(4,128)S(1)}, u32[]{:S(2)}, u32[]{:S(2)}) collective-permute-start(s32[3,384]{1,0:T(4,128)S(1)} %add_add_fusion), channel_id=1, source_target_pairs={{0,8},{2,10},{4,12},{6,14},{8,0},{10,2},{12,4},{14,6},{1,9},{3,11}... | collective-permute-start | bytes 13832 | tf_op jit(solution)/shard_map/ppermute | solution.py:299
  6.4 2.6 %constant_dynamic-slice_fusion = (bf16[24,64,128]{2,1,0:T(8,128)(2,1)}, bf16[24,64,128]{2,1,0:T(8,128)(2,1)}, bf16[24,64,128]{2,1,0:T(8,128)(2,1)}, bf16[24,64,128]{2,1,0:T(8,128)(2,1)}) fusion(bf16[384,64,128]{2,1,0:T(8,128)(2,1)} %refs_4_.1, s32[]{:T(128)S(6)} %select_n.278, s32[]{:T(128)S(6)} %select_n.277, s32[]{:T(128)S(6)} %select_n.276, s32[]{:T(128)S(6)} %select_n.270), kind=kLoop, calls=%fused_computation.51 | loop fusion | bytes 3145744 | tf_op jit(solution)/shard_map/dynamic_slice | solution.py:322
  9.0 2.9 %collective-permute-start.6 = (bf16[24,64,128]{2,1,0:T(8,128)(2,1)}, bf16[24,64,128]{2,1,0:T(8,128)(2,1)}, u32[]{:S(2)}, u32[]{:S(2)}) collective-permute-start(bf16[24,64,128]{2,1,0:T(8,128)(2,1)} %get-tuple-element.48), channel_id=1, source_target_pairs={{0,8},{2,10},{4,12},{6,14},{8,0},{10,2},{12,4},{14,6},{1,9},{3,11}... | collective-permute-start | bytes 1179656 | tf_op jit(solution)/shard_map/ppermute | solution.py:325
  11.9 2.9 %collective-permute-start.1 = (bf16[24,64,128]{2,1,0:T(8,128)(2,1)}, bf16[24,64,128]{2,1,0:T(8,128)(2,1)}, u32[]{:S(2)}, u32[]{:S(2)}) collective-permute-start(bf16[24,64,128]{2,1,0:T(8,128)(2,1)} %get-tuple-element.50), channel_id=1, source_target_pairs={{0,8},{2,10},{4,12},{6,14},{8,0},{10,2},{12,4},{14,6},{1,9},{3,11}... | collective-permute-start | bytes 1179656 | tf_op jit(solution)/shard_map/ppermute | solution.py:325
  16.0 3.8 %all-to-all-start = ((bf16[32,4,4096]{2,0,1:T(8,128)(2,1)}), bf16[32,4,4096]{2,0,1:T(8,128)(2,1)S(1)}, u32[]{:S(2)}, u32[]{:S(2)}) async-start(bf16[32,4,4096]{2,0,1:T(8,128)(2,1)} %bitcast.27), calls=%async_computation | async-start | bytes 2097152 | tf_op jit(solution)/shard_map/all_to_all | solution.py:285
  21.7 2.9 %copy.21 = f32[32,128,128]{2,1,0:T(8,128)} copy(f32[32,128,128]{1,2,0:T(8,128)} %broadcast_bitcast_fusion) | data formatting | bytes 4194304 | tf_op jit(solution)/shard_map/tile | solution.py:257
  24.7 3.1 %subtract_convert_fusion.low_ref = bf16[32,128,128]{2,1,0:T(8,128)(2,1)} fusion(f32[32,128,128]{2,1,0:T(8,128)} %copy.21, pred[128,128]{1,0:T(8,128)(4,1)S(1)} %broadcast_compare_fusion), kind=kLoop, calls=%fused_computation.3 | loop fusion | flops 2621440 | bytes 3162112 | tf_op jit(solution)/shard_map/convert_element_type | solution.py:225
  30.7 23.5 %all-to-all-done = bf16[32,4,4096]{2,0,1:T(8,128)(2,1)S(1)} async-done(((bf16[32,4,4096]{2,0,1:T(8,128)(2,1)}), bf16[32,4,4096]{2,0,1:T(8,128)(2,1)S(1)}, u32[]{:S(2)}, u32[]{:S(2)}) %all-to-all-start) | async-done | bytes 1048608 | tf_op jit(solution)/shard_map/all_to_all | solution.py:285
  54.2 4.6 %all-to-all-start.1 = ((bf16[32,4,4096]{2,0,1:T(8,128)(2,1)}), bf16[32,4,4096]{2,0,1:T(8,128)(2,1)S(1)}, u32[]{:S(2)}, u32[]{:S(2)}) async-start(bf16[32,4,4096]{2,0,1:T(8,128)(2,1)} %bitcast.26), calls=%async_computation.1 | async-start | bytes 2097152 | tf_op jit(solution)/shard_map/all_to_all | solution.py:285
  61.8 2.8 %copy-done = bf16[384,64,128]{2,1,0:T(8,128)(2,1)S(1)} copy-done((bf16[384,64,128]{2,1,0:T(8,128)(2,1)S(1)}, bf16[384,64,128]{2,1,0:T(8,128)(2,1)}, u32[]{:S(2)}) %copy-start) | copy-done | bytes 6291480
  65.8 3.5 %shard_map.67.refs_4_ = f32[128,4096]{1,0:T(8,128)S(1)} custom-call(s32[1939]{0:T(1024)S(1)} %concatenate.61.meta, bf16[128,4096]{1,0:T(8,128)(2,1)S(1)} %bitcast.32, bf16[384,64,128]{2,1,0:T(8,128)(2,1)S(1)} %copy-done), custom_call_target="tpu_custom_call" | custom-call | flops 1 | bytes 1 | tf_op jit(solution)/shard_map/pallas_call | solution.py:183
  69.3 10.5 %collective-permute-done.1 = bf16[24,64,128]{2,1,0:T(8,128)(2,1)} collective-permute-done((bf16[24,64,128]{2,1,0:T(8,128)(2,1)}, bf16[24,64,128]{2,1,0:T(8,128)(2,1)}, u32[]{:S(2)}, u32[]{:S(2)}) %collective-permute-start.1) | collective-permute-done | bytes 393248 | tf_op jit(solution)/shard_map/ppermute | solution.py:325
  85.6 1.8 constant_dynamic-update-slice_fusion.3
  89.2 2.8 %collective-permute-done.2 = bf16[24,64,128]{2,1,0:T(8,128)(2,1)S(1)} collective-permute-done((bf16[24,64,128]{2,1,0:T(8,128)(2,1)}, bf16[24,64,128]{2,1,0:T(8,128)(2,1)S(1)}, u32[]{:S(2)}, u32[]{:S(2)}) %collective-permute-start.2) | collective-permute-done | bytes 393248 | tf_op jit(solution)/shard_map/ppermute | solution.py:330
  92.1 1.9 pad_maximum_fusion.refs_0_.refs_4_
  94.0 15.0 %collective-permute-done.11 = bf16[24,64,128]{2,1,0:T(8,128)(2,1)} collective-permute-done((bf16[24,64,128]{2,1,0:T(8,128)(2,1)}, bf16[24,64,128]{2,1,0:T(8,128)(2,1)}, u32[]{:S(2)}, u32[]{:S(2)}) %collective-permute-start.11) | collective-permute-done | bytes 393248 | tf_op jit(solution)/shard_map/ppermute | solution.py:330
  110.8 4.5 %collective-permute-done.7 = bf16[24,64,128]{2,1,0:T(8,128)(2,1)} collective-permute-done((bf16[24,64,128]{2,1,0:T(8,128)(2,1)}, bf16[24,64,128]{2,1,0:T(8,128)(2,1)}, u32[]{:S(2)}, u32[]{:S(2)}) %collective-permute-start.7) | collective-permute-done | bytes 393248 | tf_op jit(solution)/shard_map/ppermute | solution.py:330
  120.7 7.4 %shard_map.68.refs_2_ = f32[128,4096]{1,0:T(8,128)S(1)} custom-call(s32[1939]{0:T(1024)S(1)} %concatenate.61.meta, bf16[128,4096]{1,0:T(8,128)(2,1)S(1)} %bitcast.29, bf16[48,64,128]{2,1,0:T(8,128)(2,1)S(1)} %copy-done.2, bf16[48,64,128]{2,1,0:T(8,128)(2,1)S(1)} %collective-permute-done.9.refs_1_.refs_5_, bf16[48,64,128]{2,1,0:T(8,128)(2,1)S(1)} %copy-done.5, ...), custom_call_target="tpu_custom_call" | custom-call | flops 1 | bytes 1 | tf_op jit(solution)/shard_map/pallas_call | solution.py:183
  128.2 4.6 %shard_map.69.refs_2_ = f32[128,4096]{1,0:T(8,128)S(1)} custom-call(s32[1939]{0:T(1024)S(1)} %concatenate.61.meta, bf16[128,4096]{1,0:T(8,128)(2,1)S(1)} %bitcast.30, bf16[48,64,128]{2,1,0:T(8,128)(2,1)S(1)} %copy-done.7, bf16[48,64,128]{2,1,0:T(8,128)(2,1)S(1)} %collective-permute-done.8.refs_1_.refs_9_, f32[128,4096]{1,0:T(8,128)S(1)} %shard_map.68.refs_2_), custom_call_target="tpu_custom_call" | custom-call | flops 1 | bytes 1 | tf_op jit(solution)/shard_map/pallas_call | solution.py:183
  132.9 4.5 %shard_map.70 = (bf16[32,4096]{1,0:T(8,128)(2,1)S(1)}, bf16[32,4096]{1,0:T(8,128)(2,1)S(1)}, bf16[32,4096]{1,0:T(8,128)(2,1)S(1)}, bf16[32,4096]{1,0:T(8,128)(2,1)S(1)}) custom-call(s32[1939]{0:T(1024)S(1)} %concatenate.61.meta, bf16[128,4096]{1,0:T(8,128)(2,1)S(1)} %bitcast.31, bf16[48,64,128]{2,1,0:T(8,128)(2,1)S(1)} %copy-done.4, ...), custom_call_target="tpu_custom_call" | custom-call | flops 1 | bytes 1 | tf_op jit(solution)/shard_map/pallas_call | solution.py:183
  137.6 3.4 %collective-permute-start.15 = (bf16[32,4096]{1,0:T(8,128)(2,1)S(1)}, bf16[32,4096]{1,0:T(8,128)(2,1)S(1)}, u32[]{:S(2)}, u32[]{:S(2)}) collective-permute-start(bf16[32,4096]{1,0:T(8,128)(2,1)S(1)} %get-tuple-element.38), channel_id=1, source_target_pairs={{0,6},{2,4},{4,2},{6,0},{8,14},{10,12},{12,10},{14,8},{1,7},{3,5},... | collective-permute-start | bytes 786440 | tf_op jit(solution)/shard_map/ppermute | solution.py:277
  141.0 4.9 %collective-permute-done.13.refs_1_ = bf16[32,4096]{1,0:T(8,128)(2,1)S(1)} collective-permute-done((bf16[32,4096]{1,0:T(8,128)(2,1)S(1)}, bf16[32,4096]{1,0:T(8,128)(2,1)S(1)}, u32[]{:S(2)}, u32[]{:S(2)}) %collective-permute-start.13) | collective-permute-done | bytes 262176 | tf_op jit(solution)/shard_map/ppermute | solution.py:277
  146.7 5.9 %collective-permute-done.15.refs_3_ = bf16[32,4096]{1,0:T(8,128)(2,1)S(1)} collective-permute-done((bf16[32,4096]{1,0:T(8,128)(2,1)S(1)}, bf16[32,4096]{1,0:T(8,128)(2,1)S(1)}, u32[]{:S(2)}, u32[]{:S(2)}) %collective-permute-start.15) | collective-permute-done | bytes 262176 | tf_op jit(solution)/shard_map/ppermute | solution.py:277
  157.1 6.8 %collective-permute-done.18.refs_3_ = bf16[32,4096]{1,0:T(8,128)(2,1)} collective-permute-done((bf16[32,4096]{1,0:T(8,128)(2,1)S(1)}, bf16[32,4096]{1,0:T(8,128)(2,1)}, u32[]{:S(2)}, u32[]{:S(2)}) %collective-permute-start.18) | collective-permute-done | bytes 262176 | tf_op jit(solution)/shard_map/ppermute | solution.py:277
  163.9 2.8 %collective-permute-done.17.refs_2_ = bf16[32,4096]{1,0:T(8,128)(2,1)} collective-permute-done((bf16[32,4096]{1,0:T(8,128)(2,1)S(1)}, bf16[32,4096]{1,0:T(8,128)(2,1)}, u32[]{:S(2)}, u32[]{:S(2)}) %collective-permute-start.17) | collective-permute-done | bytes 262176 | tf_op jit(solution)/shard_map/ppermute | solution.py:277
  172.0 15.5 %shard_map.72 = (bf16[32,4096]{1,0:T(8,128)(2,1)S(1)}, bf16[32,4096]{1,0:T(8,128)(2,1)S(1)}, bf16[32,4096]{1,0:T(8,128)(2,1)S(1)}, bf16[32,4096]{1,0:T(8,128)(2,1)S(1)}) custom-call(s32[1939]{0:T(1024)S(1)} %concatenate.61.meta, bf16[32,4096]{1,0:T(8,128)(2,1)S(1)} %shard_map.71.refs_0_, bf16[32,4096]{1,0:T(8,128)(2,1)} %collective-permute-done.16.refs_1_, ...), custom_call_target="tpu_custom_call" | custom-call | flops 1 | bytes 1 | tf_op jit(solution)/shard_map/pallas_call | solution.py:205
  187.7 3.4 %collective-permute-start.21 = (bf16[32,4096]{1,0:T(8,128)(2,1)S(1)}, bf16[32,4096]{1,0:T(8,128)(2,1)S(1)}, u32[]{:S(2)}, u32[]{:S(2)}) collective-permute-start(bf16[32,4096]{1,0:T(8,128)(2,1)S(1)} %get-tuple-element.42), channel_id=1, source_target_pairs={{0,6},{2,4},{4,2},{6,0},{8,14},{10,12},{12,10},{14,8},{1,7},{3,5},... | collective-permute-start | bytes 786440 | tf_op jit(solution)/shard_map/ppermute | solution.py:277
  191.1 2.8 %copy-done.1 = bf16[384,64,128]{2,1,0:T(8,128)(2,1)S(1)} copy-done((bf16[384,64,128]{2,1,0:T(8,128)(2,1)S(1)}, bf16[384,64,128]{2,1,0:T(8,128)(2,1)}, u32[]{:S(2)}) %copy-start.1) | copy-done | bytes 6291480
  193.9 4.9 %shard_map.73 = (bf16[32,4096]{1,0:T(8,128)(2,1)S(1)}, bf16[32,4096]{1,0:T(8,128)(2,1)S(1)}, bf16[32,4096]{1,0:T(8,128)(2,1)S(1)}, bf16[32,4096]{1,0:T(8,128)(2,1)S(1)}) custom-call(s32[1939]{0:T(1024)S(1)} %concatenate.61.meta, bf16[32,4096]{1,0:T(8,128)(2,1)S(1)} %shard_map.71.refs_0_, bf16[32,4096]{1,0:T(8,128)(2,1)} %collective-permute-done.16.refs_1_, ...), custom_call_target="tpu_custom_call" | custom-call | flops 1 | bytes 1 | tf_op jit(solution)/shard_map/pallas_call | solution.py:205
  198.8 2.4 %collective-permute-start.23 = (bf16[32,4096]{1,0:T(8,128)(2,1)S(1)}, bf16[32,4096]{1,0:T(8,128)(2,1)S(1)}, u32[]{:S(2)}, u32[]{:S(2)}) collective-permute-start(bf16[32,4096]{1,0:T(8,128)(2,1)S(1)} %get-tuple-element.45), channel_id=1, source_target_pairs={{0,4},{2,6},{4,0},{6,2},{8,12},{10,14},{12,8},{14,10},{1,5},{3,7},... | collective-permute-start | bytes 786440 | tf_op jit(solution)/shard_map/ppermute | solution.py:277
  203.4 6.1 %collective-permute-done.22 = bf16[32,4096]{1,0:T(8,128)(2,1)S(1)} collective-permute-done((bf16[32,4096]{1,0:T(8,128)(2,1)S(1)}, bf16[32,4096]{1,0:T(8,128)(2,1)S(1)}, u32[]{:S(2)}, u32[]{:S(2)}) %collective-permute-start.22) | collective-permute-done | bytes 262176 | tf_op jit(solution)/shard_map/ppermute | solution.py:277
  209.6 4.2 %collective-permute-done.24 = bf16[32,4096]{1,0:T(8,128)(2,1)S(1)} collective-permute-done((bf16[32,4096]{1,0:T(8,128)(2,1)S(1)}, bf16[32,4096]{1,0:T(8,128)(2,1)S(1)}, u32[]{:S(2)}, u32[]{:S(2)}) %collective-permute-start.24) | collective-permute-done | bytes 262176 | tf_op jit(solution)/shard_map/ppermute | solution.py:277
  (147 shorter events, 40.4 us)
Async XLA Ops:
  2.3 27.9 %collective-permute-start = (s32[3,384]{1,0:T(4,128)S(1)}, s32[3,384]{1,0:T(4,128)S(1)}, u32[]{:S(2)}, u32[]{:S(2)}) collective-permute-start(s32[3,384]{1,0:T(4,128)S(1)} %add_add_fusion), channel_id=1, source_target_pairs={{0,8},{2,10},{4,12},{6,14},{8,0},{10,2},{12,4},{14,6},{1,9},{3,11}... | collective-permute-start | bytes 13832 | tf_op jit(solution)/shard_map/ppermute | solution.py:299
  8.9 72.4 %collective-permute-start.10 = (bf16[24,64,128]{2,1,0:T(8,128)(2,1)}, bf16[24,64,128]{2,1,0:T(8,128)(2,1)}, u32[]{:S(2)}, u32[]{:S(2)}) collective-permute-start(bf16[24,64,128]{2,1,0:T(8,128)(2,1)} %get-tuple-element.47), channel_id=1, source_target_pairs={{0,8},{2,10},{4,12},{6,14},{8,0},{10,2},{12,4},{14,6},{1,9},{3,11}... | collective-permute-start | bytes 1179656 | tf_op jit(solution)/shard_map/ppermute | solution.py:325
  9.0 76.2 %collective-permute-start.6 = (bf16[24,64,128]{2,1,0:T(8,128)(2,1)}, bf16[24,64,128]{2,1,0:T(8,128)(2,1)}, u32[]{:S(2)}, u32[]{:S(2)}) collective-permute-start(bf16[24,64,128]{2,1,0:T(8,128)(2,1)} %get-tuple-element.48), channel_id=1, source_target_pairs={{0,8},{2,10},{4,12},{6,14},{8,0},{10,2},{12,4},{14,6},{1,9},{3,11}... | collective-permute-start | bytes 1179656 | tf_op jit(solution)/shard_map/ppermute | solution.py:325
  11.8 69.5 %collective-permute-start.3 = (bf16[24,64,128]{2,1,0:T(8,128)(2,1)}, bf16[24,64,128]{2,1,0:T(8,128)(2,1)}, u32[]{:S(2)}, u32[]{:S(2)}) collective-permute-start(bf16[24,64,128]{2,1,0:T(8,128)(2,1)} %get-tuple-element.49), channel_id=1, source_target_pairs={{0,8},{2,10},{4,12},{6,14},{8,0},{10,2},{12,4},{14,6},{1,9},{3,11}... | collective-permute-start | bytes 1179656 | tf_op jit(solution)/shard_map/ppermute | solution.py:325
  11.9 67.9 %collective-permute-start.1 = (bf16[24,64,128]{2,1,0:T(8,128)(2,1)}, bf16[24,64,128]{2,1,0:T(8,128)(2,1)}, u32[]{:S(2)}, u32[]{:S(2)}) collective-permute-start(bf16[24,64,128]{2,1,0:T(8,128)(2,1)} %get-tuple-element.50), channel_id=1, source_target_pairs={{0,8},{2,10},{4,12},{6,14},{8,0},{10,2},{12,4},{14,6},{1,9},{3,11}... | collective-permute-start | bytes 1179656 | tf_op jit(solution)/shard_map/ppermute | solution.py:325
  16.0 38.2 %all-to-all-start = ((bf16[32,4,4096]{2,0,1:T(8,128)(2,1)}), bf16[32,4,4096]{2,0,1:T(8,128)(2,1)S(1)}, u32[]{:S(2)}, u32[]{:S(2)}) async-start(bf16[32,4,4096]{2,0,1:T(8,128)(2,1)} %bitcast.27), calls=%async_computation | async-start | bytes 2097152 | tf_op jit(solution)/shard_map/all_to_all | solution.py:285
  54.2 39.8 %all-to-all-start.1 = ((bf16[32,4,4096]{2,0,1:T(8,128)(2,1)}), bf16[32,4,4096]{2,0,1:T(8,128)(2,1)S(1)}, u32[]{:S(2)}, u32[]{:S(2)}) async-start(bf16[32,4,4096]{2,0,1:T(8,128)(2,1)} %bitcast.26), calls=%async_computation.1 | async-start | bytes 2097152 | tf_op jit(solution)/shard_map/all_to_all | solution.py:285
  79.8 12.3 %collective-permute-start.2 = (bf16[24,64,128]{2,1,0:T(8,128)(2,1)}, bf16[24,64,128]{2,1,0:T(8,128)(2,1)S(1)}, u32[]{:S(2)}, u32[]{:S(2)}) collective-permute-start(bf16[24,64,128]{2,1,0:T(8,128)(2,1)} %collective-permute-done.1), channel_id=1, source_target_pairs={{0,16},{16,0},{1,17},{17,1},{2,18},{18,2},{3,19},{19,3},{4,20},{20... | collective-permute-start | bytes 1179656 | tf_op jit(solution)/shard_map/ppermute | solution.py:330
  81.3 36.3 %collective-permute-start.4 = (bf16[24,64,128]{2,1,0:T(8,128)(2,1)}, bf16[24,64,128]{2,1,0:T(8,128)(2,1)}, u32[]{:S(2)}, u32[]{:S(2)}) collective-permute-start(bf16[24,64,128]{2,1,0:T(8,128)(2,1)} %collective-permute-done.3), channel_id=1, source_target_pairs={{0,16},{16,0},{1,17},{17,1},{2,18},{18,2},{3,19},{19,3},{4,20},{20... | collective-permute-start | bytes 1179656 | tf_op jit(solution)/shard_map/ppermute | solution.py:330
  81.8 27.2 %collective-permute-start.11 = (bf16[24,64,128]{2,1,0:T(8,128)(2,1)}, bf16[24,64,128]{2,1,0:T(8,128)(2,1)}, u32[]{:S(2)}, u32[]{:S(2)}) collective-permute-start(bf16[24,64,128]{2,1,0:T(8,128)(2,1)} %collective-permute-done.10), channel_id=1, source_target_pairs={{0,16},{16,0},{1,17},{17,1},{2,18},{18,2},{3,19},{19,3},{4,20},{20... | collective-permute-start | bytes 1179656 | tf_op jit(solution)/shard_map/ppermute | solution.py:330
  85.1 30.2 %collective-permute-start.7 = (bf16[24,64,128]{2,1,0:T(8,128)(2,1)}, bf16[24,64,128]{2,1,0:T(8,128)(2,1)}, u32[]{:S(2)}, u32[]{:S(2)}) collective-permute-start(bf16[24,64,128]{2,1,0:T(8,128)(2,1)} %collective-permute-done.6), channel_id=1, source_target_pairs={{0,16},{16,0},{1,17},{17,1},{2,18},{18,2},{3,19},{19,3},{4,20},{20... | collective-permute-start | bytes 1179656 | tf_op jit(solution)/shard_map/ppermute | solution.py:330
  94.0 26.7 %copy-start.2 = (bf16[48,64,128]{2,1,0:T(8,128)(2,1)S(1)}, bf16[48,64,128]{2,1,0:T(8,128)(2,1)}, u32[]{:S(2)}) copy-start(bf16[48,64,128]{2,1,0:T(8,128)(2,1)} %pad_maximum_fusion.refs_0_.refs_4_) | copy-start | bytes 2359300
  110.8 8.6 %collective-permute-start.12 = (bf16[48,64,128]{2,1,0:T(8,128)(2,1)}, bf16[48,64,128]{2,1,0:T(8,128)(2,1)S(1)}, u32[]{:S(2)}, u32[]{:S(2)}) collective-permute-start(bf16[48,64,128]{2,1,0:T(8,128)(2,1)} %constant_dynamic-update-slice_fusion.4.refs_2_.refs_6_), channel_id=1, source_target_pairs={{0,1},{1,0},{2,3},{3,2},{4,5},{5,4},{6,7},{7,6},{8,9},{9,8},{10,11... | collective-permute-start | bytes 2359304 | tf_op jit(solution)/shard_map/ppermute | solution.py:333
  117.1 11.1 %collective-permute-start.8 = (bf16[48,64,128]{2,1,0:T(8,128)(2,1)}, bf16[48,64,128]{2,1,0:T(8,128)(2,1)S(1)}, u32[]{:S(2)}, u32[]{:S(2)}) collective-permute-start(bf16[48,64,128]{2,1,0:T(8,128)(2,1)} %constant_dynamic-update-slice_fusion.2.refs_0_.refs_8_), channel_id=1, source_target_pairs={{0,1},{1,0},{2,3},{3,2},{4,5},{5,4},{6,7},{7,6},{8,9},{9,8},{10,11... | collective-permute-start | bytes 2359304 | tf_op jit(solution)/shard_map/ppermute | solution.py:333
  117.1 3.6 %collective-permute-start.9 = (bf16[48,64,128]{2,1,0:T(8,128)(2,1)}, bf16[48,64,128]{2,1,0:T(8,128)(2,1)S(1)}, u32[]{:S(2)}, u32[]{:S(2)}) collective-permute-start(bf16[48,64,128]{2,1,0:T(8,128)(2,1)} %pad_maximum_fusion.refs_0_.refs_4_), channel_id=1, source_target_pairs={{0,1},{1,0},{2,3},{3,2},{4,5},{5,4},{6,7},{7,6},{8,9},{9,8},{10,11... | collective-permute-start | bytes 2359304 | tf_op jit(solution)/shard_map/ppermute | solution.py:333
  119.4 13.5 %collective-permute-start.5 = (bf16[48,64,128]{2,1,0:T(8,128)(2,1)}, bf16[48,64,128]{2,1,0:T(8,128)(2,1)S(1)}, u32[]{:S(2)}, u32[]{:S(2)}) collective-permute-start(bf16[48,64,128]{2,1,0:T(8,128)(2,1)} %constant_dynamic-update-slice_fusion.refs_0_.refs_10_), channel_id=1, source_target_pairs={{0,1},{1,0},{2,3},{3,2},{4,5},{5,4},{6,7},{7,6},{8,9},{9,8},{10,11... | collective-permute-start | bytes 2359304 | tf_op jit(solution)/shard_map/ppermute | solution.py:333
  132.8 19.8 %copy-start.9 = (bf16[32,128,128]{2,1,0:T(8,128)(2,1)S(1)}, bf16[32,128,128]{2,1,0:T(8,128)(2,1)}, u32[]{:S(2)}) copy-start(bf16[32,128,128]{2,1,0:T(8,128)(2,1)} %subtract_convert_fusion.low_ref) | copy-start | bytes 3145732
  137.4 30.0 %copy-start.3 = (bf16[48,64,128]{2,1,0:T(8,128)(2,1)S(1)}, bf16[48,64,128]{2,1,0:T(8,128)(2,1)}, u32[]{:S(2)}) copy-start(bf16[48,64,128]{2,1,0:T(8,128)(2,1)} %pad_maximum_fusion.refs_0_.refs_4_) | copy-start | bytes 2359300
  137.4 30.0 %copy-start.6 = (bf16[48,64,128]{2,1,0:T(8,128)(2,1)S(1)}, bf16[48,64,128]{2,1,0:T(8,128)(2,1)}, u32[]{:S(2)}) copy-start(bf16[48,64,128]{2,1,0:T(8,128)(2,1)} %constant_dynamic-update-slice_fusion.4.refs_2_.refs_6_) | copy-start | bytes 2359300
  137.4 30.0 %copy-start.8 = (bf16[48,64,128]{2,1,0:T(8,128)(2,1)S(1)}, bf16[48,64,128]{2,1,0:T(8,128)(2,1)}, u32[]{:S(2)}) copy-start(bf16[48,64,128]{2,1,0:T(8,128)(2,1)} %constant_dynamic-update-slice_fusion.2.refs_0_.refs_8_) | copy-start | bytes 2359300
  137.4 8.4 %collective-permute-start.13 = (bf16[32,4096]{1,0:T(8,128)(2,1)S(1)}, bf16[32,4096]{1,0:T(8,128)(2,1)S(1)}, u32[]{:S(2)}, u32[]{:S(2)}) collective-permute-start(bf16[32,4096]{1,0:T(8,128)(2,1)S(1)} %get-tuple-element.36), channel_id=1, source_target_pairs={{0,2},{2,0},{4,6},{6,4},{8,10},{10,8},{12,14},{14,12},{1,3},{3,1},... | collective-permute-start | bytes 786440 | tf_op jit(solution)/shard_map/ppermute | solution.py:277
  137.5 9.2 %collective-permute-start.14 = (bf16[32,4096]{1,0:T(8,128)(2,1)S(1)}, bf16[32,4096]{1,0:T(8,128)(2,1)S(1)}, u32[]{:S(2)}, u32[]{:S(2)}) collective-permute-start(bf16[32,4096]{1,0:T(8,128)(2,1)S(1)} %get-tuple-element.37), channel_id=1, source_target_pairs={{0,4},{2,6},{4,0},{6,2},{8,12},{10,14},{12,8},{14,10},{1,5},{3,7},... | collective-permute-start | bytes 786440 | tf_op jit(solution)/shard_map/ppermute | solution.py:277
  137.6 15.1 %collective-permute-start.15 = (bf16[32,4096]{1,0:T(8,128)(2,1)S(1)}, bf16[32,4096]{1,0:T(8,128)(2,1)S(1)}, u32[]{:S(2)}, u32[]{:S(2)}) collective-permute-start(bf16[32,4096]{1,0:T(8,128)(2,1)S(1)} %get-tuple-element.38), channel_id=1, source_target_pairs={{0,6},{2,4},{4,2},{6,0},{8,14},{10,12},{12,10},{14,8},{1,7},{3,5},... | collective-permute-start | bytes 786440 | tf_op jit(solution)/shard_map/ppermute | solution.py:277
  153.6 10.3 %collective-permute-start.18 = (bf16[32,4096]{1,0:T(8,128)(2,1)S(1)}, bf16[32,4096]{1,0:T(8,128)(2,1)}, u32[]{:S(2)}, u32[]{:S(2)}) collective-permute-start(bf16[32,4096]{1,0:T(8,128)(2,1)S(1)} %shard_map.71.refs_0_), channel_id=1, source_target_pairs={{0,6},{2,4},{4,2},{6,0},{8,14},{10,12},{12,10},{14,8},{1,7},{3,5},... | collective-permute-start | bytes 786440 | tf_op jit(solution)/shard_map/ppermute | solution.py:277
  153.7 13.0 %collective-permute-start.17 = (bf16[32,4096]{1,0:T(8,128)(2,1)S(1)}, bf16[32,4096]{1,0:T(8,128)(2,1)}, u32[]{:S(2)}, u32[]{:S(2)}) collective-permute-start(bf16[32,4096]{1,0:T(8,128)(2,1)S(1)} %shard_map.71.refs_0_), channel_id=1, source_target_pairs={{0,4},{2,6},{4,0},{6,2},{8,12},{10,14},{12,8},{14,10},{1,5},{3,7},... | collective-permute-start | bytes 786440 | tf_op jit(solution)/shard_map/ppermute | solution.py:277
  155.4 12.0 %collective-permute-start.16 = (bf16[32,4096]{1,0:T(8,128)(2,1)S(1)}, bf16[32,4096]{1,0:T(8,128)(2,1)}, u32[]{:S(2)}, u32[]{:S(2)}) collective-permute-start(bf16[32,4096]{1,0:T(8,128)(2,1)S(1)} %shard_map.71.refs_0_), channel_id=1, source_target_pairs={{0,2},{2,0},{4,6},{6,4},{8,10},{10,8},{12,14},{14,12},{1,3},{3,1},... | collective-permute-start | bytes 786440 | tf_op jit(solution)/shard_map/ppermute | solution.py:277
  187.5 13.9 %collective-permute-start.19 = (bf16[32,4096]{1,0:T(8,128)(2,1)S(1)}, bf16[32,4096]{1,0:T(8,128)(2,1)S(1)}, u32[]{:S(2)}, u32[]{:S(2)}) collective-permute-start(bf16[32,4096]{1,0:T(8,128)(2,1)S(1)} %get-tuple-element.40), channel_id=1, source_target_pairs={{0,2},{2,0},{4,6},{6,4},{8,10},{10,8},{12,14},{14,12},{1,3},{3,1},... | collective-permute-start | bytes 786440 | tf_op jit(solution)/shard_map/ppermute | solution.py:277
  187.6 15.0 %collective-permute-start.20 = (bf16[32,4096]{1,0:T(8,128)(2,1)S(1)}, bf16[32,4096]{1,0:T(8,128)(2,1)S(1)}, u32[]{:S(2)}, u32[]{:S(2)}) collective-permute-start(bf16[32,4096]{1,0:T(8,128)(2,1)S(1)} %get-tuple-element.41), channel_id=1, source_target_pairs={{0,4},{2,6},{4,0},{6,2},{8,12},{10,14},{12,8},{14,10},{1,5},{3,7},... | collective-permute-start | bytes 786440 | tf_op jit(solution)/shard_map/ppermute | solution.py:277
  187.7 15.7 %collective-permute-start.21 = (bf16[32,4096]{1,0:T(8,128)(2,1)S(1)}, bf16[32,4096]{1,0:T(8,128)(2,1)S(1)}, u32[]{:S(2)}, u32[]{:S(2)}) collective-permute-start(bf16[32,4096]{1,0:T(8,128)(2,1)S(1)} %get-tuple-element.42), channel_id=1, source_target_pairs={{0,6},{2,4},{4,2},{6,0},{8,14},{10,12},{12,10},{14,8},{1,7},{3,5},... | collective-permute-start | bytes 786440 | tf_op jit(solution)/shard_map/ppermute | solution.py:277
  198.8 10.8 %collective-permute-start.22 = (bf16[32,4096]{1,0:T(8,128)(2,1)S(1)}, bf16[32,4096]{1,0:T(8,128)(2,1)S(1)}, u32[]{:S(2)}, u32[]{:S(2)}) collective-permute-start(bf16[32,4096]{1,0:T(8,128)(2,1)S(1)} %get-tuple-element.44), channel_id=1, source_target_pairs={{0,2},{2,0},{4,6},{6,4},{8,10},{10,8},{12,14},{14,12},{1,3},{3,1},... | collective-permute-start | bytes 786440 | tf_op jit(solution)/shard_map/ppermute | solution.py:277
  198.8 10.7 %collective-permute-start.23 = (bf16[32,4096]{1,0:T(8,128)(2,1)S(1)}, bf16[32,4096]{1,0:T(8,128)(2,1)S(1)}, u32[]{:S(2)}, u32[]{:S(2)}) collective-permute-start(bf16[32,4096]{1,0:T(8,128)(2,1)S(1)} %get-tuple-element.45), channel_id=1, source_target_pairs={{0,4},{2,6},{4,0},{6,2},{8,12},{10,14},{12,8},{14,10},{1,5},{3,7},... | collective-permute-start | bytes 786440 | tf_op jit(solution)/shard_map/ppermute | solution.py:277
  201.4 12.4 %collective-permute-start.24 = (bf16[32,4096]{1,0:T(8,128)(2,1)S(1)}, bf16[32,4096]{1,0:T(8,128)(2,1)S(1)}, u32[]{:S(2)}, u32[]{:S(2)}) collective-permute-start(bf16[32,4096]{1,0:T(8,128)(2,1)S(1)} %get-tuple-element.46), channel_id=1, source_target_pairs={{0,6},{2,4},{4,2},{6,0},{8,14},{10,12},{12,10},{14,8},{1,7},{3,5},... | collective-permute-start | bytes 786440 | tf_op jit(solution)/shard_map/ppermute | solution.py:277
  (22 other events, 117.4 us)

commit v8 on v7

--- a/solution.py
+++ b/solution.py
@@ -11,8 +11,8 @@
 PAIR = 2 * TILE
 UNROLL = 4
 VMEM_LIMIT = 16 * 1024 * 1024
-PARTS = 4
-RANGES = ((0, 2), (2, 3), (3, 4))
+PARTS = 3
+RANGES = ((0, 2), (2, 3))
 OWN_FORWARD, OWN_BACKWARD, OTHER_FORWARD, OTHER_BACKWARD = range(4)
 BOUNDS = 3
 STEPS = len(RANGES) + 1
@@ -57,7 +57,7 @@
     )
 
 
-def pair_loop(sizes, meta, ref, proj, which, first, last, origin, step):
+def pair_loop(sizes, meta, ref, proj, which, first, last, origin, product, sums):
     tiles, segments, blocks = sizes
     begin, end = (meta[BOUNDS + STEPS * which + number] for number in (first, last))
     base = LISTS + which * (tiles + len(RANGES) * blocks)
@@ -75,11 +75,14 @@
         return points, lanes, padded_tile(ref[jnp.maximum(index, 0)], half)
 
     def group(index, carry):
+        terms = []
         for lane in range(UNROLL):
             pair = begin + index * UNROLL + lane
             live = pair < end
             pair = jnp.minimum(pair, end - 1)
-            step(tile(2 * pair, live), tile(2 * pair + 1, live))
+            terms.append(product(tile(2 * pair, live), tile(2 * pair + 1, live)))
+        for lanes, term in terms:
+            sums[:, lanes] += term
         return carry
 
     lax.fori_loop(0, (end - begin + UNROLL - 1) // UNROLL, group, 0)
@@ -116,12 +119,12 @@
     total = refs[-1]
     total[...] = jnp.zeros_like(total) if first else refs[0][...]
 
-    def step(one, two):
+    def product(one, two):
         waves = jnp.concatenate([wave[:, one[0]], wave[:, two[0]]], axis=1)
         tiles = jnp.concatenate([one[2], two[2]], axis=0)
-        total[:, one[1]] += jnp.dot(waves, tiles, preferred_element_type=jnp.float32)
-
-    pair_loop(sizes, meta, values, proj, *spot, step)
+        return one[1], jnp.dot(waves, tiles, preferred_element_type=jnp.float32)
+
+    pair_loop(sizes, meta, values, proj, *spot, product, total)
     if last:
         outs = refs[1:-1]
         rows = outs[0].shape[0]
@@ -141,21 +144,22 @@
     outs, field = refs[:-1], refs[-1]
     field[...] = jnp.zeros_like(field)
 
-    def step(one, two):
+    def product(one, two):
         rows = jnp.concatenate([rows_of(applied, one[1]), rows_of(applied, two[1])], axis=1)
         tiles = jnp.concatenate([one[2], two[2]], axis=1)
-        field[:, one[0]] += lax.dot_general(
+        return one[0], lax.dot_general(
             rows, tiles, (((1,), (1,)), ((), ())), preferred_element_type=jnp.float32
         )
 
-    pair_loop(sizes, meta, values, proj, which, 0, len(RANGES), 0, step)
+    pair_loop(sizes, meta, values, proj, which, 0, len(RANGES), 0, product, field)
     store_rows(outs, field)
 
 
 WHOLE = pl.BlockSpec(memory_space=pltpu.VMEM)
 
 
-COST = pl.CostEstimate(flops=1, bytes_accessed=1, transcendentals=0)
+def cost(us):
+    return pl.CostEstimate(flops=1 + us * 10**9, bytes_accessed=1, transcendentals=0)
 
 
 def join_small(blocks):
@@ -173,7 +177,7 @@
     return [pltpu.VMEM((len(pieces) * shape[0],) + shape[1:], jnp.bfloat16)]
 
 
-def project(sizes, meta, wave, pieces, count, width, spot, total=None, last=False):
+def project(sizes, meta, wave, pieces, count, width, spot, total=None, last=False, us=0):
     rows = wave.shape[0]
     bands = rows // count
     split = bands % 16 == 0
@@ -194,7 +198,7 @@
         ),
         out_shape=out_shape if last else jax.ShapeDtypeStruct((rows, width), jnp.float32),
         compiler_params=pltpu.CompilerParams(vmem_limit_bytes=VMEM_LIMIT),
-        cost_estimate=COST,
+        cost_estimate=cost(us),
     )(meta, *operands)
 
 
@@ -215,7 +219,7 @@
             jax.ShapeDtypeStruct((block.shape[0], points), jnp.bfloat16) for block in applied
         ],
         compiler_params=pltpu.CompilerParams(vmem_limit_bytes=VMEM_LIMIT),
-        cost_estimate=COST,
+        cost_estimate=cost(0),
     )(meta, *applied, *pieces)
     return split_small(result, count)
 
@@ -247,7 +251,7 @@
         out_specs=WHOLE,
         out_shape=jax.ShapeDtypeStruct(parts[0].shape, jnp.bfloat16),
         compiler_params=pltpu.CompilerParams(vmem_limit_bytes=VMEM_LIMIT),
-        cost_estimate=COST,
+        cost_estimate=cost(0),
     )(high, low, *parts)
 
 
@@ -314,22 +318,25 @@
     own_wave = to_bricks(side)
     other_wave = to_bricks(1 - side)
     spot = (OWN_FORWARD, 0, len(RANGES), 0)
-    own_total = project(sizes, meta, own_wave, [projectors], half, width, spot)
+    own_total = project(sizes, meta, own_wave, [projectors], half, width, spot, us=10)
     matrix = two_parts(coupling_matrix(coupling))
 
-    pieces = []
+    pieces, mine, across = [], None, None
     for part in range(PARTS):
-        mine = lax.dynamic_slice_in_dim(
-            projectors, part * size + (2 * group + core) * share, share, 0
-        )
-        mine = lax.ppermute(mine, "grid", partners)
+        start = part * size + (2 * group + core) * share
+        sent = lax.dynamic_slice_in_dim(projectors, start, share, 0)
+        if part > 0:
+            sent = lax.optimization_barrier((sent, mine))[0]
+        mine = lax.ppermute(sent, "grid", partners)
+        sent = mine
         if part == 0:
-            mine, total, matrix = lax.optimization_barrier((mine, own_total, matrix))
+            sent, matrix, meta = lax.optimization_barrier((sent, matrix, meta))
         else:
-            mine = lax.optimization_barrier((mine, own_total))[0]
-        both = jnp.concatenate([mine, lax.ppermute(mine, "groups", swap)])
+            sent = lax.optimization_barrier((sent, across))[0]
+        across = lax.ppermute(sent, "groups", swap)
+        both = jnp.concatenate([mine, across])
         if part == 0:
-            both, other_wave = lax.optimization_barrier((both, other_wave))
+            both, total = lax.optimization_barrier((both, own_total))
         pieces += [both, lax.ppermute(both, "band", swap)]
 
     for number, (first, end) in enumerate(RANGES):
@@ -343,6 +350,7 @@
             (OTHER_FORWARD, number, number + 1, first * size),
             total,
             last=end == PARTS,
+            us=8 if end < PARTS else 0,
         )
     if len(total) < half:
         total = [lax.dynamic_slice_in_dim(total[0], (place ^ d) * bands, bands, 0) for d in range(half)]

time: 215 us -> 198 us (0.921)
  Pallas kernels: 41.4 us -> 26.6 us
  starting transfers between devices: 37.1 us -> 50.5 us
  local copies, waits for them, and re-layouts: 35.6 us -> 25 us
  waiting for transfers between devices: 90.8 us -> 88.2 us
    all_to_all x2, waiting for transfers between devices: 23.5 us -> 0.01 us  [to_bricks(): lax.all_to_all(part, 'grid', split_axis=1, concat_axis=0, tiled=True, axi...]
    ppermute x8 -> x6, waiting for transfers between devices: 32.9 us -> 56.2 us  [the longest x3 30.9 us: body(): across = lax.ppermute(sent, 'groups', swap)]
    ppermute x12, starting transfers between devices: 14.2 us -> 34 us  [exchange(): lax.ppermute(blocks[d], 'grid', [(i, i // half * half + (i % half ^ d)) f...]
    pallas_call x2, Pallas kernels: 20.4 us -> 11.9 us  [spread(): pl.pallas_call(functools.partial(spread_kernel, sizes, len(applied), len(...]
    ppermute x8 -> x6, starting transfers between devices: 9.92 us -> 3.52 us  [the longest x3 3.49 us: body(): across = lax.ppermute(sent, 'groups', swap)]
    pallas_call x4 -> x3, Pallas kernels: 20 us -> 13.7 us  [project(): pl.pallas_call(functools.partial(project_kernel, sizes, len(pieces), spot...]
    unnamed x57 -> x22, local copies, waits for them, and re-layouts: 16.7 us -> 10.9 us
    concatenate x3 -> x2, local copies, waits for them, and re-layouts: 5.34 us -> 0.9 us  [body(): both = jnp.concatenate([mine, across])]
  transfers between devices with their start and end apart: 27 -> 24, of which waited for: 15 -> 13; matrix products, arithmetic and copies ran while one was open for 14% -> 10% of each run, Pallas kernels for 10% -> 7%
where the time goes in v8:
time: 198 us
  waiting for transfers between devices  88.2 us (45%)
  starting transfers between devices  50.5 us (26%)
  Pallas kernels  26.6 us (13%)
  local copies, waits for them, and re-layouts  25 us (13%)
  other arithmetic  6.36 us (3%)
    ppermute x12, starting transfers between devices, exchange(): lax.ppermute(blocks[d], 'grid', [(i, i // half * half + (i % half ^ d)) f...  34 us
    ppermute x12, waiting for transfers between devices, exchange(): lax.ppermute(blocks[d], 'grid', [(i, i // half * half + (i % half ^ d)) f...  32 us
    ppermute x3, waiting for transfers between devices, body(): across = lax.ppermute(sent, 'groups', swap)  30.9 us
    ppermute x3, waiting for transfers between devices, body(): mine = lax.ppermute(sent, 'grid', partners)  25.3 us
    pallas_call x3, Pallas kernels, project(): pl.pallas_call(functools.partial(project_kernel, sizes, len(pieces), spot...  13.7 us
    pallas_call x2, Pallas kernels, spread(): pl.pallas_call(functools.partial(spread_kernel, sizes, len(applied), len(...  11.9 us
    unnamed x22, local copies, waits for them, and re-layouts  10.9 us
    all_to_all x2, starting transfers between devices, to_bricks(): lax.all_to_all(part, 'grid', split_axis=1, concat_axis=0, tiled=True, axi...  8.37 us
  transfers between devices with their start and end apart: 24, of which 13 were waited for; matrix products, arithmetic and copies ran while one was open for 10% of the time, Pallas kernels for 7%

profile of v8, /device:TPU:0, one launch (start us, length us, event | category | flops | bytes accessed | tf_op | source)
XLA Modules:
  0.0 197.9 jit_solution(3813119141990175242)
XLA Ops:
  2.3 4.0 %collective-permute-start.1 = (s32[3,384]{1,0:T(4,128)S(1)}, s32[3,384]{1,0:T(4,128)S(1)}, u32[]{:S(2)}, u32[]{:S(2)}) collective-permute-start(s32[3,384]{1,0:T(4,128)S(1)} %add_add_fusion), channel_id=1, source_target_pairs={{0,8},{2,10},{4,12},{6,14},{8,0},{10,2},{12,4},{14,6},{1,9},{3,11}... | collective-permute-start | bytes 13832 | tf_op jit(solution)/shard_map/ppermute | solution.py:303
  6.4 2.5 %constant_dynamic-slice_fusion.1 = (bf16[32,64,128]{2,1,0:T(8,128)(2,1)}, bf16[32,64,128]{2,1,0:T(8,128)(2,1)}, bf16[32,64,128]{2,1,0:T(8,128)(2,1)}) fusion(bf16[384,64,128]{2,1,0:T(8,128)(2,1)} %refs_4_.1, s32[]{:T(128)S(6)} %select_n.262, s32[]{:T(128)S(6)} %select_n.261, s32[]{:T(128)S(6)} %select_n.241), kind=kLoop, calls=%fused_computation.55 | loop fusion | bytes 3145740 | tf_op jit(solution)/shard_map/dynamic_slice | solution.py:327
  11.1 4.1 %all-to-all-start.1 = ((bf16[32,4,4096]{2,0,1:T(8,128)(2,1)}), bf16[32,4,4096]{2,0,1:T(8,128)(2,1)S(1)}, u32[]{:S(2)}, u32[]{:S(2)}) async-start(bf16[32,4,4096]{2,0,1:T(8,128)(2,1)} %bitcast.26), calls=%async_computation.1 | async-start | bytes 2097152 | tf_op jit(solution)/shard_map/all_to_all | solution.py:289
  15.7 1.8 copy.19
  17.6 2.0 %select_convert_fusion.high_ref = bf16[32,128,128]{2,1,0:T(8,128)(2,1)S(1)} fusion(f32[32,128,128]{2,1,0:T(8,128)} %copy.19, pred[128,128]{1,0:T(8,128)(4,1)S(1)} %broadcast_compare_fusion), kind=kLoop, calls=%fused_computation.4 | loop fusion | flops 524288 | bytes 3162112 | tf_op jit(solution)/shard_map/convert_element_type | solution.py:228
  23.8 11.1 %collective-permute-done = bf16[32,64,128]{2,1,0:T(8,128)(2,1)} collective-permute-done((bf16[32,64,128]{2,1,0:T(8,128)(2,1)}, bf16[32,64,128]{2,1,0:T(8,128)(2,1)}, u32[]{:S(2)}, u32[]{:S(2)}) %collective-permute-start) | collective-permute-done | bytes 524320 | tf_op jit(solution)/shard_map/ppermute | solution.py:330
  36.3 11.4 %collective-permute-done.4 = bf16[32,64,128]{2,1,0:T(8,128)(2,1)S(1)} collective-permute-done((bf16[32,64,128]{2,1,0:T(8,128)(2,1)}, bf16[32,64,128]{2,1,0:T(8,128)(2,1)S(1)}, u32[]{:S(2)}, u32[]{:S(2)}) %collective-permute-start.4) | collective-permute-done | bytes 524320 | tf_op jit(solution)/shard_map/ppermute | solution.py:336
  47.7 13.0 %collective-permute-done.2 = bf16[32,64,128]{2,1,0:T(8,128)(2,1)S(1)} collective-permute-done((bf16[32,64,128]{2,1,0:T(8,128)(2,1)}, bf16[32,64,128]{2,1,0:T(8,128)(2,1)S(1)}, u32[]{:S(2)}, u32[]{:S(2)}) %collective-permute-start.2) | collective-permute-done | bytes 524320 | tf_op jit(solution)/shard_map/ppermute | solution.py:330
  61.3 2.3 %copy.29 = bf16[4,4,8,4096]{3,2,0,1:T(8,128)(2,1)} copy(bf16[4,4,8,4096]{3,2,1,0:T(8,128)(2,1)} %bitcast.30) | data formatting | bytes 2097152 | tf_op jit(solution)/shard_map/all_to_all | solution.py:289
  64.4 2.1 %pad_maximum_fusion.refs_0_.refs_4_ = bf16[64,64,128]{2,1,0:T(8,128)(2,1)} fusion(bf16[32,64,128]{2,1,0:T(8,128)(2,1)S(1)} %collective-permute-done.4, bf16[32,64,128]{2,1,0:T(8,128)(2,1)} %collective-permute-done), kind=kLoop, calls=%fused_computation.7 | loop fusion | flops 524288 | bytes 2097152 | tf_op jit(solution)/shard_map/concatenate | solution.py:337
  66.5 8.1 %collective-permute-done.5 = bf16[32,64,128]{2,1,0:T(8,128)(2,1)S(1)} collective-permute-done((bf16[32,64,128]{2,1,0:T(8,128)(2,1)S(1)}, bf16[32,64,128]{2,1,0:T(8,128)(2,1)S(1)}, u32[]{:S(2)}, u32[]{:S(2)}) %collective-permute-start.5) | collective-permute-done | bytes 524320 | tf_op jit(solution)/shard_map/ppermute | solution.py:336
  75.4 4.3 %all-to-all-start = ((bf16[32,4,4096]{2,0,1:T(8,128)(2,1)}), bf16[32,4,4096]{2,0,1:T(8,128)(2,1)}, u32[]{:S(2)}, u32[]{:S(2)}) async-start(bf16[32,4,4096]{2,0,1:T(8,128)(2,1)} %bitcast.32), calls=%async_computation | async-start | bytes 2097152 | tf_op jit(solution)/shard_map/all_to_all | solution.py:289
  79.7 2.8 %copy-done = bf16[384,64,128]{2,1,0:T(8,128)(2,1)S(1)} copy-done((bf16[384,64,128]{2,1,0:T(8,128)(2,1)S(1)}, bf16[384,64,128]{2,1,0:T(8,128)(2,1)}, u32[]{:S(2)}) %copy-start) | copy-done | bytes 6291480
  82.5 3.0 %shard_map.67.refs_4_ = f32[128,4096]{1,0:T(8,128)S(1)} custom-call(s32[1807]{0:T(1024)S(1)} %concatenate.58.meta, bf16[128,4096]{1,0:T(8,128)(2,1)S(1)} %bitcast.29, bf16[384,64,128]{2,1,0:T(8,128)(2,1)S(1)} %copy-done), custom_call_target="tpu_custom_call" | custom-call | flops 10000000000 | bytes 1 | tf_op jit(solution)/shard_map/pallas_call | solution.py:187
  91.2 11.4 %collective-permute-done.6 = bf16[32,64,128]{2,1,0:T(8,128)(2,1)S(1)} collective-permute-done((bf16[32,64,128]{2,1,0:T(8,128)(2,1)}, bf16[32,64,128]{2,1,0:T(8,128)(2,1)S(1)}, u32[]{:S(2)}, u32[]{:S(2)}) %collective-permute-start.6) | collective-permute-done | bytes 524320 | tf_op jit(solution)/shard_map/ppermute | solution.py:336
  104.4 8.2 %shard_map.68.refs_2_ = f32[128,4096]{1,0:T(8,128)S(1)} custom-call(s32[1807]{0:T(1024)S(1)} %concatenate.58.meta, bf16[128,4096]{1,0:T(8,128)(2,1)} %bitcast.10.wave, bf16[64,64,128]{2,1,0:T(8,128)(2,1)} %pad_maximum_fusion.refs_0_.refs_4_, bf16[64,64,128]{2,1,0:T(8,128)(2,1)} %collective-permute-done.8.refs_1_.refs_5_, ...), custom_call_target="tpu_custom_call" | custom-call | flops 8000000000 | bytes 1 | tf_op jit(solution)/shard_map/pallas_call | solution.py:187
  112.7 2.4 %shard_map.69 = (bf16[32,4096]{1,0:T(8,128)(2,1)S(1)}, bf16[32,4096]{1,0:T(8,128)(2,1)S(1)}, bf16[32,4096]{1,0:T(8,128)(2,1)S(1)}, bf16[32,4096]{1,0:T(8,128)(2,1)S(1)}) custom-call(s32[1807]{0:T(1024)S(1)} %concatenate.58.meta, bf16[128,4096]{1,0:T(8,128)(2,1)} %bitcast.10.wave, bf16[64,64,128]{2,1,0:T(8,128)(2,1)S(1)} %constant_dynamic-update-slice_fusion.refs_0_.refs_8_, ...), custom_call_target="tpu_custom_call" | custom-call | flops 1 | bytes 1 | tf_op jit(solution)/shard_map/pallas_call | solution.py:187
  116.8 11.0 %collective-permute-start.11 = (bf16[32,4096]{1,0:T(8,128)(2,1)S(1)}, bf16[32,4096]{1,0:T(8,128)(2,1)S(1)}, u32[]{:S(2)}, u32[]{:S(2)}) collective-permute-start(bf16[32,4096]{1,0:T(8,128)(2,1)S(1)} %get-tuple-element.39), channel_id=1, source_target_pairs={{0,4},{2,6},{4,0},{6,2},{8,12},{10,14},{12,8},{14,10},{1,5},{3,7},... | collective-permute-start | bytes 786440 | tf_op jit(solution)/shard_map/ppermute | solution.py:281
  127.8 7.1 %collective-permute-done.11.refs_2_ = bf16[32,4096]{1,0:T(8,128)(2,1)S(1)} collective-permute-done((bf16[32,4096]{1,0:T(8,128)(2,1)S(1)}, bf16[32,4096]{1,0:T(8,128)(2,1)S(1)}, u32[]{:S(2)}, u32[]{:S(2)}) %collective-permute-start.11) | collective-permute-done | bytes 262176 | tf_op jit(solution)/shard_map/ppermute | solution.py:281
  134.9 5.0 %collective-permute-done.12.refs_3_ = bf16[32,4096]{1,0:T(8,128)(2,1)S(1)} collective-permute-done((bf16[32,4096]{1,0:T(8,128)(2,1)S(1)}, bf16[32,4096]{1,0:T(8,128)(2,1)S(1)}, u32[]{:S(2)}, u32[]{:S(2)}) %collective-permute-start.12) | collective-permute-done | bytes 262176 | tf_op jit(solution)/shard_map/ppermute | solution.py:281
  142.5 1.7 collective-permute-start.14
  144.3 4.8 %collective-permute-done.13.refs_1_ = bf16[32,4096]{1,0:T(8,128)(2,1)S(1)} collective-permute-done((bf16[32,4096]{1,0:T(8,128)(2,1)S(1)}, bf16[32,4096]{1,0:T(8,128)(2,1)S(1)}, u32[]{:S(2)}, u32[]{:S(2)}) %collective-permute-start.13) | collective-permute-done | bytes 262176 | tf_op jit(solution)/shard_map/ppermute | solution.py:281
  149.1 2.6 %collective-permute-done.14.refs_2_ = bf16[32,4096]{1,0:T(8,128)(2,1)S(1)} collective-permute-done((bf16[32,4096]{1,0:T(8,128)(2,1)S(1)}, bf16[32,4096]{1,0:T(8,128)(2,1)S(1)}, u32[]{:S(2)}, u32[]{:S(2)}) %collective-permute-start.14) | collective-permute-done | bytes 262176 | tf_op jit(solution)/shard_map/ppermute | solution.py:281
  151.7 4.0 %collective-permute-done.15.refs_3_ = bf16[32,4096]{1,0:T(8,128)(2,1)S(1)} collective-permute-done((bf16[32,4096]{1,0:T(8,128)(2,1)S(1)}, bf16[32,4096]{1,0:T(8,128)(2,1)S(1)}, u32[]{:S(2)}, u32[]{:S(2)}) %collective-permute-start.15) | collective-permute-done | bytes 262176 | tf_op jit(solution)/shard_map/ppermute | solution.py:281
  155.7 8.7 %shard_map.71 = (bf16[32,4096]{1,0:T(8,128)(2,1)S(1)}, bf16[32,4096]{1,0:T(8,128)(2,1)S(1)}, bf16[32,4096]{1,0:T(8,128)(2,1)S(1)}, bf16[32,4096]{1,0:T(8,128)(2,1)S(1)}) custom-call(s32[1807]{0:T(1024)S(1)} %concatenate.58.meta, bf16[32,4096]{1,0:T(8,128)(2,1)S(1)} %shard_map.70.refs_0_, bf16[32,4096]{1,0:T(8,128)(2,1)S(1)} %collective-permute-done.13.refs_1_, ...), custom_call_target="tpu_custom_call" | custom-call | flops 1 | bytes 1 | tf_op jit(solution)/shard_map/pallas_call | solution.py:209
  164.5 3.4 %collective-permute-start.17 = (bf16[32,4096]{1,0:T(8,128)(2,1)S(1)}, bf16[32,4096]{1,0:T(8,128)(2,1)S(1)}, u32[]{:S(2)}, u32[]{:S(2)}) collective-permute-start(bf16[32,4096]{1,0:T(8,128)(2,1)S(1)} %get-tuple-element.43), channel_id=1, source_target_pairs={{0,4},{2,6},{4,0},{6,2},{8,12},{10,14},{12,8},{14,10},{1,5},{3,7},... | collective-permute-start | bytes 786440 | tf_op jit(solution)/shard_map/ppermute | solution.py:281
  168.5 2.8 %copy-done.1 = bf16[384,64,128]{2,1,0:T(8,128)(2,1)S(1)} copy-done((bf16[384,64,128]{2,1,0:T(8,128)(2,1)S(1)}, bf16[384,64,128]{2,1,0:T(8,128)(2,1)}, u32[]{:S(2)}) %copy-start.1) | copy-done | bytes 6291480
  171.3 3.2 %shard_map.72 = (bf16[32,4096]{1,0:T(8,128)(2,1)S(1)}, bf16[32,4096]{1,0:T(8,128)(2,1)S(1)}, bf16[32,4096]{1,0:T(8,128)(2,1)S(1)}, bf16[32,4096]{1,0:T(8,128)(2,1)S(1)}) custom-call(s32[1807]{0:T(1024)S(1)} %concatenate.58.meta, bf16[32,4096]{1,0:T(8,128)(2,1)S(1)} %shard_map.70.refs_0_, bf16[32,4096]{1,0:T(8,128)(2,1)S(1)} %collective-permute-done.13.refs_1_, ...), custom_call_target="tpu_custom_call" | custom-call | flops 1 | bytes 1 | tf_op jit(solution)/shard_map/pallas_call | solution.py:209
  174.6 4.3 %collective-permute-start.19 = (bf16[32,4096]{1,0:T(8,128)(2,1)S(1)}, bf16[32,4096]{1,0:T(8,128)(2,1)S(1)}, u32[]{:S(2)}, u32[]{:S(2)}) collective-permute-start(bf16[32,4096]{1,0:T(8,128)(2,1)S(1)} %get-tuple-element.46), channel_id=1, source_target_pairs={{0,2},{2,0},{4,6},{6,4},{8,10},{10,8},{12,14},{14,12},{1,3},{3,1},... | collective-permute-start | bytes 786440 | tf_op jit(solution)/shard_map/ppermute | solution.py:281
  178.9 9.4 %collective-permute-start.20 = (bf16[32,4096]{1,0:T(8,128)(2,1)S(1)}, bf16[32,4096]{1,0:T(8,128)(2,1)S(1)}, u32[]{:S(2)}, u32[]{:S(2)}) collective-permute-start(bf16[32,4096]{1,0:T(8,128)(2,1)S(1)} %get-tuple-element.47), channel_id=1, source_target_pairs={{0,4},{2,6},{4,0},{6,2},{8,12},{10,14},{12,8},{14,10},{1,5},{3,7},... | collective-permute-start | bytes 786440 | tf_op jit(solution)/shard_map/ppermute | solution.py:281
  188.7 5.9 %collective-permute-done.20 = bf16[32,4096]{1,0:T(8,128)(2,1)S(1)} collective-permute-done((bf16[32,4096]{1,0:T(8,128)(2,1)S(1)}, bf16[32,4096]{1,0:T(8,128)(2,1)S(1)}, u32[]{:S(2)}, u32[]{:S(2)}) %collective-permute-start.20) | collective-permute-done | bytes 262176 | tf_op jit(solution)/shard_map/ppermute | solution.py:281
  194.6 2.6 %collective-permute-done.21 = bf16[32,4096]{1,0:T(8,128)(2,1)S(1)} collective-permute-done((bf16[32,4096]{1,0:T(8,128)(2,1)S(1)}, bf16[32,4096]{1,0:T(8,128)(2,1)S(1)}, u32[]{:S(2)}, u32[]{:S(2)}) %collective-permute-start.21) | collective-permute-done | bytes 262176 | tf_op jit(solution)/shard_map/ppermute | solution.py:281
  (105 shorter events, 25.6 us)
Async XLA Ops:
  0.0 8.9 %copy-start.5 = (bf16[32,32768]{1,0:T(8,128)(2,1)S(1)}, bf16[32,32768]{1,0:T(8,128)(2,1)}, u32[]{:S(2)}) copy-start(bf16[32,32768]{1,0:T(8,128)(2,1)} %param.6) | copy-start | bytes 6291460
  2.3 18.1 %collective-permute-start.1 = (s32[3,384]{1,0:T(4,128)S(1)}, s32[3,384]{1,0:T(4,128)S(1)}, u32[]{:S(2)}, u32[]{:S(2)}) collective-permute-start(s32[3,384]{1,0:T(4,128)S(1)} %add_add_fusion), channel_id=1, source_target_pairs={{0,8},{2,10},{4,12},{6,14},{8,0},{10,2},{12,4},{14,6},{1,9},{3,11}... | collective-permute-start | bytes 13832 | tf_op jit(solution)/shard_map/ppermute | solution.py:303
  8.9 25.9 %collective-permute-start = (bf16[32,64,128]{2,1,0:T(8,128)(2,1)}, bf16[32,64,128]{2,1,0:T(8,128)(2,1)}, u32[]{:S(2)}, u32[]{:S(2)}) collective-permute-start(bf16[32,64,128]{2,1,0:T(8,128)(2,1)} %get-tuple-element.51), channel_id=1, source_target_pairs={{0,8},{2,10},{4,12},{6,14},{8,0},{10,2},{12,4},{14,6},{1,9},{3,11}... | collective-permute-start | bytes 1572872 | tf_op jit(solution)/shard_map/ppermute | solution.py:330
  10.0 5.3 %copy-start.7 = (f32[32,16,8,8]{0,3,2,1:T(8,128)S(1)}, f32[32,16,8,8]{0,3,2,1:T(8,128)}, u32[]{:S(2)}) copy-start(f32[32,16,8,8]{0,3,2,1:T(8,128)} %param.11) | copy-start | bytes 393220
  11.1 64.4 %all-to-all-start.1 = ((bf16[32,4,4096]{2,0,1:T(8,128)(2,1)}), bf16[32,4,4096]{2,0,1:T(8,128)(2,1)S(1)}, u32[]{:S(2)}, u32[]{:S(2)}) async-start(bf16[32,4,4096]{2,0,1:T(8,128)(2,1)} %bitcast.26), calls=%async_computation.1 | async-start | bytes 2097152 | tf_op jit(solution)/shard_map/all_to_all | solution.py:289
  17.5 2.2 %copy-start.4 = (f32[32,128,128]{2,1,0:T(8,128)S(1)}, f32[32,128,128]{2,1,0:T(8,128)}, u32[]{:S(2)}) copy-start(f32[32,128,128]{2,1,0:T(8,128)} %copy.19) | copy-start | bytes 6291460
  34.8 12.9 %collective-permute-start.4 = (bf16[32,64,128]{2,1,0:T(8,128)(2,1)}, bf16[32,64,128]{2,1,0:T(8,128)(2,1)S(1)}, u32[]{:S(2)}, u32[]{:S(2)}) collective-permute-start(bf16[32,64,128]{2,1,0:T(8,128)(2,1)} %collective-permute-done), channel_id=1, source_target_pairs={{0,16},{16,0},{1,17},{17,1},{2,18},{18,2},{3,19},{19,3},{4,20},{20... | collective-permute-start | bytes 1572872 | tf_op jit(solution)/shard_map/ppermute | solution.py:336
  36.3 24.4 %collective-permute-start.2 = (bf16[32,64,128]{2,1,0:T(8,128)(2,1)}, bf16[32,64,128]{2,1,0:T(8,128)(2,1)S(1)}, u32[]{:S(2)}, u32[]{:S(2)}) collective-permute-start(bf16[32,64,128]{2,1,0:T(8,128)(2,1)} %get-tuple-element.30), channel_id=1, source_target_pairs={{0,8},{2,10},{4,12},{6,14},{8,0},{10,2},{12,4},{14,6},{1,9},{3,11}... | collective-permute-start | bytes 1572872 | tf_op jit(solution)/shard_map/ppermute | solution.py:330
  60.8 13.8 %collective-permute-start.5 = (bf16[32,64,128]{2,1,0:T(8,128)(2,1)S(1)}, bf16[32,64,128]{2,1,0:T(8,128)(2,1)S(1)}, u32[]{:S(2)}, u32[]{:S(2)}) collective-permute-start(bf16[32,64,128]{2,1,0:T(8,128)(2,1)S(1)} %collective-permute-done.2), channel_id=1, source_target_pairs={{0,16},{16,0},{1,17},{17,1},{2,18},{18,2},{3,19},{19,3},{4,20},{20... | collective-permute-start | bytes 1572872 | tf_op jit(solution)/shard_map/ppermute | solution.py:336
  63.6 25.0 %collective-permute-start.3 = (bf16[32,64,128]{2,1,0:T(8,128)(2,1)}, bf16[32,64,128]{2,1,0:T(8,128)(2,1)}, u32[]{:S(2)}, u32[]{:S(2)}) collective-permute-start(bf16[32,64,128]{2,1,0:T(8,128)(2,1)} %get-tuple-element.31), channel_id=1, source_target_pairs={{0,8},{2,10},{4,12},{6,14},{8,0},{10,2},{12,4},{14,6},{1,9},{3,11}... | collective-permute-start | bytes 1572872 | tf_op jit(solution)/shard_map/ppermute | solution.py:330
  75.4 27.4 %collective-permute-start.9 = (bf16[64,64,128]{2,1,0:T(8,128)(2,1)}, bf16[64,64,128]{2,1,0:T(8,128)(2,1)}, u32[]{:S(2)}, u32[]{:S(2)}) collective-permute-start(bf16[64,64,128]{2,1,0:T(8,128)(2,1)} %constant_dynamic-update-slice_fusion.2.refs_2_.refs_6_), channel_id=1, source_target_pairs={{0,1},{1,0},{2,3},{3,2},{4,5},{5,4},{6,7},{7,6},{8,9},{9,8},{10,11... | collective-permute-start | bytes 3145736 | tf_op jit(solution)/shard_map/ppermute | solution.py:340
  75.4 27.3 %all-to-all-start = ((bf16[32,4,4096]{2,0,1:T(8,128)(2,1)}), bf16[32,4,4096]{2,0,1:T(8,128)(2,1)}, u32[]{:S(2)}, u32[]{:S(2)}) async-start(bf16[32,4,4096]{2,0,1:T(8,128)(2,1)} %bitcast.32), calls=%async_computation | async-start | bytes 2097152 | tf_op jit(solution)/shard_map/all_to_all | solution.py:289
  79.7 2.8 %copy-start = (bf16[384,64,128]{2,1,0:T(8,128)(2,1)S(1)}, bf16[384,64,128]{2,1,0:T(8,128)(2,1)}, u32[]{:S(2)}) copy-start(bf16[384,64,128]{2,1,0:T(8,128)(2,1)} %refs_4_.1) | copy-start | bytes 18874372
  85.5 1.3 copy-start.2
  86.8 16.0 %collective-permute-start.8 = (bf16[64,64,128]{2,1,0:T(8,128)(2,1)}, bf16[64,64,128]{2,1,0:T(8,128)(2,1)}, u32[]{:S(2)}, u32[]{:S(2)}) collective-permute-start(bf16[64,64,128]{2,1,0:T(8,128)(2,1)} %pad_maximum_fusion.refs_0_.refs_4_), channel_id=1, source_target_pairs={{0,1},{1,0},{2,3},{3,2},{4,5},{5,4},{6,7},{7,6},{8,9},{9,8},{10,11... | collective-permute-start | bytes 3145736 | tf_op jit(solution)/shard_map/ppermute | solution.py:340
  88.6 14.0 %collective-permute-start.6 = (bf16[32,64,128]{2,1,0:T(8,128)(2,1)}, bf16[32,64,128]{2,1,0:T(8,128)(2,1)S(1)}, u32[]{:S(2)}, u32[]{:S(2)}) collective-permute-start(bf16[32,64,128]{2,1,0:T(8,128)(2,1)} %collective-permute-done.3), channel_id=1, source_target_pairs={{0,16},{16,0},{1,17},{17,1},{2,18},{18,2},{3,19},{19,3},{4,20},{20... | collective-permute-start | bytes 1572872 | tf_op jit(solution)/shard_map/ppermute | solution.py:336
  102.7 10.0 %collective-permute-start.7 = (bf16[64,64,128]{2,1,0:T(8,128)(2,1)S(1)}, bf16[64,64,128]{2,1,0:T(8,128)(2,1)}, u32[]{:S(2)}, u32[]{:S(2)}) collective-permute-start(bf16[64,64,128]{2,1,0:T(8,128)(2,1)S(1)} %constant_dynamic-update-slice_fusion.refs_0_.refs_8_), channel_id=1, source_target_pairs={{0,1},{1,0},{2,3},{3,2},{4,5},{5,4},{6,7},{7,6},{8,9},{9,8},{10,11... | collective-permute-start | bytes 3145736 | tf_op jit(solution)/shard_map/ppermute | solution.py:340
  102.8 1.6 copy-start.3
  115.1 12.7 %collective-permute-start.10 = (bf16[32,4096]{1,0:T(8,128)(2,1)S(1)}, bf16[32,4096]{1,0:T(8,128)(2,1)S(1)}, u32[]{:S(2)}, u32[]{:S(2)}) collective-permute-start(bf16[32,4096]{1,0:T(8,128)(2,1)S(1)} %get-tuple-element.38), channel_id=1, source_target_pairs={{0,2},{2,0},{4,6},{6,4},{8,10},{10,8},{12,14},{14,12},{1,3},{3,1},... | collective-permute-start | bytes 786440 | tf_op jit(solution)/shard_map/ppermute | solution.py:281
  116.8 18.1 %collective-permute-start.11 = (bf16[32,4096]{1,0:T(8,128)(2,1)S(1)}, bf16[32,4096]{1,0:T(8,128)(2,1)S(1)}, u32[]{:S(2)}, u32[]{:S(2)}) collective-permute-start(bf16[32,4096]{1,0:T(8,128)(2,1)S(1)} %get-tuple-element.39), channel_id=1, source_target_pairs={{0,4},{2,6},{4,0},{6,2},{8,12},{10,14},{12,8},{14,10},{1,5},{3,7},... | collective-permute-start | bytes 786440 | tf_op jit(solution)/shard_map/ppermute | solution.py:281
  127.8 12.1 %collective-permute-start.12 = (bf16[32,4096]{1,0:T(8,128)(2,1)S(1)}, bf16[32,4096]{1,0:T(8,128)(2,1)S(1)}, u32[]{:S(2)}, u32[]{:S(2)}) collective-permute-start(bf16[32,4096]{1,0:T(8,128)(2,1)S(1)} %get-tuple-element.40), channel_id=1, source_target_pairs={{0,6},{2,4},{4,2},{6,0},{8,14},{10,12},{12,10},{14,8},{1,7},{3,5},... | collective-permute-start | bytes 786440 | tf_op jit(solution)/shard_map/ppermute | solution.py:281
  140.8 8.3 %collective-permute-start.13 = (bf16[32,4096]{1,0:T(8,128)(2,1)S(1)}, bf16[32,4096]{1,0:T(8,128)(2,1)S(1)}, u32[]{:S(2)}, u32[]{:S(2)}) collective-permute-start(bf16[32,4096]{1,0:T(8,128)(2,1)S(1)} %shard_map.70.refs_0_), channel_id=1, source_target_pairs={{0,2},{2,0},{4,6},{6,4},{8,10},{10,8},{12,14},{14,12},{1,3},{3,1},... | collective-permute-start | bytes 786440 | tf_op jit(solution)/shard_map/ppermute | solution.py:281
  142.5 9.2 %collective-permute-start.14 = (bf16[32,4096]{1,0:T(8,128)(2,1)S(1)}, bf16[32,4096]{1,0:T(8,128)(2,1)S(1)}, u32[]{:S(2)}, u32[]{:S(2)}) collective-permute-start(bf16[32,4096]{1,0:T(8,128)(2,1)S(1)} %shard_map.70.refs_0_), channel_id=1, source_target_pairs={{0,4},{2,6},{4,0},{6,2},{8,12},{10,14},{12,8},{14,10},{1,5},{3,7},... | collective-permute-start | bytes 786440 | tf_op jit(solution)/shard_map/ppermute | solution.py:281
  144.2 11.5 %collective-permute-start.15 = (bf16[32,4096]{1,0:T(8,128)(2,1)S(1)}, bf16[32,4096]{1,0:T(8,128)(2,1)S(1)}, u32[]{:S(2)}, u32[]{:S(2)}) collective-permute-start(bf16[32,4096]{1,0:T(8,128)(2,1)S(1)} %shard_map.70.refs_0_), channel_id=1, source_target_pairs={{0,6},{2,4},{4,2},{6,0},{8,14},{10,12},{12,10},{14,8},{1,7},{3,5},... | collective-permute-start | bytes 786440 | tf_op jit(solution)/shard_map/ppermute | solution.py:281
  164.4 24.0 %collective-permute-start.16 = (bf16[32,4096]{1,0:T(8,128)(2,1)S(1)}, bf16[32,4096]{1,0:T(8,128)(2,1)S(1)}, u32[]{:S(2)}, u32[]{:S(2)}) collective-permute-start(bf16[32,4096]{1,0:T(8,128)(2,1)S(1)} %get-tuple-element.42), channel_id=1, source_target_pairs={{0,2},{2,0},{4,6},{6,4},{8,10},{10,8},{12,14},{14,12},{1,3},{3,1},... | collective-permute-start | bytes 786440 | tf_op jit(solution)/shard_map/ppermute | solution.py:281
  164.5 24.1 %collective-permute-start.17 = (bf16[32,4096]{1,0:T(8,128)(2,1)S(1)}, bf16[32,4096]{1,0:T(8,128)(2,1)S(1)}, u32[]{:S(2)}, u32[]{:S(2)}) collective-permute-start(bf16[32,4096]{1,0:T(8,128)(2,1)S(1)} %get-tuple-element.43), channel_id=1, source_target_pairs={{0,4},{2,6},{4,0},{6,2},{8,12},{10,14},{12,8},{14,10},{1,5},{3,7},... | collective-permute-start | bytes 786440 | tf_op jit(solution)/shard_map/ppermute | solution.py:281
  167.9 20.7 %collective-permute-start.18 = (bf16[32,4096]{1,0:T(8,128)(2,1)S(1)}, bf16[32,4096]{1,0:T(8,128)(2,1)S(1)}, u32[]{:S(2)}, u32[]{:S(2)}) collective-permute-start(bf16[32,4096]{1,0:T(8,128)(2,1)S(1)} %get-tuple-element.44), channel_id=1, source_target_pairs={{0,6},{2,4},{4,2},{6,0},{8,14},{10,12},{12,10},{14,8},{1,7},{3,5},... | collective-permute-start | bytes 786440 | tf_op jit(solution)/shard_map/ppermute | solution.py:281
  168.5 2.8 %copy-start.1 = (bf16[384,64,128]{2,1,0:T(8,128)(2,1)S(1)}, bf16[384,64,128]{2,1,0:T(8,128)(2,1)}, u32[]{:S(2)}) copy-start(bf16[384,64,128]{2,1,0:T(8,128)(2,1)} %refs_4_.1) | copy-start | bytes 18874372
  174.6 14.1 %collective-permute-start.19 = (bf16[32,4096]{1,0:T(8,128)(2,1)S(1)}, bf16[32,4096]{1,0:T(8,128)(2,1)S(1)}, u32[]{:S(2)}, u32[]{:S(2)}) collective-permute-start(bf16[32,4096]{1,0:T(8,128)(2,1)S(1)} %get-tuple-element.46), channel_id=1, source_target_pairs={{0,2},{2,0},{4,6},{6,4},{8,10},{10,8},{12,14},{14,12},{1,3},{3,1},... | collective-permute-start | bytes 786440 | tf_op jit(solution)/shard_map/ppermute | solution.py:281
  178.9 15.7 %collective-permute-start.20 = (bf16[32,4096]{1,0:T(8,128)(2,1)S(1)}, bf16[32,4096]{1,0:T(8,128)(2,1)S(1)}, u32[]{:S(2)}, u32[]{:S(2)}) collective-permute-start(bf16[32,4096]{1,0:T(8,128)(2,1)S(1)} %get-tuple-element.47), channel_id=1, source_target_pairs={{0,4},{2,6},{4,0},{6,2},{8,12},{10,14},{12,8},{14,10},{1,5},{3,7},... | collective-permute-start | bytes 786440 | tf_op jit(solution)/shard_map/ppermute | solution.py:281
  188.4 8.8 %collective-permute-start.21 = (bf16[32,4096]{1,0:T(8,128)(2,1)S(1)}, bf16[32,4096]{1,0:T(8,128)(2,1)S(1)}, u32[]{:S(2)}, u32[]{:S(2)}) collective-permute-start(bf16[32,4096]{1,0:T(8,128)(2,1)S(1)} %get-tuple-element.48), channel_id=1, source_target_pairs={{0,6},{2,4},{4,2},{6,0},{8,14},{10,12},{12,10},{14,8},{1,7},{3,5},... | collective-permute-start | bytes 786440 | tf_op jit(solution)/shard_map/ppermute | solution.py:281
  194.6 2.6 %copy-start.6 = (bf16[32,32768]{1,0:T(8,128)(2,1)}, bf16[32,32768]{1,0:T(8,128)(2,1)S(1)}, u32[]{:S(2)}) copy-start(bf16[32,32768]{1,0:T(8,128)(2,1)S(1)} %constant_dynamic-update-slice_fusion.5) | copy-start | bytes 6291460
  (2 other events, 1.4 us)

commit v9 on v8

--- a/solution.py
+++ b/solution.py
@@ -10,7 +10,8 @@
 TILE = 64
 PAIR = 2 * TILE
 UNROLL = 4
-VMEM_LIMIT = 16 * 1024 * 1024
+OWN_COPIES = 8
+VMEM_LIMIT = 24 * 1024 * 1024
 PARTS = 3
 RANGES = ((0, 2), (2, 3))
 OWN_FORWARD, OWN_BACKWARD, OTHER_FORWARD, OTHER_BACKWARD = range(4)
@@ -23,15 +24,29 @@
     return max(1, (count - 1).bit_length())
 
 
+def list_length(tiles, blocks):
+    return tiles + len(RANGES) * (blocks + 2 * UNROLL)
+
+
 def pair_lists(codes, keys, live, blocks, absent):
     n_lists, tiles = codes.shape
     n_keys = len(RANGES) * blocks
     order = jnp.arange(tiles, dtype=jnp.int32)
     key_range = jnp.arange(n_keys, dtype=jnp.int32)
+    ranges = jnp.arange(STEPS, dtype=jnp.int32)
     mine = (keys[:, None, :] == key_range[None, :, None]) & live[:, None, :]
     pairs = (jnp.sum(mine, axis=2, dtype=jnp.int32) + 1) // 2
-    lower = key_range[None, :, None] < key_range[None, None, :]
+    in_range = key_range[:, None] // blocks == ranges[None, :]
+    totals = jnp.sum(jnp.where(in_range, pairs[:, :, None], 0), axis=1, dtype=jnp.int32)
+    totals = (totals + UNROLL - 1) // UNROLL * UNROLL
+    bounds = jnp.sum(
+        jnp.where(ranges[:, None] < ranges[None, :], totals[:, :, None], 0), axis=1, dtype=jnp.int32
+    )
+    lower = (key_range[:, None] < key_range[None, :]) & (
+        key_range[:, None] // blocks == key_range[None, :] // blocks
+    )
     starts = jnp.sum(jnp.where(lower, pairs[:, :, None], 0), axis=1, dtype=jnp.int32)
+    starts += jnp.sum(jnp.where(in_range, bounds[:, None, :], 0), axis=2, dtype=jnp.int32)
     before = (
         (keys[:, :, None] == keys[:, None, :]) & live[:, :, None] & (order[:, None] < order[None, :])
     )
@@ -39,62 +54,79 @@
         jnp.where(mine, starts[:, :, None], 0), axis=1, dtype=jnp.int32
     )
     entry = jnp.where(live, entry, -1)
-    found = entry[:, :, None] == jnp.arange(tiles + n_keys, dtype=jnp.int32)
+    found = entry[:, :, None] == jnp.arange(list_length(tiles, blocks), dtype=jnp.int32)
     entries = absent + jnp.sum(
         jnp.where(found, codes[:, :, None] - absent, 0), axis=1, dtype=jnp.int32
     )
-    ends = jnp.arange(STEPS, dtype=jnp.int32) * blocks
-    bounds = jnp.sum(
-        jnp.where(key_range[None, :, None] < ends, pairs[:, :, None], 0), axis=1, dtype=jnp.int32
-    )
     return jnp.concatenate([bounds.reshape(-1), entries.reshape(-1)])
 
 
-def padded_tile(values, half):
-    zero = jnp.zeros_like(values)
-    return jnp.concatenate(
-        [jnp.where(half == 0, values, zero), jnp.where(half == 1, values, zero)], axis=0
-    )
-
-
-def pair_loop(sizes, meta, ref, proj, which, first, last, origin, product, sums):
+def pair_loop(sizes, meta, held, proj, which, first, last, origin, product, sums):
     tiles, segments, blocks = sizes
     begin, end = (meta[BOUNDS + STEPS * which + number] for number in (first, last))
-    base = LISTS + which * (tiles + len(RANGES) * blocks)
-
-    def tile(entry, live):
+    base = LISTS + which * list_length(tiles, blocks)
+    final = 2 * (held.shape[0] - 1)
+
+    def tile(entry):
         code = meta[base + entry]
-        index = jnp.where(live, (code & ((1 << bits(tiles)) - 1)) - origin, 0)
-        code = code >> bits(tiles)
-        segment = code & ((1 << bits(segments)) - 1)
-        code = code >> bits(segments)
-        block = code & ((1 << bits(blocks)) - 1)
-        half = jnp.where(live, (segment & 1) + 2 * (code >> bits(blocks)), 2)
-        points = pl.ds(pl.multiple_of((segment >> 1) * PAIR, PAIR), PAIR)
-        lanes = pl.ds(pl.multiple_of(block * proj, proj), proj)
-        return points, lanes, padded_tile(ref[jnp.maximum(index, 0)], half)
+        window = jnp.minimum((code & ((1 << bits(2 * tiles + 1)) - 1)) - 2 * origin, final)
+        code = code >> bits(2 * tiles + 1)
+        points = pl.ds(pl.multiple_of((code & ((1 << bits(segments // 2)) - 1)) * PAIR, PAIR), PAIR)
+        lanes = pl.ds(pl.multiple_of((code >> bits(segments // 2)) * proj, proj), proj)
+        values = [held[at >> 1, at & 1] for at in (window, window + 1)]
+        return points, lanes, jnp.concatenate(values, axis=0)
 
     def group(index, carry):
         terms = []
         for lane in range(UNROLL):
             pair = begin + index * UNROLL + lane
-            live = pair < end
-            pair = jnp.minimum(pair, end - 1)
-            terms.append(product(tile(2 * pair, live), tile(2 * pair + 1, live)))
+            terms.append(product(tile(2 * pair), tile(2 * pair + 1)))
         for lanes, term in terms:
             sums[:, lanes] += term
         return carry
 
-    lax.fori_loop(0, (end - begin + UNROLL - 1) // UNROLL, group, 0)
-
-
-def join_pieces(meta, pieces, joined, first):
+    lax.fori_loop(0, (end - begin) // UNROLL, group, 0)
+
+
+def hold_pieces(meta, pieces, held, first):
     size = pieces[0].shape[0]
     for number, ref in enumerate(pieces):
+        held[number * size, 0] = jnp.zeros(held.shape[2:], held.dtype)
 
         @pl.when(meta[2] > first + number // 2 * 2 * size)
         def copy(number=number, ref=ref):
-            joined[number * size : (number + 1) * size] = ref[...]
+            at = slice(number * size, (number + 1) * size)
+            held[at, 0] = jnp.zeros_like(ref)
+            held[at, 1] = ref[...]
+
+    held[held.shape[0] - 1] = jnp.zeros(held.shape[1:], held.dtype)
+
+
+def hold_own(meta, projectors, held, sems):
+    tiles = projectors.shape[0]
+    size = tiles // OWN_COPIES
+    copies = []
+    for number in range(OWN_COPIES):
+        at = pl.ds(number * size, size)
+        copies.append(
+            pltpu.make_async_copy(projectors.at[at], held.at[at, 1], sems.at[number])
+        )
+        pl.when(meta[1] > number * size)(copies[number].start)
+    for number in range(OWN_COPIES):
+        at = slice(number * size, (number + 1) * size)
+        held[number * size, 0] = jnp.zeros(held.shape[2:], held.dtype)
+
+        @pl.when(meta[1] > number * size)
+        def fill(at=at):
+            held[at, 0] = jnp.zeros((size,) + held.shape[2:], held.dtype)
+
+    held[tiles] = jnp.zeros(held.shape[1:], held.dtype)
+    return copies, size
+
+
+def wait_own(meta, copies, size):
+    for number, copy in enumerate(copies):
+        pl.when(meta[1] > number * size)(copy.wait)
 
 
 def rows_of(refs, lanes):
@@ -112,19 +144,23 @@
 def project_kernel(sizes, n_pieces, spot, first, last, meta, wave, *refs):
     pieces, refs = refs[:n_pieces], refs[n_pieces:]
     proj = pieces[0].shape[2]
-    values = pieces[0]
     if n_pieces > 1:
-        values, refs = refs[-1], refs[:-1]
-        join_pieces(meta, pieces, values, spot[-1])
+        held, refs = refs[-1], refs[:-1]
+        hold_pieces(meta, pieces, held, spot[-1])
+    else:
+        (held, sems), refs = refs[-2:], refs[:-2]
+        copies = hold_own(meta, pieces[0], held, sems)
     total = refs[-1]
     total[...] = jnp.zeros_like(total) if first else refs[0][...]
+    if n_pieces == 1:
+        wait_own(meta, *copies)
 
     def product(one, two):
         waves = jnp.concatenate([wave[:, one[0]], wave[:, two[0]]], axis=1)
         tiles = jnp.concatenate([one[2], two[2]], axis=0)
         return one[1], jnp.dot(waves, tiles, preferred_element_type=jnp.float32)
 
-    pair_loop(sizes, meta, values, proj, *spot, product, total)
+    pair_loop(sizes, meta, held, proj, *spot, product, total)
     if last:
         outs = refs[1:-1]
         rows = outs[0].shape[0]
@@ -137,12 +173,16 @@
     applied, refs = refs[:n_rows], refs[n_rows:]
     pieces, refs = refs[:n_pieces], refs[n_pieces:]
     proj = pieces[0].shape[2]
-    values = pieces[0]
     if n_pieces > 1:
-        values, refs = refs[-1], refs[:-1]
-        join_pieces(meta, pieces, values, 0)
+        held, refs = refs[-1], refs[:-1]
+        hold_pieces(meta, pieces, held, 0)
+    else:
+        (held, sems), refs = refs[-2:], refs[:-2]
+        copies = hold_own(meta, pieces[0], held, sems)
     outs, field = refs[:-1], refs[-1]
     field[...] = jnp.zeros_like(field)
+    if n_pieces == 1:
+        wait_own(meta, *copies)
 
     def product(one, two):
         rows = jnp.concatenate([rows_of(applied, one[1]), rows_of(applied, two[1])], axis=1)
@@ -151,7 +191,7 @@
             rows, tiles, (((1,), (1,)), ((), ())), preferred_element_type=jnp.float32
         )
 
-    pair_loop(sizes, meta, values, proj, which, 0, len(RANGES), 0, product, field)
+    pair_loop(sizes, meta, held, proj, which, 0, len(RANGES), 0, product, field)
     store_rows(outs, field)
 
 
@@ -170,11 +210,15 @@
     return blocks if len(blocks) == count else jnp.split(blocks[0], count)
 
 
-def joined_shape(pieces):
-    if len(pieces) == 1:
-        return []
+def held_shape(pieces):
     shape = pieces[0].shape
-    return [pltpu.VMEM((len(pieces) * shape[0],) + shape[1:], jnp.bfloat16)]
+    shape = (len(pieces) * shape[0] + 1, 2) + shape[1:]
+    sems = [pltpu.SemaphoreType.DMA((OWN_COPIES,))] if len(pieces) == 1 else []
+    return [pltpu.VMEM(shape, jnp.bfloat16)] + sems
+
+
+def piece_specs(pieces):
+    return [pl.BlockSpec(memory_space=pltpu.HBM) if len(pieces) == 1 else WHOLE] * len(pieces)
 
 
 def project(sizes, meta, wave, pieces, count, width, spot, total=None, last=False, us=0):
@@ -191,10 +235,10 @@
         grid_spec=pltpu.PrefetchScalarGridSpec(
             num_scalar_prefetch=1,
             grid=(1,),
-            in_specs=[WHOLE] * len(operands),
+            in_specs=[WHOLE] + piece_specs(pieces) + [WHOLE] * (total is not None),
             out_specs=[WHOLE] * outs if last else WHOLE,
             scratch_shapes=([pltpu.VMEM((rows, width), jnp.float32)] if last else [])
-            + joined_shape(pieces),
+            + held_shape(pieces),
         ),
         out_shape=out_shape if last else jax.ShapeDtypeStruct((rows, width), jnp.float32),
         compiler_params=pltpu.CompilerParams(vmem_limit_bytes=VMEM_LIMIT),
@@ -211,9 +255,9 @@
         grid_spec=pltpu.PrefetchScalarGridSpec(
             num_scalar_prefetch=1,
             grid=(1,),
-            in_specs=[WHOLE] * (len(applied) + len(pieces)),
+            in_specs=[WHOLE] * len(applied) + piece_specs(pieces),
             out_specs=[WHOLE] * len(applied),
-            scratch_shapes=[pltpu.VMEM((rows, points), jnp.float32)] + joined_shape(pieces),
+            scratch_shapes=[pltpu.VMEM((rows, points), jnp.float32)] + held_shape(pieces),
         ),
         out_shape=[
             jax.ShapeDtypeStruct((block.shape[0], points), jnp.bfloat16) for block in applied
@@ -301,9 +345,11 @@
 
     numbers = jnp.stack([tile_segment, tile_block, jnp.broadcast_to(tile_count, (tiles,))])
     others = lax.ppermute(numbers, "grid", partners)
-    absent = 1 << (bits(tiles) + bits(segments) + bits(blocks))
+    absent = 2 * tiles
     segment, block = (jnp.stack([numbers[i], others[i]]) for i in (0, 1))
-    codes = jnp.stack([slots, held]) + ((segment + (block << bits(segments))) << bits(tiles))
+    codes = 2 * jnp.stack([slots, held]) + 1 - segment % 2
+    places = segment // 2 + (block << bits(segments // 2))
+    codes += places << bits(2 * tiles + 1)
     live = slots < jnp.stack([numbers[2], others[2]])
     group_of = sum(jnp.where(part >= first, 1, 0) for first, end in RANGES[1:])
     keys = jnp.stack([block + blocks * jnp.stack([0 * part, group_of]), segment // 2], axis=1)

time: 198 us -> 202 us (1.020)
  Pallas kernels: 26.6 us -> 34.3 us
  starting transfers between devices: 50.5 us -> 48.3 us
    pallas_call x2, Pallas kernels: 11.9 us -> 15.9 us  [spread(): pl.pallas_call(functools.partial(spread_kernel, sizes, len(applied), len(...]
    pallas_call x3, Pallas kernels: 13.7 us -> 17.5 us  [project(): pl.pallas_call(functools.partial(project_kernel, sizes, len(pieces), spot...]
  transfers between devices with their start and end apart: 24 -> 24, of which waited for: 13 -> 14; matrix products, arithmetic and copies ran while one was open for 10% -> 10% of each run, Pallas kernels for 7% -> 10%
where the time goes in v9:
time: 202 us; the launch traced here: 203 us
  waiting for transfers between devices  87.9 us (44%)
  starting transfers between devices  48.3 us (24%)
  Pallas kernels  34.3 us (17%)
  local copies, waits for them, and re-layouts  25 us (12%)
  other arithmetic  6.59 us (3%)
    ppermute x12, starting transfers between devices, exchange(): lax.ppermute(blocks[d], 'grid', [(i, i // half * half + (i % half ^ d)) f...  32.8 us
    ppermute x12, waiting for transfers between devices, exchange(): lax.ppermute(blocks[d], 'grid', [(i, i // half * half + (i % half ^ d)) f...  32.2 us
    ppermute x3, waiting for transfers between devices, body(): across = lax.ppermute(sent, 'groups', swap)  32 us
    ppermute x3, waiting for transfers between devices, body(): mine = lax.ppermute(sent, 'grid', partners)  23.8 us
    pallas_call x3, Pallas kernels, project(): pl.pallas_call(functools.partial(project_kernel, sizes, len(pieces), spot...  17.5 us
    pallas_call x2, Pallas kernels, spread(): pl.pallas_call(functools.partial(spread_kernel, sizes, len(applied), len(...  15.9 us
    unnamed x22, local copies, waits for them, and re-layouts  10.9 us
    all_to_all x2, starting transfers between devices, to_bricks(): lax.all_to_all(part, 'grid', split_axis=1, concat_axis=0, tiled=True, axi...  8.36 us
  transfers between devices with their start and end apart: 24, of which 14 were waited for; matrix products, arithmetic and copies ran while one was open for 10% of the time, Pallas kernels for 10%

profile of v9, /device:TPU:0, one launch (start us, length us, event | category | flops | bytes accessed | tf_op | source)
XLA Modules:
  0.0 203.4 jit_solution(8579177987855353881)
XLA Ops:
  2.3 4.0 %collective-permute-start.1 = (s32[3,384]{1,0:T(4,128)S(1)}, s32[3,384]{1,0:T(4,128)S(1)}, u32[]{:S(2)}, u32[]{:S(2)}) collective-permute-start(s32[3,384]{1,0:T(4,128)S(1)} %add_add_fusion), channel_id=1, source_target_pairs={{0,8},{2,10},{4,12},{6,14},{8,0},{10,2},{12,4},{14,6},{1,9},{3,11}... | collective-permute-start | bytes 13832 | tf_op jit(solution)/shard_map/ppermute | solution.py:347
  6.4 2.5 %constant_dynamic-slice_fusion.1 = (bf16[32,64,128]{2,1,0:T(8,128)(2,1)}, bf16[32,64,128]{2,1,0:T(8,128)(2,1)}, bf16[32,64,128]{2,1,0:T(8,128)(2,1)}) fusion(bf16[384,64,128]{2,1,0:T(8,128)(2,1)} %refs_4_.1, s32[]{:T(128)S(6)} %select_n.325, s32[]{:T(128)S(6)} %select_n.324, s32[]{:T(128)S(6)} %select_n.299), kind=kLoop, calls=%fused_computation.59 | loop fusion | bytes 3145740 | tf_op jit(solution)/shard_map/dynamic_slice | solution.py:373
  11.1 4.1 %all-to-all-start.1 = ((bf16[32,4,4096]{2,0,1:T(8,128)(2,1)}), bf16[32,4,4096]{2,0,1:T(8,128)(2,1)S(1)}, u32[]{:S(2)}, u32[]{:S(2)}) async-start(bf16[32,4,4096]{2,0,1:T(8,128)(2,1)} %bitcast.26), calls=%async_computation.1 | async-start | bytes 2097152 | tf_op jit(solution)/shard_map/all_to_all | solution.py:333
  15.8 1.8 copy.19
  17.7 2.0 select_convert_fusion.high_ref
  24.0 10.7 %collective-permute-done = bf16[32,64,128]{2,1,0:T(8,128)(2,1)} collective-permute-done((bf16[32,64,128]{2,1,0:T(8,128)(2,1)}, bf16[32,64,128]{2,1,0:T(8,128)(2,1)}, u32[]{:S(2)}, u32[]{:S(2)}) %collective-permute-start) | collective-permute-done | bytes 524320 | tf_op jit(solution)/shard_map/ppermute | solution.py:376
  36.3 11.4 %collective-permute-done.4 = bf16[32,64,128]{2,1,0:T(8,128)(2,1)S(1)} collective-permute-done((bf16[32,64,128]{2,1,0:T(8,128)(2,1)}, bf16[32,64,128]{2,1,0:T(8,128)(2,1)S(1)}, u32[]{:S(2)}, u32[]{:S(2)}) %collective-permute-start.4) | collective-permute-done | bytes 524320 | tf_op jit(solution)/shard_map/ppermute | solution.py:382
  47.7 13.0 %collective-permute-done.2 = bf16[32,64,128]{2,1,0:T(8,128)(2,1)S(1)} collective-permute-done((bf16[32,64,128]{2,1,0:T(8,128)(2,1)}, bf16[32,64,128]{2,1,0:T(8,128)(2,1)S(1)}, u32[]{:S(2)}, u32[]{:S(2)}) %collective-permute-start.2) | collective-permute-done | bytes 524320 | tf_op jit(solution)/shard_map/ppermute | solution.py:376
  61.2 2.3 %copy.29 = bf16[4,4,8,4096]{3,2,0,1:T(8,128)(2,1)} copy(bf16[4,4,8,4096]{3,2,1,0:T(8,128)(2,1)} %bitcast.30) | data formatting | bytes 2097152 | tf_op jit(solution)/shard_map/all_to_all | solution.py:333
  64.4 2.1 %pad_maximum_fusion.refs_0_.refs_4_ = bf16[64,64,128]{2,1,0:T(8,128)(2,1)} fusion(bf16[32,64,128]{2,1,0:T(8,128)(2,1)S(1)} %collective-permute-done.4, bf16[32,64,128]{2,1,0:T(8,128)(2,1)} %collective-permute-done), kind=kLoop, calls=%fused_computation.7 | loop fusion | flops 524288 | bytes 2097152 | tf_op jit(solution)/shard_map/concatenate | solution.py:383
  66.5 8.1 %collective-permute-done.5 = bf16[32,64,128]{2,1,0:T(8,128)(2,1)S(1)} collective-permute-done((bf16[32,64,128]{2,1,0:T(8,128)(2,1)S(1)}, bf16[32,64,128]{2,1,0:T(8,128)(2,1)S(1)}, u32[]{:S(2)}, u32[]{:S(2)}) %collective-permute-start.5) | collective-permute-done | bytes 524320 | tf_op jit(solution)/shard_map/ppermute | solution.py:382
  75.4 4.3 %all-to-all-start = ((bf16[32,4,4096]{2,0,1:T(8,128)(2,1)}), bf16[32,4,4096]{2,0,1:T(8,128)(2,1)}, u32[]{:S(2)}, u32[]{:S(2)}) async-start(bf16[32,4,4096]{2,0,1:T(8,128)(2,1)} %bitcast.32), calls=%async_computation | async-start | bytes 2097152 | tf_op jit(solution)/shard_map/all_to_all | solution.py:333
  79.7 2.8 %copy-done = bf16[384,64,128]{2,1,0:T(8,128)(2,1)S(1)} copy-done((bf16[384,64,128]{2,1,0:T(8,128)(2,1)S(1)}, bf16[384,64,128]{2,1,0:T(8,128)(2,1)}, u32[]{:S(2)}) %copy-start) | copy-done | bytes 6291480
  82.5 5.7 %shard_map.67.refs_4_ = f32[128,4096]{1,0:T(8,128)S(1)} custom-call(s32[1871]{0:T(1024)S(1)} %concatenate.70.meta, bf16[128,4096]{1,0:T(8,128)(2,1)S(1)} %bitcast.29, bf16[384,64,128]{2,1,0:T(8,128)(2,1)S(1)} %copy-done), custom_call_target="tpu_custom_call" | custom-call | flops 10000000000 | bytes 1 | tf_op jit(solution)/shard_map/pallas_call | solution.py:231
  91.7 12.4 %collective-permute-done.6 = bf16[32,64,128]{2,1,0:T(8,128)(2,1)S(1)} collective-permute-done((bf16[32,64,128]{2,1,0:T(8,128)(2,1)}, bf16[32,64,128]{2,1,0:T(8,128)(2,1)S(1)}, u32[]{:S(2)}, u32[]{:S(2)}) %collective-permute-start.6) | collective-permute-done | bytes 524320 | tf_op jit(solution)/shard_map/ppermute | solution.py:382
  105.9 9.3 %shard_map.68.refs_2_ = f32[128,4096]{1,0:T(8,128)S(1)} custom-call(s32[1871]{0:T(1024)S(1)} %concatenate.70.meta, bf16[128,4096]{1,0:T(8,128)(2,1)} %bitcast.10.wave, bf16[64,64,128]{2,1,0:T(8,128)(2,1)} %pad_maximum_fusion.refs_0_.refs_4_, bf16[64,64,128]{2,1,0:T(8,128)(2,1)} %collective-permute-done.8.refs_1_.refs_5_, ...), custom_call_target="tpu_custom_call" | custom-call | flops 8000000000 | bytes 1 | tf_op jit(solution)/shard_map/pallas_call | solution.py:231
  115.2 2.4 %shard_map.69 = (bf16[32,4096]{1,0:T(8,128)(2,1)S(1)}, bf16[32,4096]{1,0:T(8,128)(2,1)S(1)}, bf16[32,4096]{1,0:T(8,128)(2,1)S(1)}, bf16[32,4096]{1,0:T(8,128)(2,1)S(1)}) custom-call(s32[1871]{0:T(1024)S(1)} %concatenate.70.meta, bf16[128,4096]{1,0:T(8,128)(2,1)} %bitcast.10.wave, bf16[64,64,128]{2,1,0:T(8,128)(2,1)S(1)} %constant_dynamic-update-slice_fusion.refs_0_.refs_8_, ...), custom_call_target="tpu_custom_call" | custom-call | flops 1 | bytes 1 | tf_op jit(solution)/shard_map/pallas_call | solution.py:231
  117.6 11.2 %collective-permute-start.10 = (bf16[32,4096]{1,0:T(8,128)(2,1)S(1)}, bf16[32,4096]{1,0:T(8,128)(2,1)S(1)}, u32[]{:S(2)}, u32[]{:S(2)}) collective-permute-start(bf16[32,4096]{1,0:T(8,128)(2,1)S(1)} %get-tuple-element.38), channel_id=1, source_target_pairs={{0,2},{2,0},{4,6},{6,4},{8,10},{10,8},{12,14},{14,12},{1,3},{3,1},... | collective-permute-start | bytes 786440 | tf_op jit(solution)/shard_map/ppermute | solution.py:325
  130.4 5.4 %collective-permute-done.10.refs_1_ = bf16[32,4096]{1,0:T(8,128)(2,1)S(1)} collective-permute-done((bf16[32,4096]{1,0:T(8,128)(2,1)S(1)}, bf16[32,4096]{1,0:T(8,128)(2,1)S(1)}, u32[]{:S(2)}, u32[]{:S(2)}) %collective-permute-start.10) | collective-permute-done | bytes 262176 | tf_op jit(solution)/shard_map/ppermute | solution.py:325
  135.8 2.2 %collective-permute-done.11.refs_2_ = bf16[32,4096]{1,0:T(8,128)(2,1)S(1)} collective-permute-done((bf16[32,4096]{1,0:T(8,128)(2,1)S(1)}, bf16[32,4096]{1,0:T(8,128)(2,1)S(1)}, u32[]{:S(2)}, u32[]{:S(2)}) %collective-permute-start.11) | collective-permute-done | bytes 262176 | tf_op jit(solution)/shard_map/ppermute | solution.py:325
  138.0 4.7 %collective-permute-done.12.refs_3_ = bf16[32,4096]{1,0:T(8,128)(2,1)S(1)} collective-permute-done((bf16[32,4096]{1,0:T(8,128)(2,1)S(1)}, bf16[32,4096]{1,0:T(8,128)(2,1)S(1)}, u32[]{:S(2)}, u32[]{:S(2)}) %collective-permute-start.12) | collective-permute-done | bytes 262176 | tf_op jit(solution)/shard_map/ppermute | solution.py:325
  143.6 1.7 collective-permute-start.13
  147.1 4.8 %collective-permute-done.13.refs_1_ = bf16[32,4096]{1,0:T(8,128)(2,1)S(1)} collective-permute-done((bf16[32,4096]{1,0:T(8,128)(2,1)S(1)}, bf16[32,4096]{1,0:T(8,128)(2,1)S(1)}, u32[]{:S(2)}, u32[]{:S(2)}) %collective-permute-start.13) | collective-permute-done | bytes 262176 | tf_op jit(solution)/shard_map/ppermute | solution.py:325
  152.0 2.6 %collective-permute-done.14.refs_2_ = bf16[32,4096]{1,0:T(8,128)(2,1)S(1)} collective-permute-done((bf16[32,4096]{1,0:T(8,128)(2,1)S(1)}, bf16[32,4096]{1,0:T(8,128)(2,1)S(1)}, u32[]{:S(2)}, u32[]{:S(2)}) %collective-permute-start.14) | collective-permute-done | bytes 262176 | tf_op jit(solution)/shard_map/ppermute | solution.py:325
  154.5 3.8 %collective-permute-done.15.refs_3_ = bf16[32,4096]{1,0:T(8,128)(2,1)S(1)} collective-permute-done((bf16[32,4096]{1,0:T(8,128)(2,1)S(1)}, bf16[32,4096]{1,0:T(8,128)(2,1)S(1)}, u32[]{:S(2)}, u32[]{:S(2)}) %collective-permute-start.15) | collective-permute-done | bytes 262176 | tf_op jit(solution)/shard_map/ppermute | solution.py:325
  158.3 9.8 %shard_map.71 = (bf16[32,4096]{1,0:T(8,128)(2,1)S(1)}, bf16[32,4096]{1,0:T(8,128)(2,1)S(1)}, bf16[32,4096]{1,0:T(8,128)(2,1)S(1)}, bf16[32,4096]{1,0:T(8,128)(2,1)S(1)}) custom-call(s32[1871]{0:T(1024)S(1)} %concatenate.70.meta, bf16[32,4096]{1,0:T(8,128)(2,1)S(1)} %shard_map.70.refs_0_, bf16[32,4096]{1,0:T(8,128)(2,1)S(1)} %collective-permute-done.13.refs_1_, ...), custom_call_target="tpu_custom_call" | custom-call | flops 1 | bytes 1 | tf_op jit(solution)/shard_map/pallas_call | solution.py:253
  169.8 1.9 collective-permute-start.18
  171.7 2.8 %copy-done.1 = bf16[384,64,128]{2,1,0:T(8,128)(2,1)S(1)} copy-done((bf16[384,64,128]{2,1,0:T(8,128)(2,1)S(1)}, bf16[384,64,128]{2,1,0:T(8,128)(2,1)}, u32[]{:S(2)}) %copy-start.1) | copy-done | bytes 6291480
  174.5 6.1 %shard_map.72 = (bf16[32,4096]{1,0:T(8,128)(2,1)S(1)}, bf16[32,4096]{1,0:T(8,128)(2,1)S(1)}, bf16[32,4096]{1,0:T(8,128)(2,1)S(1)}, bf16[32,4096]{1,0:T(8,128)(2,1)S(1)}) custom-call(s32[1871]{0:T(1024)S(1)} %concatenate.70.meta, bf16[32,4096]{1,0:T(8,128)(2,1)S(1)} %shard_map.70.refs_0_, bf16[32,4096]{1,0:T(8,128)(2,1)S(1)} %collective-permute-done.13.refs_1_, ...), custom_call_target="tpu_custom_call" | custom-call | flops 1 | bytes 1 | tf_op jit(solution)/shard_map/pallas_call | solution.py:253
  180.6 11.4 %collective-permute-start.19 = (bf16[32,4096]{1,0:T(8,128)(2,1)S(1)}, bf16[32,4096]{1,0:T(8,128)(2,1)S(1)}, u32[]{:S(2)}, u32[]{:S(2)}) collective-permute-start(bf16[32,4096]{1,0:T(8,128)(2,1)S(1)} %get-tuple-element.46), channel_id=1, source_target_pairs={{0,2},{2,0},{4,6},{6,4},{8,10},{10,8},{12,14},{14,12},{1,3},{3,1},... | collective-permute-start | bytes 786440 | tf_op jit(solution)/shard_map/ppermute | solution.py:325
  193.9 5.2 %collective-permute-done.19 = bf16[32,4096]{1,0:T(8,128)(2,1)S(1)} collective-permute-done((bf16[32,4096]{1,0:T(8,128)(2,1)S(1)}, bf16[32,4096]{1,0:T(8,128)(2,1)S(1)}, u32[]{:S(2)}, u32[]{:S(2)}) %collective-permute-start.19) | collective-permute-done | bytes 262176 | tf_op jit(solution)/shard_map/ppermute | solution.py:325
  200.1 2.5 %collective-permute-done.21 = bf16[32,4096]{1,0:T(8,128)(2,1)S(1)} collective-permute-done((bf16[32,4096]{1,0:T(8,128)(2,1)S(1)}, bf16[32,4096]{1,0:T(8,128)(2,1)S(1)}, u32[]{:S(2)}, u32[]{:S(2)}) %collective-permute-start.21) | collective-permute-done | bytes 262176 | tf_op jit(solution)/shard_map/ppermute | solution.py:325
  (110 shorter events, 27.0 us)
Async XLA Ops:
  0.0 8.9 %copy-start.5 = (bf16[32,32768]{1,0:T(8,128)(2,1)S(1)}, bf16[32,32768]{1,0:T(8,128)(2,1)}, u32[]{:S(2)}) copy-start(bf16[32,32768]{1,0:T(8,128)(2,1)} %param.6) | copy-start | bytes 6291460
  2.3 18.2 %collective-permute-start.1 = (s32[3,384]{1,0:T(4,128)S(1)}, s32[3,384]{1,0:T(4,128)S(1)}, u32[]{:S(2)}, u32[]{:S(2)}) collective-permute-start(s32[3,384]{1,0:T(4,128)S(1)} %add_add_fusion), channel_id=1, source_target_pairs={{0,8},{2,10},{4,12},{6,14},{8,0},{10,2},{12,4},{14,6},{1,9},{3,11}... | collective-permute-start | bytes 13832 | tf_op jit(solution)/shard_map/ppermute | solution.py:347
  8.9 25.9 %collective-permute-start = (bf16[32,64,128]{2,1,0:T(8,128)(2,1)}, bf16[32,64,128]{2,1,0:T(8,128)(2,1)}, u32[]{:S(2)}, u32[]{:S(2)}) collective-permute-start(bf16[32,64,128]{2,1,0:T(8,128)(2,1)} %get-tuple-element.53), channel_id=1, source_target_pairs={{0,8},{2,10},{4,12},{6,14},{8,0},{10,2},{12,4},{14,6},{1,9},{3,11}... | collective-permute-start | bytes 1572872 | tf_op jit(solution)/shard_map/ppermute | solution.py:376
  10.0 5.4 %copy-start.7 = (f32[32,16,8,8]{0,3,2,1:T(8,128)S(1)}, f32[32,16,8,8]{0,3,2,1:T(8,128)}, u32[]{:S(2)}) copy-start(f32[32,16,8,8]{0,3,2,1:T(8,128)} %param.11) | copy-start | bytes 393220
  11.1 64.4 %all-to-all-start.1 = ((bf16[32,4,4096]{2,0,1:T(8,128)(2,1)}), bf16[32,4,4096]{2,0,1:T(8,128)(2,1)S(1)}, u32[]{:S(2)}, u32[]{:S(2)}) async-start(bf16[32,4,4096]{2,0,1:T(8,128)(2,1)} %bitcast.26), calls=%async_computation.1 | async-start | bytes 2097152 | tf_op jit(solution)/shard_map/all_to_all | solution.py:333
  17.6 2.2 %copy-start.4 = (f32[32,128,128]{2,1,0:T(8,128)S(1)}, f32[32,128,128]{2,1,0:T(8,128)}, u32[]{:S(2)}) copy-start(f32[32,128,128]{2,1,0:T(8,128)} %copy.19) | copy-start | bytes 6291460
  34.8 12.9 %collective-permute-start.4 = (bf16[32,64,128]{2,1,0:T(8,128)(2,1)}, bf16[32,64,128]{2,1,0:T(8,128)(2,1)S(1)}, u32[]{:S(2)}, u32[]{:S(2)}) collective-permute-start(bf16[32,64,128]{2,1,0:T(8,128)(2,1)} %collective-permute-done), channel_id=1, source_target_pairs={{0,16},{16,0},{1,17},{17,1},{2,18},{18,2},{3,19},{19,3},{4,20},{20... | collective-permute-start | bytes 1572872 | tf_op jit(solution)/shard_map/ppermute | solution.py:382
  36.3 24.5 %collective-permute-start.2 = (bf16[32,64,128]{2,1,0:T(8,128)(2,1)}, bf16[32,64,128]{2,1,0:T(8,128)(2,1)S(1)}, u32[]{:S(2)}, u32[]{:S(2)}) collective-permute-start(bf16[32,64,128]{2,1,0:T(8,128)(2,1)} %get-tuple-element.30), channel_id=1, source_target_pairs={{0,8},{2,10},{4,12},{6,14},{8,0},{10,2},{12,4},{14,6},{1,9},{3,11}... | collective-permute-start | bytes 1572872 | tf_op jit(solution)/shard_map/ppermute | solution.py:376
  60.7 13.8 %collective-permute-start.5 = (bf16[32,64,128]{2,1,0:T(8,128)(2,1)S(1)}, bf16[32,64,128]{2,1,0:T(8,128)(2,1)S(1)}, u32[]{:S(2)}, u32[]{:S(2)}) collective-permute-start(bf16[32,64,128]{2,1,0:T(8,128)(2,1)S(1)} %collective-permute-done.2), channel_id=1, source_target_pairs={{0,16},{16,0},{1,17},{17,1},{2,18},{18,2},{3,19},{19,3},{4,20},{20... | collective-permute-start | bytes 1572872 | tf_op jit(solution)/shard_map/ppermute | solution.py:382
  63.5 26.5 %collective-permute-start.3 = (bf16[32,64,128]{2,1,0:T(8,128)(2,1)}, bf16[32,64,128]{2,1,0:T(8,128)(2,1)}, u32[]{:S(2)}, u32[]{:S(2)}) collective-permute-start(bf16[32,64,128]{2,1,0:T(8,128)(2,1)} %get-tuple-element.31), channel_id=1, source_target_pairs={{0,8},{2,10},{4,12},{6,14},{8,0},{10,2},{12,4},{14,6},{1,9},{3,11}... | collective-permute-start | bytes 1572872 | tf_op jit(solution)/shard_map/ppermute | solution.py:376
  75.4 28.8 %collective-permute-start.9 = (bf16[64,64,128]{2,1,0:T(8,128)(2,1)}, bf16[64,64,128]{2,1,0:T(8,128)(2,1)}, u32[]{:S(2)}, u32[]{:S(2)}) collective-permute-start(bf16[64,64,128]{2,1,0:T(8,128)(2,1)} %constant_dynamic-update-slice_fusion.2.refs_2_.refs_6_), channel_id=1, source_target_pairs={{0,1},{1,0},{2,3},{3,2},{4,5},{5,4},{6,7},{7,6},{8,9},{9,8},{10,11... | collective-permute-start | bytes 3145736 | tf_op jit(solution)/shard_map/ppermute | solution.py:386
  75.4 28.8 %all-to-all-start = ((bf16[32,4,4096]{2,0,1:T(8,128)(2,1)}), bf16[32,4,4096]{2,0,1:T(8,128)(2,1)}, u32[]{:S(2)}, u32[]{:S(2)}) async-start(bf16[32,4,4096]{2,0,1:T(8,128)(2,1)} %bitcast.32), calls=%async_computation | async-start | bytes 2097152 | tf_op jit(solution)/shard_map/all_to_all | solution.py:333
  79.7 2.8 %copy-start = (bf16[384,64,128]{2,1,0:T(8,128)(2,1)S(1)}, bf16[384,64,128]{2,1,0:T(8,128)(2,1)}, u32[]{:S(2)}) copy-start(bf16[384,64,128]{2,1,0:T(8,128)(2,1)} %refs_4_.1) | copy-start | bytes 18874372
  88.2 1.3 copy-start.2
  89.5 14.7 %collective-permute-start.8 = (bf16[64,64,128]{2,1,0:T(8,128)(2,1)}, bf16[64,64,128]{2,1,0:T(8,128)(2,1)}, u32[]{:S(2)}, u32[]{:S(2)}) collective-permute-start(bf16[64,64,128]{2,1,0:T(8,128)(2,1)} %pad_maximum_fusion.refs_0_.refs_4_), channel_id=1, source_target_pairs={{0,1},{1,0},{2,3},{3,2},{4,5},{5,4},{6,7},{7,6},{8,9},{9,8},{10,11... | collective-permute-start | bytes 3145736 | tf_op jit(solution)/shard_map/ppermute | solution.py:386
  90.0 14.0 %collective-permute-start.6 = (bf16[32,64,128]{2,1,0:T(8,128)(2,1)}, bf16[32,64,128]{2,1,0:T(8,128)(2,1)S(1)}, u32[]{:S(2)}, u32[]{:S(2)}) collective-permute-start(bf16[32,64,128]{2,1,0:T(8,128)(2,1)} %collective-permute-done.3), channel_id=1, source_target_pairs={{0,16},{16,0},{1,17},{17,1},{2,18},{18,2},{3,19},{19,3},{4,20},{20... | collective-permute-start | bytes 1572872 | tf_op jit(solution)/shard_map/ppermute | solution.py:382
  104.2 11.0 %collective-permute-start.7 = (bf16[64,64,128]{2,1,0:T(8,128)(2,1)S(1)}, bf16[64,64,128]{2,1,0:T(8,128)(2,1)}, u32[]{:S(2)}, u32[]{:S(2)}) collective-permute-start(bf16[64,64,128]{2,1,0:T(8,128)(2,1)S(1)} %constant_dynamic-update-slice_fusion.refs_0_.refs_8_), channel_id=1, source_target_pairs={{0,1},{1,0},{2,3},{3,2},{4,5},{5,4},{6,7},{7,6},{8,9},{9,8},{10,11... | collective-permute-start | bytes 3145736 | tf_op jit(solution)/shard_map/ppermute | solution.py:386
  104.3 1.6 copy-start.3
  117.6 18.2 %collective-permute-start.10 = (bf16[32,4096]{1,0:T(8,128)(2,1)S(1)}, bf16[32,4096]{1,0:T(8,128)(2,1)S(1)}, u32[]{:S(2)}, u32[]{:S(2)}) collective-permute-start(bf16[32,4096]{1,0:T(8,128)(2,1)S(1)} %get-tuple-element.38), channel_id=1, source_target_pairs={{0,2},{2,0},{4,6},{6,4},{8,10},{10,8},{12,14},{14,12},{1,3},{3,1},... | collective-permute-start | bytes 786440 | tf_op jit(solution)/shard_map/ppermute | solution.py:325
  128.9 9.1 %collective-permute-start.11 = (bf16[32,4096]{1,0:T(8,128)(2,1)S(1)}, bf16[32,4096]{1,0:T(8,128)(2,1)S(1)}, u32[]{:S(2)}, u32[]{:S(2)}) collective-permute-start(bf16[32,4096]{1,0:T(8,128)(2,1)S(1)} %get-tuple-element.39), channel_id=1, source_target_pairs={{0,4},{2,6},{4,0},{6,2},{8,12},{10,14},{12,8},{14,10},{1,5},{3,7},... | collective-permute-start | bytes 786440 | tf_op jit(solution)/shard_map/ppermute | solution.py:325
  128.9 13.8 %collective-permute-start.12 = (bf16[32,4096]{1,0:T(8,128)(2,1)S(1)}, bf16[32,4096]{1,0:T(8,128)(2,1)S(1)}, u32[]{:S(2)}, u32[]{:S(2)}) collective-permute-start(bf16[32,4096]{1,0:T(8,128)(2,1)S(1)} %get-tuple-element.40), channel_id=1, source_target_pairs={{0,6},{2,4},{4,2},{6,0},{8,14},{10,12},{12,10},{14,8},{1,7},{3,5},... | collective-permute-start | bytes 786440 | tf_op jit(solution)/shard_map/ppermute | solution.py:325
  143.6 8.4 %collective-permute-start.13 = (bf16[32,4096]{1,0:T(8,128)(2,1)S(1)}, bf16[32,4096]{1,0:T(8,128)(2,1)S(1)}, u32[]{:S(2)}, u32[]{:S(2)}) collective-permute-start(bf16[32,4096]{1,0:T(8,128)(2,1)S(1)} %shard_map.70.refs_0_), channel_id=1, source_target_pairs={{0,2},{2,0},{4,6},{6,4},{8,10},{10,8},{12,14},{14,12},{1,3},{3,1},... | collective-permute-start | bytes 786440 | tf_op jit(solution)/shard_map/ppermute | solution.py:325
  145.3 9.2 %collective-permute-start.14 = (bf16[32,4096]{1,0:T(8,128)(2,1)S(1)}, bf16[32,4096]{1,0:T(8,128)(2,1)S(1)}, u32[]{:S(2)}, u32[]{:S(2)}) collective-permute-start(bf16[32,4096]{1,0:T(8,128)(2,1)S(1)} %shard_map.70.refs_0_), channel_id=1, source_target_pairs={{0,4},{2,6},{4,0},{6,2},{8,12},{10,14},{12,8},{14,10},{1,5},{3,7},... | collective-permute-start | bytes 786440 | tf_op jit(solution)/shard_map/ppermute | solution.py:325
  145.6 12.8 %collective-permute-start.15 = (bf16[32,4096]{1,0:T(8,128)(2,1)S(1)}, bf16[32,4096]{1,0:T(8,128)(2,1)S(1)}, u32[]{:S(2)}, u32[]{:S(2)}) collective-permute-start(bf16[32,4096]{1,0:T(8,128)(2,1)S(1)} %shard_map.70.refs_0_), channel_id=1, source_target_pairs={{0,6},{2,4},{4,2},{6,0},{8,14},{10,12},{12,10},{14,8},{1,7},{3,5},... | collective-permute-start | bytes 786440 | tf_op jit(solution)/shard_map/ppermute | solution.py:325
  168.1 24.0 %collective-permute-start.16 = (bf16[32,4096]{1,0:T(8,128)(2,1)S(1)}, bf16[32,4096]{1,0:T(8,128)(2,1)S(1)}, u32[]{:S(2)}, u32[]{:S(2)}) collective-permute-start(bf16[32,4096]{1,0:T(8,128)(2,1)S(1)} %get-tuple-element.42), channel_id=1, source_target_pairs={{0,2},{2,0},{4,6},{6,4},{8,10},{10,8},{12,14},{14,12},{1,3},{3,1},... | collective-permute-start | bytes 786440 | tf_op jit(solution)/shard_map/ppermute | solution.py:325
  169.8 24.0 %collective-permute-start.17 = (bf16[32,4096]{1,0:T(8,128)(2,1)S(1)}, bf16[32,4096]{1,0:T(8,128)(2,1)S(1)}, u32[]{:S(2)}, u32[]{:S(2)}) collective-permute-start(bf16[32,4096]{1,0:T(8,128)(2,1)S(1)} %get-tuple-element.43), channel_id=1, source_target_pairs={{0,4},{2,6},{4,0},{6,2},{8,12},{10,14},{12,8},{14,10},{1,5},{3,7},... | collective-permute-start | bytes 786440 | tf_op jit(solution)/shard_map/ppermute | solution.py:325
  169.8 24.1 %collective-permute-start.18 = (bf16[32,4096]{1,0:T(8,128)(2,1)S(1)}, bf16[32,4096]{1,0:T(8,128)(2,1)S(1)}, u32[]{:S(2)}, u32[]{:S(2)}) collective-permute-start(bf16[32,4096]{1,0:T(8,128)(2,1)S(1)} %get-tuple-element.44), channel_id=1, source_target_pairs={{0,6},{2,4},{4,2},{6,0},{8,14},{10,12},{12,10},{14,8},{1,7},{3,5},... | collective-permute-start | bytes 786440 | tf_op jit(solution)/shard_map/ppermute | solution.py:325
  171.7 2.8 %copy-start.1 = (bf16[384,64,128]{2,1,0:T(8,128)(2,1)S(1)}, bf16[384,64,128]{2,1,0:T(8,128)(2,1)}, u32[]{:S(2)}) copy-start(bf16[384,64,128]{2,1,0:T(8,128)(2,1)} %refs_4_.1) | copy-start | bytes 18874372
  180.6 18.6 %collective-permute-start.19 = (bf16[32,4096]{1,0:T(8,128)(2,1)S(1)}, bf16[32,4096]{1,0:T(8,128)(2,1)S(1)}, u32[]{:S(2)}, u32[]{:S(2)}) collective-permute-start(bf16[32,4096]{1,0:T(8,128)(2,1)S(1)} %get-tuple-element.46), channel_id=1, source_target_pairs={{0,2},{2,0},{4,6},{6,4},{8,10},{10,8},{12,14},{14,12},{1,3},{3,1},... | collective-permute-start | bytes 786440 | tf_op jit(solution)/shard_map/ppermute | solution.py:325
  192.0 8.1 %collective-permute-start.20 = (bf16[32,4096]{1,0:T(8,128)(2,1)S(1)}, bf16[32,4096]{1,0:T(8,128)(2,1)S(1)}, u32[]{:S(2)}, u32[]{:S(2)}) collective-permute-start(bf16[32,4096]{1,0:T(8,128)(2,1)S(1)} %get-tuple-element.47), channel_id=1, source_target_pairs={{0,4},{2,6},{4,0},{6,2},{8,12},{10,14},{12,8},{14,10},{1,5},{3,7},... | collective-permute-start | bytes 786440 | tf_op jit(solution)/shard_map/ppermute | solution.py:325
  192.2 10.5 %collective-permute-start.21 = (bf16[32,4096]{1,0:T(8,128)(2,1)S(1)}, bf16[32,4096]{1,0:T(8,128)(2,1)S(1)}, u32[]{:S(2)}, u32[]{:S(2)}) collective-permute-start(bf16[32,4096]{1,0:T(8,128)(2,1)S(1)} %get-tuple-element.48), channel_id=1, source_target_pairs={{0,6},{2,4},{4,2},{6,0},{8,14},{10,12},{12,10},{14,8},{1,7},{3,5},... | collective-permute-start | bytes 786440 | tf_op jit(solution)/shard_map/ppermute | solution.py:325
  200.1 2.5 %copy-start.6 = (bf16[32,32768]{1,0:T(8,128)(2,1)}, bf16[32,32768]{1,0:T(8,128)(2,1)S(1)}, u32[]{:S(2)}) copy-start(bf16[32,32768]{1,0:T(8,128)(2,1)S(1)} %constant_dynamic-update-slice_fusion.5) | copy-start | bytes 6291460
  (2 other events, 1.4 us)

commit v10 on v8

--- a/solution.py
+++ b/solution.py
@@ -9,83 +9,83 @@
 
 TILE = 64
 PAIR = 2 * TILE
-UNROLL = 4
-VMEM_LIMIT = 16 * 1024 * 1024
+GROUP = 4
+UNROLL = 2
+VMEM_LIMIT = 20 * 1024 * 1024
 PARTS = 3
 RANGES = ((0, 2), (2, 3))
-OWN_FORWARD, OWN_BACKWARD, OTHER_FORWARD, OTHER_BACKWARD = range(4)
+OWN, OTHER = range(2)
 BOUNDS = 3
 STEPS = len(RANGES) + 1
-LISTS = BOUNDS + 4 * STEPS
+LISTS = BOUNDS + 2 * STEPS
 
 
 def bits(count):
     return max(1, (count - 1).bit_length())
 
 
-def pair_lists(codes, keys, live, blocks, absent):
+def list_length(tiles, blocks):
+    return tiles + len(RANGES) * ((GROUP - 1) * blocks + GROUP * UNROLL)
+
+
+def group_lists(codes, keys, live, blocks, absent):
     n_lists, tiles = codes.shape
     n_keys = len(RANGES) * blocks
     order = jnp.arange(tiles, dtype=jnp.int32)
     key_range = jnp.arange(n_keys, dtype=jnp.int32)
+    ranges = jnp.arange(STEPS, dtype=jnp.int32)
     mine = (keys[:, None, :] == key_range[None, :, None]) & live[:, None, :]
-    pairs = (jnp.sum(mine, axis=2, dtype=jnp.int32) + 1) // 2
-    lower = key_range[None, :, None] < key_range[None, None, :]
-    starts = jnp.sum(jnp.where(lower, pairs[:, :, None], 0), axis=1, dtype=jnp.int32)
+    groups = (jnp.sum(mine, axis=2, dtype=jnp.int32) + GROUP - 1) // GROUP
+    in_range = key_range[:, None] // blocks == ranges[None, :]
+    totals = jnp.sum(jnp.where(in_range, groups[:, :, None], 0), axis=1, dtype=jnp.int32)
+    totals = (totals + UNROLL - 1) // UNROLL * UNROLL
+    bounds = jnp.sum(
+        jnp.where(ranges[:, None] < ranges[None, :], totals[:, :, None], 0), axis=1, dtype=jnp.int32
+    )
+    lower = (key_range[:, None] < key_range[None, :]) & (
+        key_range[:, None] // blocks == key_range[None, :] // blocks
+    )
+    starts = jnp.sum(jnp.where(lower, groups[:, :, None], 0), axis=1, dtype=jnp.int32)
+    starts += jnp.sum(jnp.where(in_range, bounds[:, None, :], 0), axis=2, dtype=jnp.int32)
     before = (
         (keys[:, :, None] == keys[:, None, :]) & live[:, :, None] & (order[:, None] < order[None, :])
     )
-    entry = jnp.sum(before, axis=1, dtype=jnp.int32) + 2 * jnp.sum(
+    entry = jnp.sum(before, axis=1, dtype=jnp.int32) + GROUP * jnp.sum(
         jnp.where(mine, starts[:, :, None], 0), axis=1, dtype=jnp.int32
     )
     entry = jnp.where(live, entry, -1)
-    found = entry[:, :, None] == jnp.arange(tiles + n_keys, dtype=jnp.int32)
+    found = entry[:, :, None] == jnp.arange(list_length(tiles, blocks), dtype=jnp.int32)
     entries = absent + jnp.sum(
         jnp.where(found, codes[:, :, None] - absent, 0), axis=1, dtype=jnp.int32
     )
-    ends = jnp.arange(STEPS, dtype=jnp.int32) * blocks
-    bounds = jnp.sum(
-        jnp.where(key_range[None, :, None] < ends, pairs[:, :, None], 0), axis=1, dtype=jnp.int32
-    )
     return jnp.concatenate([bounds.reshape(-1), entries.reshape(-1)])
 
 
-def padded_tile(values, half):
-    zero = jnp.zeros_like(values)
-    return jnp.concatenate(
-        [jnp.where(half == 0, values, zero), jnp.where(half == 1, values, zero)], axis=0
-    )
-
-
-def pair_loop(sizes, meta, ref, proj, which, first, last, origin, product, sums):
+def group_loop(sizes, meta, values, proj, which, first, last, origin, product):
     tiles, segments, blocks = sizes
     begin, end = (meta[BOUNDS + STEPS * which + number] for number in (first, last))
-    base = LISTS + which * (tiles + len(RANGES) * blocks)
-
-    def tile(entry, live):
-        code = meta[base + entry]
-        index = jnp.where(live, (code & ((1 << bits(tiles)) - 1)) - origin, 0)
-        code = code >> bits(tiles)
-        segment = code & ((1 << bits(segments)) - 1)
-        code = code >> bits(segments)
-        block = code & ((1 << bits(blocks)) - 1)
-        half = jnp.where(live, (segment & 1) + 2 * (code >> bits(blocks)), 2)
-        points = pl.ds(pl.multiple_of((segment >> 1) * PAIR, PAIR), PAIR)
+    base = LISTS + which * list_length(tiles, blocks)
+
+    def group(number):
+        places = []
+        for entry in range(GROUP):
+            code = meta[base + GROUP * number + entry]
+            index = jnp.maximum((code & ((1 << bits(tiles)) - 1)) - origin, 0)
+            code = code >> bits(tiles)
+            places.append((code & ((1 << bits(segments + 1)) - 1), values[index]))
+            if entry == 0:
+                block = code >> bits(segments + 1)
         lanes = pl.ds(pl.multiple_of(block * proj, proj), proj)
-        return points, lanes, padded_tile(ref[jnp.maximum(index, 0)], half)
-
-    def group(index, carry):
-        terms = []
-        for lane in range(UNROLL):
-            pair = begin + index * UNROLL + lane
-            live = pair < end
-            pair = jnp.minimum(pair, end - 1)
-            terms.append(product(tile(2 * pair, live), tile(2 * pair + 1, live)))
-        for lanes, term in terms:
-            sums[:, lanes] += term
+        return product(lanes, [at for at, tile in places], [tile for at, tile in places])
+
+    def step(index, carry):
+        sums = [group(begin + index * UNROLL + lane) for lane in range(UNROLL)]
+        for additions in sums:
+            for ref, rows, lanes, term in additions:
+                ref[rows, lanes] += term
         return carry
 
-    lax.fori_loop(0, (end - begin + UNROLL - 1) // UNROLL, group, 0)
+    lax.fori_loop(0, (end - begin) // UNROLL, step, 0)
 
 
 def join_pieces(meta, pieces, joined, first):
@@ -101,16 +101,18 @@
     return jnp.concatenate([ref[:, lanes] for ref in refs], axis=0)
 
 
-def store_rows(refs, values):
-    start = 0
-    for ref in refs:
-        rows = ref.shape[0]
-        ref[...] = values[start : start + rows].astype(ref.dtype)
-        start += rows
+def turn_waves(wave, turned, segments):
+    for pair in range(segments // 2):
+        values = wave[:, pair * PAIR : (pair + 1) * PAIR]
+        turned[0, pair] = values
+        turned[1, pair] = pltpu.roll(values.astype(jnp.float32), TILE, 1).astype(values.dtype)
+    for way in range(2):
+        turned[way, segments // 2] = jnp.zeros(turned.shape[2:], turned.dtype)
 
 
 def project_kernel(sizes, n_pieces, spot, first, last, meta, wave, *refs):
     pieces, refs = refs[:n_pieces], refs[n_pieces:]
+    turned, refs = refs[-1], refs[:-1]
     proj = pieces[0].shape[2]
     values = pieces[0]
     if n_pieces > 1:
@@ -118,13 +120,30 @@
         join_pieces(meta, pieces, values, spot[-1])
     total = refs[-1]
     total[...] = jnp.zeros_like(total) if first else refs[0][...]
-
-    def product(one, two):
-        waves = jnp.concatenate([wave[:, one[0]], wave[:, two[0]]], axis=1)
-        tiles = jnp.concatenate([one[2], two[2]], axis=0)
-        return one[1], jnp.dot(waves, tiles, preferred_element_type=jnp.float32)
-
-    pair_loop(sizes, meta, values, proj, *spot, product, total)
+    every = slice(None)
+
+    def product(lanes, segments, tiles):
+        low = lax.broadcasted_iota(jnp.int32, turned.shape[2:], 1) < TILE
+        waves = [
+            jnp.where(
+                low,
+                turned[segments[at] & 1, segments[at] >> 1],
+                turned[1 - (segments[at + 1] & 1), segments[at + 1] >> 1],
+            )
+            for at in range(0, GROUP, 2)
+        ]
+        term = jnp.dot(
+            jnp.concatenate(waves, axis=1),
+            jnp.concatenate(tiles, axis=0),
+            preferred_element_type=jnp.float32,
+        )
+        return [(total, every, lanes, term)]
+
+    @pl.when(meta[1 + spot[0]] > spot[-1])
+    def loop():
+        turn_waves(wave, turned, sizes[1])
+        group_loop(sizes, meta, values, proj, *spot, product)
+
     if last:
         outs = refs[1:-1]
         rows = outs[0].shape[0]
@@ -143,16 +162,32 @@
         join_pieces(meta, pieces, values, 0)
     outs, field = refs[:-1], refs[-1]
     field[...] = jnp.zeros_like(field)
-
-    def product(one, two):
-        rows = jnp.concatenate([rows_of(applied, one[1]), rows_of(applied, two[1])], axis=1)
-        tiles = jnp.concatenate([one[2], two[2]], axis=1)
-        return one[0], lax.dot_general(
-            rows, tiles, (((1,), (1,)), ((), ())), preferred_element_type=jnp.float32
+    every = slice(None)
+
+    def product(lanes, segments, tiles):
+        terms = lax.dot_general(
+            jnp.concatenate(tiles, axis=0),
+            rows_of(applied, lanes),
+            (((1,), (1,)), ((), ())),
+            preferred_element_type=jnp.float32,
         )
-
-    pair_loop(sizes, meta, values, proj, which, 0, len(RANGES), 0, product, field)
-    store_rows(outs, field)
+        return [
+            (
+                field,
+                pl.ds(pl.multiple_of(at * TILE, TILE), TILE),
+                every,
+                terms[number * TILE : (number + 1) * TILE],
+            )
+            for number, at in enumerate(segments)
+        ]
+
+    group_loop(sizes, meta, values, proj, which, 0, len(RANGES), 0, product)
+    for pair in range(sizes[1] // 2):
+        points = slice(pair * PAIR, (pair + 1) * PAIR)
+        values, start = field[points, :].T, 0
+        for out in outs:
+            out[:, points] = values[start : start + out.shape[0]].astype(out.dtype)
+            start += out.shape[0]
 
 
 WHOLE = pl.BlockSpec(memory_space=pltpu.VMEM)
@@ -194,7 +229,8 @@
             in_specs=[WHOLE] * len(operands),
             out_specs=[WHOLE] * outs if last else WHOLE,
             scratch_shapes=([pltpu.VMEM((rows, width), jnp.float32)] if last else [])
-            + joined_shape(pieces),
+            + joined_shape(pieces)
+            + [pltpu.VMEM((2, sizes[1] // 2 + 1, rows, PAIR), jnp.bfloat16)],
         ),
         out_shape=out_shape if last else jax.ShapeDtypeStruct((rows, width), jnp.float32),
         compiler_params=pltpu.CompilerParams(vmem_limit_bytes=VMEM_LIMIT),
@@ -213,7 +249,7 @@
             grid=(1,),
             in_specs=[WHOLE] * (len(applied) + len(pieces)),
             out_specs=[WHOLE] * len(applied),
-            scratch_shapes=[pltpu.VMEM((rows, points), jnp.float32)] + joined_shape(pieces),
+            scratch_shapes=[pltpu.VMEM((points + TILE, rows), jnp.float32)] + joined_shape(pieces),
         ),
         out_shape=[
             jax.ShapeDtypeStruct((block.shape[0], points), jnp.bfloat16) for block in applied
@@ -301,23 +337,23 @@
 
     numbers = jnp.stack([tile_segment, tile_block, jnp.broadcast_to(tile_count, (tiles,))])
     others = lax.ppermute(numbers, "grid", partners)
-    absent = 1 << (bits(tiles) + bits(segments) + bits(blocks))
+    absent = segments << bits(tiles)
     segment, block = (jnp.stack([numbers[i], others[i]]) for i in (0, 1))
-    codes = jnp.stack([slots, held]) + ((segment + (block << bits(segments))) << bits(tiles))
+    codes = jnp.stack([slots, held])
+    codes += (segment + (block << bits(segments + 1))) << bits(tiles)
     live = slots < jnp.stack([numbers[2], others[2]])
-    group_of = sum(jnp.where(part >= first, 1, 0) for first, end in RANGES[1:])
-    keys = jnp.stack([block + blocks * jnp.stack([0 * part, group_of]), segment // 2], axis=1)
-    codes, live = (jnp.stack([values] * 2, axis=1) for values in (codes, live))
+    range_of = sum(jnp.where(part >= first, 1, 0) for first, end in RANGES[1:])
+    keys = block + blocks * jnp.stack([0 * part, range_of])
     meta = jnp.concatenate(
         [
             jnp.stack([place, numbers[2, 0], others[2, 0]]),
-            pair_lists(*(v.reshape(4, tiles) for v in (codes, keys, live)), blocks, absent),
+            group_lists(codes, keys, live, blocks, absent),
         ]
     )
 
     own_wave = to_bricks(side)
     other_wave = to_bricks(1 - side)
-    spot = (OWN_FORWARD, 0, len(RANGES), 0)
+    spot = (OWN, 0, len(RANGES), 0)
     own_total = project(sizes, meta, own_wave, [projectors], half, width, spot, us=10)
     matrix = two_parts(coupling_matrix(coupling))
 
@@ -347,7 +383,7 @@
             pieces[2 * first : 2 * end],
             half,
             width,
-            (OTHER_FORWARD, number, number + 1, first * size),
+            (OTHER, number, number + 1, first * size),
             total,
             last=end == PARTS,
             us=8 if end < PARTS else 0,
@@ -360,8 +396,8 @@
 
     result = jnp.zeros((bands, npts), jnp.bfloat16)
     for which, field in (
-        (1 - side, spread(sizes, meta, applied, pieces, points, OTHER_BACKWARD)),
-        (side, spread(sizes, meta, applied, [projectors], points, OWN_BACKWARD)),
+        (1 - side, spread(sizes, meta, applied, pieces, points, OTHER)),
+        (side, spread(sizes, meta, applied, [projectors], points, OWN)),
     ):
         for d, block in enumerate(exchange(field)):
             start = (which * half + (place ^ d)) * points

time: 198 us -> 198 us (level)
  Pallas kernels: 26.6 us -> 31.1 us
  starting transfers between devices: 50.5 us -> 46.7 us
    ppermute x12, starting transfers between devices: 34 us -> 31.2 us  [exchange(): lax.ppermute(blocks[d], 'grid', [(i, i // half * half + (i % half ^ d)) f...]
    pallas_call x2, Pallas kernels: 11.9 us -> 14.3 us  [spread(): pl.pallas_call(functools.partial(spread_kernel, sizes, len(applied), len(...]
    pallas_call x3, Pallas kernels: 13.7 us -> 15.8 us  [project(): pl.pallas_call(functools.partial(project_kernel, sizes, len(pieces), spot...]
    unnamed x22 -> x18, local copies, waits for them, and re-layouts: 10.9 us -> 10.6 us
  transfers between devices with their start and end apart: 24 -> 24, of which waited for: 13 -> 13; matrix products, arithmetic and copies ran while one was open for 10% -> 10% of each run, Pallas kernels for 7% -> 10%
where the time goes in v10:
time: 198 us; the launch traced here: 199 us
  waiting for transfers between devices  88.9 us (45%)
  starting transfers between devices  46.7 us (24%)
  Pallas kernels  31.1 us (16%)
  local copies, waits for them, and re-layouts  24.6 us (12%)
  other arithmetic  6.05 us (3%)
    ppermute x12, waiting for transfers between devices, exchange(): lax.ppermute(blocks[d], 'grid', [(i, i // half * half + (i % half ^ d)) f...  32.1 us
    ppermute x3, waiting for transfers between devices, body(): across = lax.ppermute(sent, 'groups', swap)  31.9 us
    ppermute x12, starting transfers between devices, exchange(): lax.ppermute(blocks[d], 'grid', [(i, i // half * half + (i % half ^ d)) f...  31.2 us
    ppermute x3, waiting for transfers between devices, body(): mine = lax.ppermute(sent, 'grid', partners)  24.8 us
    pallas_call x3, Pallas kernels, project(): pl.pallas_call(functools.partial(project_kernel, sizes, len(pieces), spot...  15.8 us
    pallas_call x2, Pallas kernels, spread(): pl.pallas_call(functools.partial(spread_kernel, sizes, len(applied), len(...  14.3 us
    unnamed x18, local copies, waits for them, and re-layouts  10.6 us
    all_to_all x2, starting transfers between devices, to_bricks(): lax.all_to_all(part, 'grid', split_axis=1, concat_axis=0, tiled=True, axi...  8.39 us
  transfers between devices with their start and end apart: 24, of which 13 were waited for; matrix products, arithmetic and copies ran while one was open for 10% of the time, Pallas kernels for 10%

profile of v10, /device:TPU:0, one launch (start us, length us, event | category | flops | bytes accessed | tf_op | source)
XLA Modules:
  0.0 198.6 jit_solution(16921062930589101378)
XLA Ops:
  2.3 4.0 %collective-permute-start.1 = (s32[3,384]{1,0:T(4,128)S(1)}, s32[3,384]{1,0:T(4,128)S(1)}, u32[]{:S(2)}, u32[]{:S(2)}) collective-permute-start(s32[3,384]{1,0:T(4,128)S(1)} %add_add_fusion), channel_id=1, source_target_pairs={{0,8},{2,10},{4,12},{6,14},{8,0},{10,2},{12,4},{14,6},{1,9},{3,11}... | collective-permute-start | bytes 13832 | tf_op jit(solution)/shard_map/ppermute | solution.py:339
  6.4 2.5 %constant_dynamic-slice_fusion.1 = (bf16[32,64,128]{2,1,0:T(8,128)(2,1)}, bf16[32,64,128]{2,1,0:T(8,128)(2,1)}, bf16[32,64,128]{2,1,0:T(8,128)(2,1)}) fusion(bf16[384,64,128]{2,1,0:T(8,128)(2,1)} %refs_4_.1, s32[]{:T(128)S(6)} %select_n.265, s32[]{:T(128)S(6)} %select_n.264, s32[]{:T(128)S(6)} %select_n.241), kind=kLoop, calls=%fused_computation.45 | loop fusion | bytes 3145740 | tf_op jit(solution)/shard_map/dynamic_slice | solution.py:363
  11.1 4.1 %all-to-all-start.1 = ((bf16[32,4,4096]{2,0,1:T(8,128)(2,1)}), bf16[32,4,4096]{2,0,1:T(8,128)(2,1)S(1)}, u32[]{:S(2)}, u32[]{:S(2)}) async-start(bf16[32,4,4096]{2,0,1:T(8,128)(2,1)} %bitcast.18), calls=%async_computation.1 | async-start | bytes 2097152 | tf_op jit(solution)/shard_map/all_to_all | solution.py:325
  15.8 1.8 copy.17
  17.7 2.0 select_convert_fusion.high_ref
  23.1 11.8 %collective-permute-done = bf16[32,64,128]{2,1,0:T(8,128)(2,1)} collective-permute-done((bf16[32,64,128]{2,1,0:T(8,128)(2,1)}, bf16[32,64,128]{2,1,0:T(8,128)(2,1)}, u32[]{:S(2)}, u32[]{:S(2)}) %collective-permute-start) | collective-permute-done | bytes 524320 | tf_op jit(solution)/shard_map/ppermute | solution.py:366
  36.3 11.4 %collective-permute-done.4 = bf16[32,64,128]{2,1,0:T(8,128)(2,1)S(1)} collective-permute-done((bf16[32,64,128]{2,1,0:T(8,128)(2,1)}, bf16[32,64,128]{2,1,0:T(8,128)(2,1)S(1)}, u32[]{:S(2)}, u32[]{:S(2)}) %collective-permute-start.4) | collective-permute-done | bytes 524320 | tf_op jit(solution)/shard_map/ppermute | solution.py:372
  47.8 13.0 %collective-permute-done.2 = bf16[32,64,128]{2,1,0:T(8,128)(2,1)S(1)} collective-permute-done((bf16[32,64,128]{2,1,0:T(8,128)(2,1)}, bf16[32,64,128]{2,1,0:T(8,128)(2,1)S(1)}, u32[]{:S(2)}, u32[]{:S(2)}) %collective-permute-start.2) | collective-permute-done | bytes 524320 | tf_op jit(solution)/shard_map/ppermute | solution.py:366
  61.3 2.3 %copy.26 = bf16[4,4,8,4096]{3,2,0,1:T(8,128)(2,1)} copy(bf16[4,4,8,4096]{3,2,1,0:T(8,128)(2,1)} %bitcast.23) | data formatting | bytes 2097152 | tf_op jit(solution)/shard_map/all_to_all | solution.py:325
  64.4 2.1 %pad_maximum_fusion.refs_0_.refs_4_ = bf16[64,64,128]{2,1,0:T(8,128)(2,1)} fusion(bf16[32,64,128]{2,1,0:T(8,128)(2,1)S(1)} %collective-permute-done.4, bf16[32,64,128]{2,1,0:T(8,128)(2,1)} %collective-permute-done), kind=kLoop, calls=%fused_computation.7 | loop fusion | flops 524288 | bytes 2097152 | tf_op jit(solution)/shard_map/concatenate | solution.py:373
  66.5 8.1 %collective-permute-done.5 = bf16[32,64,128]{2,1,0:T(8,128)(2,1)S(1)} collective-permute-done((bf16[32,64,128]{2,1,0:T(8,128)(2,1)S(1)}, bf16[32,64,128]{2,1,0:T(8,128)(2,1)S(1)}, u32[]{:S(2)}, u32[]{:S(2)}) %collective-permute-start.5) | collective-permute-done | bytes 524320 | tf_op jit(solution)/shard_map/ppermute | solution.py:372
  75.5 4.3 %all-to-all-start = ((bf16[32,4,4096]{2,0,1:T(8,128)(2,1)}), bf16[32,4,4096]{2,0,1:T(8,128)(2,1)}, u32[]{:S(2)}, u32[]{:S(2)}) async-start(bf16[32,4,4096]{2,0,1:T(8,128)(2,1)} %bitcast.25), calls=%async_computation | async-start | bytes 2097152 | tf_op jit(solution)/shard_map/all_to_all | solution.py:325
  79.8 2.8 %copy-done = bf16[384,64,128]{2,1,0:T(8,128)(2,1)S(1)} copy-done((bf16[384,64,128]{2,1,0:T(8,128)(2,1)S(1)}, bf16[384,64,128]{2,1,0:T(8,128)(2,1)}, u32[]{:S(2)}) %copy-start) | copy-done | bytes 6291480
  82.5 6.7 %shard_map.67.refs_4_ = f32[128,4096]{1,0:T(8,128)S(1)} custom-call(s32[1193]{0:T(1024)S(1)} %concatenate.24.meta, bf16[128,4096]{1,0:T(8,128)(2,1)S(1)} %bitcast.22, bf16[384,64,128]{2,1,0:T(8,128)(2,1)S(1)} %copy-done), custom_call_target="tpu_custom_call" | custom-call | flops 10000000000 | bytes 1 | tf_op jit(solution)/shard_map/pallas_call | solution.py:222
  92.7 12.4 %collective-permute-done.6 = bf16[32,64,128]{2,1,0:T(8,128)(2,1)S(1)} collective-permute-done((bf16[32,64,128]{2,1,0:T(8,128)(2,1)}, bf16[32,64,128]{2,1,0:T(8,128)(2,1)S(1)}, u32[]{:S(2)}, u32[]{:S(2)}) %collective-permute-start.6) | collective-permute-done | bytes 524320 | tf_op jit(solution)/shard_map/ppermute | solution.py:372
  106.9 6.7 %shard_map.68.refs_2_ = f32[128,4096]{1,0:T(8,128)S(1)} custom-call(s32[1193]{0:T(1024)S(1)} %concatenate.24.meta, bf16[128,4096]{1,0:T(8,128)(2,1)} %bitcast.6.wave, bf16[64,64,128]{2,1,0:T(8,128)(2,1)} %pad_maximum_fusion.refs_0_.refs_4_, bf16[64,64,128]{2,1,0:T(8,128)(2,1)} %collective-permute-done.8.refs_1_.refs_5_, ...), custom_call_target="tpu_custom_call" | custom-call | flops 8000000000 | bytes 1 | tf_op jit(solution)/shard_map/pallas_call | solution.py:222
  113.6 2.4 %shard_map.69 = (bf16[32,4096]{1,0:T(8,128)(2,1)S(1)}, bf16[32,4096]{1,0:T(8,128)(2,1)S(1)}, bf16[32,4096]{1,0:T(8,128)(2,1)S(1)}, bf16[32,4096]{1,0:T(8,128)(2,1)S(1)}) custom-call(s32[1193]{0:T(1024)S(1)} %concatenate.24.meta, bf16[128,4096]{1,0:T(8,128)(2,1)} %bitcast.6.wave, bf16[64,64,128]{2,1,0:T(8,128)(2,1)S(1)} %constant_dynamic-update-slice_fusion.refs_0_.refs_8_, ...), custom_call_target="tpu_custom_call" | custom-call | flops 1 | bytes 1 | tf_op jit(solution)/shard_map/pallas_call | solution.py:222
  116.0 9.3 %collective-permute-start.10 = (bf16[32,4096]{1,0:T(8,128)(2,1)S(1)}, bf16[32,4096]{1,0:T(8,128)(2,1)S(1)}, u32[]{:S(2)}, u32[]{:S(2)}) collective-permute-start(bf16[32,4096]{1,0:T(8,128)(2,1)S(1)} %get-tuple-element.38), channel_id=1, source_target_pairs={{0,2},{2,0},{4,6},{6,4},{8,10},{10,8},{12,14},{14,12},{1,3},{3,1},... | collective-permute-start | bytes 786440 | tf_op jit(solution)/shard_map/ppermute | solution.py:317
  126.9 5.4 %collective-permute-done.10.refs_1_ = bf16[32,4096]{1,0:T(8,128)(2,1)S(1)} collective-permute-done((bf16[32,4096]{1,0:T(8,128)(2,1)S(1)}, bf16[32,4096]{1,0:T(8,128)(2,1)S(1)}, u32[]{:S(2)}, u32[]{:S(2)}) %collective-permute-start.10) | collective-permute-done | bytes 262176 | tf_op jit(solution)/shard_map/ppermute | solution.py:317
  132.3 2.2 %collective-permute-done.11.refs_2_ = bf16[32,4096]{1,0:T(8,128)(2,1)S(1)} collective-permute-done((bf16[32,4096]{1,0:T(8,128)(2,1)S(1)}, bf16[32,4096]{1,0:T(8,128)(2,1)S(1)}, u32[]{:S(2)}, u32[]{:S(2)}) %collective-permute-start.11) | collective-permute-done | bytes 262176 | tf_op jit(solution)/shard_map/ppermute | solution.py:317
  134.5 4.7 %collective-permute-done.12.refs_3_ = bf16[32,4096]{1,0:T(8,128)(2,1)S(1)} collective-permute-done((bf16[32,4096]{1,0:T(8,128)(2,1)S(1)}, bf16[32,4096]{1,0:T(8,128)(2,1)S(1)}, u32[]{:S(2)}, u32[]{:S(2)}) %collective-permute-start.12) | collective-permute-done | bytes 262176 | tf_op jit(solution)/shard_map/ppermute | solution.py:317
  140.1 1.7 collective-permute-start.13
  143.6 4.8 %collective-permute-done.13.refs_1_ = bf16[32,4096]{1,0:T(8,128)(2,1)S(1)} collective-permute-done((bf16[32,4096]{1,0:T(8,128)(2,1)S(1)}, bf16[32,4096]{1,0:T(8,128)(2,1)S(1)}, u32[]{:S(2)}, u32[]{:S(2)}) %collective-permute-start.13) | collective-permute-done | bytes 262176 | tf_op jit(solution)/shard_map/ppermute | solution.py:317
  148.5 2.6 %collective-permute-done.14.refs_2_ = bf16[32,4096]{1,0:T(8,128)(2,1)S(1)} collective-permute-done((bf16[32,4096]{1,0:T(8,128)(2,1)S(1)}, bf16[32,4096]{1,0:T(8,128)(2,1)S(1)}, u32[]{:S(2)}, u32[]{:S(2)}) %collective-permute-start.14) | collective-permute-done | bytes 262176 | tf_op jit(solution)/shard_map/ppermute | solution.py:317
  151.0 3.8 %collective-permute-done.15.refs_3_ = bf16[32,4096]{1,0:T(8,128)(2,1)S(1)} collective-permute-done((bf16[32,4096]{1,0:T(8,128)(2,1)S(1)}, bf16[32,4096]{1,0:T(8,128)(2,1)S(1)}, u32[]{:S(2)}, u32[]{:S(2)}) %collective-permute-start.15) | collective-permute-done | bytes 262176 | tf_op jit(solution)/shard_map/ppermute | solution.py:317
  154.8 7.1 %shard_map.71 = (bf16[32,4096]{1,0:T(8,128)(2,1)S(1)}, bf16[32,4096]{1,0:T(8,128)(2,1)S(1)}, bf16[32,4096]{1,0:T(8,128)(2,1)S(1)}, bf16[32,4096]{1,0:T(8,128)(2,1)S(1)}) custom-call(s32[1193]{0:T(1024)S(1)} %concatenate.24.meta, bf16[32,4096]{1,0:T(8,128)(2,1)S(1)} %shard_map.70.refs_0_, bf16[32,4096]{1,0:T(8,128)(2,1)S(1)} %collective-permute-done.13.refs_1_, ...), custom_call_target="tpu_custom_call" | custom-call | flops 1 | bytes 1 | tf_op jit(solution)/shard_map/pallas_call | solution.py:245
  161.9 11.7 %collective-permute-start.16 = (bf16[32,4096]{1,0:T(8,128)(2,1)S(1)}, bf16[32,4096]{1,0:T(8,128)(2,1)S(1)}, u32[]{:S(2)}, u32[]{:S(2)}) collective-permute-start(bf16[32,4096]{1,0:T(8,128)(2,1)S(1)} %get-tuple-element.42), channel_id=1, source_target_pairs={{0,2},{2,0},{4,6},{6,4},{8,10},{10,8},{12,14},{14,12},{1,3},{3,1},... | collective-permute-start | bytes 786440 | tf_op jit(solution)/shard_map/ppermute | solution.py:317
  175.1 2.8 %copy-done.1 = bf16[384,64,128]{2,1,0:T(8,128)(2,1)S(1)} copy-done((bf16[384,64,128]{2,1,0:T(8,128)(2,1)S(1)}, bf16[384,64,128]{2,1,0:T(8,128)(2,1)}, u32[]{:S(2)}) %copy-start.1) | copy-done | bytes 6291480
  177.9 7.2 %shard_map.72 = (bf16[32,4096]{1,0:T(8,128)(2,1)S(1)}, bf16[32,4096]{1,0:T(8,128)(2,1)S(1)}, bf16[32,4096]{1,0:T(8,128)(2,1)S(1)}, bf16[32,4096]{1,0:T(8,128)(2,1)S(1)}) custom-call(s32[1193]{0:T(1024)S(1)} %concatenate.24.meta, bf16[32,4096]{1,0:T(8,128)(2,1)S(1)} %shard_map.70.refs_0_, bf16[32,4096]{1,0:T(8,128)(2,1)S(1)} %collective-permute-done.13.refs_1_, ...), custom_call_target="tpu_custom_call" | custom-call | flops 1 | bytes 1 | tf_op jit(solution)/shard_map/pallas_call | solution.py:245
  186.3 2.7 %collective-permute-start.21 = (bf16[32,4096]{1,0:T(8,128)(2,1)S(1)}, bf16[32,4096]{1,0:T(8,128)(2,1)S(1)}, u32[]{:S(2)}, u32[]{:S(2)}) collective-permute-start(bf16[32,4096]{1,0:T(8,128)(2,1)S(1)} %get-tuple-element.48), channel_id=1, source_target_pairs={{0,6},{2,4},{4,2},{6,0},{8,14},{10,12},{12,10},{14,8},{1,7},{3,5},... | collective-permute-start | bytes 786440 | tf_op jit(solution)/shard_map/ppermute | solution.py:317
  189.1 5.3 %collective-permute-done.19 = bf16[32,4096]{1,0:T(8,128)(2,1)S(1)} collective-permute-done((bf16[32,4096]{1,0:T(8,128)(2,1)S(1)}, bf16[32,4096]{1,0:T(8,128)(2,1)S(1)}, u32[]{:S(2)}, u32[]{:S(2)}) %collective-permute-start.19) | collective-permute-done | bytes 262176 | tf_op jit(solution)/shard_map/ppermute | solution.py:317
  194.5 3.3 %collective-permute-done.21 = bf16[32,4096]{1,0:T(8,128)(2,1)S(1)} collective-permute-done((bf16[32,4096]{1,0:T(8,128)(2,1)S(1)}, bf16[32,4096]{1,0:T(8,128)(2,1)S(1)}, u32[]{:S(2)}, u32[]{:S(2)}) %collective-permute-start.21) | collective-permute-done | bytes 262176 | tf_op jit(solution)/shard_map/ppermute | solution.py:317
  (95 shorter events, 24.2 us)
Async XLA Ops:
  0.0 8.9 %copy-start.5 = (bf16[32,32768]{1,0:T(8,128)(2,1)S(1)}, bf16[32,32768]{1,0:T(8,128)(2,1)}, u32[]{:S(2)}) copy-start(bf16[32,32768]{1,0:T(8,128)(2,1)} %param.6) | copy-start | bytes 6291460
  2.3 17.9 %collective-permute-start.1 = (s32[3,384]{1,0:T(4,128)S(1)}, s32[3,384]{1,0:T(4,128)S(1)}, u32[]{:S(2)}, u32[]{:S(2)}) collective-permute-start(s32[3,384]{1,0:T(4,128)S(1)} %add_add_fusion), channel_id=1, source_target_pairs={{0,8},{2,10},{4,12},{6,14},{8,0},{10,2},{12,4},{14,6},{1,9},{3,11}... | collective-permute-start | bytes 13832 | tf_op jit(solution)/shard_map/ppermute | solution.py:339
  8.9 25.9 %collective-permute-start = (bf16[32,64,128]{2,1,0:T(8,128)(2,1)}, bf16[32,64,128]{2,1,0:T(8,128)(2,1)}, u32[]{:S(2)}, u32[]{:S(2)}) collective-permute-start(bf16[32,64,128]{2,1,0:T(8,128)(2,1)} %get-tuple-element.51), channel_id=1, source_target_pairs={{0,8},{2,10},{4,12},{6,14},{8,0},{10,2},{12,4},{14,6},{1,9},{3,11}... | collective-permute-start | bytes 1572872 | tf_op jit(solution)/shard_map/ppermute | solution.py:366
  10.1 5.4 %copy-start.7 = (f32[32,16,8,8]{0,3,2,1:T(8,128)S(1)}, f32[32,16,8,8]{0,3,2,1:T(8,128)}, u32[]{:S(2)}) copy-start(f32[32,16,8,8]{0,3,2,1:T(8,128)} %param.11) | copy-start | bytes 393220
  11.1 64.3 %all-to-all-start.1 = ((bf16[32,4,4096]{2,0,1:T(8,128)(2,1)}), bf16[32,4,4096]{2,0,1:T(8,128)(2,1)S(1)}, u32[]{:S(2)}, u32[]{:S(2)}) async-start(bf16[32,4,4096]{2,0,1:T(8,128)(2,1)} %bitcast.18), calls=%async_computation.1 | async-start | bytes 2097152 | tf_op jit(solution)/shard_map/all_to_all | solution.py:325
  17.6 2.2 %copy-start.4 = (f32[32,128,128]{2,1,0:T(8,128)S(1)}, f32[32,128,128]{2,1,0:T(8,128)}, u32[]{:S(2)}) copy-start(f32[32,128,128]{2,1,0:T(8,128)} %copy.17) | copy-start | bytes 6291460
  34.8 12.9 %collective-permute-start.4 = (bf16[32,64,128]{2,1,0:T(8,128)(2,1)}, bf16[32,64,128]{2,1,0:T(8,128)(2,1)S(1)}, u32[]{:S(2)}, u32[]{:S(2)}) collective-permute-start(bf16[32,64,128]{2,1,0:T(8,128)(2,1)} %collective-permute-done), channel_id=1, source_target_pairs={{0,16},{16,0},{1,17},{17,1},{2,18},{18,2},{3,19},{19,3},{4,20},{20... | collective-permute-start | bytes 1572872 | tf_op jit(solution)/shard_map/ppermute | solution.py:372
  36.3 24.4 %collective-permute-start.2 = (bf16[32,64,128]{2,1,0:T(8,128)(2,1)}, bf16[32,64,128]{2,1,0:T(8,128)(2,1)S(1)}, u32[]{:S(2)}, u32[]{:S(2)}) collective-permute-start(bf16[32,64,128]{2,1,0:T(8,128)(2,1)} %get-tuple-element.30), channel_id=1, source_target_pairs={{0,8},{2,10},{4,12},{6,14},{8,0},{10,2},{12,4},{14,6},{1,9},{3,11}... | collective-permute-start | bytes 1572872 | tf_op jit(solution)/shard_map/ppermute | solution.py:366
  60.8 13.8 %collective-permute-start.5 = (bf16[32,64,128]{2,1,0:T(8,128)(2,1)S(1)}, bf16[32,64,128]{2,1,0:T(8,128)(2,1)S(1)}, u32[]{:S(2)}, u32[]{:S(2)}) collective-permute-start(bf16[32,64,128]{2,1,0:T(8,128)(2,1)S(1)} %collective-permute-done.2), channel_id=1, source_target_pairs={{0,16},{16,0},{1,17},{17,1},{2,18},{18,2},{3,19},{19,3},{4,20},{20... | collective-permute-start | bytes 1572872 | tf_op jit(solution)/shard_map/ppermute | solution.py:372
  63.6 27.5 %collective-permute-start.3 = (bf16[32,64,128]{2,1,0:T(8,128)(2,1)}, bf16[32,64,128]{2,1,0:T(8,128)(2,1)}, u32[]{:S(2)}, u32[]{:S(2)}) collective-permute-start(bf16[32,64,128]{2,1,0:T(8,128)(2,1)} %get-tuple-element.31), channel_id=1, source_target_pairs={{0,8},{2,10},{4,12},{6,14},{8,0},{10,2},{12,4},{14,6},{1,9},{3,11}... | collective-permute-start | bytes 1572872 | tf_op jit(solution)/shard_map/ppermute | solution.py:366
  75.4 29.8 %collective-permute-start.9 = (bf16[64,64,128]{2,1,0:T(8,128)(2,1)}, bf16[64,64,128]{2,1,0:T(8,128)(2,1)}, u32[]{:S(2)}, u32[]{:S(2)}) collective-permute-start(bf16[64,64,128]{2,1,0:T(8,128)(2,1)} %constant_dynamic-update-slice_fusion.2.refs_2_.refs_6_), channel_id=1, source_target_pairs={{0,1},{1,0},{2,3},{3,2},{4,5},{5,4},{6,7},{7,6},{8,9},{9,8},{10,11... | collective-permute-start | bytes 3145736 | tf_op jit(solution)/shard_map/ppermute | solution.py:376
  75.5 29.8 %all-to-all-start = ((bf16[32,4,4096]{2,0,1:T(8,128)(2,1)}), bf16[32,4,4096]{2,0,1:T(8,128)(2,1)}, u32[]{:S(2)}, u32[]{:S(2)}) async-start(bf16[32,4,4096]{2,0,1:T(8,128)(2,1)} %bitcast.25), calls=%async_computation | async-start | bytes 2097152 | tf_op jit(solution)/shard_map/all_to_all | solution.py:325
  79.7 2.8 %copy-start = (bf16[384,64,128]{2,1,0:T(8,128)(2,1)S(1)}, bf16[384,64,128]{2,1,0:T(8,128)(2,1)}, u32[]{:S(2)}) copy-start(bf16[384,64,128]{2,1,0:T(8,128)(2,1)} %refs_4_.1) | copy-start | bytes 18874372
  89.2 1.3 copy-start.2
  90.6 14.7 %collective-permute-start.8 = (bf16[64,64,128]{2,1,0:T(8,128)(2,1)}, bf16[64,64,128]{2,1,0:T(8,128)(2,1)}, u32[]{:S(2)}, u32[]{:S(2)}) collective-permute-start(bf16[64,64,128]{2,1,0:T(8,128)(2,1)} %pad_maximum_fusion.refs_0_.refs_4_), channel_id=1, source_target_pairs={{0,1},{1,0},{2,3},{3,2},{4,5},{5,4},{6,7},{7,6},{8,9},{9,8},{10,11... | collective-permute-start | bytes 3145736 | tf_op jit(solution)/shard_map/ppermute | solution.py:376
  91.1 14.0 %collective-permute-start.6 = (bf16[32,64,128]{2,1,0:T(8,128)(2,1)}, bf16[32,64,128]{2,1,0:T(8,128)(2,1)S(1)}, u32[]{:S(2)}, u32[]{:S(2)}) collective-permute-start(bf16[32,64,128]{2,1,0:T(8,128)(2,1)} %collective-permute-done.3), channel_id=1, source_target_pairs={{0,16},{16,0},{1,17},{17,1},{2,18},{18,2},{3,19},{19,3},{4,20},{20... | collective-permute-start | bytes 1572872 | tf_op jit(solution)/shard_map/ppermute | solution.py:372
  105.2 8.5 %collective-permute-start.7 = (bf16[64,64,128]{2,1,0:T(8,128)(2,1)S(1)}, bf16[64,64,128]{2,1,0:T(8,128)(2,1)}, u32[]{:S(2)}, u32[]{:S(2)}) collective-permute-start(bf16[64,64,128]{2,1,0:T(8,128)(2,1)S(1)} %constant_dynamic-update-slice_fusion.refs_0_.refs_8_), channel_id=1, source_target_pairs={{0,1},{1,0},{2,3},{3,2},{4,5},{5,4},{6,7},{7,6},{8,9},{9,8},{10,11... | collective-permute-start | bytes 3145736 | tf_op jit(solution)/shard_map/ppermute | solution.py:376
  105.3 1.6 copy-start.3
  116.0 16.3 %collective-permute-start.10 = (bf16[32,4096]{1,0:T(8,128)(2,1)S(1)}, bf16[32,4096]{1,0:T(8,128)(2,1)S(1)}, u32[]{:S(2)}, u32[]{:S(2)}) collective-permute-start(bf16[32,4096]{1,0:T(8,128)(2,1)S(1)} %get-tuple-element.38), channel_id=1, source_target_pairs={{0,2},{2,0},{4,6},{6,4},{8,10},{10,8},{12,14},{14,12},{1,3},{3,1},... | collective-permute-start | bytes 786440 | tf_op jit(solution)/shard_map/ppermute | solution.py:317
  125.4 9.1 %collective-permute-start.11 = (bf16[32,4096]{1,0:T(8,128)(2,1)S(1)}, bf16[32,4096]{1,0:T(8,128)(2,1)S(1)}, u32[]{:S(2)}, u32[]{:S(2)}) collective-permute-start(bf16[32,4096]{1,0:T(8,128)(2,1)S(1)} %get-tuple-element.39), channel_id=1, source_target_pairs={{0,4},{2,6},{4,0},{6,2},{8,12},{10,14},{12,8},{14,10},{1,5},{3,7},... | collective-permute-start | bytes 786440 | tf_op jit(solution)/shard_map/ppermute | solution.py:317
  125.4 13.8 %collective-permute-start.12 = (bf16[32,4096]{1,0:T(8,128)(2,1)S(1)}, bf16[32,4096]{1,0:T(8,128)(2,1)S(1)}, u32[]{:S(2)}, u32[]{:S(2)}) collective-permute-start(bf16[32,4096]{1,0:T(8,128)(2,1)S(1)} %get-tuple-element.40), channel_id=1, source_target_pairs={{0,6},{2,4},{4,2},{6,0},{8,14},{10,12},{12,10},{14,8},{1,7},{3,5},... | collective-permute-start | bytes 786440 | tf_op jit(solution)/shard_map/ppermute | solution.py:317
  140.1 8.4 %collective-permute-start.13 = (bf16[32,4096]{1,0:T(8,128)(2,1)S(1)}, bf16[32,4096]{1,0:T(8,128)(2,1)S(1)}, u32[]{:S(2)}, u32[]{:S(2)}) collective-permute-start(bf16[32,4096]{1,0:T(8,128)(2,1)S(1)} %shard_map.70.refs_0_), channel_id=1, source_target_pairs={{0,2},{2,0},{4,6},{6,4},{8,10},{10,8},{12,14},{14,12},{1,3},{3,1},... | collective-permute-start | bytes 786440 | tf_op jit(solution)/shard_map/ppermute | solution.py:317
  141.8 9.2 %collective-permute-start.14 = (bf16[32,4096]{1,0:T(8,128)(2,1)S(1)}, bf16[32,4096]{1,0:T(8,128)(2,1)S(1)}, u32[]{:S(2)}, u32[]{:S(2)}) collective-permute-start(bf16[32,4096]{1,0:T(8,128)(2,1)S(1)} %shard_map.70.refs_0_), channel_id=1, source_target_pairs={{0,4},{2,6},{4,0},{6,2},{8,12},{10,14},{12,8},{14,10},{1,5},{3,7},... | collective-permute-start | bytes 786440 | tf_op jit(solution)/shard_map/ppermute | solution.py:317
  142.1 12.8 %collective-permute-start.15 = (bf16[32,4096]{1,0:T(8,128)(2,1)S(1)}, bf16[32,4096]{1,0:T(8,128)(2,1)S(1)}, u32[]{:S(2)}, u32[]{:S(2)}) collective-permute-start(bf16[32,4096]{1,0:T(8,128)(2,1)S(1)} %shard_map.70.refs_0_), channel_id=1, source_target_pairs={{0,6},{2,4},{4,2},{6,0},{8,14},{10,12},{12,10},{14,8},{1,7},{3,5},... | collective-permute-start | bytes 786440 | tf_op jit(solution)/shard_map/ppermute | solution.py:317
  161.9 24.4 %collective-permute-start.16 = (bf16[32,4096]{1,0:T(8,128)(2,1)S(1)}, bf16[32,4096]{1,0:T(8,128)(2,1)S(1)}, u32[]{:S(2)}, u32[]{:S(2)}) collective-permute-start(bf16[32,4096]{1,0:T(8,128)(2,1)S(1)} %get-tuple-element.42), channel_id=1, source_target_pairs={{0,2},{2,0},{4,6},{6,4},{8,10},{10,8},{12,14},{14,12},{1,3},{3,1},... | collective-permute-start | bytes 786440 | tf_op jit(solution)/shard_map/ppermute | solution.py:317
  173.6 15.4 %collective-permute-start.17 = (bf16[32,4096]{1,0:T(8,128)(2,1)S(1)}, bf16[32,4096]{1,0:T(8,128)(2,1)S(1)}, u32[]{:S(2)}, u32[]{:S(2)}) collective-permute-start(bf16[32,4096]{1,0:T(8,128)(2,1)S(1)} %get-tuple-element.43), channel_id=1, source_target_pairs={{0,4},{2,6},{4,0},{6,2},{8,12},{10,14},{12,8},{14,10},{1,5},{3,7},... | collective-permute-start | bytes 786440 | tf_op jit(solution)/shard_map/ppermute | solution.py:317
  173.6 15.4 %collective-permute-start.18 = (bf16[32,4096]{1,0:T(8,128)(2,1)S(1)}, bf16[32,4096]{1,0:T(8,128)(2,1)S(1)}, u32[]{:S(2)}, u32[]{:S(2)}) collective-permute-start(bf16[32,4096]{1,0:T(8,128)(2,1)S(1)} %get-tuple-element.44), channel_id=1, source_target_pairs={{0,6},{2,4},{4,2},{6,0},{8,14},{10,12},{12,10},{14,8},{1,7},{3,5},... | collective-permute-start | bytes 786440 | tf_op jit(solution)/shard_map/ppermute | solution.py:317
  175.1 2.8 %copy-start.1 = (bf16[384,64,128]{2,1,0:T(8,128)(2,1)S(1)}, bf16[384,64,128]{2,1,0:T(8,128)(2,1)}, u32[]{:S(2)}) copy-start(bf16[384,64,128]{2,1,0:T(8,128)(2,1)} %refs_4_.1) | copy-start | bytes 18874372
  185.2 9.2 %collective-permute-start.19 = (bf16[32,4096]{1,0:T(8,128)(2,1)S(1)}, bf16[32,4096]{1,0:T(8,128)(2,1)S(1)}, u32[]{:S(2)}, u32[]{:S(2)}) collective-permute-start(bf16[32,4096]{1,0:T(8,128)(2,1)S(1)} %get-tuple-element.46), channel_id=1, source_target_pairs={{0,2},{2,0},{4,6},{6,4},{8,10},{10,8},{12,14},{14,12},{1,3},{3,1},... | collective-permute-start | bytes 786440 | tf_op jit(solution)/shard_map/ppermute | solution.py:317
  185.3 9.2 %collective-permute-start.20 = (bf16[32,4096]{1,0:T(8,128)(2,1)S(1)}, bf16[32,4096]{1,0:T(8,128)(2,1)S(1)}, u32[]{:S(2)}, u32[]{:S(2)}) collective-permute-start(bf16[32,4096]{1,0:T(8,128)(2,1)S(1)} %get-tuple-element.47), channel_id=1, source_target_pairs={{0,4},{2,6},{4,0},{6,2},{8,12},{10,14},{12,8},{14,10},{1,5},{3,7},... | collective-permute-start | bytes 786440 | tf_op jit(solution)/shard_map/ppermute | solution.py:317
  186.3 11.6 %collective-permute-start.21 = (bf16[32,4096]{1,0:T(8,128)(2,1)S(1)}, bf16[32,4096]{1,0:T(8,128)(2,1)S(1)}, u32[]{:S(2)}, u32[]{:S(2)}) collective-permute-start(bf16[32,4096]{1,0:T(8,128)(2,1)S(1)} %get-tuple-element.48), channel_id=1, source_target_pairs={{0,6},{2,4},{4,2},{6,0},{8,14},{10,12},{12,10},{14,8},{1,7},{3,5},... | collective-permute-start | bytes 786440 | tf_op jit(solution)/shard_map/ppermute | solution.py:317
  194.5 3.4 %copy-start.6 = (bf16[32,32768]{1,0:T(8,128)(2,1)}, bf16[32,32768]{1,0:T(8,128)(2,1)S(1)}, u32[]{:S(2)}) copy-start(bf16[32,32768]{1,0:T(8,128)(2,1)S(1)} %constant_dynamic-update-slice_fusion.5) | copy-start | bytes 6291460

commit v11 on v10

--- a/solution.py
+++ b/solution.py
@@ -10,9 +10,9 @@
 TILE = 64
 PAIR = 2 * TILE
 GROUP = 4
-UNROLL = 2
-VMEM_LIMIT = 20 * 1024 * 1024
-PARTS = 3
+UNROLL = 4
+VMEM_LIMIT = 14 * 1024 * 1024
+PARTS = (3, 5, 4)
 RANGES = ((0, 2), (2, 3))
 OWN, OTHER = range(2)
 BOUNDS = 3
@@ -89,12 +89,13 @@
 
 
 def join_pieces(meta, pieces, joined, first):
-    size = pieces[0].shape[0]
+    end = 0
     for number, ref in enumerate(pieces):
-
-        @pl.when(meta[2] > first + number // 2 * 2 * size)
-        def copy(number=number, ref=ref):
-            joined[number * size : (number + 1) * size] = ref[...]
+        start, end = end, end + ref.shape[0]
+
+        @pl.when(meta[2] > first + (start if number % 2 == 0 else start - ref.shape[0]))
+        def copy(start=start, end=end, ref=ref):
+            joined[start:end] = ref[...]
 
 
 def rows_of(refs, lanes):
@@ -208,8 +209,8 @@
 def joined_shape(pieces):
     if len(pieces) == 1:
         return []
-    shape = pieces[0].shape
-    return [pltpu.VMEM((len(pieces) * shape[0],) + shape[1:], jnp.bfloat16)]
+    count = sum(piece.shape[0] for piece in pieces)
+    return [pltpu.VMEM((count,) + pieces[0].shape[1:], jnp.bfloat16)]
 
 
 def project(sizes, meta, wave, pieces, count, width, spot, total=None, last=False, us=0):
@@ -328,12 +329,16 @@
 
     segments, blocks = points // TILE, coupling.shape[0]
     sizes = (tiles, segments, blocks)
-    size = tiles // PARTS
-    share = size // 4
     slots = jnp.arange(tiles, dtype=jnp.int32)
-    part, quarter = slots // size, slots % size // share
-    held = part * size + slots % share
-    held += share * ((quarter // 2 ^ group) + 2 * (quarter % 2 ^ core))
+    starts = [tiles * sum(PARTS[:number]) // sum(PARTS) for number in range(len(PARTS) + 1)]
+    held, range_of = slots, 0
+    for start, end in zip(starts, starts[1:]):
+        share = (end - start) // 4
+        quarter, rest = (slots - start) // share, (slots - start) % share
+        at = start + rest + share * ((quarter // 2 ^ group) + 2 * (quarter % 2 ^ core))
+        held = jnp.where((slots >= start) & (slots < end), at, held)
+    for first, end in RANGES[1:]:
+        range_of += jnp.where(slots >= starts[first], 1, 0)
 
     numbers = jnp.stack([tile_segment, tile_block, jnp.broadcast_to(tile_count, (tiles,))])
     others = lax.ppermute(numbers, "grid", partners)
@@ -342,8 +347,7 @@
     codes = jnp.stack([slots, held])
     codes += (segment + (block << bits(segments + 1))) << bits(tiles)
     live = slots < jnp.stack([numbers[2], others[2]])
-    range_of = sum(jnp.where(part >= first, 1, 0) for first, end in RANGES[1:])
-    keys = block + blocks * jnp.stack([0 * part, range_of])
+    keys = block + blocks * jnp.stack([jnp.zeros_like(slots), range_of])
     meta = jnp.concatenate(
         [
             jnp.stack([place, numbers[2, 0], others[2, 0]]),
@@ -353,26 +357,30 @@
 
     own_wave = to_bricks(side)
     other_wave = to_bricks(1 - side)
+    matrix = two_parts(coupling_matrix(coupling))
+
+    arrived, pieces, across = [], [], None
+    source = projectors
+    for number, (start, end) in enumerate(zip(starts, starts[1:])):
+        share = (end - start) // 4
+        start += (2 * group + core) * share
+        sent = lax.dynamic_slice_in_dim(source, start, share, 0)
+        if number == 0:
+            sent, source = lax.optimization_barrier((sent, source))
+        if number > 1:
+            sent = lax.optimization_barrier((sent, arrived[number - 2]))[0]
+        arrived.append(lax.ppermute(sent, "grid", partners))
+    own_wave, late = lax.optimization_barrier((own_wave, arrived[-1]))
     spot = (OWN, 0, len(RANGES), 0)
-    own_total = project(sizes, meta, own_wave, [projectors], half, width, spot, us=10)
-    matrix = two_parts(coupling_matrix(coupling))
-
-    pieces, mine, across = [], None, None
-    for part in range(PARTS):
-        start = part * size + (2 * group + core) * share
-        sent = lax.dynamic_slice_in_dim(projectors, start, share, 0)
-        if part > 0:
-            sent = lax.optimization_barrier((sent, mine))[0]
-        mine = lax.ppermute(sent, "grid", partners)
+    total = project(sizes, meta, own_wave, [projectors], half, width, spot, us=10)
+    for number, mine in enumerate(arrived):
         sent = mine
-        if part == 0:
-            sent, matrix, meta = lax.optimization_barrier((sent, matrix, meta))
-        else:
-            sent = lax.optimization_barrier((sent, across))[0]
+        if number == 1:
+            sent, across, matrix, meta = lax.optimization_barrier((sent, across, matrix, meta))
+        if number > 1:
+            sent, across = lax.optimization_barrier((sent, across))
         across = lax.ppermute(sent, "groups", swap)
         both = jnp.concatenate([mine, across])
-        if part == 0:
-            both, total = lax.optimization_barrier((both, own_total))
         pieces += [both, lax.ppermute(both, "band", swap)]
 
     for number, (first, end) in enumerate(RANGES):
@@ -383,10 +391,10 @@
             pieces[2 * first : 2 * end],
             half,
             width,
-            (OTHER, number, number + 1, first * size),
+            (OTHER, number, number + 1, starts[first]),
             total,
-            last=end == PARTS,
-            us=8 if end < PARTS else 0,
+            last=end == len(PARTS),
+            us=8 if end < len(PARTS) else 0,
         )
     if len(total) < half:
         total = [lax.dynamic_slice_in_dim(total[0], (place ^ d) * bands, bands, 0) for d in range(half)]

time: 198 us -> 199 us (level); the launches traced: 199 us -> 197 us
  local copies, waits for them, and re-layouts: 24.6 us -> 35.3 us
  Pallas kernels: 31.1 us -> 24.2 us
  starting transfers between devices: 46.7 us -> 40.9 us
  waiting for transfers between devices: 88.9 us -> 91.9 us
  other arithmetic: 6.05 us -> 3.93 us
    ppermute x3, waiting for transfers between devices: 24.8 us -> 54.8 us  [body(): arrived.append(lax.ppermute(sent, 'grid', partners))]
    ppermute x3, waiting for transfers between devices: 31.9 us -> 4.82 us  [body(): across = lax.ppermute(sent, 'groups', swap)]
    ppermute x12, starting transfers between devices: 31.2 us -> 21.7 us  [exchange(): lax.ppermute(blocks[d], 'grid', [(i, i // half * half + (i % half ^ d)) f...]
    pallas_call x2, Pallas kernels: 14.3 us -> 10.7 us  [spread(): pl.pallas_call(functools.partial(spread_kernel, sizes, len(applied), len(...]
    pallas_call x3, Pallas kernels: 15.8 us -> 12.5 us  [project(): pl.pallas_call(functools.partial(project_kernel, sizes, len(pieces), spot...]
    unnamed x18 -> x27, local copies, waits for them, and re-layouts: 10.6 us -> 13.6 us
    concatenate x2 -> x3, local copies, waits for them, and re-layouts: 0.9 us -> 3.86 us  [body(): both = jnp.concatenate([mine, across])]
    ppermute x3, starting transfers between devices: 0.03 us -> 3 us  [body(): arrived.append(lax.ppermute(sent, 'grid', partners))]
  transfers between devices with their start and end apart: 24 -> 24, of which waited for: 13 -> 13; matrix products, arithmetic and copies ran while one was open for 10% -> 14% of each run, Pallas kernels for 10% -> 7%
where the time goes in v11:
time: 199 us; the launch traced here: 197 us
  waiting for transfers between devices  91.9 us (46%)
  starting transfers between devices  40.9 us (21%)
  local copies, waits for them, and re-layouts  35.3 us (18%)
  Pallas kernels  24.2 us (12%)
  other arithmetic  3.93 us (2%)
    ppermute x3, waiting for transfers between devices, body(): arrived.append(lax.ppermute(sent, 'grid', partners))  54.8 us
    ppermute x12, waiting for transfers between devices, exchange(): lax.ppermute(blocks[d], 'grid', [(i, i // half * half + (i % half ^ d)) f...  32.3 us
    ppermute x12, starting transfers between devices, exchange(): lax.ppermute(blocks[d], 'grid', [(i, i // half * half + (i % half ^ d)) f...  21.7 us
    unnamed x27, local copies, waits for them, and re-layouts  13.6 us
    pallas_call x3, Pallas kernels, project(): pl.pallas_call(functools.partial(project_kernel, sizes, len(pieces), spot...  12.5 us
    pallas_call x2, Pallas kernels, spread(): pl.pallas_call(functools.partial(spread_kernel, sizes, len(applied), len(...  10.7 us
    all_to_all x2, starting transfers between devices, to_bricks(): lax.all_to_all(part, 'grid', split_axis=1, concat_axis=0, tiled=True, axi...  8.04 us
    dynamic_slice x3, local copies, waits for them, and re-layouts, body(): sent = lax.dynamic_slice_in_dim(source, start, share, 0)  4.82 us
  transfers between devices with their start and end apart: 24, of which 13 were waited for; matrix products, arithmetic and copies ran while one was open for 14% of the time, Pallas kernels for 7%

profile of v11, /device:TPU:0, one launch (start us, length us, event | category | flops | bytes accessed | tf_op | source)
XLA Modules:
  0.0 197.3 jit_solution(14372935273049326295)
XLA Ops:
  2.3 4.0 %collective-permute-start.3 = (s32[3,384]{1,0:T(4,128)S(1)}, s32[3,384]{1,0:T(4,128)S(1)}, u32[]{:S(2)}, u32[]{:S(2)}) collective-permute-start(s32[3,384]{1,0:T(4,128)S(1)} %add_add_fusion), channel_id=1, source_target_pairs={{0,8},{2,10},{4,12},{6,14},{8,0},{10,2},{12,4},{14,6},{1,9},{3,11}... | collective-permute-start | bytes 13832 | tf_op jit(solution)/shard_map/ppermute | solution.py:344
  6.4 1.8 constant_dynamic-slice_fusion.4
  8.1 2.0 %constant_dynamic-slice_fusion.3 = bf16[40,64,128]{2,1,0:T(8,128)(2,1)} fusion(bf16[384,64,128]{2,1,0:T(8,128)(2,1)} %refs_4_.1, s32[]{:T(128)S(6)} %select_n.349), kind=kLoop, calls=%fused_computation.62 | loop fusion | bytes 1310724 | tf_op jit(solution)/shard_map/dynamic_slice | solution.py:367
  10.1 2.9 %collective-permute-start.1 = (bf16[24,64,128]{2,1,0:T(8,128)(2,1)}, bf16[24,64,128]{2,1,0:T(8,128)(2,1)}, u32[]{:S(2)}, u32[]{:S(2)}) collective-permute-start(bf16[24,64,128]{2,1,0:T(8,128)(2,1)} %constant_dynamic-slice_fusion.4), channel_id=1, source_target_pairs={{0,8},{2,10},{4,12},{6,14},{8,0},{10,2},{12,4},{14,6},{1,9},{3,11}... | collective-permute-start | bytes 1179656 | tf_op jit(solution)/shard_map/ppermute | solution.py:372
  15.2 3.8 %all-to-all-start.1 = ((bf16[32,4,4096]{2,0,1:T(8,128)(2,1)}), bf16[32,4,4096]{2,0,1:T(8,128)(2,1)S(1)}, u32[]{:S(2)}, u32[]{:S(2)}) async-start(bf16[32,4,4096]{2,0,1:T(8,128)(2,1)} %bitcast.18), calls=%async_computation.1 | async-start | bytes 2097152 | tf_op jit(solution)/shard_map/all_to_all | solution.py:326
  19.6 1.8 copy.17
  21.5 2.0 %select_convert_fusion.high_ref = bf16[32,128,128]{2,1,0:T(8,128)(2,1)S(1)} fusion(f32[32,128,128]{2,1,0:T(8,128)} %copy.17, pred[128,128]{1,0:T(8,128)(4,1)S(1)} %broadcast_compare_fusion), kind=kLoop, calls=%fused_computation.1 | loop fusion | flops 524288 | bytes 3162112 | tf_op jit(solution)/shard_map/convert_element_type | solution.py:265
  25.2 33.2 %collective-permute-done.1 = bf16[24,64,128]{2,1,0:T(8,128)(2,1)} collective-permute-done((bf16[24,64,128]{2,1,0:T(8,128)(2,1)}, bf16[24,64,128]{2,1,0:T(8,128)(2,1)}, u32[]{:S(2)}, u32[]{:S(2)}) %collective-permute-start.1) | collective-permute-done | bytes 393248 | tf_op jit(solution)/shard_map/ppermute | solution.py:372
  64.1 4.5 %collective-permute-done.2 = bf16[24,64,128]{2,1,0:T(8,128)(2,1)S(1)} collective-permute-done((bf16[24,64,128]{2,1,0:T(8,128)(2,1)}, bf16[24,64,128]{2,1,0:T(8,128)(2,1)S(1)}, u32[]{:S(2)}, u32[]{:S(2)}) %collective-permute-start.2) | collective-permute-done | bytes 393248 | tf_op jit(solution)/shard_map/ppermute | solution.py:382
  71.2 2.3 %copy.26 = bf16[4,4,8,4096]{3,2,0,1:T(8,128)(2,1)} copy(bf16[4,4,8,4096]{3,2,1,0:T(8,128)(2,1)} %bitcast.23) | data formatting | bytes 2097152 | tf_op jit(solution)/shard_map/all_to_all | solution.py:326
  73.5 21.5 %collective-permute-done.4 = bf16[32,64,128]{2,1,0:T(8,128)(2,1)} collective-permute-done((bf16[32,64,128]{2,1,0:T(8,128)(2,1)S(1)}, bf16[32,64,128]{2,1,0:T(8,128)(2,1)}, u32[]{:S(2)}, u32[]{:S(2)}) %collective-permute-start.4) | collective-permute-done | bytes 524320 | tf_op jit(solution)/shard_map/ppermute | solution.py:372
  95.6 4.2 %all-to-all-start = ((bf16[32,4,4096]{2,0,1:T(8,128)(2,1)}), bf16[32,4,4096]{2,0,1:T(8,128)(2,1)}, u32[]{:S(2)}, u32[]{:S(2)}) async-start(bf16[32,4,4096]{2,0,1:T(8,128)(2,1)} %bitcast.25), calls=%async_computation | async-start | bytes 2097152 | tf_op jit(solution)/shard_map/all_to_all | solution.py:326
  99.8 2.0 %constant_dynamic-update-slice_fusion.5 = bf16[80,64,128]{2,1,0:T(8,128)(2,1)} fusion(bf16[40,64,128]{2,1,0:T(8,128)(2,1)} %collective-permute-done), kind=kLoop, calls=%fused_computation.22 | loop fusion | bytes 1310720
  101.8 2.0 constant_dynamic-update-slice_fusion.4.refs_2_.refs_6_
  103.8 1.9 constant_dynamic-update-slice_fusion.3
  109.5 2.8 %copy-done = bf16[384,64,128]{2,1,0:T(8,128)(2,1)S(1)} copy-done((bf16[384,64,128]{2,1,0:T(8,128)(2,1)S(1)}, bf16[384,64,128]{2,1,0:T(8,128)(2,1)}, u32[]{:S(2)}) %copy-start) | copy-done | bytes 6291480
  112.3 3.1 %shard_map.67.refs_4_ = f32[128,4096]{1,0:T(8,128)S(1)} custom-call(s32[1225]{0:T(1024)S(1)} %concatenate.24.meta, bf16[128,4096]{1,0:T(8,128)(2,1)S(1)} %bitcast.22, bf16[384,64,128]{2,1,0:T(8,128)(2,1)S(1)} %copy-done), custom_call_target="tpu_custom_call" | custom-call | flops 10000000000 | bytes 1 | tf_op jit(solution)/shard_map/pallas_call | solution.py:223
  118.3 7.1 %shard_map.68.refs_2_ = f32[128,4096]{1,0:T(8,128)S(1)} custom-call(s32[1225]{0:T(1024)S(1)} %concatenate.24.meta, bf16[128,4096]{1,0:T(8,128)(2,1)} %bitcast.6.wave, bf16[48,64,128]{2,1,0:T(8,128)(2,1)} %constant_dynamic-update-slice_fusion.2.refs_0_.refs_4_, bf16[48,64,128]{2,1,0:T(8,128)(2,1)} %collective-permute-done.8.refs_1_.refs_5_, ...), custom_call_target="tpu_custom_call" | custom-call | flops 8000000000 | bytes 1 | tf_op jit(solution)/shard_map/pallas_call | solution.py:223
  125.4 2.4 %shard_map.69 = (bf16[32,4096]{1,0:T(8,128)(2,1)S(1)}, bf16[32,4096]{1,0:T(8,128)(2,1)S(1)}, bf16[32,4096]{1,0:T(8,128)(2,1)S(1)}, bf16[32,4096]{1,0:T(8,128)(2,1)S(1)}) custom-call(s32[1225]{0:T(1024)S(1)} %concatenate.24.meta, bf16[128,4096]{1,0:T(8,128)(2,1)} %bitcast.6.wave, bf16[64,64,128]{2,1,0:T(8,128)(2,1)S(1)} %constant_dynamic-update-slice_fusion.refs_0_.refs_8_, ...), custom_call_target="tpu_custom_call" | custom-call | flops 1 | bytes 1 | tf_op jit(solution)/shard_map/pallas_call | solution.py:223
  127.8 5.6 %collective-permute-start.10 = (bf16[32,4096]{1,0:T(8,128)(2,1)S(1)}, bf16[32,4096]{1,0:T(8,128)(2,1)S(1)}, u32[]{:S(2)}, u32[]{:S(2)}) collective-permute-start(bf16[32,4096]{1,0:T(8,128)(2,1)S(1)} %get-tuple-element.36), channel_id=1, source_target_pairs={{0,2},{2,0},{4,6},{6,4},{8,10},{10,8},{12,14},{14,12},{1,3},{3,1},... | collective-permute-start | bytes 786440 | tf_op jit(solution)/shard_map/ppermute | solution.py:318
  135.0 5.4 %collective-permute-done.10.refs_1_ = bf16[32,4096]{1,0:T(8,128)(2,1)S(1)} collective-permute-done((bf16[32,4096]{1,0:T(8,128)(2,1)S(1)}, bf16[32,4096]{1,0:T(8,128)(2,1)S(1)}, u32[]{:S(2)}, u32[]{:S(2)}) %collective-permute-start.10) | collective-permute-done | bytes 262176 | tf_op jit(solution)/shard_map/ppermute | solution.py:318
  140.4 2.2 %collective-permute-done.11.refs_2_ = bf16[32,4096]{1,0:T(8,128)(2,1)S(1)} collective-permute-done((bf16[32,4096]{1,0:T(8,128)(2,1)S(1)}, bf16[32,4096]{1,0:T(8,128)(2,1)S(1)}, u32[]{:S(2)}, u32[]{:S(2)}) %collective-permute-start.11) | collective-permute-done | bytes 262176 | tf_op jit(solution)/shard_map/ppermute | solution.py:318
  142.6 4.7 %collective-permute-done.12.refs_3_ = bf16[32,4096]{1,0:T(8,128)(2,1)S(1)} collective-permute-done((bf16[32,4096]{1,0:T(8,128)(2,1)S(1)}, bf16[32,4096]{1,0:T(8,128)(2,1)S(1)}, u32[]{:S(2)}, u32[]{:S(2)}) %collective-permute-start.12) | collective-permute-done | bytes 262176 | tf_op jit(solution)/shard_map/ppermute | solution.py:318
  151.7 4.8 %collective-permute-done.13.refs_1_ = bf16[32,4096]{1,0:T(8,128)(2,1)S(1)} collective-permute-done((bf16[32,4096]{1,0:T(8,128)(2,1)S(1)}, bf16[32,4096]{1,0:T(8,128)(2,1)S(1)}, u32[]{:S(2)}, u32[]{:S(2)}) %collective-permute-start.13) | collective-permute-done | bytes 262176 | tf_op jit(solution)/shard_map/ppermute | solution.py:318
  156.6 2.6 %collective-permute-done.14.refs_2_ = bf16[32,4096]{1,0:T(8,128)(2,1)S(1)} collective-permute-done((bf16[32,4096]{1,0:T(8,128)(2,1)S(1)}, bf16[32,4096]{1,0:T(8,128)(2,1)S(1)}, u32[]{:S(2)}, u32[]{:S(2)}) %collective-permute-start.14) | collective-permute-done | bytes 262176 | tf_op jit(solution)/shard_map/ppermute | solution.py:318
  159.2 3.8 %collective-permute-done.15.refs_3_ = bf16[32,4096]{1,0:T(8,128)(2,1)S(1)} collective-permute-done((bf16[32,4096]{1,0:T(8,128)(2,1)S(1)}, bf16[32,4096]{1,0:T(8,128)(2,1)S(1)}, u32[]{:S(2)}, u32[]{:S(2)}) %collective-permute-start.15) | collective-permute-done | bytes 262176 | tf_op jit(solution)/shard_map/ppermute | solution.py:318
  162.9 7.4 %shard_map.71 = (bf16[32,4096]{1,0:T(8,128)(2,1)S(1)}, bf16[32,4096]{1,0:T(8,128)(2,1)S(1)}, bf16[32,4096]{1,0:T(8,128)(2,1)S(1)}, bf16[32,4096]{1,0:T(8,128)(2,1)S(1)}) custom-call(s32[1225]{0:T(1024)S(1)} %concatenate.24.meta, bf16[32,4096]{1,0:T(8,128)(2,1)S(1)} %shard_map.70.refs_0_, bf16[32,4096]{1,0:T(8,128)(2,1)S(1)} %collective-permute-done.13.refs_1_, ...), custom_call_target="tpu_custom_call" | custom-call | flops 1 | bytes 1 | tf_op jit(solution)/shard_map/pallas_call | solution.py:246
  173.9 2.8 %copy-done.1 = bf16[384,64,128]{2,1,0:T(8,128)(2,1)S(1)} copy-done((bf16[384,64,128]{2,1,0:T(8,128)(2,1)S(1)}, bf16[384,64,128]{2,1,0:T(8,128)(2,1)}, u32[]{:S(2)}) %copy-start.1) | copy-done | bytes 6291480
  176.7 3.3 %shard_map.72 = (bf16[32,4096]{1,0:T(8,128)(2,1)S(1)}, bf16[32,4096]{1,0:T(8,128)(2,1)S(1)}, bf16[32,4096]{1,0:T(8,128)(2,1)S(1)}, bf16[32,4096]{1,0:T(8,128)(2,1)S(1)}) custom-call(s32[1225]{0:T(1024)S(1)} %concatenate.24.meta, bf16[32,4096]{1,0:T(8,128)(2,1)S(1)} %shard_map.70.refs_0_, bf16[32,4096]{1,0:T(8,128)(2,1)S(1)} %collective-permute-done.13.refs_1_, ...), custom_call_target="tpu_custom_call" | custom-call | flops 1 | bytes 1 | tf_op jit(solution)/shard_map/pallas_call | solution.py:246
  180.0 5.8 %collective-permute-start.19 = (bf16[32,4096]{1,0:T(8,128)(2,1)S(1)}, bf16[32,4096]{1,0:T(8,128)(2,1)S(1)}, u32[]{:S(2)}, u32[]{:S(2)}) collective-permute-start(bf16[32,4096]{1,0:T(8,128)(2,1)S(1)} %get-tuple-element.44), channel_id=1, source_target_pairs={{0,2},{2,0},{4,6},{6,4},{8,10},{10,8},{12,14},{14,12},{1,3},{3,1},... | collective-permute-start | bytes 786440 | tf_op jit(solution)/shard_map/ppermute | solution.py:318
  187.7 5.2 %collective-permute-done.19 = bf16[32,4096]{1,0:T(8,128)(2,1)S(1)} collective-permute-done((bf16[32,4096]{1,0:T(8,128)(2,1)S(1)}, bf16[32,4096]{1,0:T(8,128)(2,1)S(1)}, u32[]{:S(2)}, u32[]{:S(2)}) %collective-permute-start.19) | collective-permute-done | bytes 262176 | tf_op jit(solution)/shard_map/ppermute | solution.py:318
  194.1 2.5 %collective-permute-done.21 = bf16[32,4096]{1,0:T(8,128)(2,1)S(1)} collective-permute-done((bf16[32,4096]{1,0:T(8,128)(2,1)S(1)}, bf16[32,4096]{1,0:T(8,128)(2,1)S(1)}, u32[]{:S(2)}, u32[]{:S(2)}) %collective-permute-start.21) | collective-permute-done | bytes 262176 | tf_op jit(solution)/shard_map/ppermute | solution.py:318
  (106 shorter events, 34.7 us)
Async XLA Ops:
  0.0 13.0 %copy-start.7 = (bf16[32,32768]{1,0:T(8,128)(2,1)S(1)}, bf16[32,32768]{1,0:T(8,128)(2,1)}, u32[]{:S(2)}) copy-start(bf16[32,32768]{1,0:T(8,128)(2,1)} %param.6) | copy-start | bytes 6291460
  2.3 21.7 %collective-permute-start.3 = (s32[3,384]{1,0:T(4,128)S(1)}, s32[3,384]{1,0:T(4,128)S(1)}, u32[]{:S(2)}, u32[]{:S(2)}) collective-permute-start(s32[3,384]{1,0:T(4,128)S(1)} %add_add_fusion), channel_id=1, source_target_pairs={{0,8},{2,10},{4,12},{6,14},{8,0},{10,2},{12,4},{14,6},{1,9},{3,11}... | collective-permute-start | bytes 13832 | tf_op jit(solution)/shard_map/ppermute | solution.py:344
  10.1 54.0 %collective-permute-start = (bf16[40,64,128]{2,1,0:T(8,128)(2,1)}, bf16[40,64,128]{2,1,0:T(8,128)(2,1)}, u32[]{:S(2)}, u32[]{:S(2)}) collective-permute-start(bf16[40,64,128]{2,1,0:T(8,128)(2,1)} %constant_dynamic-slice_fusion.3), channel_id=1, source_target_pairs={{0,8},{2,10},{4,12},{6,14},{8,0},{10,2},{12,4},{14,6},{1,9},{3,11}... | collective-permute-start | bytes 1966088 | tf_op jit(solution)/shard_map/ppermute | solution.py:372
  10.1 48.3 %collective-permute-start.1 = (bf16[24,64,128]{2,1,0:T(8,128)(2,1)}, bf16[24,64,128]{2,1,0:T(8,128)(2,1)}, u32[]{:S(2)}, u32[]{:S(2)}) collective-permute-start(bf16[24,64,128]{2,1,0:T(8,128)(2,1)} %constant_dynamic-slice_fusion.4), channel_id=1, source_target_pairs={{0,8},{2,10},{4,12},{6,14},{8,0},{10,2},{12,4},{14,6},{1,9},{3,11}... | collective-permute-start | bytes 1179656 | tf_op jit(solution)/shard_map/ppermute | solution.py:372
  14.1 5.1 %copy-start.9 = (f32[32,16,8,8]{0,3,2,1:T(8,128)S(1)}, f32[32,16,8,8]{0,3,2,1:T(8,128)}, u32[]{:S(2)}) copy-start(f32[32,16,8,8]{0,3,2,1:T(8,128)} %param.11) | copy-start | bytes 393220
  15.2 80.4 %all-to-all-start.1 = ((bf16[32,4,4096]{2,0,1:T(8,128)(2,1)}), bf16[32,4,4096]{2,0,1:T(8,128)(2,1)S(1)}, u32[]{:S(2)}, u32[]{:S(2)}) async-start(bf16[32,4,4096]{2,0,1:T(8,128)(2,1)} %bitcast.18), calls=%async_computation.1 | async-start | bytes 2097152 | tf_op jit(solution)/shard_map/all_to_all | solution.py:326
  21.4 2.2 %copy-start.6 = (f32[32,128,128]{2,1,0:T(8,128)S(1)}, f32[32,128,128]{2,1,0:T(8,128)}, u32[]{:S(2)}) copy-start(f32[32,128,128]{2,1,0:T(8,128)} %copy.17) | copy-start | bytes 6291460
  58.4 10.2 %collective-permute-start.2 = (bf16[24,64,128]{2,1,0:T(8,128)(2,1)}, bf16[24,64,128]{2,1,0:T(8,128)(2,1)S(1)}, u32[]{:S(2)}, u32[]{:S(2)}) collective-permute-start(bf16[24,64,128]{2,1,0:T(8,128)(2,1)} %collective-permute-done.1), channel_id=1, source_target_pairs={{0,16},{16,0},{1,17},{17,1},{2,18},{18,2},{3,19},{19,3},{4,20},{20... | collective-permute-start | bytes 1179656 | tf_op jit(solution)/shard_map/ppermute | solution.py:382
  68.6 26.5 %collective-permute-start.5 = (bf16[40,64,128]{2,1,0:T(8,128)(2,1)}, bf16[40,64,128]{2,1,0:T(8,128)(2,1)}, u32[]{:S(2)}, u32[]{:S(2)}) collective-permute-start(bf16[40,64,128]{2,1,0:T(8,128)(2,1)} %collective-permute-done), channel_id=1, source_target_pairs={{0,16},{16,0},{1,17},{17,1},{2,18},{18,2},{3,19},{19,3},{4,20},{20... | collective-permute-start | bytes 1966088 | tf_op jit(solution)/shard_map/ppermute | solution.py:382
  71.2 23.9 %collective-permute-start.4 = (bf16[32,64,128]{2,1,0:T(8,128)(2,1)S(1)}, bf16[32,64,128]{2,1,0:T(8,128)(2,1)}, u32[]{:S(2)}, u32[]{:S(2)}) collective-permute-start(bf16[32,64,128]{2,1,0:T(8,128)(2,1)S(1)} %constant_dynamic-slice_fusion.1), channel_id=1, source_target_pairs={{0,8},{2,10},{4,12},{6,14},{8,0},{10,2},{12,4},{14,6},{1,9},{3,11}... | collective-permute-start | bytes 1572872 | tf_op jit(solution)/shard_map/ppermute | solution.py:372
  95.0 13.3 %collective-permute-start.6 = (bf16[32,64,128]{2,1,0:T(8,128)(2,1)}, bf16[32,64,128]{2,1,0:T(8,128)(2,1)}, u32[]{:S(2)}, u32[]{:S(2)}) collective-permute-start(bf16[32,64,128]{2,1,0:T(8,128)(2,1)} %collective-permute-done.4), channel_id=1, source_target_pairs={{0,16},{16,0},{1,17},{17,1},{2,18},{18,2},{3,19},{19,3},{4,20},{20... | collective-permute-start | bytes 1572872 | tf_op jit(solution)/shard_map/ppermute | solution.py:382
  95.6 8.2 %copy-start.2 = (bf16[32,4,4096]{2,0,1:T(8,128)(2,1)}, bf16[32,4,4096]{2,0,1:T(8,128)(2,1)S(1)}, u32[]{:S(2)}) copy-start(bf16[32,4,4096]{2,0,1:T(8,128)(2,1)S(1)} %all-to-all-done.1) | copy-start | bytes 3145732
  95.6 21.1 %all-to-all-start = ((bf16[32,4,4096]{2,0,1:T(8,128)(2,1)}), bf16[32,4,4096]{2,0,1:T(8,128)(2,1)}, u32[]{:S(2)}, u32[]{:S(2)}) async-start(bf16[32,4,4096]{2,0,1:T(8,128)(2,1)} %bitcast.25), calls=%async_computation | async-start | bytes 2097152 | tf_op jit(solution)/shard_map/all_to_all | solution.py:326
  103.8 12.9 %collective-permute-start.9 = (bf16[80,64,128]{2,1,0:T(8,128)(2,1)}, bf16[80,64,128]{2,1,0:T(8,128)(2,1)}, u32[]{:S(2)}, u32[]{:S(2)}) collective-permute-start(bf16[80,64,128]{2,1,0:T(8,128)(2,1)} %constant_dynamic-update-slice_fusion.4.refs_2_.refs_6_), channel_id=1, source_target_pairs={{0,1},{1,0},{2,3},{3,2},{4,5},{5,4},{6,7},{7,6},{8,9},{9,8},{10,11... | collective-permute-start | bytes 3932168 | tf_op jit(solution)/shard_map/ppermute | solution.py:384
  103.8 5.7 %copy-start.3 = (bf16[32,4,4096]{2,0,1:T(8,128)(2,1)S(1)}, bf16[32,4,4096]{2,0,1:T(8,128)(2,1)}, u32[]{:S(2)}) copy-start(bf16[32,4,4096]{2,0,1:T(8,128)(2,1)} %copy-done.2) | copy-start | bytes 3145732
  106.4 10.3 %collective-permute-start.8 = (bf16[48,64,128]{2,1,0:T(8,128)(2,1)}, bf16[48,64,128]{2,1,0:T(8,128)(2,1)}, u32[]{:S(2)}, u32[]{:S(2)}) collective-permute-start(bf16[48,64,128]{2,1,0:T(8,128)(2,1)} %constant_dynamic-update-slice_fusion.2.refs_0_.refs_4_), channel_id=1, source_target_pairs={{0,1},{1,0},{2,3},{3,2},{4,5},{5,4},{6,7},{7,6},{8,9},{9,8},{10,11... | collective-permute-start | bytes 2359304 | tf_op jit(solution)/shard_map/ppermute | solution.py:384
  109.4 16.0 %collective-permute-start.7 = (bf16[64,64,128]{2,1,0:T(8,128)(2,1)S(1)}, bf16[64,64,128]{2,1,0:T(8,128)(2,1)}, u32[]{:S(2)}, u32[]{:S(2)}) collective-permute-start(bf16[64,64,128]{2,1,0:T(8,128)(2,1)S(1)} %constant_dynamic-update-slice_fusion.refs_0_.refs_8_), channel_id=1, source_target_pairs={{0,1},{1,0},{2,3},{3,2},{4,5},{5,4},{6,7},{7,6},{8,9},{9,8},{10,11... | collective-permute-start | bytes 3145736 | tf_op jit(solution)/shard_map/ppermute | solution.py:384
  109.5 2.8 %copy-start = (bf16[384,64,128]{2,1,0:T(8,128)(2,1)S(1)}, bf16[384,64,128]{2,1,0:T(8,128)(2,1)}, u32[]{:S(2)}) copy-start(bf16[384,64,128]{2,1,0:T(8,128)(2,1)} %refs_4_.1) | copy-start | bytes 18874372
  127.8 12.6 %collective-permute-start.10 = (bf16[32,4096]{1,0:T(8,128)(2,1)S(1)}, bf16[32,4096]{1,0:T(8,128)(2,1)S(1)}, u32[]{:S(2)}, u32[]{:S(2)}) collective-permute-start(bf16[32,4096]{1,0:T(8,128)(2,1)S(1)} %get-tuple-element.36), channel_id=1, source_target_pairs={{0,2},{2,0},{4,6},{6,4},{8,10},{10,8},{12,14},{14,12},{1,3},{3,1},... | collective-permute-start | bytes 786440 | tf_op jit(solution)/shard_map/ppermute | solution.py:318
  133.5 9.1 %collective-permute-start.11 = (bf16[32,4096]{1,0:T(8,128)(2,1)S(1)}, bf16[32,4096]{1,0:T(8,128)(2,1)S(1)}, u32[]{:S(2)}, u32[]{:S(2)}) collective-permute-start(bf16[32,4096]{1,0:T(8,128)(2,1)S(1)} %get-tuple-element.37), channel_id=1, source_target_pairs={{0,4},{2,6},{4,0},{6,2},{8,12},{10,14},{12,8},{14,10},{1,5},{3,7},... | collective-permute-start | bytes 786440 | tf_op jit(solution)/shard_map/ppermute | solution.py:318
  133.5 13.8 %collective-permute-start.12 = (bf16[32,4096]{1,0:T(8,128)(2,1)S(1)}, bf16[32,4096]{1,0:T(8,128)(2,1)S(1)}, u32[]{:S(2)}, u32[]{:S(2)}) collective-permute-start(bf16[32,4096]{1,0:T(8,128)(2,1)S(1)} %get-tuple-element.38), channel_id=1, source_target_pairs={{0,6},{2,4},{4,2},{6,0},{8,14},{10,12},{12,10},{14,8},{1,7},{3,5},... | collective-permute-start | bytes 786440 | tf_op jit(solution)/shard_map/ppermute | solution.py:318
  148.2 8.4 %collective-permute-start.13 = (bf16[32,4096]{1,0:T(8,128)(2,1)S(1)}, bf16[32,4096]{1,0:T(8,128)(2,1)S(1)}, u32[]{:S(2)}, u32[]{:S(2)}) collective-permute-start(bf16[32,4096]{1,0:T(8,128)(2,1)S(1)} %shard_map.70.refs_0_), channel_id=1, source_target_pairs={{0,2},{2,0},{4,6},{6,4},{8,10},{10,8},{12,14},{14,12},{1,3},{3,1},... | collective-permute-start | bytes 786440 | tf_op jit(solution)/shard_map/ppermute | solution.py:318
  149.9 9.2 %collective-permute-start.14 = (bf16[32,4096]{1,0:T(8,128)(2,1)S(1)}, bf16[32,4096]{1,0:T(8,128)(2,1)S(1)}, u32[]{:S(2)}, u32[]{:S(2)}) collective-permute-start(bf16[32,4096]{1,0:T(8,128)(2,1)S(1)} %shard_map.70.refs_0_), channel_id=1, source_target_pairs={{0,4},{2,6},{4,0},{6,2},{8,12},{10,14},{12,8},{14,10},{1,5},{3,7},... | collective-permute-start | bytes 786440 | tf_op jit(solution)/shard_map/ppermute | solution.py:318
  150.2 12.8 %collective-permute-start.15 = (bf16[32,4096]{1,0:T(8,128)(2,1)S(1)}, bf16[32,4096]{1,0:T(8,128)(2,1)S(1)}, u32[]{:S(2)}, u32[]{:S(2)}) collective-permute-start(bf16[32,4096]{1,0:T(8,128)(2,1)S(1)} %shard_map.70.refs_0_), channel_id=1, source_target_pairs={{0,6},{2,4},{4,2},{6,0},{8,14},{10,12},{12,10},{14,8},{1,7},{3,5},... | collective-permute-start | bytes 786440 | tf_op jit(solution)/shard_map/ppermute | solution.py:318
  170.3 15.7 %collective-permute-start.16 = (bf16[32,4096]{1,0:T(8,128)(2,1)S(1)}, bf16[32,4096]{1,0:T(8,128)(2,1)S(1)}, u32[]{:S(2)}, u32[]{:S(2)}) collective-permute-start(bf16[32,4096]{1,0:T(8,128)(2,1)S(1)} %get-tuple-element.40), channel_id=1, source_target_pairs={{0,2},{2,0},{4,6},{6,4},{8,10},{10,8},{12,14},{14,12},{1,3},{3,1},... | collective-permute-start | bytes 786440 | tf_op jit(solution)/shard_map/ppermute | solution.py:318
  171.0 16.6 %collective-permute-start.17 = (bf16[32,4096]{1,0:T(8,128)(2,1)S(1)}, bf16[32,4096]{1,0:T(8,128)(2,1)S(1)}, u32[]{:S(2)}, u32[]{:S(2)}) collective-permute-start(bf16[32,4096]{1,0:T(8,128)(2,1)S(1)} %get-tuple-element.41), channel_id=1, source_target_pairs={{0,4},{2,6},{4,0},{6,2},{8,12},{10,14},{12,8},{14,10},{1,5},{3,7},... | collective-permute-start | bytes 786440 | tf_op jit(solution)/shard_map/ppermute | solution.py:318
  172.4 15.2 %collective-permute-start.18 = (bf16[32,4096]{1,0:T(8,128)(2,1)S(1)}, bf16[32,4096]{1,0:T(8,128)(2,1)S(1)}, u32[]{:S(2)}, u32[]{:S(2)}) collective-permute-start(bf16[32,4096]{1,0:T(8,128)(2,1)S(1)} %get-tuple-element.42), channel_id=1, source_target_pairs={{0,6},{2,4},{4,2},{6,0},{8,14},{10,12},{12,10},{14,8},{1,7},{3,5},... | collective-permute-start | bytes 786440 | tf_op jit(solution)/shard_map/ppermute | solution.py:318
  173.9 2.8 %copy-start.1 = (bf16[384,64,128]{2,1,0:T(8,128)(2,1)S(1)}, bf16[384,64,128]{2,1,0:T(8,128)(2,1)}, u32[]{:S(2)}) copy-start(bf16[384,64,128]{2,1,0:T(8,128)(2,1)} %refs_4_.1) | copy-start | bytes 18874372
  180.0 13.0 %collective-permute-start.19 = (bf16[32,4096]{1,0:T(8,128)(2,1)S(1)}, bf16[32,4096]{1,0:T(8,128)(2,1)S(1)}, u32[]{:S(2)}, u32[]{:S(2)}) collective-permute-start(bf16[32,4096]{1,0:T(8,128)(2,1)S(1)} %get-tuple-element.44), channel_id=1, source_target_pairs={{0,2},{2,0},{4,6},{6,4},{8,10},{10,8},{12,14},{14,12},{1,3},{3,1},... | collective-permute-start | bytes 786440 | tf_op jit(solution)/shard_map/ppermute | solution.py:318
  185.8 8.2 %collective-permute-start.20 = (bf16[32,4096]{1,0:T(8,128)(2,1)S(1)}, bf16[32,4096]{1,0:T(8,128)(2,1)S(1)}, u32[]{:S(2)}, u32[]{:S(2)}) collective-permute-start(bf16[32,4096]{1,0:T(8,128)(2,1)S(1)} %get-tuple-element.45), channel_id=1, source_target_pairs={{0,4},{2,6},{4,0},{6,2},{8,12},{10,14},{12,8},{14,10},{1,5},{3,7},... | collective-permute-start | bytes 786440 | tf_op jit(solution)/shard_map/ppermute | solution.py:318
  186.0 10.6 %collective-permute-start.21 = (bf16[32,4096]{1,0:T(8,128)(2,1)S(1)}, bf16[32,4096]{1,0:T(8,128)(2,1)S(1)}, u32[]{:S(2)}, u32[]{:S(2)}) collective-permute-start(bf16[32,4096]{1,0:T(8,128)(2,1)S(1)} %get-tuple-element.46), channel_id=1, source_target_pairs={{0,6},{2,4},{4,2},{6,0},{8,14},{10,12},{12,10},{14,8},{1,7},{3,5},... | collective-permute-start | bytes 786440 | tf_op jit(solution)/shard_map/ppermute | solution.py:318
  194.0 2.5 %copy-start.8 = (bf16[32,32768]{1,0:T(8,128)(2,1)}, bf16[32,32768]{1,0:T(8,128)(2,1)S(1)}, u32[]{:S(2)}) copy-start(bf16[32,32768]{1,0:T(8,128)(2,1)S(1)} %constant_dynamic-update-slice_fusion.7) | copy-start | bytes 6291460
  (4 other events, 4.7 us)

commit v12 on v11

--- a/solution.py
+++ b/solution.py
@@ -1,4 +1,5 @@
 import functools
+import math
 
 import jax
 import jax.numpy as jnp
@@ -11,8 +12,8 @@
 PAIR = 2 * TILE
 GROUP = 4
 UNROLL = 4
-VMEM_LIMIT = 14 * 1024 * 1024
-PARTS = (3, 5, 4)
+VMEM_SLACK = 10 * 1024 * 1024
+PARTS = (15, 17, 16)
 RANGES = ((0, 2), (2, 3))
 OWN, OTHER = range(2)
 BOUNDS = 3
@@ -93,7 +94,7 @@
     for number, ref in enumerate(pieces):
         start, end = end, end + ref.shape[0]
 
-        @pl.when(meta[2] > first + (start if number % 2 == 0 else start - ref.shape[0]))
+        @pl.when(meta[2] > first + start - number % 4 * ref.shape[0])
         def copy(start=start, end=end, ref=ref):
             joined[start:end] = ref[...]
 
@@ -114,13 +115,14 @@
 def project_kernel(sizes, n_pieces, spot, first, last, meta, wave, *refs):
     pieces, refs = refs[:n_pieces], refs[n_pieces:]
     turned, refs = refs[-1], refs[:-1]
-    proj = pieces[0].shape[2]
+    if not first:
+        before, refs = refs[0], refs[1:]
     values = pieces[0]
     if n_pieces > 1:
-        values, refs = refs[-1], refs[:-1]
+        values, refs = refs[0], refs[1:]
         join_pieces(meta, pieces, values, spot[-1])
     total = refs[-1]
-    total[...] = jnp.zeros_like(total) if first else refs[0][...]
+    total[...] = jnp.zeros_like(total) if first else before[...]
     every = slice(None)
 
     def product(lanes, segments, tiles):
@@ -143,24 +145,19 @@
     @pl.when(meta[1 + spot[0]] > spot[-1])
     def loop():
         turn_waves(wave, turned, sizes[1])
-        group_loop(sizes, meta, values, proj, *spot, product)
+        group_loop(sizes, meta, values, values.shape[2], *spot, product)
 
     if last:
-        outs = refs[1:-1]
+        outs = refs[:-1]
         rows = outs[0].shape[0]
         for d, out in enumerate(outs):
             start = 0 if len(outs) == 1 else pl.multiple_of((meta[0] ^ d) * rows, rows)
             out[...] = total[pl.ds(start, rows), :].astype(out.dtype)
 
 
-def spread_kernel(sizes, n_rows, n_pieces, which, meta, *refs):
+def spread_kernel(sizes, n_rows, spots, meta, *refs):
     applied, refs = refs[:n_rows], refs[n_rows:]
-    pieces, refs = refs[:n_pieces], refs[n_pieces:]
-    proj = pieces[0].shape[2]
-    values = pieces[0]
-    if n_pieces > 1:
-        values, refs = refs[-1], refs[:-1]
-        join_pieces(meta, pieces, values, 0)
+    lists, refs = refs[: len(spots)], refs[len(spots) :]
     outs, field = refs[:-1], refs[-1]
     field[...] = jnp.zeros_like(field)
     every = slice(None)
@@ -182,7 +179,8 @@
             for number, at in enumerate(segments)
         ]
 
-    group_loop(sizes, meta, values, proj, which, 0, len(RANGES), 0, product)
+    for values, spot in zip(lists, spots):
+        group_loop(sizes, meta, values, values.shape[2], *spot, product)
     for pair in range(sizes[1] // 2):
         points = slice(pair * PAIR, (pair + 1) * PAIR)
         values, start = field[points, :].T, 0
@@ -206,58 +204,62 @@
     return blocks if len(blocks) == count else jnp.split(blocks[0], count)
 
 
-def joined_shape(pieces):
-    if len(pieces) == 1:
-        return []
-    count = sum(piece.shape[0] for piece in pieces)
-    return [pltpu.VMEM((count,) + pieces[0].shape[1:], jnp.bfloat16)]
+def vmem(scratch):
+    size = sum(math.prod(ref.shape) * jnp.dtype(ref.dtype).itemsize for ref in scratch)
+    return pltpu.CompilerParams(vmem_limit_bytes=size + VMEM_SLACK)
 
 
 def project(sizes, meta, wave, pieces, count, width, spot, total=None, last=False, us=0):
     rows = wave.shape[0]
-    bands = rows // count
-    split = bands % 16 == 0
     operands = [wave, *pieces] + ([] if total is None else [total])
-    outs = count if split else 1
-    out_shape = [jax.ShapeDtypeStruct((rows // outs, width), jnp.bfloat16)] * outs
-    return pl.pallas_call(
-        functools.partial(
-            project_kernel, sizes, len(pieces), spot, total is None, last
-        ),
+    shapes = []
+    if len(pieces) > 1:
+        held = sum(piece.shape[0] for piece in pieces)
+        shapes.append(jax.ShapeDtypeStruct((held,) + pieces[0].shape[1:], jnp.bfloat16))
+    scratch = [pltpu.VMEM((2, sizes[1] // 2 + 1, rows, PAIR), jnp.bfloat16)]
+    if last:
+        outs = count if rows // count % 16 == 0 else 1
+        shapes += [jax.ShapeDtypeStruct((rows // outs, width), jnp.bfloat16)] * outs
+        scratch = [pltpu.VMEM((rows, width), jnp.float32)] + scratch
+    else:
+        shapes.append(jax.ShapeDtypeStruct((rows, width), jnp.float32))
+    result = pl.pallas_call(
+        functools.partial(project_kernel, sizes, len(pieces), spot, total is None, last),
         grid_spec=pltpu.PrefetchScalarGridSpec(
             num_scalar_prefetch=1,
             grid=(1,),
             in_specs=[WHOLE] * len(operands),
-            out_specs=[WHOLE] * outs if last else WHOLE,
-            scratch_shapes=([pltpu.VMEM((rows, width), jnp.float32)] if last else [])
-            + joined_shape(pieces)
-            + [pltpu.VMEM((2, sizes[1] // 2 + 1, rows, PAIR), jnp.bfloat16)],
+            out_specs=[WHOLE] * len(shapes),
+            scratch_shapes=scratch,
         ),
-        out_shape=out_shape if last else jax.ShapeDtypeStruct((rows, width), jnp.float32),
-        compiler_params=pltpu.CompilerParams(vmem_limit_bytes=VMEM_LIMIT),
+        out_shape=shapes,
+        compiler_params=vmem(scratch),
         cost_estimate=cost(us),
     )(meta, *operands)
-
-
-def spread(sizes, meta, applied, pieces, points, which):
+    joined, result = (result[0], result[1:]) if len(pieces) > 1 else (pieces[0], result)
+    return (list(result) if last else result[0]), joined
+
+
+def spread(sizes, meta, applied, lists, points, spots):
     count = len(applied)
     applied = join_small(applied)
     rows = sum(block.shape[0] for block in applied)
+    scratch = [pltpu.VMEM((points + TILE, rows), jnp.float32)]
     result = pl.pallas_call(
-        functools.partial(spread_kernel, sizes, len(applied), len(pieces), which),
+        functools.partial(spread_kernel, sizes, len(applied), spots),
         grid_spec=pltpu.PrefetchScalarGridSpec(
             num_scalar_prefetch=1,
             grid=(1,),
-            in_specs=[WHOLE] * (len(applied) + len(pieces)),
+            in_specs=[WHOLE] * (len(applied) + len(lists)),
             out_specs=[WHOLE] * len(applied),
-            scratch_shapes=[pltpu.VMEM((points + TILE, rows), jnp.float32)] + joined_shape(pieces),
+            scratch_shapes=scratch,
         ),
         out_shape=[
             jax.ShapeDtypeStruct((block.shape[0], points), jnp.bfloat16) for block in applied
         ],
-        compiler_params=pltpu.CompilerParams(vmem_limit_bytes=VMEM_LIMIT),
+        compiler_params=vmem(scratch),
         cost_estimate=cost(0),
-    )(meta, *applied, *pieces)
+    )(meta, *applied, *lists)
     return split_small(result, count)
 
 
@@ -287,7 +289,7 @@
         in_specs=[WHOLE] * (2 + len(parts)),
         out_specs=WHOLE,
         out_shape=jax.ShapeDtypeStruct(parts[0].shape, jnp.bfloat16),
-        compiler_params=pltpu.CompilerParams(vmem_limit_bytes=VMEM_LIMIT),
+        compiler_params=vmem([]),
         cost_estimate=cost(0),
     )(high, low, *parts)
 
@@ -340,7 +342,24 @@
     for first, end in RANGES[1:]:
         range_of += jnp.where(slots >= starts[first], 1, 0)
 
+    own_wave = to_bricks(side)
+    other_wave = to_bricks(1 - side)
+    matrix = two_parts(coupling_matrix(coupling))
+
+    arrived, pieces, across = [], [], None
+    source = projectors
+    for number, (start, end) in enumerate(zip(starts, starts[1:])):
+        share = (end - start) // 4
+        start += (2 * group + core) * share
+        sent = lax.dynamic_slice_in_dim(source, start, share, 0)
+        if number == 0:
+            sent, source = lax.optimization_barrier((sent, source))
+        if number > 0:
+            sent = lax.optimization_barrier((sent, arrived[0]))[0]
+        arrived.append(lax.ppermute(sent, "grid", partners))
+
     numbers = jnp.stack([tile_segment, tile_block, jnp.broadcast_to(tile_count, (tiles,))])
+    numbers = lax.optimization_barrier((numbers, arrived[0]))[0]
     others = lax.ppermute(numbers, "grid", partners)
     absent = segments << bits(tiles)
     segment, block = (jnp.stack([numbers[i], others[i]]) for i in (0, 1))
@@ -355,47 +374,38 @@
         ]
     )
 
-    own_wave = to_bricks(side)
-    other_wave = to_bricks(1 - side)
-    matrix = two_parts(coupling_matrix(coupling))
-
-    arrived, pieces, across = [], [], None
-    source = projectors
-    for number, (start, end) in enumerate(zip(starts, starts[1:])):
-        share = (end - start) // 4
-        start += (2 * group + core) * share
-        sent = lax.dynamic_slice_in_dim(source, start, share, 0)
-        if number == 0:
-            sent, source = lax.optimization_barrier((sent, source))
-        if number > 1:
-            sent = lax.optimization_barrier((sent, arrived[number - 2]))[0]
-        arrived.append(lax.ppermute(sent, "grid", partners))
-    own_wave, late = lax.optimization_barrier((own_wave, arrived[-1]))
-    spot = (OWN, 0, len(RANGES), 0)
-    total = project(sizes, meta, own_wave, [projectors], half, width, spot, us=10)
+    own_wave = lax.optimization_barrier((own_wave, arrived[-1]))[0]
+    own_spot = (OWN, 0, len(RANGES), 0)
+    total, own_tiles = project(
+        sizes, meta, own_wave, [projectors], half, width, own_spot, us=10
+    )
     for number, mine in enumerate(arrived):
         sent = mine
         if number == 1:
-            sent, across, matrix, meta = lax.optimization_barrier((sent, across, matrix, meta))
-        if number > 1:
-            sent, across = lax.optimization_barrier((sent, across))
+            sent, across, matrix = lax.optimization_barrier((sent, across, matrix))
+        if number == 2:
+            sent, across, other_wave = lax.optimization_barrier((sent, across, other_wave))
         across = lax.ppermute(sent, "groups", swap)
-        both = jnp.concatenate([mine, across])
-        pieces += [both, lax.ppermute(both, "band", swap)]
-
+        pieces += [mine, across]
+        pieces += [lax.ppermute(mine, "band", swap), lax.ppermute(across, "band", swap)]
+
+    joined, other_spots = [], []
     for number, (first, end) in enumerate(RANGES):
-        total = project(
+        other_spots.append((OTHER, number, number + 1, starts[first]))
+        last = end == len(PARTS)
+        total, tiles_held = project(
             sizes,
             meta,
             other_wave,
-            pieces[2 * first : 2 * end],
+            pieces[4 * first : 4 * end],
             half,
             width,
-            (OTHER, number, number + 1, starts[first]),
+            other_spots[-1],
             total,
-            last=end == len(PARTS),
-            us=8 if end < len(PARTS) else 0,
+            last=last,
+            us=0 if last else 8,
         )
+        joined.append(tiles_held)
     if len(total) < half:
         total = [lax.dynamic_slice_in_dim(total[0], (place ^ d) * bands, bands, 0) for d in range(half)]
 
@@ -404,8 +414,8 @@
 
     result = jnp.zeros((bands, npts), jnp.bfloat16)
     for which, field in (
-        (1 - side, spread(sizes, meta, applied, pieces, points, OTHER)),
-        (side, spread(sizes, meta, applied, [projectors], points, OWN)),
+        (1 - side, spread(sizes, meta, applied, joined, points, other_spots)),
+        (side, spread(sizes, meta, applied, [own_tiles], points, [own_spot])),
     ):
         for d, block in enumerate(exchange(field)):
             start = (which * half + (place ^ d)) * points

time: 199 us -> 177 us (0.89)
  the two profiles are of different devices: /device:TPU:0 before, /device:TPU:16 now
where the time goes in v12:
time: 177 us; the launch traced here: 175 us
  waiting for transfers between devices  55.8 us (32%)
  starting transfers between devices  53 us (30%)
  local copies, waits for them, and re-layouts  30.1 us (17%)
  Pallas kernels  29.8 us (17%)
  other arithmetic  5.38 us (3%)
    ppermute x12, waiting for transfers between devices, exchange(): lax.ppermute(blocks[d], 'grid', [(i, i // half * half + (i % half ^ d)) f...  33.8 us
    all_to_all x2, starting transfers between devices, to_bricks(): lax.all_to_all(part, 'grid', split_axis=1, concat_axis=0, tiled=True, axi...  27 us
    pallas_call x3, Pallas kernels, project(): pl.pallas_call(functools.partial(project_kernel, sizes, len(pieces), spot...  16.2 us
    ppermute x12, starting transfers between devices, exchange(): lax.ppermute(blocks[d], 'grid', [(i, i // half * half + (i % half ^ d)) f...  14.2 us
    ppermute x3, waiting for transfers between devices, body(): arrived.append(lax.ppermute(sent, 'grid', partners))  14.1 us
    unnamed x26, local copies, waits for them, and re-layouts  13.6 us
    pallas_call x2, Pallas kernels, spread(): pl.pallas_call(functools.partial(spread_kernel, sizes, len(applied), spot...  12.6 us
    all_to_all x2, waiting for transfers between devices, to_bricks(): lax.all_to_all(part, 'grid', split_axis=1, concat_axis=0, tiled=True, axi...  7.56 us
  transfers between devices with their start and end apart: 27, of which 14 were waited for; matrix products, arithmetic and copies ran while one was open for 11% of the time, Pallas kernels for 8%

profile of v12, /device:TPU:16, one launch (start us, length us, event | category | flops | bytes accessed | tf_op | source)
XLA Modules:
  0.0 175.3 jit_solution(100445665364420614)
XLA Ops:
  0.0 1.9 %constant_dynamic-slice_fusion.4 = bf16[30,64,128]{2,1,0:T(8,128)(2,1)} fusion(bf16[384,64,128]{2,1,0:T(8,128)(2,1)} %refs_4_.1, s32[]{:T(128)S(6)} %select_n.353), kind=kLoop, calls=%fused_computation.57 | loop fusion | bytes 983044 | tf_op jit(solution)/shard_map/dynamic_slice | solution.py:354
  1.9 2.6 %constant_dynamic-slice_fusion = (bf16[32,16384]{1,0:T(8,128)(2,1)S(1)}, bf16[32,16384]{1,0:T(8,128)(2,1)}) fusion(bf16[32,32768]{1,0:T(8,128)(2,1)} %param.6, s32[]{:T(128)S(6)} %select_n.386, s32[]{:T(128)S(6)} %select_n.385), kind=kLoop, calls=%fused_computation.53 | loop fusion | bytes 4194312 | tf_op jit(solution)/shard_map/dynamic_slice | solution.py:327
  5.6 4.1 %all-to-all-start.1 = ((bf16[32,4,4096]{2,0,1:T(8,128)(2,1)}), bf16[32,4,4096]{2,0,1:T(8,128)(2,1)S(1)}, u32[]{:S(2)}, u32[]{:S(2)}) async-start(bf16[32,4,4096]{2,0,1:T(8,128)(2,1)} %bitcast.19), calls=%async_computation.1 | async-start | bytes 2097152 | tf_op jit(solution)/shard_map/all_to_all | solution.py:328
  12.1 1.9 %constant_dynamic-slice_fusion.3 = bf16[34,64,128]{2,1,0:T(8,128)(2,1)} fusion(bf16[384,64,128]{2,1,0:T(8,128)(2,1)} %refs_4_.1, s32[]{:T(128)S(6)} %select_n.380), kind=kLoop, calls=%fused_computation.56 | loop fusion | bytes 1114116 | tf_op jit(solution)/shard_map/dynamic_slice | solution.py:354
  14.0 2.0 %constant_dynamic-slice_fusion.2 = bf16[32,64,128]{2,1,0:T(8,128)(2,1)} fusion(bf16[384,64,128]{2,1,0:T(8,128)(2,1)} %refs_4_.1, s32[]{:T(128)S(6)} %select_n.383), kind=kLoop, calls=%fused_computation.55 | loop fusion | bytes 1048580 | tf_op jit(solution)/shard_map/dynamic_slice | solution.py:354
  19.9 1.9 %subtract_convert_fusion.low_ref = bf16[32,128,128]{2,1,0:T(8,128)(2,1)S(1)} fusion(f32[32,128,128]{2,1,0:T(8,128)} %copy.18, pred[128,128]{1,0:T(8,128)(4,1)S(1)} %broadcast_compare_fusion), kind=kLoop, calls=%fused_computation | loop fusion | flops 2621440 | bytes 3162112 | tf_op jit(solution)/shard_map/convert_element_type | solution.py:268
  23.5 3.4 %collective-permute-start.1 = (s32[3,384]{1,0:T(4,128)S(1)}, s32[3,384]{1,0:T(4,128)S(1)}, u32[]{:S(2)}, u32[]{:S(2)}) collective-permute-start(s32[3,384]{1,0:T(4,128)S(1)} %add_add_fusion), channel_id=1, source_target_pairs={{0,8},{2,10},{4,12},{6,14},{8,0},{10,2},{12,4},{14,6},{1,9},{3,11}... | collective-permute-start | bytes 13832 | tf_op jit(solution)/shard_map/ppermute | solution.py:363
  27.5 2.9 %collective-permute-start.4 = (bf16[32,64,128]{2,1,0:T(8,128)(2,1)}, bf16[32,64,128]{2,1,0:T(8,128)(2,1)}, u32[]{:S(2)}, u32[]{:S(2)}) collective-permute-start(bf16[32,64,128]{2,1,0:T(8,128)(2,1)} %constant_dynamic-slice_fusion.2), channel_id=1, source_target_pairs={{0,8},{2,10},{4,12},{6,14},{8,0},{10,2},{12,4},{14,6},{1,9},{3,11}... | collective-permute-start | bytes 1572872 | tf_op jit(solution)/shard_map/ppermute | solution.py:359
  33.2 22.8 %all-to-all-start = ((bf16[32,4,4096]{2,0,1:T(8,128)(2,1)}), bf16[32,4,4096]{2,0,1:T(8,128)(2,1)S(1)}, u32[]{:S(2)}, u32[]{:S(2)}) async-start(bf16[32,4,4096]{2,0,1:T(8,128)(2,1)} %bitcast.26), calls=%async_computation | async-start | bytes 2097152 | tf_op jit(solution)/shard_map/all_to_all | solution.py:328
  57.1 7.1 %collective-permute-done.2.refs_4_ = bf16[34,64,128]{2,1,0:T(8,128)(2,1)} collective-permute-done((bf16[34,64,128]{2,1,0:T(8,128)(2,1)}, bf16[34,64,128]{2,1,0:T(8,128)(2,1)}, u32[]{:S(2)}, u32[]{:S(2)}) %collective-permute-start.2) | collective-permute-done | bytes 557088 | tf_op jit(solution)/shard_map/ppermute | solution.py:359
  68.5 5.2 %collective-permute-done.4.refs_0_ = bf16[32,64,128]{2,1,0:T(8,128)(2,1)} collective-permute-done((bf16[32,64,128]{2,1,0:T(8,128)(2,1)}, bf16[32,64,128]{2,1,0:T(8,128)(2,1)}, u32[]{:S(2)}, u32[]{:S(2)}) %collective-permute-start.4) | collective-permute-done | bytes 524320 | tf_op jit(solution)/shard_map/ppermute | solution.py:359
  73.7 7.6 %all-to-all-done = bf16[32,4,4096]{2,0,1:T(8,128)(2,1)S(1)} async-done(((bf16[32,4,4096]{2,0,1:T(8,128)(2,1)}), bf16[32,4,4096]{2,0,1:T(8,128)(2,1)S(1)}, u32[]{:S(2)}, u32[]{:S(2)}) %all-to-all-start) | async-done | bytes 1048608 | tf_op jit(solution)/shard_map/all_to_all | solution.py:328
  82.6 2.8 %copy-done = bf16[384,64,128]{2,1,0:T(8,128)(2,1)S(1)} copy-done((bf16[384,64,128]{2,1,0:T(8,128)(2,1)S(1)}, bf16[384,64,128]{2,1,0:T(8,128)(2,1)}, u32[]{:S(2)}) %copy-start) | copy-done | bytes 6291480
  86.6 3.1 %shard_map.67.refs_8_ = f32[128,4096]{1,0:T(8,128)S(1)} custom-call(s32[1225]{0:T(1024)S(1)} %concatenate.26.meta, bf16[128,4096]{1,0:T(8,128)(2,1)S(1)} %bitcast.23, bf16[384,64,128]{2,1,0:T(8,128)(2,1)S(1)} %copy-done), custom_call_target="tpu_custom_call" | custom-call | flops 10000000000 | bytes 1 | tf_op jit(solution)/shard_map/pallas_call | solution.py:226
  90.7 8.1 %shard_map.68 = (bf16[256,64,128]{2,1,0:T(8,128)(2,1)S(1)}, f32[128,4096]{1,0:T(8,128)S(1)}) custom-call(s32[1225]{0:T(1024)S(1)} %concatenate.26.meta, bf16[128,4096]{1,0:T(8,128)(2,1)S(1)} %bitcast.21, bf16[30,64,128]{2,1,0:T(8,128)(2,1)} %collective-permute-done.refs_0_, bf16[30,64,128]{2,1,0:T(8,128)(2,1)} %collective-permute-done.3.refs_1_, ...), custom_call_target="tpu_custom_call" | custom-call | flops 8000000000 | bytes 1 | tf_op jit(solution)/shard_map/pallas_call | solution.py:226
  98.8 2.0 %copy-done.2 = bf16[256,64,128]{2,1,0:T(8,128)(2,1)} copy-done((bf16[256,64,128]{2,1,0:T(8,128)(2,1)}, bf16[256,64,128]{2,1,0:T(8,128)(2,1)S(1)}, u32[]{:S(2)}) %copy-start.2) | copy-done | bytes 4194328
  100.8 5.1 %shard_map.69 = (bf16[128,64,128]{2,1,0:T(8,128)(2,1)S(1)}, bf16[32,4096]{1,0:T(8,128)(2,1)S(1)}, bf16[32,4096]{1,0:T(8,128)(2,1)S(1)}, bf16[32,4096]{1,0:T(8,128)(2,1)S(1)}, bf16[32,4096]{1,0:T(8,128)(2,1)S(1)}) custom-call(s32[1225]{0:T(1024)S(1)} %concatenate.26.meta, bf16[128,4096]{1,0:T(8,128)(2,1)S(1)} %bitcast.22, ...), custom_call_target="tpu_custom_call" | custom-call | flops 1 | bytes 1 | tf_op jit(solution)/shard_map/pallas_call | solution.py:226
  106.4 3.1 %collective-permute-start.15 = (bf16[32,4096]{1,0:T(8,128)(2,1)S(1)}, bf16[32,4096]{1,0:T(8,128)(2,1)S(1)}, u32[]{:S(2)}, u32[]{:S(2)}) collective-permute-start(bf16[32,4096]{1,0:T(8,128)(2,1)S(1)} %get-tuple-element.46), channel_id=1, source_target_pairs={{0,6},{2,4},{4,2},{6,0},{8,14},{10,12},{12,10},{14,8},{1,7},{3,5},... | collective-permute-start | bytes 786440 | tf_op jit(solution)/shard_map/ppermute | solution.py:320
  109.5 5.2 %collective-permute-done.13.refs_1_ = bf16[32,4096]{1,0:T(8,128)(2,1)S(1)} collective-permute-done((bf16[32,4096]{1,0:T(8,128)(2,1)S(1)}, bf16[32,4096]{1,0:T(8,128)(2,1)S(1)}, u32[]{:S(2)}, u32[]{:S(2)}) %collective-permute-start.13) | collective-permute-done | bytes 262176 | tf_op jit(solution)/shard_map/ppermute | solution.py:320
  115.2 6.3 %collective-permute-done.15.refs_3_ = bf16[32,4096]{1,0:T(8,128)(2,1)S(1)} collective-permute-done((bf16[32,4096]{1,0:T(8,128)(2,1)S(1)}, bf16[32,4096]{1,0:T(8,128)(2,1)S(1)}, u32[]{:S(2)}, u32[]{:S(2)}) %collective-permute-start.15) | collective-permute-done | bytes 262176 | tf_op jit(solution)/shard_map/ppermute | solution.py:320
  123.2 2.8 %collective-permute-start.18 = (bf16[32,4096]{1,0:T(8,128)(2,1)S(1)}, bf16[32,4096]{1,0:T(8,128)(2,1)S(1)}, u32[]{:S(2)}, u32[]{:S(2)}) collective-permute-start(bf16[32,4096]{1,0:T(8,128)(2,1)S(1)} %shard_map.70.refs_0_), channel_id=1, source_target_pairs={{0,6},{2,4},{4,2},{6,0},{8,14},{10,12},{12,10},{14,8},{1,7},{3,5},... | collective-permute-start | bytes 786440 | tf_op jit(solution)/shard_map/ppermute | solution.py:320
  126.0 4.8 %collective-permute-done.16.refs_1_ = bf16[32,4096]{1,0:T(8,128)(2,1)S(1)} collective-permute-done((bf16[32,4096]{1,0:T(8,128)(2,1)S(1)}, bf16[32,4096]{1,0:T(8,128)(2,1)S(1)}, u32[]{:S(2)}, u32[]{:S(2)}) %collective-permute-start.16) | collective-permute-done | bytes 262176 | tf_op jit(solution)/shard_map/ppermute | solution.py:320
  132.1 4.8 %collective-permute-done.18.refs_3_ = bf16[32,4096]{1,0:T(8,128)(2,1)S(1)} collective-permute-done((bf16[32,4096]{1,0:T(8,128)(2,1)S(1)}, bf16[32,4096]{1,0:T(8,128)(2,1)S(1)}, u32[]{:S(2)}, u32[]{:S(2)}) %collective-permute-start.18) | collective-permute-done | bytes 262176 | tf_op jit(solution)/shard_map/ppermute | solution.py:320
  136.9 2.2 %copy-done.3 = bf16[256,64,128]{2,1,0:T(8,128)(2,1)S(1)} copy-done((bf16[256,64,128]{2,1,0:T(8,128)(2,1)S(1)}, bf16[256,64,128]{2,1,0:T(8,128)(2,1)}, u32[]{:S(2)}) %copy-start.3) | copy-done | bytes 4194328
  140.7 9.3 %shard_map.71 = (bf16[32,4096]{1,0:T(8,128)(2,1)S(1)}, bf16[32,4096]{1,0:T(8,128)(2,1)S(1)}, bf16[32,4096]{1,0:T(8,128)(2,1)S(1)}, bf16[32,4096]{1,0:T(8,128)(2,1)S(1)}) custom-call(s32[1225]{0:T(1024)S(1)} %concatenate.26.meta, bf16[32,4096]{1,0:T(8,128)(2,1)S(1)} %shard_map.70.refs_0_, bf16[32,4096]{1,0:T(8,128)(2,1)S(1)} %collective-permute-done.16.refs_1_, ...), custom_call_target="tpu_custom_call" | custom-call | flops 1 | bytes 1 | tf_op jit(solution)/shard_map/pallas_call | solution.py:248
  150.2 3.4 %collective-permute-start.21 = (bf16[32,4096]{1,0:T(8,128)(2,1)S(1)}, bf16[32,4096]{1,0:T(8,128)(2,1)S(1)}, u32[]{:S(2)}, u32[]{:S(2)}) collective-permute-start(bf16[32,4096]{1,0:T(8,128)(2,1)S(1)} %get-tuple-element.52), channel_id=1, source_target_pairs={{0,6},{2,4},{4,2},{6,0},{8,14},{10,12},{12,10},{14,8},{1,7},{3,5},... | collective-permute-start | bytes 786440 | tf_op jit(solution)/shard_map/ppermute | solution.py:320
  153.6 2.8 %copy-done.1 = bf16[384,64,128]{2,1,0:T(8,128)(2,1)S(1)} copy-done((bf16[384,64,128]{2,1,0:T(8,128)(2,1)S(1)}, bf16[384,64,128]{2,1,0:T(8,128)(2,1)}, u32[]{:S(2)}) %copy-start.1) | copy-done | bytes 6291480
  156.4 3.3 %shard_map.72 = (bf16[32,4096]{1,0:T(8,128)(2,1)S(1)}, bf16[32,4096]{1,0:T(8,128)(2,1)S(1)}, bf16[32,4096]{1,0:T(8,128)(2,1)S(1)}, bf16[32,4096]{1,0:T(8,128)(2,1)S(1)}) custom-call(s32[1225]{0:T(1024)S(1)} %concatenate.26.meta, bf16[32,4096]{1,0:T(8,128)(2,1)S(1)} %shard_map.70.refs_0_, bf16[32,4096]{1,0:T(8,128)(2,1)S(1)} %collective-permute-done.16.refs_1_, ...), custom_call_target="tpu_custom_call" | custom-call | flops 1 | bytes 1 | tf_op jit(solution)/shard_map/pallas_call | solution.py:248
  161.0 2.5 %collective-permute-start.24 = (bf16[32,4096]{1,0:T(8,128)(2,1)S(1)}, bf16[32,4096]{1,0:T(8,128)(2,1)S(1)}, u32[]{:S(2)}, u32[]{:S(2)}) collective-permute-start(bf16[32,4096]{1,0:T(8,128)(2,1)S(1)} %get-tuple-element.56), channel_id=1, source_target_pairs={{0,6},{2,4},{4,2},{6,0},{8,14},{10,12},{12,10},{14,8},{1,7},{3,5},... | collective-permute-start | bytes 786440 | tf_op jit(solution)/shard_map/ppermute | solution.py:320
  163.6 2.1 %collective-permute-done.21 = bf16[32,4096]{1,0:T(8,128)(2,1)S(1)} collective-permute-done((bf16[32,4096]{1,0:T(8,128)(2,1)S(1)}, bf16[32,4096]{1,0:T(8,128)(2,1)S(1)}, u32[]{:S(2)}, u32[]{:S(2)}) %collective-permute-start.21) | collective-permute-done | bytes 262176 | tf_op jit(solution)/shard_map/ppermute | solution.py:320
  165.7 4.5 %collective-permute-done.22 = bf16[32,4096]{1,0:T(8,128)(2,1)S(1)} collective-permute-done((bf16[32,4096]{1,0:T(8,128)(2,1)S(1)}, bf16[32,4096]{1,0:T(8,128)(2,1)S(1)}, u32[]{:S(2)}, u32[]{:S(2)}) %collective-permute-start.22) | collective-permute-done | bytes 262176 | tf_op jit(solution)/shard_map/ppermute | solution.py:320
  170.2 4.3 %collective-permute-done.24 = bf16[32,4096]{1,0:T(8,128)(2,1)S(1)} collective-permute-done((bf16[32,4096]{1,0:T(8,128)(2,1)S(1)}, bf16[32,4096]{1,0:T(8,128)(2,1)S(1)}, u32[]{:S(2)}, u32[]{:S(2)}) %collective-permute-start.24) | collective-permute-done | bytes 262176 | tf_op jit(solution)/shard_map/ppermute | solution.py:320
  (110 shorter events, 28.2 us)
Async XLA Ops:
  1.9 21.7 %collective-permute-start = (bf16[30,64,128]{2,1,0:T(8,128)(2,1)}, bf16[30,64,128]{2,1,0:T(8,128)(2,1)}, u32[]{:S(2)}, u32[]{:S(2)}) collective-permute-start(bf16[30,64,128]{2,1,0:T(8,128)(2,1)} %constant_dynamic-slice_fusion.4), channel_id=1, source_target_pairs={{0,8},{2,10},{4,12},{6,14},{8,0},{10,2},{12,4},{14,6},{1,9},{3,11}... | collective-permute-start | bytes 1474568 | tf_op jit(solution)/shard_map/ppermute | solution.py:359
  4.5 5.3 %copy-start.10 = (f32[32,16,8,8]{0,3,2,1:T(8,128)S(1)}, f32[32,16,8,8]{0,3,2,1:T(8,128)}, u32[]{:S(2)}) copy-start(f32[32,16,8,8]{0,3,2,1:T(8,128)} %param.11) | copy-start | bytes 393220
  5.6 26.6 %all-to-all-start.1 = ((bf16[32,4,4096]{2,0,1:T(8,128)(2,1)}), bf16[32,4,4096]{2,0,1:T(8,128)(2,1)S(1)}, u32[]{:S(2)}, u32[]{:S(2)}) async-start(bf16[32,4,4096]{2,0,1:T(8,128)(2,1)} %bitcast.19), calls=%async_computation.1 | async-start | bytes 2097152 | tf_op jit(solution)/shard_map/all_to_all | solution.py:328
  12.0 4.0 %copy-start.12 = (s32[384]{0:T(512)S(1)}, s32[384]{0:T(512)}, u32[]{:S(2)}) copy-start(s32[384]{0:T(512)} %param.8) | copy-start | bytes 4612
  14.0 4.7 %copy-start.8 = (bf16[32,16384]{1,0:T(8,128)(2,1)S(1)}, bf16[32,16384]{1,0:T(8,128)(2,1)}, u32[]{:S(2)}) copy-start(bf16[32,16384]{1,0:T(8,128)(2,1)} %get-tuple-element.58) | copy-start | bytes 3145732
  23.5 8.5 %collective-permute-start.1 = (s32[3,384]{1,0:T(4,128)S(1)}, s32[3,384]{1,0:T(4,128)S(1)}, u32[]{:S(2)}, u32[]{:S(2)}) collective-permute-start(s32[3,384]{1,0:T(4,128)S(1)} %add_add_fusion), channel_id=1, source_target_pairs={{0,8},{2,10},{4,12},{6,14},{8,0},{10,2},{12,4},{14,6},{1,9},{3,11}... | collective-permute-start | bytes 13832 | tf_op jit(solution)/shard_map/ppermute | solution.py:363
  27.5 36.6 %collective-permute-start.2 = (bf16[34,64,128]{2,1,0:T(8,128)(2,1)}, bf16[34,64,128]{2,1,0:T(8,128)(2,1)}, u32[]{:S(2)}, u32[]{:S(2)}) collective-permute-start(bf16[34,64,128]{2,1,0:T(8,128)(2,1)} %constant_dynamic-slice_fusion.3), channel_id=1, source_target_pairs={{0,8},{2,10},{4,12},{6,14},{8,0},{10,2},{12,4},{14,6},{1,9},{3,11}... | collective-permute-start | bytes 1671176 | tf_op jit(solution)/shard_map/ppermute | solution.py:359
  27.5 46.2 %collective-permute-start.4 = (bf16[32,64,128]{2,1,0:T(8,128)(2,1)}, bf16[32,64,128]{2,1,0:T(8,128)(2,1)}, u32[]{:S(2)}, u32[]{:S(2)}) collective-permute-start(bf16[32,64,128]{2,1,0:T(8,128)(2,1)} %constant_dynamic-slice_fusion.2), channel_id=1, source_target_pairs={{0,8},{2,10},{4,12},{6,14},{8,0},{10,2},{12,4},{14,6},{1,9},{3,11}... | collective-permute-start | bytes 1572872 | tf_op jit(solution)/shard_map/ppermute | solution.py:359
  30.5 26.6 %collective-permute-start.3 = (bf16[30,64,128]{2,1,0:T(8,128)(2,1)}, bf16[30,64,128]{2,1,0:T(8,128)(2,1)}, u32[]{:S(2)}, u32[]{:S(2)}) collective-permute-start(bf16[30,64,128]{2,1,0:T(8,128)(2,1)} %collective-permute-done.refs_0_), channel_id=1, source_target_pairs={{0,16},{16,0},{1,17},{17,1},{2,18},{18,2},{3,19},{19,3},{4,20},{20... | collective-permute-start | bytes 1474568 | tf_op jit(solution)/shard_map/ppermute | solution.py:388
  32.0 57.7 %collective-permute-start.9 = (bf16[30,64,128]{2,1,0:T(8,128)(2,1)}, bf16[30,64,128]{2,1,0:T(8,128)(2,1)}, u32[]{:S(2)}, u32[]{:S(2)}) collective-permute-start(bf16[30,64,128]{2,1,0:T(8,128)(2,1)} %collective-permute-done.refs_0_), channel_id=1, source_target_pairs={{0,1},{1,0},{2,3},{3,2},{4,5},{5,4},{6,7},{7,6},{8,9},{9,8},{10,11... | collective-permute-start | bytes 1474568 | tf_op jit(solution)/shard_map/ppermute | solution.py:390
  33.2 48.1 %all-to-all-start = ((bf16[32,4,4096]{2,0,1:T(8,128)(2,1)}), bf16[32,4,4096]{2,0,1:T(8,128)(2,1)S(1)}, u32[]{:S(2)}, u32[]{:S(2)}) async-start(bf16[32,4,4096]{2,0,1:T(8,128)(2,1)} %bitcast.26), calls=%async_computation | async-start | bytes 2097152 | tf_op jit(solution)/shard_map/all_to_all | solution.py:328
  64.1 17.2 %collective-permute-start.5 = (bf16[34,64,128]{2,1,0:T(8,128)(2,1)}, bf16[34,64,128]{2,1,0:T(8,128)(2,1)}, u32[]{:S(2)}, u32[]{:S(2)}) collective-permute-start(bf16[34,64,128]{2,1,0:T(8,128)(2,1)} %collective-permute-done.2.refs_4_), channel_id=1, source_target_pairs={{0,16},{16,0},{1,17},{17,1},{2,18},{18,2},{3,19},{19,3},{4,20},{20... | collective-permute-start | bytes 1671176 | tf_op jit(solution)/shard_map/ppermute | solution.py:388
  68.0 22.8 %collective-permute-start.10 = (bf16[30,64,128]{2,1,0:T(8,128)(2,1)}, bf16[30,64,128]{2,1,0:T(8,128)(2,1)}, u32[]{:S(2)}, u32[]{:S(2)}) collective-permute-start(bf16[30,64,128]{2,1,0:T(8,128)(2,1)} %collective-permute-done.3.refs_1_), channel_id=1, source_target_pairs={{0,1},{1,0},{2,3},{3,2},{4,5},{5,4},{6,7},{7,6},{8,9},{9,8},{10,11... | collective-permute-start | bytes 1474568 | tf_op jit(solution)/shard_map/ppermute | solution.py:390
  68.0 22.7 %collective-permute-start.11 = (bf16[34,64,128]{2,1,0:T(8,128)(2,1)}, bf16[34,64,128]{2,1,0:T(8,128)(2,1)}, u32[]{:S(2)}, u32[]{:S(2)}) collective-permute-start(bf16[34,64,128]{2,1,0:T(8,128)(2,1)} %collective-permute-done.2.refs_4_), channel_id=1, source_target_pairs={{0,1},{1,0},{2,3},{3,2},{4,5},{5,4},{6,7},{7,6},{8,9},{9,8},{10,11... | collective-permute-start | bytes 1671176 | tf_op jit(solution)/shard_map/ppermute | solution.py:390
  81.3 9.4 %collective-permute-start.6 = (bf16[32,64,128]{2,1,0:T(8,128)(2,1)}, bf16[32,64,128]{2,1,0:T(8,128)(2,1)S(1)}, u32[]{:S(2)}, u32[]{:S(2)}) collective-permute-start(bf16[32,64,128]{2,1,0:T(8,128)(2,1)} %collective-permute-done.4.refs_0_), channel_id=1, source_target_pairs={{0,16},{16,0},{1,17},{17,1},{2,18},{18,2},{3,19},{19,3},{4,20},{20... | collective-permute-start | bytes 1572872 | tf_op jit(solution)/shard_map/ppermute | solution.py:388
  82.6 8.1 %collective-permute-start.12 = (bf16[34,64,128]{2,1,0:T(8,128)(2,1)}, bf16[34,64,128]{2,1,0:T(8,128)(2,1)S(1)}, u32[]{:S(2)}, u32[]{:S(2)}) collective-permute-start(bf16[34,64,128]{2,1,0:T(8,128)(2,1)} %collective-permute-done.5.refs_5_), channel_id=1, source_target_pairs={{0,1},{1,0},{2,3},{3,2},{4,5},{5,4},{6,7},{7,6},{8,9},{9,8},{10,11... | collective-permute-start | bytes 1671176 | tf_op jit(solution)/shard_map/ppermute | solution.py:390
  89.7 11.1 %collective-permute-start.7 = (bf16[32,64,128]{2,1,0:T(8,128)(2,1)}, bf16[32,64,128]{2,1,0:T(8,128)(2,1)S(1)}, u32[]{:S(2)}, u32[]{:S(2)}) collective-permute-start(bf16[32,64,128]{2,1,0:T(8,128)(2,1)} %collective-permute-done.4.refs_0_), channel_id=1, source_target_pairs={{0,1},{1,0},{2,3},{3,2},{4,5},{5,4},{6,7},{7,6},{8,9},{9,8},{10,11... | collective-permute-start | bytes 1572872 | tf_op jit(solution)/shard_map/ppermute | solution.py:390
  90.7 10.1 %collective-permute-start.8 = (bf16[32,64,128]{2,1,0:T(8,128)(2,1)S(1)}, bf16[32,64,128]{2,1,0:T(8,128)(2,1)S(1)}, u32[]{:S(2)}, u32[]{:S(2)}) collective-permute-start(bf16[32,64,128]{2,1,0:T(8,128)(2,1)S(1)} %collective-permute-done.6.refs_1_), channel_id=1, source_target_pairs={{0,1},{1,0},{2,3},{3,2},{4,5},{5,4},{6,7},{7,6},{8,9},{9,8},{10,11... | collective-permute-start | bytes 1572872 | tf_op jit(solution)/shard_map/ppermute | solution.py:390
  106.0 16.9 %copy-start.4 = (bf16[128,64,128]{2,1,0:T(8,128)(2,1)}, bf16[128,64,128]{2,1,0:T(8,128)(2,1)S(1)}, u32[]{:S(2)}) copy-start(bf16[128,64,128]{2,1,0:T(8,128)(2,1)S(1)} %get-tuple-element.48.refs_5_) | copy-start | bytes 6291460
  106.0 8.8 %collective-permute-start.13 = (bf16[32,4096]{1,0:T(8,128)(2,1)S(1)}, bf16[32,4096]{1,0:T(8,128)(2,1)S(1)}, u32[]{:S(2)}, u32[]{:S(2)}) collective-permute-start(bf16[32,4096]{1,0:T(8,128)(2,1)S(1)} %get-tuple-element.44), channel_id=1, source_target_pairs={{0,2},{2,0},{4,6},{6,4},{8,10},{10,8},{12,14},{14,12},{1,3},{3,1},... | collective-permute-start | bytes 786440 | tf_op jit(solution)/shard_map/ppermute | solution.py:320
  106.1 9.2 %collective-permute-start.14 = (bf16[32,4096]{1,0:T(8,128)(2,1)S(1)}, bf16[32,4096]{1,0:T(8,128)(2,1)S(1)}, u32[]{:S(2)}, u32[]{:S(2)}) collective-permute-start(bf16[32,4096]{1,0:T(8,128)(2,1)S(1)} %get-tuple-element.45), channel_id=1, source_target_pairs={{0,4},{2,6},{4,0},{6,2},{8,12},{10,14},{12,8},{14,10},{1,5},{3,7},... | collective-permute-start | bytes 786440 | tf_op jit(solution)/shard_map/ppermute | solution.py:320
  106.4 15.1 %collective-permute-start.15 = (bf16[32,4096]{1,0:T(8,128)(2,1)S(1)}, bf16[32,4096]{1,0:T(8,128)(2,1)S(1)}, u32[]{:S(2)}, u32[]{:S(2)}) collective-permute-start(bf16[32,4096]{1,0:T(8,128)(2,1)S(1)} %get-tuple-element.46), channel_id=1, source_target_pairs={{0,6},{2,4},{4,2},{6,0},{8,14},{10,12},{12,10},{14,8},{1,7},{3,5},... | collective-permute-start | bytes 786440 | tf_op jit(solution)/shard_map/ppermute | solution.py:320
  122.5 8.3 %collective-permute-start.16 = (bf16[32,4096]{1,0:T(8,128)(2,1)S(1)}, bf16[32,4096]{1,0:T(8,128)(2,1)S(1)}, u32[]{:S(2)}, u32[]{:S(2)}) collective-permute-start(bf16[32,4096]{1,0:T(8,128)(2,1)S(1)} %shard_map.70.refs_0_), channel_id=1, source_target_pairs={{0,2},{2,0},{4,6},{6,4},{8,10},{10,8},{12,14},{14,12},{1,3},{3,1},... | collective-permute-start | bytes 786440 | tf_op jit(solution)/shard_map/ppermute | solution.py:320
  122.9 9.2 %collective-permute-start.17 = (bf16[32,4096]{1,0:T(8,128)(2,1)S(1)}, bf16[32,4096]{1,0:T(8,128)(2,1)S(1)}, u32[]{:S(2)}, u32[]{:S(2)}) collective-permute-start(bf16[32,4096]{1,0:T(8,128)(2,1)S(1)} %shard_map.70.refs_0_), channel_id=1, source_target_pairs={{0,4},{2,6},{4,0},{6,2},{8,12},{10,14},{12,8},{14,10},{1,5},{3,7},... | collective-permute-start | bytes 786440 | tf_op jit(solution)/shard_map/ppermute | solution.py:320
  123.2 13.8 %collective-permute-start.18 = (bf16[32,4096]{1,0:T(8,128)(2,1)S(1)}, bf16[32,4096]{1,0:T(8,128)(2,1)S(1)}, u32[]{:S(2)}, u32[]{:S(2)}) collective-permute-start(bf16[32,4096]{1,0:T(8,128)(2,1)S(1)} %shard_map.70.refs_0_), channel_id=1, source_target_pairs={{0,6},{2,4},{4,2},{6,0},{8,14},{10,12},{12,10},{14,8},{1,7},{3,5},... | collective-permute-start | bytes 786440 | tf_op jit(solution)/shard_map/ppermute | solution.py:320
  150.0 11.0 %collective-permute-start.19 = (bf16[32,4096]{1,0:T(8,128)(2,1)S(1)}, bf16[32,4096]{1,0:T(8,128)(2,1)S(1)}, u32[]{:S(2)}, u32[]{:S(2)}) collective-permute-start(bf16[32,4096]{1,0:T(8,128)(2,1)S(1)} %get-tuple-element.50), channel_id=1, source_target_pairs={{0,2},{2,0},{4,6},{6,4},{8,10},{10,8},{12,14},{14,12},{1,3},{3,1},... | collective-permute-start | bytes 786440 | tf_op jit(solution)/shard_map/ppermute | solution.py:320
  150.1 13.4 %collective-permute-start.20 = (bf16[32,4096]{1,0:T(8,128)(2,1)S(1)}, bf16[32,4096]{1,0:T(8,128)(2,1)S(1)}, u32[]{:S(2)}, u32[]{:S(2)}) collective-permute-start(bf16[32,4096]{1,0:T(8,128)(2,1)S(1)} %get-tuple-element.51), channel_id=1, source_target_pairs={{0,4},{2,6},{4,0},{6,2},{8,12},{10,14},{12,8},{14,10},{1,5},{3,7},... | collective-permute-start | bytes 786440 | tf_op jit(solution)/shard_map/ppermute | solution.py:320
  150.2 15.5 %collective-permute-start.21 = (bf16[32,4096]{1,0:T(8,128)(2,1)S(1)}, bf16[32,4096]{1,0:T(8,128)(2,1)S(1)}, u32[]{:S(2)}, u32[]{:S(2)}) collective-permute-start(bf16[32,4096]{1,0:T(8,128)(2,1)S(1)} %get-tuple-element.52), channel_id=1, source_target_pairs={{0,6},{2,4},{4,2},{6,0},{8,14},{10,12},{12,10},{14,8},{1,7},{3,5},... | collective-permute-start | bytes 786440 | tf_op jit(solution)/shard_map/ppermute | solution.py:320
  159.7 10.5 %collective-permute-start.22 = (bf16[32,4096]{1,0:T(8,128)(2,1)S(1)}, bf16[32,4096]{1,0:T(8,128)(2,1)S(1)}, u32[]{:S(2)}, u32[]{:S(2)}) collective-permute-start(bf16[32,4096]{1,0:T(8,128)(2,1)S(1)} %get-tuple-element.54), channel_id=1, source_target_pairs={{0,2},{2,0},{4,6},{6,4},{8,10},{10,8},{12,14},{14,12},{1,3},{3,1},... | collective-permute-start | bytes 786440 | tf_op jit(solution)/shard_map/ppermute | solution.py:320
  159.8 10.4 %collective-permute-start.23 = (bf16[32,4096]{1,0:T(8,128)(2,1)S(1)}, bf16[32,4096]{1,0:T(8,128)(2,1)S(1)}, u32[]{:S(2)}, u32[]{:S(2)}) collective-permute-start(bf16[32,4096]{1,0:T(8,128)(2,1)S(1)} %get-tuple-element.55), channel_id=1, source_target_pairs={{0,4},{2,6},{4,0},{6,2},{8,12},{10,14},{12,8},{14,10},{1,5},{3,7},... | collective-permute-start | bytes 786440 | tf_op jit(solution)/shard_map/ppermute | solution.py:320
  161.0 13.5 %collective-permute-start.24 = (bf16[32,4096]{1,0:T(8,128)(2,1)S(1)}, bf16[32,4096]{1,0:T(8,128)(2,1)S(1)}, u32[]{:S(2)}, u32[]{:S(2)}) collective-permute-start(bf16[32,4096]{1,0:T(8,128)(2,1)S(1)} %get-tuple-element.56), channel_id=1, source_target_pairs={{0,6},{2,4},{4,2},{6,0},{8,14},{10,12},{12,10},{14,8},{1,7},{3,5},... | collective-permute-start | bytes 786440 | tf_op jit(solution)/shard_map/ppermute | solution.py:320
  170.2 4.3 %copy-start.9 = (bf16[32,32768]{1,0:T(8,128)(2,1)}, bf16[32,32768]{1,0:T(8,128)(2,1)S(1)}, u32[]{:S(2)}) copy-start(bf16[32,32768]{1,0:T(8,128)(2,1)S(1)} %constant_dynamic-update-slice_fusion.1) | copy-start | bytes 6291460
  (8 other events, 17.6 us)

commit v13 on v12

--- a/solution.py
+++ b/solution.py
@@ -13,7 +13,8 @@
 GROUP = 4
 UNROLL = 4
 VMEM_SLACK = 10 * 1024 * 1024
-PARTS = (15, 17, 16)
+PARTS = (1, 1, 2)
+ORDER = (0, 2, 1)
 RANGES = ((0, 2), (2, 3))
 OWN, OTHER = range(2)
 BOUNDS = 3
@@ -89,12 +90,12 @@
     lax.fori_loop(0, (end - begin) // UNROLL, step, 0)
 
 
-def join_pieces(meta, pieces, joined, first):
+def join_pieces(meta, pieces, joined, firsts):
     end = 0
-    for number, ref in enumerate(pieces):
+    for first, ref in zip(firsts, pieces):
         start, end = end, end + ref.shape[0]
 
-        @pl.when(meta[2] > first + start - number % 4 * ref.shape[0])
+        @pl.when(meta[2] > first)
         def copy(start=start, end=end, ref=ref):
             joined[start:end] = ref[...]
 
@@ -112,7 +113,8 @@
         turned[way, segments // 2] = jnp.zeros(turned.shape[2:], turned.dtype)
 
 
-def project_kernel(sizes, n_pieces, spot, first, last, meta, wave, *refs):
+def project_kernel(sizes, firsts, spot, first, last, meta, wave, *refs):
+    n_pieces = max(1, len(firsts))
     pieces, refs = refs[:n_pieces], refs[n_pieces:]
     turned, refs = refs[-1], refs[:-1]
     if not first:
@@ -120,7 +122,7 @@
     values = pieces[0]
     if n_pieces > 1:
         values, refs = refs[0], refs[1:]
-        join_pieces(meta, pieces, values, spot[-1])
+        join_pieces(meta, pieces, values, firsts)
     total = refs[-1]
     total[...] = jnp.zeros_like(total) if first else before[...]
     every = slice(None)
@@ -142,7 +144,9 @@
         )
         return [(total, every, lanes, term)]
 
-    @pl.when(meta[1 + spot[0]] > spot[-1])
+    begin, end = (meta[BOUNDS + STEPS * spot[0] + number] for number in spot[1:3])
+
+    @pl.when(end > begin)
     def loop():
         turn_waves(wave, turned, sizes[1])
         group_loop(sizes, meta, values, values.shape[2], *spot, product)
@@ -209,7 +213,9 @@
     return pltpu.CompilerParams(vmem_limit_bytes=size + VMEM_SLACK)
 
 
-def project(sizes, meta, wave, pieces, count, width, spot, total=None, last=False, us=0):
+def project(
+    sizes, meta, wave, pieces, count, width, spot, firsts=(), total=None, last=False, us=0
+):
     rows = wave.shape[0]
     operands = [wave, *pieces] + ([] if total is None else [total])
     shapes = []
@@ -224,7 +230,7 @@
     else:
         shapes.append(jax.ShapeDtypeStruct((rows, width), jnp.float32))
     result = pl.pallas_call(
-        functools.partial(project_kernel, sizes, len(pieces), spot, total is None, last),
+        functools.partial(project_kernel, sizes, firsts, spot, total is None, last),
         grid_spec=pltpu.PrefetchScalarGridSpec(
             num_scalar_prefetch=1,
             grid=(1,),
@@ -323,8 +329,9 @@
             for d in range(1, half)
         ]
 
-    def to_bricks(which):
+    def to_bricks(which, after):
         part = lax.dynamic_slice_in_dim(wavefunctions, which * half * points, half * points, 1)
+        part = lax.optimization_barrier((part, after))[0]
         return lax.all_to_all(
             part, "grid", split_axis=1, concat_axis=0, tiled=True, axis_index_groups=pools
         )
@@ -333,33 +340,44 @@
     sizes = (tiles, segments, blocks)
     slots = jnp.arange(tiles, dtype=jnp.int32)
     starts = [tiles * sum(PARTS[:number]) // sum(PARTS) for number in range(len(PARTS) + 1)]
-    held, range_of = slots, 0
-    for start, end in zip(starts, starts[1:]):
+    held, range_of, bases = slots, 0, [0]
+    for part in ORDER:
+        start, end = starts[part], starts[part + 1]
         share = (end - start) // 4
         quarter, rest = (slots - start) // share, (slots - start) % share
-        at = start + rest + share * ((quarter // 2 ^ group) + 2 * (quarter % 2 ^ core))
-        held = jnp.where((slots >= start) & (slots < end), at, held)
-    for first, end in RANGES[1:]:
-        range_of += jnp.where(slots >= starts[first], 1, 0)
-
-    own_wave = to_bricks(side)
-    other_wave = to_bricks(1 - side)
+        at = bases[-1] + rest + share * ((quarter // 2 ^ group) + 2 * (quarter % 2 ^ core))
+        inside = (slots >= start) & (slots < end)
+        held = jnp.where(inside, at, held)
+        later = sum(len(bases) > first for first, end in RANGES[1:])
+        range_of += jnp.where(inside, later, 0)
+        bases.append(bases[-1] + end - start)
+
     matrix = two_parts(coupling_matrix(coupling))
 
-    arrived, pieces, across = [], [], None
-    source = projectors
-    for number, (start, end) in enumerate(zip(starts, starts[1:])):
+    neighbours = [
+        (i, i // half * half + (i % half ^ max(1, half // 2))) for i in range(n_grid)
+    ]
+
+    def quarter_of(source, start, end):
         share = (end - start) // 4
-        start += (2 * group + core) * share
-        sent = lax.dynamic_slice_in_dim(source, start, share, 0)
-        if number == 0:
-            sent, source = lax.optimization_barrier((sent, source))
-        if number > 0:
-            sent = lax.optimization_barrier((sent, arrived[0]))[0]
-        arrived.append(lax.ppermute(sent, "grid", partners))
-
+        return lax.dynamic_slice_in_dim(source, start + (2 * group + core) * share, share, 0)
+
+    first = quarter_of(projectors, starts[0], starts[1])
+    first, source = lax.optimization_barrier((first, projectors))
+    first = lax.ppermute(first, "grid", partners)
+    upper = quarter_of(source, starts[2], starts[3])
+    middle = upper.shape[0] // 2
+    taken = lax.ppermute(upper[middle:], "grid", neighbours)
+    upper = jnp.where(tile_count[0] > starts[2], upper[:middle], taken)
+    upper = lax.ppermute(lax.optimization_barrier((upper, first))[0], "grid", partners)
+    second = quarter_of(source, starts[1], starts[2])
+    second = lax.ppermute(lax.optimization_barrier((second, first))[0], "grid", partners)
+    rest = lax.ppermute(upper, "grid", neighbours)
+
+    own_wave = to_bricks(side, first)
+    other_wave = to_bricks(1 - side, first)
     numbers = jnp.stack([tile_segment, tile_block, jnp.broadcast_to(tile_count, (tiles,))])
-    numbers = lax.optimization_barrier((numbers, arrived[0]))[0]
+    numbers = lax.optimization_barrier((numbers, first))[0]
     others = lax.ppermute(numbers, "grid", partners)
     absent = segments << bits(tiles)
     segment, block = (jnp.stack([numbers[i], others[i]]) for i in (0, 1))
@@ -374,33 +392,37 @@
         ]
     )
 
-    own_wave = lax.optimization_barrier((own_wave, arrived[-1]))[0]
     own_spot = (OWN, 0, len(RANGES), 0)
     total, own_tiles = project(
         sizes, meta, own_wave, [projectors], half, width, own_spot, us=10
     )
-    for number, mine in enumerate(arrived):
-        sent = mine
-        if number == 1:
-            sent, across, matrix = lax.optimization_barrier((sent, across, matrix))
-        if number == 2:
-            sent, across, other_wave = lax.optimization_barrier((sent, across, other_wave))
-        across = lax.ppermute(sent, "groups", swap)
-        pieces += [mine, across]
-        pieces += [lax.ppermute(mine, "band", swap), lax.ppermute(across, "band", swap)]
+
+    def over_groups(block):
+        return lax.ppermute(block, "groups", swap)
+
+    def to_core(blocks):
+        return blocks + [lax.ppermute(block, "band", swap) for block in blocks]
+
+    held_first = [first, over_groups(first)]
+    sent, total, matrix, held_first = lax.optimization_barrier((second, total, matrix, held_first))
+    held_second = [second, over_groups(sent)]
+    held_second, other_wave = lax.optimization_barrier((held_second, other_wave))
+    held_upper = [upper, rest, over_groups(upper), over_groups(rest)]
+    pieces = [to_core(blocks) for blocks in (held_first, held_upper, held_second)]
 
     joined, other_spots = [], []
     for number, (first, end) in enumerate(RANGES):
-        other_spots.append((OTHER, number, number + 1, starts[first]))
+        other_spots.append((OTHER, number, number + 1, bases[first]))
         last = end == len(PARTS)
         total, tiles_held = project(
             sizes,
             meta,
             other_wave,
-            pieces[4 * first : 4 * end],
+            sum(pieces[first:end], []),
             half,
             width,
             other_spots[-1],
+            sum(([starts[ORDER[at]]] * len(pieces[at]) for at in range(first, end)), []),
             total,
             last=last,
             us=0 if last else 8,

time: 177 us -> 193 us (1.090)
  the two profiles are of different devices: /device:TPU:16 before, /device:TPU:26 now
where the time goes in v13:
time: 193 us; the launch traced here: 192 us
  waiting for transfers between devices  70.7 us (37%)
  local copies, waits for them, and re-layouts  43 us (22%)
  starting transfers between devices  32.9 us (17%)
  Pallas kernels  29.6 us (15%)
  other arithmetic  14.9 us (8%)
    ppermute x12, waiting for transfers between devices, exchange(): lax.ppermute(blocks[d], 'grid', [(i, i // half * half + (i % half ^ d)) f...  32.9 us
    ppermute x1, waiting for transfers between devices, body(): lax.ppermute(lax.optimization_barrier((upper, first))[0], 'grid', partners)  24 us
    unnamed x54, local copies, waits for them, and re-layouts  19.7 us
    pallas_call x3, Pallas kernels, project(): pl.pallas_call(functools.partial(project_kernel, sizes, firsts, spot, tot...  15.8 us
    ppermute x12, starting transfers between devices, exchange(): lax.ppermute(blocks[d], 'grid', [(i, i // half * half + (i % half ^ d)) f...  14.2 us
    pallas_call x2, Pallas kernels, spread(): pl.pallas_call(functools.partial(spread_kernel, sizes, len(applied), spot...  12.9 us
    all_to_all x2, starting transfers between devices, to_bricks(): lax.all_to_all(part, 'grid', split_axis=1, concat_axis=0, tiled=True, axi...  10.3 us
    ppermute x4, waiting for transfers between devices, over_groups(): return lax.ppermute(block, 'groups', swap)  9.41 us
  transfers between devices with their start and end apart: 32, of which 15 were waited for; matrix products, arithmetic and copies ran while one was open for 19% of the time, Pallas kernels for 8%

profile of v13, /device:TPU:26, one launch (start us, length us, event | category | flops | bytes accessed | tf_op | source)
XLA Modules:
  0.0 192.1 jit_solution(16109753757018510630)
XLA Ops:
  1.4 1.8 constant_dynamic-slice_fusion
  6.8 1.9 copy.17
  10.4 1.9 subtract_convert_fusion.low_ref
  13.8 2.7 %constant_dynamic-slice_fusion.1 = (bf16[32,16384]{1,0:T(8,128)(2,1)}, bf16[32,16384]{1,0:T(8,128)(2,1)S(1)}) fusion(bf16[32,32768]{1,0:T(8,128)(2,1)} %param.6, s32[]{:T(128)S(6)} %select_n.395, s32[]{:T(128)S(6)} %select_n.392), kind=kLoop, calls=%fused_computation.43 | loop fusion | bytes 4194312 | tf_op jit(solution)/shard_map/dynamic_slice | solution.py:333
  19.5 1.8 collective-permute-done.refs_0_
  24.5 5.1 %all-to-all-start = ((bf16[32,4,4096]{2,0,1:T(8,128)(2,1)}), bf16[32,4,4096]{2,0,1:T(8,128)(2,1)S(1)}, u32[]{:S(2)}, u32[]{:S(2)}) async-start(bf16[32,4,4096]{2,0,1:T(8,128)(2,1)} %bitcast.28), calls=%async_computation | async-start | bytes 2097152 | tf_op jit(solution)/shard_map/all_to_all | solution.py:335
  30.4 2.2 %dynamic-slice_select_fusion = (bf16[24,64,128]{2,1,0:T(8,128)(2,1)}, bf16[24,64,128]{2,1,0:T(8,128)(2,1)}) fusion(bf16[24,64,128]{2,1,0:T(8,128)(2,1)} %collective-permute-done.9, bf16[384,64,128]{2,1,0:T(8,128)(2,1)} %refs_4_.1, s32[]{:T(128)S(6)} %select_n.397, pred[]{:T(512)S(6)} %gt.3, s32[]{:T(128)S(6)} %select_n.390), kind=kLoop, calls=%fused_computation.9 | loop fusion | flops 196608 | bytes 1966089 | tf_op jit(solution)/shard_map/jit(_where)/select_n | solution.py:371
  34.9 1.7 collective-permute-start.10
  44.9 24.0 %collective-permute-done.10.refs_4_ = bf16[24,64,128]{2,1,0:T(8,128)(2,1)} collective-permute-done((bf16[24,64,128]{2,1,0:T(8,128)(2,1)}, bf16[24,64,128]{2,1,0:T(8,128)(2,1)}, u32[]{:S(2)}, u32[]{:S(2)}) %collective-permute-start.10) | collective-permute-done | bytes 393248 | tf_op jit(solution)/shard_map/ppermute | solution.py:372
  74.3 2.0 %concatenate.26.meta = s32[1225]{0:T(1024)S(1)} concatenate(s32[1]{0:T(128)} %bitcast, s32[1]{0:T(128)} %bitcast.2, s32[1]{0:T(128)} %bitcast.3, s32[6]{0:T(128)} %reshape.790, s32[1216]{0:T(1024)S(1)} %add.471), dimensions={0} | concatenate | bytes 9800 | tf_op jit(solution)/shard_map/concatenate | solution.py:388
  79.5 5.3 %all-to-all-start.1 = ((bf16[32,4,4096]{2,0,1:T(8,128)(2,1)}), bf16[32,4,4096]{2,0,1:T(8,128)(2,1)S(1)}, u32[]{:S(2)}, u32[]{:S(2)}) async-start(bf16[32,4,4096]{2,0,1:T(8,128)(2,1)} %bitcast.27), calls=%async_computation.1 | async-start | bytes 2097152 | tf_op jit(solution)/shard_map/all_to_all | solution.py:335
  84.8 2.8 %copy-done = bf16[384,64,128]{2,1,0:T(8,128)(2,1)S(1)} copy-done((bf16[384,64,128]{2,1,0:T(8,128)(2,1)S(1)}, bf16[384,64,128]{2,1,0:T(8,128)(2,1)}, u32[]{:S(2)}) %copy-start) | copy-done | bytes 6291480
  88.8 2.8 %shard_map.67.refs_12_ = f32[128,4096]{1,0:T(8,128)S(1)} custom-call(s32[1225]{0:T(1024)S(1)} %concatenate.26.meta, bf16[128,4096]{1,0:T(8,128)(2,1)S(1)} %bitcast.24, bf16[384,64,128]{2,1,0:T(8,128)(2,1)S(1)} %copy-done), custom_call_target="tpu_custom_call" | custom-call | flops 10000000000 | bytes 1 | tf_op jit(solution)/shard_map/pallas_call | solution.py:232
  94.5 9.4 %collective-permute-done.4.refs_1_ = bf16[24,64,128]{2,1,0:T(8,128)(2,1)S(1)} collective-permute-done((bf16[24,64,128]{2,1,0:T(8,128)(2,1)S(1)}, bf16[24,64,128]{2,1,0:T(8,128)(2,1)S(1)}, u32[]{:S(2)}, u32[]{:S(2)}) %collective-permute-start.4) | collective-permute-done | bytes 393248 | tf_op jit(solution)/shard_map/ppermute | solution.py:401
  108.4 9.2 %shard_map.68 = (bf16[288,64,128]{2,1,0:T(8,128)(2,1)S(1)}, f32[128,4096]{1,0:T(8,128)S(1)}) custom-call(s32[1225]{0:T(1024)S(1)} %concatenate.26.meta, bf16[128,4096]{1,0:T(8,128)(2,1)S(1)} %bitcast.22, bf16[24,64,128]{2,1,0:T(8,128)(2,1)} %collective-permute-done.refs_0_, bf16[24,64,128]{2,1,0:T(8,128)(2,1)} %collective-permute-done.3.refs_1_, ...), custom_call_target="tpu_custom_call" | custom-call | flops 8000000000 | bytes 1 | tf_op jit(solution)/shard_map/pallas_call | solution.py:232
  117.6 2.1 %copy-done.2 = bf16[288,64,128]{2,1,0:T(8,128)(2,1)} copy-done((bf16[288,64,128]{2,1,0:T(8,128)(2,1)}, bf16[288,64,128]{2,1,0:T(8,128)(2,1)S(1)}, u32[]{:S(2)}) %copy-start.2) | copy-done | bytes 4718616
  119.7 3.8 %shard_map.69 = (bf16[96,64,128]{2,1,0:T(8,128)(2,1)S(1)}, bf16[32,4096]{1,0:T(8,128)(2,1)S(1)}, bf16[32,4096]{1,0:T(8,128)(2,1)S(1)}, bf16[32,4096]{1,0:T(8,128)(2,1)S(1)}, bf16[32,4096]{1,0:T(8,128)(2,1)S(1)}) custom-call(s32[1225]{0:T(1024)S(1)} %concatenate.26.meta, bf16[128,4096]{1,0:T(8,128)(2,1)S(1)} %bitcast.23, ...), custom_call_target="tpu_custom_call" | custom-call | flops 1 | bytes 1 | tf_op jit(solution)/shard_map/pallas_call | solution.py:232
  123.7 3.4 %collective-permute-start.20 = (bf16[32,4096]{1,0:T(8,128)(2,1)S(1)}, bf16[32,4096]{1,0:T(8,128)(2,1)S(1)}, u32[]{:S(2)}, u32[]{:S(2)}) collective-permute-start(bf16[32,4096]{1,0:T(8,128)(2,1)S(1)} %get-tuple-element.56), channel_id=1, source_target_pairs={{0,6},{2,4},{4,2},{6,0},{8,14},{10,12},{12,10},{14,8},{1,7},{3,5},... | collective-permute-start | bytes 786440 | tf_op jit(solution)/shard_map/ppermute | solution.py:326
  127.1 4.9 %collective-permute-done.18.refs_1_ = bf16[32,4096]{1,0:T(8,128)(2,1)S(1)} collective-permute-done((bf16[32,4096]{1,0:T(8,128)(2,1)S(1)}, bf16[32,4096]{1,0:T(8,128)(2,1)S(1)}, u32[]{:S(2)}, u32[]{:S(2)}) %collective-permute-start.18) | collective-permute-done | bytes 262176 | tf_op jit(solution)/shard_map/ppermute | solution.py:326
  132.8 5.9 %collective-permute-done.20.refs_3_ = bf16[32,4096]{1,0:T(8,128)(2,1)S(1)} collective-permute-done((bf16[32,4096]{1,0:T(8,128)(2,1)S(1)}, bf16[32,4096]{1,0:T(8,128)(2,1)S(1)}, u32[]{:S(2)}, u32[]{:S(2)}) %collective-permute-start.20) | collective-permute-done | bytes 262176 | tf_op jit(solution)/shard_map/ppermute | solution.py:326
  140.3 2.8 %collective-permute-start.23 = (bf16[32,4096]{1,0:T(8,128)(2,1)S(1)}, bf16[32,4096]{1,0:T(8,128)(2,1)S(1)}, u32[]{:S(2)}, u32[]{:S(2)}) collective-permute-start(bf16[32,4096]{1,0:T(8,128)(2,1)S(1)} %shard_map.70.refs_0_), channel_id=1, source_target_pairs={{0,6},{2,4},{4,2},{6,0},{8,14},{10,12},{12,10},{14,8},{1,7},{3,5},... | collective-permute-start | bytes 786440 | tf_op jit(solution)/shard_map/ppermute | solution.py:326
  143.2 4.8 %collective-permute-done.21.refs_1_ = bf16[32,4096]{1,0:T(8,128)(2,1)S(1)} collective-permute-done((bf16[32,4096]{1,0:T(8,128)(2,1)S(1)}, bf16[32,4096]{1,0:T(8,128)(2,1)S(1)}, u32[]{:S(2)}, u32[]{:S(2)}) %collective-permute-start.21) | collective-permute-done | bytes 262176 | tf_op jit(solution)/shard_map/ppermute | solution.py:326
  149.3 4.4 %collective-permute-done.23.refs_3_ = bf16[32,4096]{1,0:T(8,128)(2,1)S(1)} collective-permute-done((bf16[32,4096]{1,0:T(8,128)(2,1)S(1)}, bf16[32,4096]{1,0:T(8,128)(2,1)S(1)}, u32[]{:S(2)}, u32[]{:S(2)}) %collective-permute-start.23) | collective-permute-done | bytes 262176 | tf_op jit(solution)/shard_map/ppermute | solution.py:326
  153.7 2.3 %copy-done.3 = bf16[288,64,128]{2,1,0:T(8,128)(2,1)S(1)} copy-done((bf16[288,64,128]{2,1,0:T(8,128)(2,1)S(1)}, bf16[288,64,128]{2,1,0:T(8,128)(2,1)}, u32[]{:S(2)}) %copy-start.3) | copy-done | bytes 4718616
  157.4 9.9 %shard_map.71 = (bf16[32,4096]{1,0:T(8,128)(2,1)S(1)}, bf16[32,4096]{1,0:T(8,128)(2,1)S(1)}, bf16[32,4096]{1,0:T(8,128)(2,1)S(1)}, bf16[32,4096]{1,0:T(8,128)(2,1)S(1)}) custom-call(s32[1225]{0:T(1024)S(1)} %concatenate.26.meta, bf16[32,4096]{1,0:T(8,128)(2,1)S(1)} %shard_map.70.refs_0_, bf16[32,4096]{1,0:T(8,128)(2,1)S(1)} %collective-permute-done.21.refs_1_, ...), custom_call_target="tpu_custom_call" | custom-call | flops 1 | bytes 1 | tf_op jit(solution)/shard_map/pallas_call | solution.py:254
  167.5 3.4 %collective-permute-start.26 = (bf16[32,4096]{1,0:T(8,128)(2,1)S(1)}, bf16[32,4096]{1,0:T(8,128)(2,1)S(1)}, u32[]{:S(2)}, u32[]{:S(2)}) collective-permute-start(bf16[32,4096]{1,0:T(8,128)(2,1)S(1)} %get-tuple-element.62), channel_id=1, source_target_pairs={{0,6},{2,4},{4,2},{6,0},{8,14},{10,12},{12,10},{14,8},{1,7},{3,5},... | collective-permute-start | bytes 786440 | tf_op jit(solution)/shard_map/ppermute | solution.py:326
  170.9 2.8 %copy-done.1 = bf16[384,64,128]{2,1,0:T(8,128)(2,1)S(1)} copy-done((bf16[384,64,128]{2,1,0:T(8,128)(2,1)S(1)}, bf16[384,64,128]{2,1,0:T(8,128)(2,1)}, u32[]{:S(2)}) %copy-start.1) | copy-done | bytes 6291480
  173.7 3.0 %shard_map.72 = (bf16[32,4096]{1,0:T(8,128)(2,1)S(1)}, bf16[32,4096]{1,0:T(8,128)(2,1)S(1)}, bf16[32,4096]{1,0:T(8,128)(2,1)S(1)}, bf16[32,4096]{1,0:T(8,128)(2,1)S(1)}) custom-call(s32[1225]{0:T(1024)S(1)} %concatenate.26.meta, bf16[32,4096]{1,0:T(8,128)(2,1)S(1)} %shard_map.70.refs_0_, bf16[32,4096]{1,0:T(8,128)(2,1)S(1)} %collective-permute-done.21.refs_1_, ...), custom_call_target="tpu_custom_call" | custom-call | flops 1 | bytes 1 | tf_op jit(solution)/shard_map/pallas_call | solution.py:254
  178.4 2.1 %collective-permute-start.29 = (bf16[32,4096]{1,0:T(8,128)(2,1)S(1)}, bf16[32,4096]{1,0:T(8,128)(2,1)S(1)}, u32[]{:S(2)}, u32[]{:S(2)}) collective-permute-start(bf16[32,4096]{1,0:T(8,128)(2,1)S(1)} %get-tuple-element.66), channel_id=1, source_target_pairs={{0,6},{2,4},{4,2},{6,0},{8,14},{10,12},{12,10},{14,8},{1,7},{3,5},... | collective-permute-start | bytes 786440 | tf_op jit(solution)/shard_map/ppermute | solution.py:326
  180.5 2.2 %collective-permute-done.26 = bf16[32,4096]{1,0:T(8,128)(2,1)S(1)} collective-permute-done((bf16[32,4096]{1,0:T(8,128)(2,1)S(1)}, bf16[32,4096]{1,0:T(8,128)(2,1)S(1)}, u32[]{:S(2)}, u32[]{:S(2)}) %collective-permute-start.26) | collective-permute-done | bytes 262176 | tf_op jit(solution)/shard_map/ppermute | solution.py:326
  182.8 3.9 %collective-permute-done.27 = bf16[32,4096]{1,0:T(8,128)(2,1)S(1)} collective-permute-done((bf16[32,4096]{1,0:T(8,128)(2,1)S(1)}, bf16[32,4096]{1,0:T(8,128)(2,1)S(1)}, u32[]{:S(2)}, u32[]{:S(2)}) %collective-permute-start.27) | collective-permute-done | bytes 262176 | tf_op jit(solution)/shard_map/ppermute | solution.py:326
  187.5 3.9 %collective-permute-done.29 = bf16[32,4096]{1,0:T(8,128)(2,1)S(1)} collective-permute-done((bf16[32,4096]{1,0:T(8,128)(2,1)S(1)}, bf16[32,4096]{1,0:T(8,128)(2,1)S(1)}, u32[]{:S(2)}, u32[]{:S(2)}) %collective-permute-start.29) | collective-permute-done | bytes 262176 | tf_op jit(solution)/shard_map/ppermute | solution.py:326
  (148 shorter events, 51.0 us)
Async XLA Ops:
  1.0 20.3 %collective-permute-start = (bf16[24,64,128]{2,1,0:T(8,128)(2,1)S(1)}, bf16[24,64,128]{2,1,0:T(8,128)(2,1)}, u32[]{:S(2)}, u32[]{:S(2)}) collective-permute-start(bf16[24,64,128]{2,1,0:T(8,128)(2,1)S(1)} %constant_dynamic-slice_fusion.4), channel_id=1, source_target_pairs={{0,8},{2,10},{4,12},{6,14},{8,0},{10,2},{12,4},{14,6},{1,9},{3,11}... | collective-permute-start | bytes 1179656 | tf_op jit(solution)/shard_map/ppermute | solution.py:367
  3.2 27.2 %collective-permute-start.9 = (bf16[24,64,128]{2,1,0:T(8,128)(2,1)}, bf16[24,64,128]{2,1,0:T(8,128)(2,1)}, u32[]{:S(2)}, u32[]{:S(2)}) collective-permute-start(bf16[24,64,128]{2,1,0:T(8,128)(2,1)} %constant_dynamic-slice_fusion), channel_id=1, source_target_pairs={{0,4},{2,6},{4,0},{6,2},{8,12},{10,14},{12,8},{14,10},{1,5},{3,7},... | collective-permute-start | bytes 1179656 | tf_op jit(solution)/shard_map/ppermute | solution.py:370
  21.4 15.7 %collective-permute-start.1 = (s32[3,384]{1,0:T(4,128)}, s32[3,384]{1,0:T(4,128)}, u32[]{:S(2)}, u32[]{:S(2)}) collective-permute-start(s32[3,384]{1,0:T(4,128)} %add_add_fusion), channel_id=1, source_target_pairs={{0,8},{2,10},{4,12},{6,14},{8,0},{10,2},{12,4},{14,6},{1,9},{3,11}... | collective-permute-start | bytes 13832 | tf_op jit(solution)/shard_map/ppermute | solution.py:381
  24.5 54.1 %all-to-all-start = ((bf16[32,4,4096]{2,0,1:T(8,128)(2,1)}), bf16[32,4,4096]{2,0,1:T(8,128)(2,1)S(1)}, u32[]{:S(2)}, u32[]{:S(2)}) async-start(bf16[32,4,4096]{2,0,1:T(8,128)(2,1)} %bitcast.28), calls=%async_computation | async-start | bytes 2097152 | tf_op jit(solution)/shard_map/all_to_all | solution.py:335
  32.6 60.4 %collective-permute-start.2 = (bf16[24,64,128]{2,1,0:T(8,128)(2,1)}, bf16[24,64,128]{2,1,0:T(8,128)(2,1)S(1)}, u32[]{:S(2)}, u32[]{:S(2)}) collective-permute-start(bf16[24,64,128]{2,1,0:T(8,128)(2,1)} %get-tuple-element.39), channel_id=1, source_target_pairs={{0,8},{2,10},{4,12},{6,14},{8,0},{10,2},{12,4},{14,6},{1,9},{3,11}... | collective-permute-start | bytes 1179656 | tf_op jit(solution)/shard_map/ppermute | solution.py:374
  34.9 34.0 %collective-permute-start.10 = (bf16[24,64,128]{2,1,0:T(8,128)(2,1)}, bf16[24,64,128]{2,1,0:T(8,128)(2,1)}, u32[]{:S(2)}, u32[]{:S(2)}) collective-permute-start(bf16[24,64,128]{2,1,0:T(8,128)(2,1)} %get-tuple-element.50), channel_id=1, source_target_pairs={{0,8},{2,10},{4,12},{6,14},{8,0},{10,2},{12,4},{14,6},{1,9},{3,11}... | collective-permute-start | bytes 1179656 | tf_op jit(solution)/shard_map/ppermute | solution.py:372
  36.6 56.4 %collective-permute-start.3 = (bf16[24,64,128]{2,1,0:T(8,128)(2,1)}, bf16[24,64,128]{2,1,0:T(8,128)(2,1)}, u32[]{:S(2)}, u32[]{:S(2)}) collective-permute-start(bf16[24,64,128]{2,1,0:T(8,128)(2,1)} %collective-permute-done.refs_0_), channel_id=1, source_target_pairs={{0,16},{16,0},{1,17},{17,1},{2,18},{18,2},{3,19},{19,3},{4,20},{20... | collective-permute-start | bytes 1179656 | tf_op jit(solution)/shard_map/ppermute | solution.py:401
  68.8 9.2 %collective-permute-start.11 = (bf16[24,64,128]{2,1,0:T(8,128)(2,1)}, bf16[24,64,128]{2,1,0:T(8,128)(2,1)}, u32[]{:S(2)}, u32[]{:S(2)}) collective-permute-start(bf16[24,64,128]{2,1,0:T(8,128)(2,1)} %collective-permute-done.10.refs_4_), channel_id=1, source_target_pairs={{0,4},{2,6},{4,0},{6,2},{8,12},{10,14},{12,8},{14,10},{1,5},{3,7},... | collective-permute-start | bytes 1179656 | tf_op jit(solution)/shard_map/ppermute | solution.py:375
  76.3 17.2 %collective-permute-start.12 = (bf16[24,64,128]{2,1,0:T(8,128)(2,1)}, bf16[24,64,128]{2,1,0:T(8,128)(2,1)}, u32[]{:S(2)}, u32[]{:S(2)}) collective-permute-start(bf16[24,64,128]{2,1,0:T(8,128)(2,1)} %collective-permute-done.10.refs_4_), channel_id=1, source_target_pairs={{0,16},{16,0},{1,17},{17,1},{2,18},{18,2},{3,19},{19,3},{4,20},{20... | collective-permute-start | bytes 1179656 | tf_op jit(solution)/shard_map/ppermute | solution.py:401
  76.8 17.3 %collective-permute-start.14 = (bf16[24,64,128]{2,1,0:T(8,128)(2,1)}, bf16[24,64,128]{2,1,0:T(8,128)(2,1)}, u32[]{:S(2)}, u32[]{:S(2)}) collective-permute-start(bf16[24,64,128]{2,1,0:T(8,128)(2,1)} %collective-permute-done.10.refs_4_), channel_id=1, source_target_pairs={{0,1},{1,0},{2,3},{3,2},{4,5},{5,4},{6,7},{7,6},{8,9},{9,8},{10,11... | collective-permute-start | bytes 1179656 | tf_op jit(solution)/shard_map/ppermute | solution.py:404
  78.0 16.0 %collective-permute-start.13 = (bf16[24,64,128]{2,1,0:T(8,128)(2,1)}, bf16[24,64,128]{2,1,0:T(8,128)(2,1)}, u32[]{:S(2)}, u32[]{:S(2)}) collective-permute-start(bf16[24,64,128]{2,1,0:T(8,128)(2,1)} %collective-permute-done.11.refs_5_), channel_id=1, source_target_pairs={{0,16},{16,0},{1,17},{17,1},{2,18},{18,2},{3,19},{19,3},{4,20},{20... | collective-permute-start | bytes 1179656 | tf_op jit(solution)/shard_map/ppermute | solution.py:401
  79.5 25.2 %all-to-all-start.1 = ((bf16[32,4,4096]{2,0,1:T(8,128)(2,1)}), bf16[32,4,4096]{2,0,1:T(8,128)(2,1)S(1)}, u32[]{:S(2)}, u32[]{:S(2)}) async-start(bf16[32,4,4096]{2,0,1:T(8,128)(2,1)} %bitcast.27), calls=%async_computation.1 | async-start | bytes 2097152 | tf_op jit(solution)/shard_map/all_to_all | solution.py:335
  93.0 11.0 %collective-permute-start.4 = (bf16[24,64,128]{2,1,0:T(8,128)(2,1)S(1)}, bf16[24,64,128]{2,1,0:T(8,128)(2,1)S(1)}, u32[]{:S(2)}, u32[]{:S(2)}) collective-permute-start(bf16[24,64,128]{2,1,0:T(8,128)(2,1)S(1)} %collective-permute-done.2.refs_0_), channel_id=1, source_target_pairs={{0,16},{16,0},{1,17},{17,1},{2,18},{18,2},{3,19},{19,3},{4,20},{20... | collective-permute-start | bytes 1179656 | tf_op jit(solution)/shard_map/ppermute | solution.py:401
  93.5 11.2 %collective-permute-start.15 = (bf16[24,64,128]{2,1,0:T(8,128)(2,1)}, bf16[24,64,128]{2,1,0:T(8,128)(2,1)}, u32[]{:S(2)}, u32[]{:S(2)}) collective-permute-start(bf16[24,64,128]{2,1,0:T(8,128)(2,1)} %collective-permute-done.11.refs_5_), channel_id=1, source_target_pairs={{0,1},{1,0},{2,3},{3,2},{4,5},{5,4},{6,7},{7,6},{8,9},{9,8},{10,11... | collective-permute-start | bytes 1179656 | tf_op jit(solution)/shard_map/ppermute | solution.py:404
  93.5 11.8 %collective-permute-start.16 = (bf16[24,64,128]{2,1,0:T(8,128)(2,1)}, bf16[24,64,128]{2,1,0:T(8,128)(2,1)}, u32[]{:S(2)}, u32[]{:S(2)}) collective-permute-start(bf16[24,64,128]{2,1,0:T(8,128)(2,1)} %collective-permute-done.12.refs_6_), channel_id=1, source_target_pairs={{0,1},{1,0},{2,3},{3,2},{4,5},{5,4},{6,7},{7,6},{8,9},{9,8},{10,11... | collective-permute-start | bytes 1179656 | tf_op jit(solution)/shard_map/ppermute | solution.py:404
  94.0 11.4 %collective-permute-start.17 = (bf16[24,64,128]{2,1,0:T(8,128)(2,1)}, bf16[24,64,128]{2,1,0:T(8,128)(2,1)}, u32[]{:S(2)}, u32[]{:S(2)}) collective-permute-start(bf16[24,64,128]{2,1,0:T(8,128)(2,1)} %collective-permute-done.13.refs_7_), channel_id=1, source_target_pairs={{0,1},{1,0},{2,3},{3,2},{4,5},{5,4},{6,7},{7,6},{8,9},{9,8},{10,11... | collective-permute-start | bytes 1179656 | tf_op jit(solution)/shard_map/ppermute | solution.py:404
  94.1 11.3 %collective-permute-start.7 = (bf16[24,64,128]{2,1,0:T(8,128)(2,1)}, bf16[24,64,128]{2,1,0:T(8,128)(2,1)}, u32[]{:S(2)}, u32[]{:S(2)}) collective-permute-start(bf16[24,64,128]{2,1,0:T(8,128)(2,1)} %collective-permute-done.refs_0_), channel_id=1, source_target_pairs={{0,1},{1,0},{2,3},{3,2},{4,5},{5,4},{6,7},{7,6},{8,9},{9,8},{10,11... | collective-permute-start | bytes 1179656 | tf_op jit(solution)/shard_map/ppermute | solution.py:404
  104.7 2.1 %collective-permute-start.8 = (bf16[24,64,128]{2,1,0:T(8,128)(2,1)}, bf16[24,64,128]{2,1,0:T(8,128)(2,1)}, u32[]{:S(2)}, u32[]{:S(2)}) collective-permute-start(bf16[24,64,128]{2,1,0:T(8,128)(2,1)} %collective-permute-done.3.refs_1_), channel_id=1, source_target_pairs={{0,1},{1,0},{2,3},{3,2},{4,5},{5,4},{6,7},{7,6},{8,9},{9,8},{10,11... | collective-permute-start | bytes 1179656 | tf_op jit(solution)/shard_map/ppermute | solution.py:404
  104.7 15.0 %collective-permute-start.5 = (bf16[24,64,128]{2,1,0:T(8,128)(2,1)S(1)}, bf16[24,64,128]{2,1,0:T(8,128)(2,1)S(1)}, u32[]{:S(2)}, u32[]{:S(2)}) collective-permute-start(bf16[24,64,128]{2,1,0:T(8,128)(2,1)S(1)} %collective-permute-done.2.refs_0_), channel_id=1, source_target_pairs={{0,1},{1,0},{2,3},{3,2},{4,5},{5,4},{6,7},{7,6},{8,9},{9,8},{10,11... | collective-permute-start | bytes 1179656 | tf_op jit(solution)/shard_map/ppermute | solution.py:404
  105.3 14.4 %collective-permute-start.6 = (bf16[24,64,128]{2,1,0:T(8,128)(2,1)}, bf16[24,64,128]{2,1,0:T(8,128)(2,1)S(1)}, u32[]{:S(2)}, u32[]{:S(2)}) collective-permute-start(bf16[24,64,128]{2,1,0:T(8,128)(2,1)} %copy-done.8), channel_id=1, source_target_pairs={{0,1},{1,0},{2,3},{3,2},{4,5},{5,4},{6,7},{7,6},{8,9},{9,8},{10,11... | collective-permute-start | bytes 1179656 | tf_op jit(solution)/shard_map/ppermute | solution.py:404
  123.5 8.4 %collective-permute-start.18 = (bf16[32,4096]{1,0:T(8,128)(2,1)S(1)}, bf16[32,4096]{1,0:T(8,128)(2,1)S(1)}, u32[]{:S(2)}, u32[]{:S(2)}) collective-permute-start(bf16[32,4096]{1,0:T(8,128)(2,1)S(1)} %get-tuple-element.54), channel_id=1, source_target_pairs={{0,2},{2,0},{4,6},{6,4},{8,10},{10,8},{12,14},{14,12},{1,3},{3,1},... | collective-permute-start | bytes 786440 | tf_op jit(solution)/shard_map/ppermute | solution.py:326
  123.6 9.2 %collective-permute-start.19 = (bf16[32,4096]{1,0:T(8,128)(2,1)S(1)}, bf16[32,4096]{1,0:T(8,128)(2,1)S(1)}, u32[]{:S(2)}, u32[]{:S(2)}) collective-permute-start(bf16[32,4096]{1,0:T(8,128)(2,1)S(1)} %get-tuple-element.55), channel_id=1, source_target_pairs={{0,4},{2,6},{4,0},{6,2},{8,12},{10,14},{12,8},{14,10},{1,5},{3,7},... | collective-permute-start | bytes 786440 | tf_op jit(solution)/shard_map/ppermute | solution.py:326
  123.7 15.1 %collective-permute-start.20 = (bf16[32,4096]{1,0:T(8,128)(2,1)S(1)}, bf16[32,4096]{1,0:T(8,128)(2,1)S(1)}, u32[]{:S(2)}, u32[]{:S(2)}) collective-permute-start(bf16[32,4096]{1,0:T(8,128)(2,1)S(1)} %get-tuple-element.56), channel_id=1, source_target_pairs={{0,6},{2,4},{4,2},{6,0},{8,14},{10,12},{12,10},{14,8},{1,7},{3,5},... | collective-permute-start | bytes 786440 | tf_op jit(solution)/shard_map/ppermute | solution.py:326
  139.7 8.3 %collective-permute-start.21 = (bf16[32,4096]{1,0:T(8,128)(2,1)S(1)}, bf16[32,4096]{1,0:T(8,128)(2,1)S(1)}, u32[]{:S(2)}, u32[]{:S(2)}) collective-permute-start(bf16[32,4096]{1,0:T(8,128)(2,1)S(1)} %shard_map.70.refs_0_), channel_id=1, source_target_pairs={{0,2},{2,0},{4,6},{6,4},{8,10},{10,8},{12,14},{14,12},{1,3},{3,1},... | collective-permute-start | bytes 786440 | tf_op jit(solution)/shard_map/ppermute | solution.py:326
  140.0 9.2 %collective-permute-start.22 = (bf16[32,4096]{1,0:T(8,128)(2,1)S(1)}, bf16[32,4096]{1,0:T(8,128)(2,1)S(1)}, u32[]{:S(2)}, u32[]{:S(2)}) collective-permute-start(bf16[32,4096]{1,0:T(8,128)(2,1)S(1)} %shard_map.70.refs_0_), channel_id=1, source_target_pairs={{0,4},{2,6},{4,0},{6,2},{8,12},{10,14},{12,8},{14,10},{1,5},{3,7},... | collective-permute-start | bytes 786440 | tf_op jit(solution)/shard_map/ppermute | solution.py:326
  140.3 13.3 %collective-permute-start.23 = (bf16[32,4096]{1,0:T(8,128)(2,1)S(1)}, bf16[32,4096]{1,0:T(8,128)(2,1)S(1)}, u32[]{:S(2)}, u32[]{:S(2)}) collective-permute-start(bf16[32,4096]{1,0:T(8,128)(2,1)S(1)} %shard_map.70.refs_0_), channel_id=1, source_target_pairs={{0,6},{2,4},{4,2},{6,0},{8,14},{10,12},{12,10},{14,8},{1,7},{3,5},... | collective-permute-start | bytes 786440 | tf_op jit(solution)/shard_map/ppermute | solution.py:326
  167.3 11.1 %collective-permute-start.24 = (bf16[32,4096]{1,0:T(8,128)(2,1)S(1)}, bf16[32,4096]{1,0:T(8,128)(2,1)S(1)}, u32[]{:S(2)}, u32[]{:S(2)}) collective-permute-start(bf16[32,4096]{1,0:T(8,128)(2,1)S(1)} %get-tuple-element.60), channel_id=1, source_target_pairs={{0,2},{2,0},{4,6},{6,4},{8,10},{10,8},{12,14},{14,12},{1,3},{3,1},... | collective-permute-start | bytes 786440 | tf_op jit(solution)/shard_map/ppermute | solution.py:326
  167.4 13.1 %collective-permute-start.25 = (bf16[32,4096]{1,0:T(8,128)(2,1)S(1)}, bf16[32,4096]{1,0:T(8,128)(2,1)S(1)}, u32[]{:S(2)}, u32[]{:S(2)}) collective-permute-start(bf16[32,4096]{1,0:T(8,128)(2,1)S(1)} %get-tuple-element.61), channel_id=1, source_target_pairs={{0,4},{2,6},{4,0},{6,2},{8,12},{10,14},{12,8},{14,10},{1,5},{3,7},... | collective-permute-start | bytes 786440 | tf_op jit(solution)/shard_map/ppermute | solution.py:326
  167.5 15.3 %collective-permute-start.26 = (bf16[32,4096]{1,0:T(8,128)(2,1)S(1)}, bf16[32,4096]{1,0:T(8,128)(2,1)S(1)}, u32[]{:S(2)}, u32[]{:S(2)}) collective-permute-start(bf16[32,4096]{1,0:T(8,128)(2,1)S(1)} %get-tuple-element.62), channel_id=1, source_target_pairs={{0,6},{2,4},{4,2},{6,0},{8,14},{10,12},{12,10},{14,8},{1,7},{3,5},... | collective-permute-start | bytes 786440 | tf_op jit(solution)/shard_map/ppermute | solution.py:326
  176.7 10.1 %collective-permute-start.27 = (bf16[32,4096]{1,0:T(8,128)(2,1)S(1)}, bf16[32,4096]{1,0:T(8,128)(2,1)S(1)}, u32[]{:S(2)}, u32[]{:S(2)}) collective-permute-start(bf16[32,4096]{1,0:T(8,128)(2,1)S(1)} %get-tuple-element.64), channel_id=1, source_target_pairs={{0,2},{2,0},{4,6},{6,4},{8,10},{10,8},{12,14},{14,12},{1,3},{3,1},... | collective-permute-start | bytes 786440 | tf_op jit(solution)/shard_map/ppermute | solution.py:326
  178.2 9.2 %collective-permute-start.28 = (bf16[32,4096]{1,0:T(8,128)(2,1)S(1)}, bf16[32,4096]{1,0:T(8,128)(2,1)S(1)}, u32[]{:S(2)}, u32[]{:S(2)}) collective-permute-start(bf16[32,4096]{1,0:T(8,128)(2,1)S(1)} %get-tuple-element.65), channel_id=1, source_target_pairs={{0,4},{2,6},{4,0},{6,2},{8,12},{10,14},{12,8},{14,10},{1,5},{3,7},... | collective-permute-start | bytes 786440 | tf_op jit(solution)/shard_map/ppermute | solution.py:326
  178.4 13.0 %collective-permute-start.29 = (bf16[32,4096]{1,0:T(8,128)(2,1)S(1)}, bf16[32,4096]{1,0:T(8,128)(2,1)S(1)}, u32[]{:S(2)}, u32[]{:S(2)}) collective-permute-start(bf16[32,4096]{1,0:T(8,128)(2,1)S(1)} %get-tuple-element.66), channel_id=1, source_target_pairs={{0,6},{2,4},{4,2},{6,0},{8,14},{10,12},{12,10},{14,8},{1,7},{3,5},... | collective-permute-start | bytes 786440 | tf_op jit(solution)/shard_map/ppermute | solution.py:326
  (27 other events, 121.6 us)

commit v14 on v13

--- a/solution.py
+++ b/solution.py
@@ -370,15 +370,15 @@
     taken = lax.ppermute(upper[middle:], "grid", neighbours)
     upper = jnp.where(tile_count[0] > starts[2], upper[:middle], taken)
     upper = lax.ppermute(lax.optimization_barrier((upper, first))[0], "grid", partners)
+    rest = lax.ppermute(upper, "grid", neighbours)
     second = quarter_of(source, starts[1], starts[2])
-    second = lax.ppermute(lax.optimization_barrier((second, first))[0], "grid", partners)
-    rest = lax.ppermute(upper, "grid", neighbours)
 
     own_wave = to_bricks(side, first)
     other_wave = to_bricks(1 - side, first)
     numbers = jnp.stack([tile_segment, tile_block, jnp.broadcast_to(tile_count, (tiles,))])
     numbers = lax.optimization_barrier((numbers, first))[0]
     others = lax.ppermute(numbers, "grid", partners)
+    second = lax.ppermute(lax.optimization_barrier((second, others))[0], "grid", partners)
     absent = segments << bits(tiles)
     segment, block = (jnp.stack([numbers[i], others[i]]) for i in (0, 1))
     codes = jnp.stack([slots, held])
@@ -392,9 +392,10 @@
         ]
     )
 
+    own_wave = lax.optimization_barrier((own_wave, upper))[0]
     own_spot = (OWN, 0, len(RANGES), 0)
     total, own_tiles = project(
-        sizes, meta, own_wave, [projectors], half, width, own_spot, us=10
+        sizes, meta, own_wave, [projectors], half, width, own_spot, us=5
     )
 
     def over_groups(block):
@@ -404,7 +405,7 @@
         return blocks + [lax.ppermute(block, "band", swap) for block in blocks]
 
     held_first = [first, over_groups(first)]
-    sent, total, matrix, held_first = lax.optimization_barrier((second, total, matrix, held_first))
+    sent, matrix = lax.optimization_barrier((second, matrix))
     held_second = [second, over_groups(sent)]
     held_second, other_wave = lax.optimization_barrier((held_second, other_wave))
     held_upper = [upper, rest, over_groups(upper), over_groups(rest)]

time: 193 us -> 188 us (0.974)
  the two profiles are of different devices: /device:TPU:26 before, /device:TPU:0 now
where the time goes in v14:
time: 188 us; the launch traced here: 185 us
  waiting for transfers between devices  62.7 us (33%)
  starting transfers between devices  45.3 us (24%)
  local copies, waits for them, and re-layouts  34.3 us (18%)
  Pallas kernels  24.6 us (13%)
  other arithmetic  16.7 us (9%)
    ppermute x12, waiting for transfers between devices, exchange(): lax.ppermute(blocks[d], 'grid', [(i, i // half * half + (i % half ^ d)) f...  32.6 us
    ppermute x12, starting transfers between devices, exchange(): lax.ppermute(blocks[d], 'grid', [(i, i // half * half + (i % half ^ d)) f...  18.2 us
    pallas_call x3, Pallas kernels, project(): pl.pallas_call(functools.partial(project_kernel, sizes, firsts, spot, tot...  14.3 us
    ppermute x1, waiting for transfers between devices, body(): lax.ppermute(lax.optimization_barrier((upper, first))[0], 'grid', partners)  13.2 us
    unnamed x30, local copies, waits for them, and re-layouts  12.1 us
    pallas_call x2, Pallas kernels, spread(): pl.pallas_call(functools.partial(spread_kernel, sizes, len(applied), spot...  9.35 us
    all_to_all x2, starting transfers between devices, to_bricks(): lax.all_to_all(part, 'grid', split_axis=1, concat_axis=0, tiled=True, axi...  7.75 us
    ppermute x1, waiting for transfers between devices, body(): rest = lax.ppermute(upper, 'grid', neighbours)  7.61 us
  transfers between devices with their start and end apart: 32, of which 15 were waited for; matrix products, arithmetic and copies ran while one was open for 20% of the time, Pallas kernels for 8%

profile of v14, /device:TPU:0, one launch (start us, length us, event | category | flops | bytes accessed | tf_op | source)
XLA Modules:
  0.0 184.6 jit_solution(12542153288450230986)
XLA Ops:
  1.8 4.0 %collective-permute-start = (bf16[24,64,128]{2,1,0:T(8,128)(2,1)}, bf16[24,64,128]{2,1,0:T(8,128)(2,1)}, u32[]{:S(2)}, u32[]{:S(2)}) collective-permute-start(bf16[24,64,128]{2,1,0:T(8,128)(2,1)} %constant_dynamic-slice_fusion.4), channel_id=1, source_target_pairs={{0,8},{2,10},{4,12},{6,14},{8,0},{10,2},{12,4},{14,6},{1,9},{3,11}... | collective-permute-start | bytes 1179656 | tf_op jit(solution)/shard_map/ppermute | solution.py:367
  16.5 3.3 %constant_dynamic-slice_fusion = (bf16[32,16384]{1,0:T(8,128)(2,1)}, bf16[32,16384]{1,0:T(8,128)(2,1)S(1)}) fusion(bf16[32,32768]{1,0:T(8,128)(2,1)} %param.6, s32[]{:T(128)S(6)} %select_n.398, s32[]{:T(128)S(6)} %select_n.394), kind=kLoop, calls=%fused_computation.42 | loop fusion | bytes 4194312 | tf_op jit(solution)/shard_map/dynamic_slice | solution.py:333
  21.4 2.4 %collective-permute-done.refs_0_ = bf16[24,64,128]{2,1,0:T(8,128)(2,1)} collective-permute-done((bf16[24,64,128]{2,1,0:T(8,128)(2,1)}, bf16[24,64,128]{2,1,0:T(8,128)(2,1)}, u32[]{:S(2)}, u32[]{:S(2)}) %collective-permute-start) | collective-permute-done | bytes 393248 | tf_op jit(solution)/shard_map/ppermute | solution.py:367
  24.8 3.5 %all-to-all-start = ((bf16[32,4,4096]{2,0,1:T(8,128)(2,1)}), bf16[32,4,4096]{2,0,1:T(8,128)(2,1)S(1)}, u32[]{:S(2)}, u32[]{:S(2)}) async-start(bf16[32,4,4096]{2,0,1:T(8,128)(2,1)} %bitcast.20), calls=%async_computation | async-start | bytes 2097152 | tf_op jit(solution)/shard_map/all_to_all | solution.py:335
  28.9 2.0 %subtract_convert_fusion.low_ref = bf16[32,128,128]{2,1,0:T(8,128)(2,1)S(1)} fusion(f32[32,128,128]{2,1,0:T(8,128)} %copy-done.6, pred[128,128]{1,0:T(8,128)(4,1)S(1)} %broadcast_compare_fusion), kind=kLoop, calls=%fused_computation | loop fusion | flops 2621440 | bytes 3162112 | tf_op jit(solution)/shard_map/convert_element_type | solution.py:274
  30.9 2.8 %collective-permute-start.1 = (s32[3,384]{1,0:T(4,128)}, s32[3,384]{1,0:T(4,128)S(1)}, u32[]{:S(2)}, u32[]{:S(2)}) collective-permute-start(s32[3,384]{1,0:T(4,128)} %add_add_fusion), channel_id=1, source_target_pairs={{0,8},{2,10},{4,12},{6,14},{8,0},{10,2},{12,4},{14,6},{1,9},{3,11}... | collective-permute-start | bytes 13832 | tf_op jit(solution)/shard_map/ppermute | solution.py:380
  33.8 2.2 %dynamic-slice_select_fusion = (bf16[24,64,128]{2,1,0:T(8,128)(2,1)}, bf16[24,64,128]{2,1,0:T(8,128)(2,1)}) fusion(bf16[24,64,128]{2,1,0:T(8,128)(2,1)} %collective-permute-done.9, bf16[384,64,128]{2,1,0:T(8,128)(2,1)} %refs_4_.1, s32[]{:T(128)S(6)} %select_n.396, pred[]{:T(512)S(6)} %gt.3, s32[]{:T(128)S(6)} %select_n.390), kind=kLoop, calls=%fused_computation.9 | loop fusion | flops 196608 | bytes 1966089 | tf_op jit(solution)/shard_map/jit(_where)/select_n | solution.py:371
  41.1 3.5 %collective-permute-start.2 = (bf16[24,64,128]{2,1,0:T(8,128)(2,1)}, bf16[24,64,128]{2,1,0:T(8,128)(2,1)S(1)}, u32[]{:S(2)}, u32[]{:S(2)}) collective-permute-start(bf16[24,64,128]{2,1,0:T(8,128)(2,1)} %get-tuple-element.37), channel_id=1, source_target_pairs={{0,8},{2,10},{4,12},{6,14},{8,0},{10,2},{12,4},{14,6},{1,9},{3,11}... | collective-permute-start | bytes 1179656 | tf_op jit(solution)/shard_map/ppermute | solution.py:381
  45.9 4.2 %all-to-all-start.1 = ((bf16[32,4,4096]{2,0,1:T(8,128)(2,1)}), bf16[32,4,4096]{2,0,1:T(8,128)(2,1)}, u32[]{:S(2)}, u32[]{:S(2)}) async-start(bf16[32,4,4096]{2,0,1:T(8,128)(2,1)} %bitcast.26), calls=%async_computation.1 | async-start | bytes 2097152 | tf_op jit(solution)/shard_map/all_to_all | solution.py:335
  54.8 13.2 %collective-permute-done.10.refs_4_ = bf16[24,64,128]{2,1,0:T(8,128)(2,1)} collective-permute-done((bf16[24,64,128]{2,1,0:T(8,128)(2,1)}, bf16[24,64,128]{2,1,0:T(8,128)(2,1)}, u32[]{:S(2)}, u32[]{:S(2)}) %collective-permute-start.10) | collective-permute-done | bytes 393248 | tf_op jit(solution)/shard_map/ppermute | solution.py:372
  72.4 2.3 %collective-permute-done.2.refs_0_ = bf16[24,64,128]{2,1,0:T(8,128)(2,1)S(1)} collective-permute-done((bf16[24,64,128]{2,1,0:T(8,128)(2,1)}, bf16[24,64,128]{2,1,0:T(8,128)(2,1)S(1)}, u32[]{:S(2)}, u32[]{:S(2)}) %collective-permute-start.2) | collective-permute-done | bytes 393248 | tf_op jit(solution)/shard_map/ppermute | solution.py:381
  76.2 7.6 %collective-permute-done.11.refs_5_ = bf16[24,64,128]{2,1,0:T(8,128)(2,1)} collective-permute-done((bf16[24,64,128]{2,1,0:T(8,128)(2,1)}, bf16[24,64,128]{2,1,0:T(8,128)(2,1)}, u32[]{:S(2)}, u32[]{:S(2)}) %collective-permute-start.11) | collective-permute-done | bytes 393248 | tf_op jit(solution)/shard_map/ppermute | solution.py:373
  93.3 2.7 %collective-permute-done.13.refs_7_ = bf16[24,64,128]{2,1,0:T(8,128)(2,1)} collective-permute-done((bf16[24,64,128]{2,1,0:T(8,128)(2,1)}, bf16[24,64,128]{2,1,0:T(8,128)(2,1)}, u32[]{:S(2)}, u32[]{:S(2)}) %collective-permute-start.13) | collective-permute-done | bytes 393248 | tf_op jit(solution)/shard_map/ppermute | solution.py:402
  96.0 2.8 %copy-done = bf16[384,64,128]{2,1,0:T(8,128)(2,1)S(1)} copy-done((bf16[384,64,128]{2,1,0:T(8,128)(2,1)S(1)}, bf16[384,64,128]{2,1,0:T(8,128)(2,1)}, u32[]{:S(2)}) %copy-start) | copy-done | bytes 6291480
  98.7 5.0 %shard_map.67.refs_12_ = f32[128,4096]{1,0:T(8,128)S(1)} custom-call(s32[1225]{0:T(1024)S(1)} %concatenate.26.meta, bf16[128,4096]{1,0:T(8,128)(2,1)} %bitcast.9.wave, bf16[384,64,128]{2,1,0:T(8,128)(2,1)S(1)} %copy-done), custom_call_target="tpu_custom_call" | custom-call | flops 5000000000 | bytes 1 | tf_op jit(solution)/shard_map/pallas_call | solution.py:232
  104.4 5.5 %shard_map.68 = (bf16[288,64,128]{2,1,0:T(8,128)(2,1)S(1)}, f32[128,4096]{1,0:T(8,128)S(1)}) custom-call(s32[1225]{0:T(1024)S(1)} %concatenate.26.meta, bf16[128,4096]{1,0:T(8,128)(2,1)S(1)} %bitcast.22, bf16[24,64,128]{2,1,0:T(8,128)(2,1)} %collective-permute-done.refs_0_, bf16[24,64,128]{2,1,0:T(8,128)(2,1)} %collective-permute-done.6.refs_1_, ...), custom_call_target="tpu_custom_call" | custom-call | flops 8000000000 | bytes 1 | tf_op jit(solution)/shard_map/pallas_call | solution.py:232
  109.9 2.1 %copy-done.2 = bf16[288,64,128]{2,1,0:T(8,128)(2,1)} copy-done((bf16[288,64,128]{2,1,0:T(8,128)(2,1)}, bf16[288,64,128]{2,1,0:T(8,128)(2,1)S(1)}, u32[]{:S(2)}) %copy-start.2) | copy-done | bytes 4718616
  112.1 3.8 %shard_map.69 = (bf16[96,64,128]{2,1,0:T(8,128)(2,1)S(1)}, bf16[32,4096]{1,0:T(8,128)(2,1)S(1)}, bf16[32,4096]{1,0:T(8,128)(2,1)S(1)}, bf16[32,4096]{1,0:T(8,128)(2,1)S(1)}, bf16[32,4096]{1,0:T(8,128)(2,1)S(1)}) custom-call(s32[1225]{0:T(1024)S(1)} %concatenate.26.meta, bf16[128,4096]{1,0:T(8,128)(2,1)S(1)} %bitcast.23, ...), custom_call_target="tpu_custom_call" | custom-call | flops 1 | bytes 1 | tf_op jit(solution)/shard_map/pallas_call | solution.py:232
  116.0 3.7 %collective-permute-start.19 = (bf16[32,4096]{1,0:T(8,128)(2,1)S(1)}, bf16[32,4096]{1,0:T(8,128)(2,1)S(1)}, u32[]{:S(2)}, u32[]{:S(2)}) collective-permute-start(bf16[32,4096]{1,0:T(8,128)(2,1)S(1)} %get-tuple-element.51), channel_id=1, source_target_pairs={{0,4},{2,6},{4,0},{6,2},{8,12},{10,14},{12,8},{14,10},{1,5},{3,7},... | collective-permute-start | bytes 786440 | tf_op jit(solution)/shard_map/ppermute | solution.py:326
  121.1 3.5 %collective-permute-done.18.refs_1_ = bf16[32,4096]{1,0:T(8,128)(2,1)S(1)} collective-permute-done((bf16[32,4096]{1,0:T(8,128)(2,1)S(1)}, bf16[32,4096]{1,0:T(8,128)(2,1)S(1)}, u32[]{:S(2)}, u32[]{:S(2)}) %collective-permute-start.18) | collective-permute-done | bytes 262176 | tf_op jit(solution)/shard_map/ppermute | solution.py:326
  124.6 2.3 %collective-permute-done.19.refs_2_ = bf16[32,4096]{1,0:T(8,128)(2,1)S(1)} collective-permute-done((bf16[32,4096]{1,0:T(8,128)(2,1)S(1)}, bf16[32,4096]{1,0:T(8,128)(2,1)S(1)}, u32[]{:S(2)}, u32[]{:S(2)}) %collective-permute-start.19) | collective-permute-done | bytes 262176 | tf_op jit(solution)/shard_map/ppermute | solution.py:326
  126.8 6.5 %collective-permute-done.20.refs_3_ = bf16[32,4096]{1,0:T(8,128)(2,1)S(1)} collective-permute-done((bf16[32,4096]{1,0:T(8,128)(2,1)S(1)}, bf16[32,4096]{1,0:T(8,128)(2,1)S(1)}, u32[]{:S(2)}, u32[]{:S(2)}) %collective-permute-start.20) | collective-permute-done | bytes 262176 | tf_op jit(solution)/shard_map/ppermute | solution.py:326
  137.8 4.8 %collective-permute-done.21.refs_1_ = bf16[32,4096]{1,0:T(8,128)(2,1)S(1)} collective-permute-done((bf16[32,4096]{1,0:T(8,128)(2,1)S(1)}, bf16[32,4096]{1,0:T(8,128)(2,1)S(1)}, u32[]{:S(2)}, u32[]{:S(2)}) %collective-permute-start.21) | collective-permute-done | bytes 262176 | tf_op jit(solution)/shard_map/ppermute | solution.py:326
  143.8 5.1 %collective-permute-done.23.refs_3_ = bf16[32,4096]{1,0:T(8,128)(2,1)S(1)} collective-permute-done((bf16[32,4096]{1,0:T(8,128)(2,1)S(1)}, bf16[32,4096]{1,0:T(8,128)(2,1)S(1)}, u32[]{:S(2)}, u32[]{:S(2)}) %collective-permute-start.23) | collective-permute-done | bytes 262176 | tf_op jit(solution)/shard_map/ppermute | solution.py:326
  148.9 2.3 %copy-done.3 = bf16[288,64,128]{2,1,0:T(8,128)(2,1)S(1)} copy-done((bf16[288,64,128]{2,1,0:T(8,128)(2,1)S(1)}, bf16[288,64,128]{2,1,0:T(8,128)(2,1)}, u32[]{:S(2)}) %copy-start.3) | copy-done | bytes 4718616
  152.7 5.2 %shard_map.71 = (bf16[32,4096]{1,0:T(8,128)(2,1)S(1)}, bf16[32,4096]{1,0:T(8,128)(2,1)S(1)}, bf16[32,4096]{1,0:T(8,128)(2,1)S(1)}, bf16[32,4096]{1,0:T(8,128)(2,1)S(1)}) custom-call(s32[1225]{0:T(1024)S(1)} %concatenate.26.meta, bf16[32,4096]{1,0:T(8,128)(2,1)S(1)} %shard_map.70.refs_0_, bf16[32,4096]{1,0:T(8,128)(2,1)S(1)} %collective-permute-done.21.refs_1_, ...), custom_call_target="tpu_custom_call" | custom-call | flops 1 | bytes 1 | tf_op jit(solution)/shard_map/pallas_call | solution.py:254
  158.7 2.8 %collective-permute-start.26 = (bf16[32,4096]{1,0:T(8,128)(2,1)S(1)}, bf16[32,4096]{1,0:T(8,128)(2,1)S(1)}, u32[]{:S(2)}, u32[]{:S(2)}) collective-permute-start(bf16[32,4096]{1,0:T(8,128)(2,1)S(1)} %get-tuple-element.58), channel_id=1, source_target_pairs={{0,6},{2,4},{4,2},{6,0},{8,14},{10,12},{12,10},{14,8},{1,7},{3,5},... | collective-permute-start | bytes 786440 | tf_op jit(solution)/shard_map/ppermute | solution.py:326
  161.5 2.8 %copy-done.1 = bf16[384,64,128]{2,1,0:T(8,128)(2,1)S(1)} copy-done((bf16[384,64,128]{2,1,0:T(8,128)(2,1)S(1)}, bf16[384,64,128]{2,1,0:T(8,128)(2,1)}, u32[]{:S(2)}) %copy-start.1) | copy-done | bytes 6291480
  164.3 4.1 %shard_map.72 = (bf16[32,4096]{1,0:T(8,128)(2,1)S(1)}, bf16[32,4096]{1,0:T(8,128)(2,1)S(1)}, bf16[32,4096]{1,0:T(8,128)(2,1)S(1)}, bf16[32,4096]{1,0:T(8,128)(2,1)S(1)}) custom-call(s32[1225]{0:T(1024)S(1)} %concatenate.26.meta, bf16[32,4096]{1,0:T(8,128)(2,1)S(1)} %shard_map.70.refs_0_, bf16[32,4096]{1,0:T(8,128)(2,1)S(1)} %collective-permute-done.21.refs_1_, ...), custom_call_target="tpu_custom_call" | custom-call | flops 1 | bytes 1 | tf_op jit(solution)/shard_map/pallas_call | solution.py:254
  168.5 4.4 %collective-permute-start.28 = (bf16[32,4096]{1,0:T(8,128)(2,1)S(1)}, bf16[32,4096]{1,0:T(8,128)(2,1)S(1)}, u32[]{:S(2)}, u32[]{:S(2)}) collective-permute-start(bf16[32,4096]{1,0:T(8,128)(2,1)S(1)} %get-tuple-element.61), channel_id=1, source_target_pairs={{0,4},{2,6},{4,0},{6,2},{8,12},{10,14},{12,8},{14,10},{1,5},{3,7},... | collective-permute-start | bytes 786440 | tf_op jit(solution)/shard_map/ppermute | solution.py:326
  174.6 4.3 %collective-permute-done.27 = bf16[32,4096]{1,0:T(8,128)(2,1)S(1)} collective-permute-done((bf16[32,4096]{1,0:T(8,128)(2,1)S(1)}, bf16[32,4096]{1,0:T(8,128)(2,1)S(1)}, u32[]{:S(2)}, u32[]{:S(2)}) %collective-permute-start.27) | collective-permute-done | bytes 262176 | tf_op jit(solution)/shard_map/ppermute | solution.py:326
  180.0 3.9 %collective-permute-done.29 = bf16[32,4096]{1,0:T(8,128)(2,1)S(1)} collective-permute-done((bf16[32,4096]{1,0:T(8,128)(2,1)S(1)}, bf16[32,4096]{1,0:T(8,128)(2,1)S(1)}, u32[]{:S(2)}, u32[]{:S(2)}) %collective-permute-start.29) | collective-permute-done | bytes 262176 | tf_op jit(solution)/shard_map/ppermute | solution.py:326
  (124 shorter events, 54.8 us)
Async XLA Ops:
  1.8 22.0 %collective-permute-start = (bf16[24,64,128]{2,1,0:T(8,128)(2,1)}, bf16[24,64,128]{2,1,0:T(8,128)(2,1)}, u32[]{:S(2)}, u32[]{:S(2)}) collective-permute-start(bf16[24,64,128]{2,1,0:T(8,128)(2,1)} %constant_dynamic-slice_fusion.4), channel_id=1, source_target_pairs={{0,8},{2,10},{4,12},{6,14},{8,0},{10,2},{12,4},{14,6},{1,9},{3,11}... | collective-permute-start | bytes 1179656 | tf_op jit(solution)/shard_map/ppermute | solution.py:367
  6.8 27.0 %collective-permute-start.9 = (bf16[24,64,128]{2,1,0:T(8,128)(2,1)S(1)}, bf16[24,64,128]{2,1,0:T(8,128)(2,1)}, u32[]{:S(2)}, u32[]{:S(2)}) collective-permute-start(bf16[24,64,128]{2,1,0:T(8,128)(2,1)S(1)} %constant_dynamic-slice_fusion.1), channel_id=1, source_target_pairs={{0,4},{2,6},{4,0},{6,2},{8,12},{10,14},{12,8},{14,10},{1,5},{3,7},... | collective-permute-start | bytes 1179656 | tf_op jit(solution)/shard_map/ppermute | solution.py:370
  24.8 21.1 %all-to-all-start = ((bf16[32,4,4096]{2,0,1:T(8,128)(2,1)}), bf16[32,4,4096]{2,0,1:T(8,128)(2,1)S(1)}, u32[]{:S(2)}, u32[]{:S(2)}) async-start(bf16[32,4,4096]{2,0,1:T(8,128)(2,1)} %bitcast.20), calls=%async_computation | async-start | bytes 2097152 | tf_op jit(solution)/shard_map/all_to_all | solution.py:335
  30.9 10.2 %collective-permute-start.1 = (s32[3,384]{1,0:T(4,128)}, s32[3,384]{1,0:T(4,128)S(1)}, u32[]{:S(2)}, u32[]{:S(2)}) collective-permute-start(s32[3,384]{1,0:T(4,128)} %add_add_fusion), channel_id=1, source_target_pairs={{0,8},{2,10},{4,12},{6,14},{8,0},{10,2},{12,4},{14,6},{1,9},{3,11}... | collective-permute-start | bytes 13832 | tf_op jit(solution)/shard_map/ppermute | solution.py:380
  37.6 30.4 %collective-permute-start.10 = (bf16[24,64,128]{2,1,0:T(8,128)(2,1)}, bf16[24,64,128]{2,1,0:T(8,128)(2,1)}, u32[]{:S(2)}, u32[]{:S(2)}) collective-permute-start(bf16[24,64,128]{2,1,0:T(8,128)(2,1)} %get-tuple-element.45), channel_id=1, source_target_pairs={{0,8},{2,10},{4,12},{6,14},{8,0},{10,2},{12,4},{14,6},{1,9},{3,11}... | collective-permute-start | bytes 1179656 | tf_op jit(solution)/shard_map/ppermute | solution.py:372
  37.8 54.4 %collective-permute-start.6 = (bf16[24,64,128]{2,1,0:T(8,128)(2,1)}, bf16[24,64,128]{2,1,0:T(8,128)(2,1)}, u32[]{:S(2)}, u32[]{:S(2)}) collective-permute-start(bf16[24,64,128]{2,1,0:T(8,128)(2,1)} %collective-permute-done.refs_0_), channel_id=1, source_target_pairs={{0,16},{16,0},{1,17},{17,1},{2,18},{18,2},{3,19},{19,3},{4,20},{20... | collective-permute-start | bytes 1179656 | tf_op jit(solution)/shard_map/ppermute | solution.py:402
  39.3 53.4 %collective-permute-start.7 = (bf16[24,64,128]{2,1,0:T(8,128)(2,1)}, bf16[24,64,128]{2,1,0:T(8,128)(2,1)}, u32[]{:S(2)}, u32[]{:S(2)}) collective-permute-start(bf16[24,64,128]{2,1,0:T(8,128)(2,1)} %collective-permute-done.refs_0_), channel_id=1, source_target_pairs={{0,1},{1,0},{2,3},{3,2},{4,5},{5,4},{6,7},{7,6},{8,9},{9,8},{10,11... | collective-permute-start | bytes 1179656 | tf_op jit(solution)/shard_map/ppermute | solution.py:405
  41.1 33.6 %collective-permute-start.2 = (bf16[24,64,128]{2,1,0:T(8,128)(2,1)}, bf16[24,64,128]{2,1,0:T(8,128)(2,1)S(1)}, u32[]{:S(2)}, u32[]{:S(2)}) collective-permute-start(bf16[24,64,128]{2,1,0:T(8,128)(2,1)} %get-tuple-element.37), channel_id=1, source_target_pairs={{0,8},{2,10},{4,12},{6,14},{8,0},{10,2},{12,4},{14,6},{1,9},{3,11}... | collective-permute-start | bytes 1179656 | tf_op jit(solution)/shard_map/ppermute | solution.py:381
  45.9 46.8 %all-to-all-start.1 = ((bf16[32,4,4096]{2,0,1:T(8,128)(2,1)}), bf16[32,4,4096]{2,0,1:T(8,128)(2,1)}, u32[]{:S(2)}, u32[]{:S(2)}) async-start(bf16[32,4,4096]{2,0,1:T(8,128)(2,1)} %bitcast.26), calls=%async_computation.1 | async-start | bytes 2097152 | tf_op jit(solution)/shard_map/all_to_all | solution.py:335
  68.0 15.8 %collective-permute-start.11 = (bf16[24,64,128]{2,1,0:T(8,128)(2,1)}, bf16[24,64,128]{2,1,0:T(8,128)(2,1)}, u32[]{:S(2)}, u32[]{:S(2)}) collective-permute-start(bf16[24,64,128]{2,1,0:T(8,128)(2,1)} %collective-permute-done.10.refs_4_), channel_id=1, source_target_pairs={{0,4},{2,6},{4,0},{6,2},{8,12},{10,14},{12,8},{14,10},{1,5},{3,7},... | collective-permute-start | bytes 1179656 | tf_op jit(solution)/shard_map/ppermute | solution.py:373
  70.8 22.0 %collective-permute-start.12 = (bf16[24,64,128]{2,1,0:T(8,128)(2,1)}, bf16[24,64,128]{2,1,0:T(8,128)(2,1)}, u32[]{:S(2)}, u32[]{:S(2)}) collective-permute-start(bf16[24,64,128]{2,1,0:T(8,128)(2,1)} %collective-permute-done.10.refs_4_), channel_id=1, source_target_pairs={{0,16},{16,0},{1,17},{17,1},{2,18},{18,2},{3,19},{19,3},{4,20},{20... | collective-permute-start | bytes 1179656 | tf_op jit(solution)/shard_map/ppermute | solution.py:402
  74.7 17.5 %collective-permute-start.3 = (bf16[24,64,128]{2,1,0:T(8,128)(2,1)S(1)}, bf16[24,64,128]{2,1,0:T(8,128)(2,1)}, u32[]{:S(2)}, u32[]{:S(2)}) collective-permute-start(bf16[24,64,128]{2,1,0:T(8,128)(2,1)S(1)} %collective-permute-done.2.refs_0_), channel_id=1, source_target_pairs={{0,16},{16,0},{1,17},{17,1},{2,18},{18,2},{3,19},{19,3},{4,20},{20... | collective-permute-start | bytes 1179656 | tf_op jit(solution)/shard_map/ppermute | solution.py:402
  83.8 12.1 %collective-permute-start.13 = (bf16[24,64,128]{2,1,0:T(8,128)(2,1)}, bf16[24,64,128]{2,1,0:T(8,128)(2,1)}, u32[]{:S(2)}, u32[]{:S(2)}) collective-permute-start(bf16[24,64,128]{2,1,0:T(8,128)(2,1)} %collective-permute-done.11.refs_5_), channel_id=1, source_target_pairs={{0,16},{16,0},{1,17},{17,1},{2,18},{18,2},{3,19},{19,3},{4,20},{20... | collective-permute-start | bytes 1179656 | tf_op jit(solution)/shard_map/ppermute | solution.py:402
  92.1 11.6 %collective-permute-start.14 = (bf16[24,64,128]{2,1,0:T(8,128)(2,1)}, bf16[24,64,128]{2,1,0:T(8,128)(2,1)}, u32[]{:S(2)}, u32[]{:S(2)}) collective-permute-start(bf16[24,64,128]{2,1,0:T(8,128)(2,1)} %collective-permute-done.10.refs_4_), channel_id=1, source_target_pairs={{0,1},{1,0},{2,3},{3,2},{4,5},{5,4},{6,7},{7,6},{8,9},{9,8},{10,11... | collective-permute-start | bytes 1179656 | tf_op jit(solution)/shard_map/ppermute | solution.py:405
  92.2 12.1 %collective-permute-start.8 = (bf16[24,64,128]{2,1,0:T(8,128)(2,1)}, bf16[24,64,128]{2,1,0:T(8,128)(2,1)}, u32[]{:S(2)}, u32[]{:S(2)}) collective-permute-start(bf16[24,64,128]{2,1,0:T(8,128)(2,1)} %collective-permute-done.6.refs_1_), channel_id=1, source_target_pairs={{0,1},{1,0},{2,3},{3,2},{4,5},{5,4},{6,7},{7,6},{8,9},{9,8},{10,11... | collective-permute-start | bytes 1179656 | tf_op jit(solution)/shard_map/ppermute | solution.py:405
  92.7 11.7 %collective-permute-start.15 = (bf16[24,64,128]{2,1,0:T(8,128)(2,1)}, bf16[24,64,128]{2,1,0:T(8,128)(2,1)S(1)}, u32[]{:S(2)}, u32[]{:S(2)}) collective-permute-start(bf16[24,64,128]{2,1,0:T(8,128)(2,1)} %collective-permute-done.11.refs_5_), channel_id=1, source_target_pairs={{0,1},{1,0},{2,3},{3,2},{4,5},{5,4},{6,7},{7,6},{8,9},{9,8},{10,11... | collective-permute-start | bytes 1179656 | tf_op jit(solution)/shard_map/ppermute | solution.py:405
  92.8 11.6 %collective-permute-start.16 = (bf16[24,64,128]{2,1,0:T(8,128)(2,1)}, bf16[24,64,128]{2,1,0:T(8,128)(2,1)S(1)}, u32[]{:S(2)}, u32[]{:S(2)}) collective-permute-start(bf16[24,64,128]{2,1,0:T(8,128)(2,1)} %collective-permute-done.12.refs_6_), channel_id=1, source_target_pairs={{0,1},{1,0},{2,3},{3,2},{4,5},{5,4},{6,7},{7,6},{8,9},{9,8},{10,11... | collective-permute-start | bytes 1179656 | tf_op jit(solution)/shard_map/ppermute | solution.py:405
  96.0 8.5 %collective-permute-start.17 = (bf16[24,64,128]{2,1,0:T(8,128)(2,1)}, bf16[24,64,128]{2,1,0:T(8,128)(2,1)S(1)}, u32[]{:S(2)}, u32[]{:S(2)}) collective-permute-start(bf16[24,64,128]{2,1,0:T(8,128)(2,1)} %collective-permute-done.13.refs_7_), channel_id=1, source_target_pairs={{0,1},{1,0},{2,3},{3,2},{4,5},{5,4},{6,7},{7,6},{8,9},{9,8},{10,11... | collective-permute-start | bytes 1179656 | tf_op jit(solution)/shard_map/ppermute | solution.py:405
  103.8 8.3 %collective-permute-start.4 = (bf16[24,64,128]{2,1,0:T(8,128)(2,1)S(1)}, bf16[24,64,128]{2,1,0:T(8,128)(2,1)S(1)}, u32[]{:S(2)}, u32[]{:S(2)}) collective-permute-start(bf16[24,64,128]{2,1,0:T(8,128)(2,1)S(1)} %collective-permute-done.2.refs_0_), channel_id=1, source_target_pairs={{0,1},{1,0},{2,3},{3,2},{4,5},{5,4},{6,7},{7,6},{8,9},{9,8},{10,11... | collective-permute-start | bytes 1179656 | tf_op jit(solution)/shard_map/ppermute | solution.py:405
  104.3 7.7 %collective-permute-start.5 = (bf16[24,64,128]{2,1,0:T(8,128)(2,1)}, bf16[24,64,128]{2,1,0:T(8,128)(2,1)S(1)}, u32[]{:S(2)}, u32[]{:S(2)}) collective-permute-start(bf16[24,64,128]{2,1,0:T(8,128)(2,1)} %collective-permute-done.3.refs_1_), channel_id=1, source_target_pairs={{0,1},{1,0},{2,3},{3,2},{4,5},{5,4},{6,7},{7,6},{8,9},{9,8},{10,11... | collective-permute-start | bytes 1179656 | tf_op jit(solution)/shard_map/ppermute | solution.py:405
  115.9 8.7 %collective-permute-start.18 = (bf16[32,4096]{1,0:T(8,128)(2,1)S(1)}, bf16[32,4096]{1,0:T(8,128)(2,1)S(1)}, u32[]{:S(2)}, u32[]{:S(2)}) collective-permute-start(bf16[32,4096]{1,0:T(8,128)(2,1)S(1)} %get-tuple-element.50), channel_id=1, source_target_pairs={{0,2},{2,0},{4,6},{6,4},{8,10},{10,8},{12,14},{14,12},{1,3},{3,1},... | collective-permute-start | bytes 786440 | tf_op jit(solution)/shard_map/ppermute | solution.py:326
  116.0 10.9 %collective-permute-start.19 = (bf16[32,4096]{1,0:T(8,128)(2,1)S(1)}, bf16[32,4096]{1,0:T(8,128)(2,1)S(1)}, u32[]{:S(2)}, u32[]{:S(2)}) collective-permute-start(bf16[32,4096]{1,0:T(8,128)(2,1)S(1)} %get-tuple-element.51), channel_id=1, source_target_pairs={{0,4},{2,6},{4,0},{6,2},{8,12},{10,14},{12,8},{14,10},{1,5},{3,7},... | collective-permute-start | bytes 786440 | tf_op jit(solution)/shard_map/ppermute | solution.py:326
  119.7 13.6 %collective-permute-start.20 = (bf16[32,4096]{1,0:T(8,128)(2,1)S(1)}, bf16[32,4096]{1,0:T(8,128)(2,1)S(1)}, u32[]{:S(2)}, u32[]{:S(2)}) collective-permute-start(bf16[32,4096]{1,0:T(8,128)(2,1)S(1)} %get-tuple-element.52), channel_id=1, source_target_pairs={{0,6},{2,4},{4,2},{6,0},{8,14},{10,12},{12,10},{14,8},{1,7},{3,5},... | collective-permute-start | bytes 786440 | tf_op jit(solution)/shard_map/ppermute | solution.py:326
  134.3 8.3 %collective-permute-start.21 = (bf16[32,4096]{1,0:T(8,128)(2,1)S(1)}, bf16[32,4096]{1,0:T(8,128)(2,1)S(1)}, u32[]{:S(2)}, u32[]{:S(2)}) collective-permute-start(bf16[32,4096]{1,0:T(8,128)(2,1)S(1)} %shard_map.70.refs_0_), channel_id=1, source_target_pairs={{0,2},{2,0},{4,6},{6,4},{8,10},{10,8},{12,14},{14,12},{1,3},{3,1},... | collective-permute-start | bytes 786440 | tf_op jit(solution)/shard_map/ppermute | solution.py:326
  134.6 9.2 %collective-permute-start.22 = (bf16[32,4096]{1,0:T(8,128)(2,1)S(1)}, bf16[32,4096]{1,0:T(8,128)(2,1)S(1)}, u32[]{:S(2)}, u32[]{:S(2)}) collective-permute-start(bf16[32,4096]{1,0:T(8,128)(2,1)S(1)} %shard_map.70.refs_0_), channel_id=1, source_target_pairs={{0,4},{2,6},{4,0},{6,2},{8,12},{10,14},{12,8},{14,10},{1,5},{3,7},... | collective-permute-start | bytes 786440 | tf_op jit(solution)/shard_map/ppermute | solution.py:326
  136.4 12.6 %collective-permute-start.23 = (bf16[32,4096]{1,0:T(8,128)(2,1)S(1)}, bf16[32,4096]{1,0:T(8,128)(2,1)S(1)}, u32[]{:S(2)}, u32[]{:S(2)}) collective-permute-start(bf16[32,4096]{1,0:T(8,128)(2,1)S(1)} %shard_map.70.refs_0_), channel_id=1, source_target_pairs={{0,6},{2,4},{4,2},{6,0},{8,14},{10,12},{12,10},{14,8},{1,7},{3,5},... | collective-permute-start | bytes 786440 | tf_op jit(solution)/shard_map/ppermute | solution.py:326
  157.9 15.1 %collective-permute-start.24 = (bf16[32,4096]{1,0:T(8,128)(2,1)S(1)}, bf16[32,4096]{1,0:T(8,128)(2,1)S(1)}, u32[]{:S(2)}, u32[]{:S(2)}) collective-permute-start(bf16[32,4096]{1,0:T(8,128)(2,1)S(1)} %get-tuple-element.56), channel_id=1, source_target_pairs={{0,2},{2,0},{4,6},{6,4},{8,10},{10,8},{12,14},{14,12},{1,3},{3,1},... | collective-permute-start | bytes 786440 | tf_op jit(solution)/shard_map/ppermute | solution.py:326
  158.0 16.5 %collective-permute-start.25 = (bf16[32,4096]{1,0:T(8,128)(2,1)S(1)}, bf16[32,4096]{1,0:T(8,128)(2,1)S(1)}, u32[]{:S(2)}, u32[]{:S(2)}) collective-permute-start(bf16[32,4096]{1,0:T(8,128)(2,1)S(1)} %get-tuple-element.57), channel_id=1, source_target_pairs={{0,4},{2,6},{4,0},{6,2},{8,12},{10,14},{12,8},{14,10},{1,5},{3,7},... | collective-permute-start | bytes 786440 | tf_op jit(solution)/shard_map/ppermute | solution.py:326
  158.7 15.9 %collective-permute-start.26 = (bf16[32,4096]{1,0:T(8,128)(2,1)S(1)}, bf16[32,4096]{1,0:T(8,128)(2,1)S(1)}, u32[]{:S(2)}, u32[]{:S(2)}) collective-permute-start(bf16[32,4096]{1,0:T(8,128)(2,1)S(1)} %get-tuple-element.58), channel_id=1, source_target_pairs={{0,6},{2,4},{4,2},{6,0},{8,14},{10,12},{12,10},{14,8},{1,7},{3,5},... | collective-permute-start | bytes 786440 | tf_op jit(solution)/shard_map/ppermute | solution.py:326
  168.4 10.6 %collective-permute-start.27 = (bf16[32,4096]{1,0:T(8,128)(2,1)S(1)}, bf16[32,4096]{1,0:T(8,128)(2,1)S(1)}, u32[]{:S(2)}, u32[]{:S(2)}) collective-permute-start(bf16[32,4096]{1,0:T(8,128)(2,1)S(1)} %get-tuple-element.60), channel_id=1, source_target_pairs={{0,2},{2,0},{4,6},{6,4},{8,10},{10,8},{12,14},{14,12},{1,3},{3,1},... | collective-permute-start | bytes 786440 | tf_op jit(solution)/shard_map/ppermute | solution.py:326
  168.5 11.6 %collective-permute-start.28 = (bf16[32,4096]{1,0:T(8,128)(2,1)S(1)}, bf16[32,4096]{1,0:T(8,128)(2,1)S(1)}, u32[]{:S(2)}, u32[]{:S(2)}) collective-permute-start(bf16[32,4096]{1,0:T(8,128)(2,1)S(1)} %get-tuple-element.61), channel_id=1, source_target_pairs={{0,4},{2,6},{4,0},{6,2},{8,12},{10,14},{12,8},{14,10},{1,5},{3,7},... | collective-permute-start | bytes 786440 | tf_op jit(solution)/shard_map/ppermute | solution.py:326
  173.0 10.9 %collective-permute-start.29 = (bf16[32,4096]{1,0:T(8,128)(2,1)S(1)}, bf16[32,4096]{1,0:T(8,128)(2,1)S(1)}, u32[]{:S(2)}, u32[]{:S(2)}) collective-permute-start(bf16[32,4096]{1,0:T(8,128)(2,1)S(1)} %get-tuple-element.62), channel_id=1, source_target_pairs={{0,6},{2,4},{4,2},{6,0},{8,14},{10,12},{12,10},{14,8},{1,7},{3,5},... | collective-permute-start | bytes 786440 | tf_op jit(solution)/shard_map/ppermute | solution.py:326
  (15 other events, 99.7 us)

commit v15 on v14

--- a/solution.py
+++ b/solution.py
@@ -264,7 +264,7 @@
             jax.ShapeDtypeStruct((block.shape[0], points), jnp.bfloat16) for block in applied
         ],
         compiler_params=vmem(scratch),
-        cost_estimate=cost(0),
+        cost_estimate=cost(8),
     )(meta, *applied, *lists)
     return split_small(result, count)
 
@@ -296,7 +296,7 @@
         out_specs=WHOLE,
         out_shape=jax.ShapeDtypeStruct(parts[0].shape, jnp.bfloat16),
         compiler_params=vmem([]),
-        cost_estimate=cost(0),
+        cost_estimate=cost(6),
     )(high, low, *parts)
 
 
@@ -329,7 +329,7 @@
             for d in range(1, half)
         ]
 
-    def to_bricks(which, after):
+    def to_bricks(which, after=None):
         part = lax.dynamic_slice_in_dim(wavefunctions, which * half * points, half * points, 1)
         part = lax.optimization_barrier((part, after))[0]
         return lax.all_to_all(
@@ -362,23 +362,23 @@
         share = (end - start) // 4
         return lax.dynamic_slice_in_dim(source, start + (2 * group + core) * share, share, 0)
 
-    first = quarter_of(projectors, starts[0], starts[1])
-    first, source = lax.optimization_barrier((first, projectors))
-    first = lax.ppermute(first, "grid", partners)
-    upper = quarter_of(source, starts[2], starts[3])
+    upper = quarter_of(projectors, starts[2], starts[3])
     middle = upper.shape[0] // 2
     taken = lax.ppermute(upper[middle:], "grid", neighbours)
     upper = jnp.where(tile_count[0] > starts[2], upper[:middle], taken)
-    upper = lax.ppermute(lax.optimization_barrier((upper, first))[0], "grid", partners)
+    upper = lax.ppermute(upper, "grid", partners)
+    source = lax.optimization_barrier((projectors, taken))[0]
+    first, second = (quarter_of(source, starts[at], starts[at + 1]) for at in (0, 1))
+    first, second, late = lax.optimization_barrier((first, second, upper))
+    first = lax.ppermute(first, "grid", partners)
+    second = lax.ppermute(second, "grid", partners)
     rest = lax.ppermute(upper, "grid", neighbours)
-    second = quarter_of(source, starts[1], starts[2])
-
-    own_wave = to_bricks(side, first)
-    other_wave = to_bricks(1 - side, first)
+
+    own_wave = to_bricks(side)
+    other_wave = to_bricks(1 - side, upper)
     numbers = jnp.stack([tile_segment, tile_block, jnp.broadcast_to(tile_count, (tiles,))])
-    numbers = lax.optimization_barrier((numbers, first))[0]
+    numbers = lax.optimization_barrier((numbers, taken))[0]
     others = lax.ppermute(numbers, "grid", partners)
-    second = lax.ppermute(lax.optimization_barrier((second, others))[0], "grid", partners)
     absent = segments << bits(tiles)
     segment, block = (jnp.stack([numbers[i], others[i]]) for i in (0, 1))
     codes = jnp.stack([slots, held])
@@ -404,11 +404,13 @@
     def to_core(blocks):
         return blocks + [lax.ppermute(block, "band", swap) for block in blocks]
 
+    held_upper = [upper, rest, over_groups(upper)]
     held_first = [first, over_groups(first)]
-    sent, matrix = lax.optimization_barrier((second, matrix))
+    rest, late = lax.optimization_barrier((rest, held_upper[-1]))
+    held_upper.append(over_groups(rest))
+    sent, late, matrix = lax.optimization_barrier((second, (held_upper, held_first), matrix))
     held_second = [second, over_groups(sent)]
     held_second, other_wave = lax.optimization_barrier((held_second, other_wave))
-    held_upper = [upper, rest, over_groups(upper), over_groups(rest)]
     pieces = [to_core(blocks) for blocks in (held_first, held_upper, held_second)]
 
     joined, other_spots = [], []

time: 188 us -> 186 us (0.989); the launches traced: 185 us -> 188 us
  Pallas kernels: 24.6 us -> 33.7 us
  starting transfers between devices: 45.3 us -> 37.8 us
  other arithmetic: 16.7 us -> 11.3 us
  waiting for transfers between devices: 62.7 us -> 67.9 us
    ppermute x2, waiting for transfers between devices: 15.5 us -> 23.2 us  [the longest x1 16.7 us: body(): upper = lax.ppermute(upper, 'grid', partners)]
    pallas_call x2, Pallas kernels: 9.35 us -> 14.5 us  [spread(): pl.pallas_call(functools.partial(spread_kernel, sizes, len(applied), spot...]
    unnamed x30 -> x40, local copies, waits for them, and re-layouts: 12.1 us -> 17.1 us
    ppermute x1, starting transfers between devices: 4.04 us -> 0.01 us  [body(): first = lax.ppermute(first, 'grid', partners)]
    ppermute x12, starting transfers between devices: 18.2 us -> 14.2 us  [exchange(): lax.ppermute(blocks[d], 'grid', [(i, i // half * half + (i % half ^ d)) f...]
    pallas_call x3, Pallas kernels: 14.3 us -> 18.2 us  [project(): pl.pallas_call(functools.partial(project_kernel, sizes, firsts, spot, tot...]
    ppermute x1, waiting for transfers between devices: 7.61 us -> 10.2 us  [body(): rest = lax.ppermute(upper, 'grid', neighbours)]
    another operation x3, local copies, waits for them, and re-layouts: 4.6 us -> 2.17 us  [coupling_matrix(): wide = jnp.tile(coupling.reshape(blocks, proj, width), (1, 1, atoms))]
  transfers between devices with their start and end apart: 32 -> 32, of which waited for: 15 -> 13; matrix products, arithmetic and copies ran while one was open for 20% -> 15% of each run, Pallas kernels for 8% -> 10%
where the time goes in v15:
time: 186 us; the launch traced here: 188 us
  waiting for transfers between devices  67.9 us (37%)
  starting transfers between devices  37.8 us (20%)
  local copies, waits for them, and re-layouts  35.9 us (19%)
  Pallas kernels  33.7 us (18%)
  other arithmetic  11.3 us (6%)
    ppermute x12, waiting for transfers between devices, exchange(): lax.ppermute(blocks[d], 'grid', [(i, i // half * half + (i % half ^ d)) f...  31.7 us
    pallas_call x3, Pallas kernels, project(): pl.pallas_call(functools.partial(project_kernel, sizes, firsts, spot, tot...  18.2 us
    unnamed x40, local copies, waits for them, and re-layouts  17.1 us
    ppermute x1, waiting for transfers between devices, body(): upper = lax.ppermute(upper, 'grid', partners)  16.7 us
    pallas_call x2, Pallas kernels, spread(): pl.pallas_call(functools.partial(spread_kernel, sizes, len(applied), spot...  14.5 us
    ppermute x12, starting transfers between devices, exchange(): lax.ppermute(blocks[d], 'grid', [(i, i // half * half + (i % half ^ d)) f...  14.2 us
    ppermute x1, waiting for transfers between devices, body(): rest = lax.ppermute(upper, 'grid', neighbours)  10.2 us
    all_to_all x2, starting transfers between devices, to_bricks(): lax.all_to_all(part, 'grid', split_axis=1, concat_axis=0, tiled=True, axi...  7.03 us
  transfers between devices with their start and end apart: 32, of which 13 were waited for; matrix products, arithmetic and copies ran while one was open for 15% of the time, Pallas kernels for 10%

profile of v15, /device:TPU:0, one launch (start us, length us, event | category | flops | bytes accessed | tf_op | source)
XLA Modules:
  0.0 187.7 jit_solution(12581954063147774695)
XLA Ops:
  1.8 3.0 %collective-permute-start = (bf16[24,64,128]{2,1,0:T(8,128)(2,1)}, bf16[24,64,128]{2,1,0:T(8,128)(2,1)}, u32[]{:S(2)}, u32[]{:S(2)}) collective-permute-start(bf16[24,64,128]{2,1,0:T(8,128)(2,1)} %constant_dynamic-slice_fusion.4), channel_id=1, source_target_pairs={{0,4},{2,6},{4,0},{6,2},{8,12},{10,14},{12,8},{14,10},{1,5},{3,7},... | collective-permute-start | bytes 1179656 | tf_op jit(solution)/shard_map/ppermute | solution.py:367
  4.8 2.7 %constant_dynamic-slice_fusion = (bf16[32,16384]{1,0:T(8,128)(2,1)S(1)}, bf16[32,16384]{1,0:T(8,128)(2,1)}) fusion(bf16[32,32768]{1,0:T(8,128)(2,1)} %param.6, s32[]{:T(128)S(6)} %select_n.398, s32[]{:T(128)S(6)} %select_n.397), kind=kLoop, calls=%fused_computation.42 | loop fusion | bytes 4194312 | tf_op jit(solution)/shard_map/dynamic_slice | solution.py:333
  8.5 3.5 %all-to-all-start.1 = ((bf16[32,4,4096]{2,0,1:T(8,128)(2,1)}), bf16[32,4,4096]{2,0,1:T(8,128)(2,1)S(1)}, u32[]{:S(2)}, u32[]{:S(2)}) async-start(bf16[32,4,4096]{2,0,1:T(8,128)(2,1)} %bitcast.19), calls=%async_computation.1 | async-start | bytes 2097152 | tf_op jit(solution)/shard_map/all_to_all | solution.py:335
  19.8 2.7 %collective-permute-start.1 = (s32[3,384]{1,0:T(4,128)S(1)}, s32[3,384]{1,0:T(4,128)S(1)}, u32[]{:S(2)}, u32[]{:S(2)}) collective-permute-start(s32[3,384]{1,0:T(4,128)S(1)} %add_add_fusion), channel_id=1, source_target_pairs={{0,8},{2,10},{4,12},{6,14},{8,0},{10,2},{12,4},{14,6},{1,9},{3,11}... | collective-permute-start | bytes 13832 | tf_op jit(solution)/shard_map/ppermute | solution.py:381
  24.5 2.0 %constant_dynamic-slice_fusion.2 = (bf16[24,64,128]{2,1,0:T(8,128)(2,1)}, bf16[24,64,128]{2,1,0:T(8,128)(2,1)}) fusion(bf16[384,64,128]{2,1,0:T(8,128)(2,1)} %refs_4_.1, s32[]{:T(128)S(6)} %select_n.391, s32[]{:T(128)S(6)} %select_n.390), kind=kLoop, calls=%fused_computation.44 | loop fusion | bytes 1572872 | tf_op jit(solution)/shard_map/dynamic_slice | solution.py:363
  27.3 16.7 %collective-permute-done.2.refs_4_ = bf16[24,64,128]{2,1,0:T(8,128)(2,1)} collective-permute-done((bf16[24,64,128]{2,1,0:T(8,128)(2,1)S(1)}, bf16[24,64,128]{2,1,0:T(8,128)(2,1)}, u32[]{:S(2)}, u32[]{:S(2)}) %collective-permute-start.2) | collective-permute-done | bytes 393248 | tf_op jit(solution)/shard_map/ppermute | solution.py:369
  44.1 1.9 %collective-permute-start.4 = (bf16[24,64,128]{2,1,0:T(8,128)(2,1)}, bf16[24,64,128]{2,1,0:T(8,128)(2,1)}, u32[]{:S(2)}, u32[]{:S(2)}) collective-permute-start(bf16[24,64,128]{2,1,0:T(8,128)(2,1)} %collective-permute-done.2.refs_4_), channel_id=1, source_target_pairs={{0,4},{2,6},{4,0},{6,2},{8,12},{10,14},{12,8},{14,10},{1,5},{3,7},... | collective-permute-start | bytes 1179656 | tf_op jit(solution)/shard_map/ppermute | solution.py:375
  50.0 2.3 %copy.24 = bf16[4,4,8,4096]{3,2,0,1:T(8,128)(2,1)} copy(bf16[4,4,8,4096]{3,2,1,0:T(8,128)(2,1)} %bitcast.25) | data formatting | bytes 2097152 | tf_op jit(solution)/shard_map/all_to_all | solution.py:335
  52.3 10.2 %collective-permute-done.4.refs_5_ = bf16[24,64,128]{2,1,0:T(8,128)(2,1)} collective-permute-done((bf16[24,64,128]{2,1,0:T(8,128)(2,1)}, bf16[24,64,128]{2,1,0:T(8,128)(2,1)}, u32[]{:S(2)}, u32[]{:S(2)}) %collective-permute-start.4) | collective-permute-done | bytes 393248 | tf_op jit(solution)/shard_map/ppermute | solution.py:375
  66.8 3.5 %all-to-all-start = ((bf16[32,4,4096]{2,0,1:T(8,128)(2,1)}), bf16[32,4,4096]{2,0,1:T(8,128)(2,1)S(1)}, u32[]{:S(2)}, u32[]{:S(2)}) async-start(bf16[32,4,4096]{2,0,1:T(8,128)(2,1)} %bitcast.27), calls=%async_computation | async-start | bytes 2097152 | tf_op jit(solution)/shard_map/all_to_all | solution.py:335
  73.2 6.5 %collective-permute-done.3.refs_0_ = bf16[24,64,128]{2,1,0:T(8,128)(2,1)S(1)} collective-permute-done((bf16[24,64,128]{2,1,0:T(8,128)(2,1)}, bf16[24,64,128]{2,1,0:T(8,128)(2,1)S(1)}, u32[]{:S(2)}, u32[]{:S(2)}) %collective-permute-start.3) | collective-permute-done | bytes 393248 | tf_op jit(solution)/shard_map/ppermute | solution.py:374
  85.3 1.9 %concatenate.26.meta = s32[1225]{0:T(1024)S(1)} concatenate(s32[1]{0:T(128)} %bitcast, s32[1]{0:T(128)} %bitcast.2, s32[1]{0:T(128)} %bitcast.3, s32[6]{0:T(128)} %reshape.790, s32[1216]{0:T(1024)S(1)} %add.472), dimensions={0} | concatenate | bytes 9800 | tf_op jit(solution)/shard_map/concatenate | solution.py:388
  88.3 2.4 %collective-permute-done.9.refs_1_ = bf16[24,64,128]{2,1,0:T(8,128)(2,1)} collective-permute-done((bf16[24,64,128]{2,1,0:T(8,128)(2,1)S(1)}, bf16[24,64,128]{2,1,0:T(8,128)(2,1)}, u32[]{:S(2)}, u32[]{:S(2)}) %collective-permute-start.9) | collective-permute-done | bytes 393248 | tf_op jit(solution)/shard_map/ppermute | solution.py:402
  92.0 2.8 %copy-done.2 = bf16[384,64,128]{2,1,0:T(8,128)(2,1)S(1)} copy-done((bf16[384,64,128]{2,1,0:T(8,128)(2,1)S(1)}, bf16[384,64,128]{2,1,0:T(8,128)(2,1)}, u32[]{:S(2)}) %copy-start.2) | copy-done | bytes 6291480
  94.8 4.8 %shard_map.67.refs_12_ = f32[128,4096]{1,0:T(8,128)S(1)} custom-call(s32[1225]{0:T(1024)S(1)} %concatenate.26.meta, bf16[128,4096]{1,0:T(8,128)(2,1)S(1)} %bitcast.24, bf16[384,64,128]{2,1,0:T(8,128)(2,1)S(1)} %copy-done.2), custom_call_target="tpu_custom_call" | custom-call | flops 5000000000 | bytes 1 | tf_op jit(solution)/shard_map/pallas_call | solution.py:232
  103.1 8.9 %shard_map.68 = (bf16[288,64,128]{2,1,0:T(8,128)(2,1)S(1)}, f32[128,4096]{1,0:T(8,128)S(1)}) custom-call(s32[1225]{0:T(1024)S(1)} %concatenate.26.meta, bf16[128,4096]{1,0:T(8,128)(2,1)S(1)} %bitcast.22, bf16[24,64,128]{2,1,0:T(8,128)(2,1)} %collective-permute-done.7.refs_0_, bf16[24,64,128]{2,1,0:T(8,128)(2,1)} %collective-permute-done.8.refs_1_, ...), custom_call_target="tpu_custom_call" | custom-call | flops 8000000000 | bytes 1 | tf_op jit(solution)/shard_map/pallas_call | solution.py:232
  112.0 2.1 %copy-done.8 = bf16[288,64,128]{2,1,0:T(8,128)(2,1)} copy-done((bf16[288,64,128]{2,1,0:T(8,128)(2,1)}, bf16[288,64,128]{2,1,0:T(8,128)(2,1)S(1)}, u32[]{:S(2)}) %copy-start.8) | copy-done | bytes 4718616
  114.1 4.5 %shard_map.69 = (bf16[96,64,128]{2,1,0:T(8,128)(2,1)S(1)}, bf16[32,4096]{1,0:T(8,128)(2,1)S(1)}, bf16[32,4096]{1,0:T(8,128)(2,1)S(1)}, bf16[32,4096]{1,0:T(8,128)(2,1)S(1)}, bf16[32,4096]{1,0:T(8,128)(2,1)S(1)}) custom-call(s32[1225]{0:T(1024)S(1)} %concatenate.26.meta, bf16[128,4096]{1,0:T(8,128)(2,1)S(1)} %bitcast.23, ...), custom_call_target="tpu_custom_call" | custom-call | flops 1 | bytes 1 | tf_op jit(solution)/shard_map/pallas_call | solution.py:232
  118.9 3.4 %collective-permute-start.20 = (bf16[32,4096]{1,0:T(8,128)(2,1)S(1)}, bf16[32,4096]{1,0:T(8,128)(2,1)S(1)}, u32[]{:S(2)}, u32[]{:S(2)}) collective-permute-start(bf16[32,4096]{1,0:T(8,128)(2,1)S(1)} %get-tuple-element.50), channel_id=1, source_target_pairs={{0,6},{2,4},{4,2},{6,0},{8,14},{10,12},{12,10},{14,8},{1,7},{3,5},... | collective-permute-start | bytes 786440 | tf_op jit(solution)/shard_map/ppermute | solution.py:326
  122.3 5.2 %collective-permute-done.18.refs_1_ = bf16[32,4096]{1,0:T(8,128)(2,1)S(1)} collective-permute-done((bf16[32,4096]{1,0:T(8,128)(2,1)S(1)}, bf16[32,4096]{1,0:T(8,128)(2,1)S(1)}, u32[]{:S(2)}, u32[]{:S(2)}) %collective-permute-start.18) | collective-permute-done | bytes 262176 | tf_op jit(solution)/shard_map/ppermute | solution.py:326
  128.0 6.3 %collective-permute-done.20.refs_3_ = bf16[32,4096]{1,0:T(8,128)(2,1)S(1)} collective-permute-done((bf16[32,4096]{1,0:T(8,128)(2,1)S(1)}, bf16[32,4096]{1,0:T(8,128)(2,1)S(1)}, u32[]{:S(2)}, u32[]{:S(2)}) %collective-permute-start.20) | collective-permute-done | bytes 262176 | tf_op jit(solution)/shard_map/ppermute | solution.py:326
  135.8 2.8 %collective-permute-start.23 = (bf16[32,4096]{1,0:T(8,128)(2,1)S(1)}, bf16[32,4096]{1,0:T(8,128)(2,1)S(1)}, u32[]{:S(2)}, u32[]{:S(2)}) collective-permute-start(bf16[32,4096]{1,0:T(8,128)(2,1)S(1)} %shard_map.70.refs_0_), channel_id=1, source_target_pairs={{0,6},{2,4},{4,2},{6,0},{8,14},{10,12},{12,10},{14,8},{1,7},{3,5},... | collective-permute-start | bytes 786440 | tf_op jit(solution)/shard_map/ppermute | solution.py:326
  138.7 4.8 %collective-permute-done.21.refs_1_ = bf16[32,4096]{1,0:T(8,128)(2,1)S(1)} collective-permute-done((bf16[32,4096]{1,0:T(8,128)(2,1)S(1)}, bf16[32,4096]{1,0:T(8,128)(2,1)S(1)}, u32[]{:S(2)}, u32[]{:S(2)}) %collective-permute-start.21) | collective-permute-done | bytes 262176 | tf_op jit(solution)/shard_map/ppermute | solution.py:326
  144.8 4.7 %collective-permute-done.23.refs_3_ = bf16[32,4096]{1,0:T(8,128)(2,1)S(1)} collective-permute-done((bf16[32,4096]{1,0:T(8,128)(2,1)S(1)}, bf16[32,4096]{1,0:T(8,128)(2,1)S(1)}, u32[]{:S(2)}, u32[]{:S(2)}) %collective-permute-start.23) | collective-permute-done | bytes 262176 | tf_op jit(solution)/shard_map/ppermute | solution.py:326
  150.9 2.3 %copy-done.9 = bf16[288,64,128]{2,1,0:T(8,128)(2,1)S(1)} copy-done((bf16[288,64,128]{2,1,0:T(8,128)(2,1)S(1)}, bf16[288,64,128]{2,1,0:T(8,128)(2,1)}, u32[]{:S(2)}) %copy-start.9) | copy-done | bytes 4718616
  153.3 9.3 %shard_map.71 = (bf16[32,4096]{1,0:T(8,128)(2,1)S(1)}, bf16[32,4096]{1,0:T(8,128)(2,1)S(1)}, bf16[32,4096]{1,0:T(8,128)(2,1)S(1)}, bf16[32,4096]{1,0:T(8,128)(2,1)S(1)}) custom-call(s32[1225]{0:T(1024)S(1)} %concatenate.26.meta, bf16[32,4096]{1,0:T(8,128)(2,1)S(1)} %shard_map.70.refs_0_, bf16[32,4096]{1,0:T(8,128)(2,1)S(1)} %collective-permute-done.21.refs_1_, ...), custom_call_target="tpu_custom_call" | custom-call | flops 8000000000 | bytes 1 | tf_op jit(solution)/shard_map/pallas_call | solution.py:254
  162.7 3.4 %collective-permute-start.26 = (bf16[32,4096]{1,0:T(8,128)(2,1)S(1)}, bf16[32,4096]{1,0:T(8,128)(2,1)S(1)}, u32[]{:S(2)}, u32[]{:S(2)}) collective-permute-start(bf16[32,4096]{1,0:T(8,128)(2,1)S(1)} %get-tuple-element.56), channel_id=1, source_target_pairs={{0,6},{2,4},{4,2},{6,0},{8,14},{10,12},{12,10},{14,8},{1,7},{3,5},... | collective-permute-start | bytes 786440 | tf_op jit(solution)/shard_map/ppermute | solution.py:326
  166.1 2.8 %copy-done.3 = bf16[384,64,128]{2,1,0:T(8,128)(2,1)S(1)} copy-done((bf16[384,64,128]{2,1,0:T(8,128)(2,1)S(1)}, bf16[384,64,128]{2,1,0:T(8,128)(2,1)}, u32[]{:S(2)}) %copy-start.3) | copy-done | bytes 6291480
  168.9 5.2 %shard_map.72 = (bf16[32,4096]{1,0:T(8,128)(2,1)S(1)}, bf16[32,4096]{1,0:T(8,128)(2,1)S(1)}, bf16[32,4096]{1,0:T(8,128)(2,1)S(1)}, bf16[32,4096]{1,0:T(8,128)(2,1)S(1)}) custom-call(s32[1225]{0:T(1024)S(1)} %concatenate.26.meta, bf16[32,4096]{1,0:T(8,128)(2,1)S(1)} %shard_map.70.refs_0_, bf16[32,4096]{1,0:T(8,128)(2,1)S(1)} %collective-permute-done.21.refs_1_, ...), custom_call_target="tpu_custom_call" | custom-call | flops 8000000000 | bytes 1 | tf_op jit(solution)/shard_map/pallas_call | solution.py:254
  174.5 3.5 %collective-permute-start.29 = (bf16[32,4096]{1,0:T(8,128)(2,1)S(1)}, bf16[32,4096]{1,0:T(8,128)(2,1)S(1)}, u32[]{:S(2)}, u32[]{:S(2)}) collective-permute-start(bf16[32,4096]{1,0:T(8,128)(2,1)S(1)} %get-tuple-element.60), channel_id=1, source_target_pairs={{0,6},{2,4},{4,2},{6,0},{8,14},{10,12},{12,10},{14,8},{1,7},{3,5},... | collective-permute-start | bytes 786440 | tf_op jit(solution)/shard_map/ppermute | solution.py:326
  178.1 6.1 %collective-permute-done.27 = bf16[32,4096]{1,0:T(8,128)(2,1)S(1)} collective-permute-done((bf16[32,4096]{1,0:T(8,128)(2,1)S(1)}, bf16[32,4096]{1,0:T(8,128)(2,1)S(1)}, u32[]{:S(2)}, u32[]{:S(2)}) %collective-permute-start.27) | collective-permute-done | bytes 262176 | tf_op jit(solution)/shard_map/ppermute | solution.py:326
  184.3 2.7 %collective-permute-done.29 = bf16[32,4096]{1,0:T(8,128)(2,1)S(1)} collective-permute-done((bf16[32,4096]{1,0:T(8,128)(2,1)S(1)}, bf16[32,4096]{1,0:T(8,128)(2,1)S(1)}, u32[]{:S(2)}, u32[]{:S(2)}) %collective-permute-start.29) | collective-permute-done | bytes 262176 | tf_op jit(solution)/shard_map/ppermute | solution.py:326
  (134 shorter events, 41.5 us)
Async XLA Ops:
  1.8 18.1 %collective-permute-start = (bf16[24,64,128]{2,1,0:T(8,128)(2,1)}, bf16[24,64,128]{2,1,0:T(8,128)(2,1)}, u32[]{:S(2)}, u32[]{:S(2)}) collective-permute-start(bf16[24,64,128]{2,1,0:T(8,128)(2,1)} %constant_dynamic-slice_fusion.4), channel_id=1, source_target_pairs={{0,4},{2,6},{4,0},{6,2},{8,12},{10,14},{12,8},{14,10},{1,5},{3,7},... | collective-permute-start | bytes 1179656 | tf_op jit(solution)/shard_map/ppermute | solution.py:367
  8.5 57.3 %all-to-all-start.1 = ((bf16[32,4,4096]{2,0,1:T(8,128)(2,1)}), bf16[32,4,4096]{2,0,1:T(8,128)(2,1)S(1)}, u32[]{:S(2)}, u32[]{:S(2)}) async-start(bf16[32,4,4096]{2,0,1:T(8,128)(2,1)} %bitcast.19), calls=%async_computation.1 | async-start | bytes 2097152 | tf_op jit(solution)/shard_map/all_to_all | solution.py:335
  19.8 6.7 %collective-permute-start.1 = (s32[3,384]{1,0:T(4,128)S(1)}, s32[3,384]{1,0:T(4,128)S(1)}, u32[]{:S(2)}, u32[]{:S(2)}) collective-permute-start(s32[3,384]{1,0:T(4,128)S(1)} %add_add_fusion), channel_id=1, source_target_pairs={{0,8},{2,10},{4,12},{6,14},{8,0},{10,2},{12,4},{14,6},{1,9},{3,11}... | collective-permute-start | bytes 13832 | tf_op jit(solution)/shard_map/ppermute | solution.py:381
  24.2 19.9 %collective-permute-start.2 = (bf16[24,64,128]{2,1,0:T(8,128)(2,1)S(1)}, bf16[24,64,128]{2,1,0:T(8,128)(2,1)}, u32[]{:S(2)}, u32[]{:S(2)}) collective-permute-start(bf16[24,64,128]{2,1,0:T(8,128)(2,1)S(1)} %dynamic-slice_select_fusion), channel_id=1, source_target_pairs={{0,8},{2,10},{4,12},{6,14},{8,0},{10,2},{12,4},{14,6},{1,9},{3,11}... | collective-permute-start | bytes 1179656 | tf_op jit(solution)/shard_map/ppermute | solution.py:369
  44.1 20.3 %collective-permute-start.7 = (bf16[24,64,128]{2,1,0:T(8,128)(2,1)}, bf16[24,64,128]{2,1,0:T(8,128)(2,1)}, u32[]{:S(2)}, u32[]{:S(2)}) collective-permute-start(bf16[24,64,128]{2,1,0:T(8,128)(2,1)} %get-tuple-element.37), channel_id=1, source_target_pairs={{0,8},{2,10},{4,12},{6,14},{8,0},{10,2},{12,4},{14,6},{1,9},{3,11}... | collective-permute-start | bytes 1179656 | tf_op jit(solution)/shard_map/ppermute | solution.py:373
  44.1 18.4 %collective-permute-start.4 = (bf16[24,64,128]{2,1,0:T(8,128)(2,1)}, bf16[24,64,128]{2,1,0:T(8,128)(2,1)}, u32[]{:S(2)}, u32[]{:S(2)}) collective-permute-start(bf16[24,64,128]{2,1,0:T(8,128)(2,1)} %collective-permute-done.2.refs_4_), channel_id=1, source_target_pairs={{0,4},{2,6},{4,0},{6,2},{8,12},{10,14},{12,8},{14,10},{1,5},{3,7},... | collective-permute-start | bytes 1179656 | tf_op jit(solution)/shard_map/ppermute | solution.py:375
  46.0 16.4 %collective-permute-start.5 = (bf16[24,64,128]{2,1,0:T(8,128)(2,1)}, bf16[24,64,128]{2,1,0:T(8,128)(2,1)}, u32[]{:S(2)}, u32[]{:S(2)}) collective-permute-start(bf16[24,64,128]{2,1,0:T(8,128)(2,1)} %collective-permute-done.2.refs_4_), channel_id=1, source_target_pairs={{0,16},{16,0},{1,17},{17,1},{2,18},{18,2},{3,19},{19,3},{4,20},{20... | collective-permute-start | bytes 1179656 | tf_op jit(solution)/shard_map/ppermute | solution.py:402
  49.0 30.7 %collective-permute-start.3 = (bf16[24,64,128]{2,1,0:T(8,128)(2,1)}, bf16[24,64,128]{2,1,0:T(8,128)(2,1)S(1)}, u32[]{:S(2)}, u32[]{:S(2)}) collective-permute-start(bf16[24,64,128]{2,1,0:T(8,128)(2,1)} %get-tuple-element.35), channel_id=1, source_target_pairs={{0,8},{2,10},{4,12},{6,14},{8,0},{10,2},{12,4},{14,6},{1,9},{3,11}... | collective-permute-start | bytes 1179656 | tf_op jit(solution)/shard_map/ppermute | solution.py:374
  62.4 17.2 %collective-permute-start.6 = (bf16[24,64,128]{2,1,0:T(8,128)(2,1)}, bf16[24,64,128]{2,1,0:T(8,128)(2,1)}, u32[]{:S(2)}, u32[]{:S(2)}) collective-permute-start(bf16[24,64,128]{2,1,0:T(8,128)(2,1)} %collective-permute-done.4.refs_5_), channel_id=1, source_target_pairs={{0,16},{16,0},{1,17},{17,1},{2,18},{18,2},{3,19},{19,3},{4,20},{20... | collective-permute-start | bytes 1179656 | tf_op jit(solution)/shard_map/ppermute | solution.py:402
  64.3 15.3 %collective-permute-start.8 = (bf16[24,64,128]{2,1,0:T(8,128)(2,1)}, bf16[24,64,128]{2,1,0:T(8,128)(2,1)}, u32[]{:S(2)}, u32[]{:S(2)}) collective-permute-start(bf16[24,64,128]{2,1,0:T(8,128)(2,1)} %collective-permute-done.7.refs_0_), channel_id=1, source_target_pairs={{0,16},{16,0},{1,17},{17,1},{2,18},{18,2},{3,19},{19,3},{4,20},{20... | collective-permute-start | bytes 1179656 | tf_op jit(solution)/shard_map/ppermute | solution.py:402
  66.8 34.1 %all-to-all-start = ((bf16[32,4,4096]{2,0,1:T(8,128)(2,1)}), bf16[32,4,4096]{2,0,1:T(8,128)(2,1)S(1)}, u32[]{:S(2)}, u32[]{:S(2)}) async-start(bf16[32,4,4096]{2,0,1:T(8,128)(2,1)} %bitcast.27), calls=%async_computation | async-start | bytes 2097152 | tf_op jit(solution)/shard_map/all_to_all | solution.py:335
  73.1 14.8 %collective-permute-start.14 = (bf16[24,64,128]{2,1,0:T(8,128)(2,1)}, bf16[24,64,128]{2,1,0:T(8,128)(2,1)}, u32[]{:S(2)}, u32[]{:S(2)}) collective-permute-start(bf16[24,64,128]{2,1,0:T(8,128)(2,1)} %collective-permute-done.2.refs_4_), channel_id=1, source_target_pairs={{0,1},{1,0},{2,3},{3,2},{4,5},{5,4},{6,7},{7,6},{8,9},{9,8},{10,11... | collective-permute-start | bytes 1179656 | tf_op jit(solution)/shard_map/ppermute | solution.py:405
  79.7 11.1 %collective-permute-start.9 = (bf16[24,64,128]{2,1,0:T(8,128)(2,1)S(1)}, bf16[24,64,128]{2,1,0:T(8,128)(2,1)}, u32[]{:S(2)}, u32[]{:S(2)}) collective-permute-start(bf16[24,64,128]{2,1,0:T(8,128)(2,1)S(1)} %collective-permute-done.3.refs_0_), channel_id=1, source_target_pairs={{0,16},{16,0},{1,17},{17,1},{2,18},{18,2},{3,19},{19,3},{4,20},{20... | collective-permute-start | bytes 1179656 | tf_op jit(solution)/shard_map/ppermute | solution.py:402
  87.3 13.6 %collective-permute-start.12 = (bf16[24,64,128]{2,1,0:T(8,128)(2,1)}, bf16[24,64,128]{2,1,0:T(8,128)(2,1)}, u32[]{:S(2)}, u32[]{:S(2)}) collective-permute-start(bf16[24,64,128]{2,1,0:T(8,128)(2,1)} %collective-permute-done.7.refs_0_), channel_id=1, source_target_pairs={{0,1},{1,0},{2,3},{3,2},{4,5},{5,4},{6,7},{7,6},{8,9},{9,8},{10,11... | collective-permute-start | bytes 1179656 | tf_op jit(solution)/shard_map/ppermute | solution.py:405
  87.3 14.1 %collective-permute-start.15 = (bf16[24,64,128]{2,1,0:T(8,128)(2,1)}, bf16[24,64,128]{2,1,0:T(8,128)(2,1)}, u32[]{:S(2)}, u32[]{:S(2)}) collective-permute-start(bf16[24,64,128]{2,1,0:T(8,128)(2,1)} %collective-permute-done.4.refs_5_), channel_id=1, source_target_pairs={{0,1},{1,0},{2,3},{3,2},{4,5},{5,4},{6,7},{7,6},{8,9},{9,8},{10,11... | collective-permute-start | bytes 1179656 | tf_op jit(solution)/shard_map/ppermute | solution.py:405
  87.8 13.7 %collective-permute-start.16 = (bf16[24,64,128]{2,1,0:T(8,128)(2,1)}, bf16[24,64,128]{2,1,0:T(8,128)(2,1)}, u32[]{:S(2)}, u32[]{:S(2)}) collective-permute-start(bf16[24,64,128]{2,1,0:T(8,128)(2,1)} %collective-permute-done.5.refs_6_), channel_id=1, source_target_pairs={{0,1},{1,0},{2,3},{3,2},{4,5},{5,4},{6,7},{7,6},{8,9},{9,8},{10,11... | collective-permute-start | bytes 1179656 | tf_op jit(solution)/shard_map/ppermute | solution.py:405
  87.9 13.6 %collective-permute-start.13 = (bf16[24,64,128]{2,1,0:T(8,128)(2,1)}, bf16[24,64,128]{2,1,0:T(8,128)(2,1)}, u32[]{:S(2)}, u32[]{:S(2)}) collective-permute-start(bf16[24,64,128]{2,1,0:T(8,128)(2,1)} %collective-permute-done.8.refs_1_), channel_id=1, source_target_pairs={{0,1},{1,0},{2,3},{3,2},{4,5},{5,4},{6,7},{7,6},{8,9},{9,8},{10,11... | collective-permute-start | bytes 1179656 | tf_op jit(solution)/shard_map/ppermute | solution.py:405
  90.7 10.7 %collective-permute-start.17 = (bf16[24,64,128]{2,1,0:T(8,128)(2,1)}, bf16[24,64,128]{2,1,0:T(8,128)(2,1)}, u32[]{:S(2)}, u32[]{:S(2)}) collective-permute-start(bf16[24,64,128]{2,1,0:T(8,128)(2,1)} %collective-permute-done.6.refs_7_), channel_id=1, source_target_pairs={{0,1},{1,0},{2,3},{3,2},{4,5},{5,4},{6,7},{7,6},{8,9},{9,8},{10,11... | collective-permute-start | bytes 1179656 | tf_op jit(solution)/shard_map/ppermute | solution.py:405
  100.9 13.3 %collective-permute-start.10 = (bf16[24,64,128]{2,1,0:T(8,128)(2,1)S(1)}, bf16[24,64,128]{2,1,0:T(8,128)(2,1)S(1)}, u32[]{:S(2)}, u32[]{:S(2)}) collective-permute-start(bf16[24,64,128]{2,1,0:T(8,128)(2,1)S(1)} %collective-permute-done.3.refs_0_), channel_id=1, source_target_pairs={{0,1},{1,0},{2,3},{3,2},{4,5},{5,4},{6,7},{7,6},{8,9},{9,8},{10,11... | collective-permute-start | bytes 1179656 | tf_op jit(solution)/shard_map/ppermute | solution.py:405
  101.4 12.8 %collective-permute-start.11 = (bf16[24,64,128]{2,1,0:T(8,128)(2,1)}, bf16[24,64,128]{2,1,0:T(8,128)(2,1)S(1)}, u32[]{:S(2)}, u32[]{:S(2)}) collective-permute-start(bf16[24,64,128]{2,1,0:T(8,128)(2,1)} %collective-permute-done.9.refs_1_), channel_id=1, source_target_pairs={{0,1},{1,0},{2,3},{3,2},{4,5},{5,4},{6,7},{7,6},{8,9},{9,8},{10,11... | collective-permute-start | bytes 1179656 | tf_op jit(solution)/shard_map/ppermute | solution.py:405
  118.7 8.7 %collective-permute-start.18 = (bf16[32,4096]{1,0:T(8,128)(2,1)S(1)}, bf16[32,4096]{1,0:T(8,128)(2,1)S(1)}, u32[]{:S(2)}, u32[]{:S(2)}) collective-permute-start(bf16[32,4096]{1,0:T(8,128)(2,1)S(1)} %get-tuple-element.48), channel_id=1, source_target_pairs={{0,2},{2,0},{4,6},{6,4},{8,10},{10,8},{12,14},{14,12},{1,3},{3,1},... | collective-permute-start | bytes 786440 | tf_op jit(solution)/shard_map/ppermute | solution.py:326
  118.8 9.2 %collective-permute-start.19 = (bf16[32,4096]{1,0:T(8,128)(2,1)S(1)}, bf16[32,4096]{1,0:T(8,128)(2,1)S(1)}, u32[]{:S(2)}, u32[]{:S(2)}) collective-permute-start(bf16[32,4096]{1,0:T(8,128)(2,1)S(1)} %get-tuple-element.49), channel_id=1, source_target_pairs={{0,4},{2,6},{4,0},{6,2},{8,12},{10,14},{12,8},{14,10},{1,5},{3,7},... | collective-permute-start | bytes 786440 | tf_op jit(solution)/shard_map/ppermute | solution.py:326
  118.9 15.4 %collective-permute-start.20 = (bf16[32,4096]{1,0:T(8,128)(2,1)S(1)}, bf16[32,4096]{1,0:T(8,128)(2,1)S(1)}, u32[]{:S(2)}, u32[]{:S(2)}) collective-permute-start(bf16[32,4096]{1,0:T(8,128)(2,1)S(1)} %get-tuple-element.50), channel_id=1, source_target_pairs={{0,6},{2,4},{4,2},{6,0},{8,14},{10,12},{12,10},{14,8},{1,7},{3,5},... | collective-permute-start | bytes 786440 | tf_op jit(solution)/shard_map/ppermute | solution.py:326
  135.2 8.4 %collective-permute-start.21 = (bf16[32,4096]{1,0:T(8,128)(2,1)S(1)}, bf16[32,4096]{1,0:T(8,128)(2,1)S(1)}, u32[]{:S(2)}, u32[]{:S(2)}) collective-permute-start(bf16[32,4096]{1,0:T(8,128)(2,1)S(1)} %shard_map.70.refs_0_), channel_id=1, source_target_pairs={{0,2},{2,0},{4,6},{6,4},{8,10},{10,8},{12,14},{14,12},{1,3},{3,1},... | collective-permute-start | bytes 786440 | tf_op jit(solution)/shard_map/ppermute | solution.py:326
  135.5 9.2 %collective-permute-start.22 = (bf16[32,4096]{1,0:T(8,128)(2,1)S(1)}, bf16[32,4096]{1,0:T(8,128)(2,1)S(1)}, u32[]{:S(2)}, u32[]{:S(2)}) collective-permute-start(bf16[32,4096]{1,0:T(8,128)(2,1)S(1)} %shard_map.70.refs_0_), channel_id=1, source_target_pairs={{0,4},{2,6},{4,0},{6,2},{8,12},{10,14},{12,8},{14,10},{1,5},{3,7},... | collective-permute-start | bytes 786440 | tf_op jit(solution)/shard_map/ppermute | solution.py:326
  135.8 13.7 %collective-permute-start.23 = (bf16[32,4096]{1,0:T(8,128)(2,1)S(1)}, bf16[32,4096]{1,0:T(8,128)(2,1)S(1)}, u32[]{:S(2)}, u32[]{:S(2)}) collective-permute-start(bf16[32,4096]{1,0:T(8,128)(2,1)S(1)} %shard_map.70.refs_0_), channel_id=1, source_target_pairs={{0,6},{2,4},{4,2},{6,0},{8,14},{10,12},{12,10},{14,8},{1,7},{3,5},... | collective-permute-start | bytes 786440 | tf_op jit(solution)/shard_map/ppermute | solution.py:326
  162.6 11.9 %collective-permute-start.24 = (bf16[32,4096]{1,0:T(8,128)(2,1)S(1)}, bf16[32,4096]{1,0:T(8,128)(2,1)S(1)}, u32[]{:S(2)}, u32[]{:S(2)}) collective-permute-start(bf16[32,4096]{1,0:T(8,128)(2,1)S(1)} %get-tuple-element.54), channel_id=1, source_target_pairs={{0,2},{2,0},{4,6},{6,4},{8,10},{10,8},{12,14},{14,12},{1,3},{3,1},... | collective-permute-start | bytes 786440 | tf_op jit(solution)/shard_map/ppermute | solution.py:326
  162.6 15.3 %collective-permute-start.25 = (bf16[32,4096]{1,0:T(8,128)(2,1)S(1)}, bf16[32,4096]{1,0:T(8,128)(2,1)S(1)}, u32[]{:S(2)}, u32[]{:S(2)}) collective-permute-start(bf16[32,4096]{1,0:T(8,128)(2,1)S(1)} %get-tuple-element.55), channel_id=1, source_target_pairs={{0,4},{2,6},{4,0},{6,2},{8,12},{10,14},{12,8},{14,10},{1,5},{3,7},... | collective-permute-start | bytes 786440 | tf_op jit(solution)/shard_map/ppermute | solution.py:326
  162.7 15.3 %collective-permute-start.26 = (bf16[32,4096]{1,0:T(8,128)(2,1)S(1)}, bf16[32,4096]{1,0:T(8,128)(2,1)S(1)}, u32[]{:S(2)}, u32[]{:S(2)}) collective-permute-start(bf16[32,4096]{1,0:T(8,128)(2,1)S(1)} %get-tuple-element.56), channel_id=1, source_target_pairs={{0,6},{2,4},{4,2},{6,0},{8,14},{10,12},{12,10},{14,8},{1,7},{3,5},... | collective-permute-start | bytes 786440 | tf_op jit(solution)/shard_map/ppermute | solution.py:326
  174.1 10.1 %collective-permute-start.27 = (bf16[32,4096]{1,0:T(8,128)(2,1)S(1)}, bf16[32,4096]{1,0:T(8,128)(2,1)S(1)}, u32[]{:S(2)}, u32[]{:S(2)}) collective-permute-start(bf16[32,4096]{1,0:T(8,128)(2,1)S(1)} %get-tuple-element.58), channel_id=1, source_target_pairs={{0,2},{2,0},{4,6},{6,4},{8,10},{10,8},{12,14},{14,12},{1,3},{3,1},... | collective-permute-start | bytes 786440 | tf_op jit(solution)/shard_map/ppermute | solution.py:326
  174.2 10.0 %collective-permute-start.28 = (bf16[32,4096]{1,0:T(8,128)(2,1)S(1)}, bf16[32,4096]{1,0:T(8,128)(2,1)S(1)}, u32[]{:S(2)}, u32[]{:S(2)}) collective-permute-start(bf16[32,4096]{1,0:T(8,128)(2,1)S(1)} %get-tuple-element.59), channel_id=1, source_target_pairs={{0,4},{2,6},{4,0},{6,2},{8,12},{10,14},{12,8},{14,10},{1,5},{3,7},... | collective-permute-start | bytes 786440 | tf_op jit(solution)/shard_map/ppermute | solution.py:326
  174.5 12.5 %collective-permute-start.29 = (bf16[32,4096]{1,0:T(8,128)(2,1)S(1)}, bf16[32,4096]{1,0:T(8,128)(2,1)S(1)}, u32[]{:S(2)}, u32[]{:S(2)}) collective-permute-start(bf16[32,4096]{1,0:T(8,128)(2,1)S(1)} %get-tuple-element.60), channel_id=1, source_target_pairs={{0,6},{2,4},{4,2},{6,0},{8,14},{10,12},{12,10},{14,8},{1,7},{3,5},... | collective-permute-start | bytes 786440 | tf_op jit(solution)/shard_map/ppermute | solution.py:326
  (20 other events, 167.8 us)

commit v16 on v15

--- a/solution.py
+++ b/solution.py
@@ -408,15 +408,19 @@
     held_first = [first, over_groups(first)]
     rest, late = lax.optimization_barrier((rest, held_upper[-1]))
     held_upper.append(over_groups(rest))
-    sent, late, matrix = lax.optimization_barrier((second, (held_upper, held_first), matrix))
+    sent, late, matrix, total = lax.optimization_barrier(
+        (second, (held_upper, held_first), matrix, total)
+    )
     held_second = [second, over_groups(sent)]
-    held_second, other_wave = lax.optimization_barrier((held_second, other_wave))
-    pieces = [to_core(blocks) for blocks in (held_first, held_upper, held_second)]
+    pieces = [to_core(blocks) for blocks in (held_first, held_upper)]
 
     joined, other_spots = [], []
     for number, (first, end) in enumerate(RANGES):
         other_spots.append((OTHER, number, number + 1, bases[first]))
         last = end == len(PARTS)
+        if last:
+            held_second, total = lax.optimization_barrier((held_second, total))
+            pieces.append(to_core(held_second))
         total, tiles_held = project(
             sizes,
             meta,

time: 186 us -> 212 us (1.14); the launches traced: 188 us -> 210 us
  waiting for transfers between devices: 67.9 us -> 89.2 us
  Pallas kernels: 33.7 us -> 23.1 us
  local copies, waits for them, and re-layouts: 35.9 us -> 44.6 us
  starting transfers between devices: 37.8 us -> 44.1 us
  other arithmetic: 11.3 us -> 8.29 us
    ppermute x1, waiting for transfers between devices: 0.01 us -> 12.6 us  [body(): taken = lax.ppermute(upper[middle:], 'grid', neighbours)]
    ppermute x1, waiting for transfers between devices: 10.2 us -> 18.8 us  [body(): rest = lax.ppermute(upper, 'grid', neighbours)]
    unnamed x40 -> x54, local copies, waits for them, and re-layouts: 17.1 us -> 25.5 us
    ppermute x1, waiting for transfers between devices: 6.46 us -> 0.01 us  [body(): second = lax.ppermute(second, 'grid', partners)]
    ppermute x12, starting transfers between devices: 14.2 us -> 20.1 us  [exchange(): lax.ppermute(blocks[d], 'grid', [(i, i // half * half + (i % half ^ d)) f...]
    ppermute x4, waiting for transfers between devices: 2.45 us -> 7.94 us  [over_groups(): return lax.ppermute(block, 'groups', swap)]
    pallas_call x3, Pallas kernels: 18.2 us -> 12.8 us  [project(): pl.pallas_call(functools.partial(project_kernel, sizes, firsts, spot, tot...]
    pallas_call x2, Pallas kernels: 14.5 us -> 9.32 us  [spread(): pl.pallas_call(functools.partial(spread_kernel, sizes, len(applied), spot...]
  transfers between devices with their start and end apart: 32 -> 32, of which waited for: 13 -> 14; matrix products, arithmetic and copies ran while one was open for 15% -> 11% of each run, Pallas kernels for 10% -> 6%
where the time goes in v16:
time: 212 us; the launch traced here: 210 us
  waiting for transfers between devices  89.2 us (42%)
  local copies, waits for them, and re-layouts  44.6 us (21%)
  starting transfers between devices  44.1 us (21%)
  Pallas kernels  23.1 us (11%)
  other arithmetic  8.29 us (4%)
    ppermute x12, waiting for transfers between devices, exchange(): lax.ppermute(blocks[d], 'grid', [(i, i // half * half + (i % half ^ d)) f...  32.4 us
    unnamed x54, local copies, waits for them, and re-layouts  25.5 us
    ppermute x12, starting transfers between devices, exchange(): lax.ppermute(blocks[d], 'grid', [(i, i // half * half + (i % half ^ d)) f...  20.1 us
    ppermute x1, waiting for transfers between devices, body(): rest = lax.ppermute(upper, 'grid', neighbours)  18.8 us
    ppermute x1, waiting for transfers between devices, body(): upper = lax.ppermute(upper, 'grid', partners)  15.5 us
    pallas_call x3, Pallas kernels, project(): pl.pallas_call(functools.partial(project_kernel, sizes, firsts, spot, tot...  12.8 us
    ppermute x1, waiting for transfers between devices, body(): taken = lax.ppermute(upper[middle:], 'grid', neighbours)  12.6 us
    pallas_call x2, Pallas kernels, spread(): pl.pallas_call(functools.partial(spread_kernel, sizes, len(applied), spot...  9.32 us
  transfers between devices with their start and end apart: 32, of which 14 were waited for; matrix products, arithmetic and copies ran while one was open for 11% of the time, Pallas kernels for 6%

profile of v16, /device:TPU:0, one launch (start us, length us, event | category | flops | bytes accessed | tf_op | source)
XLA Modules:
  0.0 210.3 jit_solution(10995484755491353057)
XLA Ops:
  0.0 2.6 %constant_dynamic-slice_fusion = (bf16[32,16384]{1,0:T(8,128)(2,1)}, bf16[32,16384]{1,0:T(8,128)(2,1)S(1)}) fusion(bf16[32,32768]{1,0:T(8,128)(2,1)} %param.6, s32[]{:T(128)S(6)} %select_n.398, s32[]{:T(128)S(6)} %select_n.397), kind=kLoop, calls=%fused_computation.42 | loop fusion | bytes 4194312 | tf_op jit(solution)/shard_map/dynamic_slice | solution.py:333
  3.7 5.2 %all-to-all-start = ((bf16[32,4,4096]{2,0,1:T(8,128)(2,1)}), bf16[32,4,4096]{2,0,1:T(8,128)(2,1)S(1)}, u32[]{:S(2)}, u32[]{:S(2)}) async-start(bf16[32,4,4096]{2,0,1:T(8,128)(2,1)} %bitcast.20), calls=%async_computation | async-start | bytes 2097152 | tf_op jit(solution)/shard_map/all_to_all | solution.py:335
  10.8 2.0 collective-permute-start
  16.0 2.0 select_convert_fusion.high_ref
  18.6 12.6 %collective-permute-done = bf16[24,64,128]{2,1,0:T(8,128)(2,1)} collective-permute-done((bf16[24,64,128]{2,1,0:T(8,128)(2,1)}, bf16[24,64,128]{2,1,0:T(8,128)(2,1)}, u32[]{:S(2)}, u32[]{:S(2)}) %collective-permute-start) | collective-permute-done | bytes 393248 | tf_op jit(solution)/shard_map/ppermute | solution.py:367
  31.1 2.6 %collective-permute-start.1 = (s32[3,384]{1,0:T(4,128)S(1)}, s32[3,384]{1,0:T(4,128)S(1)}, u32[]{:S(2)}, u32[]{:S(2)}) collective-permute-start(s32[3,384]{1,0:T(4,128)S(1)} %add_add_fusion), channel_id=1, source_target_pairs={{0,8},{2,10},{4,12},{6,14},{8,0},{10,2},{12,4},{14,6},{1,9},{3,11}... | collective-permute-start | bytes 13832 | tf_op jit(solution)/shard_map/ppermute | solution.py:381
  36.5 2.1 constant_dynamic-slice_fusion.2
  39.8 15.5 %collective-permute-done.2.refs_4_ = bf16[24,64,128]{2,1,0:T(8,128)(2,1)} collective-permute-done((bf16[24,64,128]{2,1,0:T(8,128)(2,1)}, bf16[24,64,128]{2,1,0:T(8,128)(2,1)}, u32[]{:S(2)}, u32[]{:S(2)}) %collective-permute-start.2) | collective-permute-done | bytes 393248 | tf_op jit(solution)/shard_map/ppermute | solution.py:369
  55.3 2.3 %copy.23 = bf16[4,4,8,4096]{3,2,0,1:T(8,128)(2,1)} copy(bf16[4,4,8,4096]{3,2,1,0:T(8,128)(2,1)} %bitcast.25) | data formatting | bytes 2097152 | tf_op jit(solution)/shard_map/all_to_all | solution.py:335
  61.0 3.5 %all-to-all-start.1 = ((bf16[32,4,4096]{2,0,1:T(8,128)(2,1)}), bf16[32,4,4096]{2,0,1:T(8,128)(2,1)S(1)}, u32[]{:S(2)}, u32[]{:S(2)}) async-start(bf16[32,4,4096]{2,0,1:T(8,128)(2,1)} %bitcast.27), calls=%async_computation.1 | async-start | bytes 2097152 | tf_op jit(solution)/shard_map/all_to_all | solution.py:335
  65.1 2.7 %collective-permute-start.3 = (bf16[24,64,128]{2,1,0:T(8,128)(2,1)}, bf16[24,64,128]{2,1,0:T(8,128)(2,1)S(1)}, u32[]{:S(2)}, u32[]{:S(2)}) collective-permute-start(bf16[24,64,128]{2,1,0:T(8,128)(2,1)} %get-tuple-element.36), channel_id=1, source_target_pairs={{0,8},{2,10},{4,12},{6,14},{8,0},{10,2},{12,4},{14,6},{1,9},{3,11}... | collective-permute-start | bytes 1179656 | tf_op jit(solution)/shard_map/ppermute | solution.py:374
  67.8 18.8 %collective-permute-done.4.refs_5_ = bf16[24,64,128]{2,1,0:T(8,128)(2,1)} collective-permute-done((bf16[24,64,128]{2,1,0:T(8,128)(2,1)}, bf16[24,64,128]{2,1,0:T(8,128)(2,1)}, u32[]{:S(2)}, u32[]{:S(2)}) %collective-permute-start.4) | collective-permute-done | bytes 393248 | tf_op jit(solution)/shard_map/ppermute | solution.py:375
  94.1 2.0 concatenate.26.meta
  96.7 7.9 %collective-permute-done.8.refs_1_ = bf16[24,64,128]{2,1,0:T(8,128)(2,1)} collective-permute-done((bf16[24,64,128]{2,1,0:T(8,128)(2,1)}, bf16[24,64,128]{2,1,0:T(8,128)(2,1)}, u32[]{:S(2)}, u32[]{:S(2)}) %collective-permute-start.8) | collective-permute-done | bytes 393248 | tf_op jit(solution)/shard_map/ppermute | solution.py:402
  106.4 2.8 %copy-done.2 = bf16[384,64,128]{2,1,0:T(8,128)(2,1)S(1)} copy-done((bf16[384,64,128]{2,1,0:T(8,128)(2,1)S(1)}, bf16[384,64,128]{2,1,0:T(8,128)(2,1)}, u32[]{:S(2)}) %copy-start.2) | copy-done | bytes 6291480
  109.2 3.3 %shard_map.67.refs_12_ = f32[128,4096]{1,0:T(8,128)S(1)} custom-call(s32[1225]{0:T(1024)S(1)} %concatenate.26.meta, bf16[128,4096]{1,0:T(8,128)(2,1)S(1)} %bitcast.24, bf16[384,64,128]{2,1,0:T(8,128)(2,1)S(1)} %copy-done.2), custom_call_target="tpu_custom_call" | custom-call | flops 5000000000 | bytes 1 | tf_op jit(solution)/shard_map/pallas_call | solution.py:232
  125.7 5.5 %shard_map.68 = (bf16[288,64,128]{2,1,0:T(8,128)(2,1)S(1)}, f32[128,4096]{1,0:T(8,128)S(1)}) custom-call(s32[1225]{0:T(1024)S(1)} %concatenate.26.meta, bf16[128,4096]{1,0:T(8,128)(2,1)S(1)} %bitcast.22, bf16[24,64,128]{2,1,0:T(8,128)(2,1)} %collective-permute-done.7.refs_0_, bf16[24,64,128]{2,1,0:T(8,128)(2,1)} %collective-permute-done.8.refs_1_, ...), custom_call_target="tpu_custom_call" | custom-call | flops 8000000000 | bytes 1 | tf_op jit(solution)/shard_map/pallas_call | solution.py:232
  131.1 2.1 %copy-done.18 = bf16[288,64,128]{2,1,0:T(8,128)(2,1)} copy-done((bf16[288,64,128]{2,1,0:T(8,128)(2,1)}, bf16[288,64,128]{2,1,0:T(8,128)(2,1)S(1)}, u32[]{:S(2)}) %copy-start.18) | copy-done | bytes 4718616
  135.8 4.1 %shard_map.69 = (bf16[96,64,128]{2,1,0:T(8,128)(2,1)S(1)}, bf16[32,4096]{1,0:T(8,128)(2,1)S(1)}, bf16[32,4096]{1,0:T(8,128)(2,1)S(1)}, bf16[32,4096]{1,0:T(8,128)(2,1)S(1)}, bf16[32,4096]{1,0:T(8,128)(2,1)S(1)}) custom-call(s32[1225]{0:T(1024)S(1)} %concatenate.26.meta, bf16[128,4096]{1,0:T(8,128)(2,1)S(1)} %bitcast.23, ...), custom_call_target="tpu_custom_call" | custom-call | flops 1 | bytes 1 | tf_op jit(solution)/shard_map/pallas_call | solution.py:232
  140.8 3.0 %collective-permute-start.19 = (bf16[32,4096]{1,0:T(8,128)(2,1)S(1)}, bf16[32,4096]{1,0:T(8,128)(2,1)S(1)}, u32[]{:S(2)}, u32[]{:S(2)}) collective-permute-start(bf16[32,4096]{1,0:T(8,128)(2,1)S(1)} %get-tuple-element.51), channel_id=1, source_target_pairs={{0,4},{2,6},{4,0},{6,2},{8,12},{10,14},{12,8},{14,10},{1,5},{3,7},... | collective-permute-start | bytes 786440 | tf_op jit(solution)/shard_map/ppermute | solution.py:326
  145.3 3.0 %collective-permute-done.18.refs_1_ = bf16[32,4096]{1,0:T(8,128)(2,1)S(1)} collective-permute-done((bf16[32,4096]{1,0:T(8,128)(2,1)S(1)}, bf16[32,4096]{1,0:T(8,128)(2,1)S(1)}, u32[]{:S(2)}, u32[]{:S(2)}) %collective-permute-start.18) | collective-permute-done | bytes 262176 | tf_op jit(solution)/shard_map/ppermute | solution.py:326
  148.3 2.7 %collective-permute-done.19.refs_2_ = bf16[32,4096]{1,0:T(8,128)(2,1)S(1)} collective-permute-done((bf16[32,4096]{1,0:T(8,128)(2,1)S(1)}, bf16[32,4096]{1,0:T(8,128)(2,1)S(1)}, u32[]{:S(2)}, u32[]{:S(2)}) %collective-permute-start.19) | collective-permute-done | bytes 262176 | tf_op jit(solution)/shard_map/ppermute | solution.py:326
  151.0 6.2 %collective-permute-done.20.refs_3_ = bf16[32,4096]{1,0:T(8,128)(2,1)S(1)} collective-permute-done((bf16[32,4096]{1,0:T(8,128)(2,1)S(1)}, bf16[32,4096]{1,0:T(8,128)(2,1)S(1)}, u32[]{:S(2)}, u32[]{:S(2)}) %collective-permute-start.20) | collective-permute-done | bytes 262176 | tf_op jit(solution)/shard_map/ppermute | solution.py:326
  161.7 4.8 %collective-permute-done.21.refs_1_ = bf16[32,4096]{1,0:T(8,128)(2,1)S(1)} collective-permute-done((bf16[32,4096]{1,0:T(8,128)(2,1)S(1)}, bf16[32,4096]{1,0:T(8,128)(2,1)S(1)}, u32[]{:S(2)}, u32[]{:S(2)}) %collective-permute-start.21) | collective-permute-done | bytes 262176 | tf_op jit(solution)/shard_map/ppermute | solution.py:326
  167.8 4.7 %collective-permute-done.23.refs_3_ = bf16[32,4096]{1,0:T(8,128)(2,1)S(1)} collective-permute-done((bf16[32,4096]{1,0:T(8,128)(2,1)S(1)}, bf16[32,4096]{1,0:T(8,128)(2,1)S(1)}, u32[]{:S(2)}, u32[]{:S(2)}) %collective-permute-start.23) | collective-permute-done | bytes 262176 | tf_op jit(solution)/shard_map/ppermute | solution.py:326
  173.9 2.3 %copy-done.19 = bf16[288,64,128]{2,1,0:T(8,128)(2,1)S(1)} copy-done((bf16[288,64,128]{2,1,0:T(8,128)(2,1)S(1)}, bf16[288,64,128]{2,1,0:T(8,128)(2,1)}, u32[]{:S(2)}) %copy-start.19) | copy-done | bytes 4718616
  176.2 5.8 %shard_map.71 = (bf16[32,4096]{1,0:T(8,128)(2,1)S(1)}, bf16[32,4096]{1,0:T(8,128)(2,1)S(1)}, bf16[32,4096]{1,0:T(8,128)(2,1)S(1)}, bf16[32,4096]{1,0:T(8,128)(2,1)S(1)}) custom-call(s32[1225]{0:T(1024)S(1)} %concatenate.26.meta, bf16[32,4096]{1,0:T(8,128)(2,1)S(1)} %shard_map.70.refs_0_, bf16[32,4096]{1,0:T(8,128)(2,1)S(1)} %collective-permute-done.21.refs_1_, ...), custom_call_target="tpu_custom_call" | custom-call | flops 8000000000 | bytes 1 | tf_op jit(solution)/shard_map/pallas_call | solution.py:254
  182.1 5.3 %collective-permute-start.25 = (bf16[32,4096]{1,0:T(8,128)(2,1)S(1)}, bf16[32,4096]{1,0:T(8,128)(2,1)S(1)}, u32[]{:S(2)}, u32[]{:S(2)}) collective-permute-start(bf16[32,4096]{1,0:T(8,128)(2,1)S(1)} %get-tuple-element.57), channel_id=1, source_target_pairs={{0,4},{2,6},{4,0},{6,2},{8,12},{10,14},{12,8},{14,10},{1,5},{3,7},... | collective-permute-start | bytes 786440 | tf_op jit(solution)/shard_map/ppermute | solution.py:326
  188.7 2.8 %copy-done.3 = bf16[384,64,128]{2,1,0:T(8,128)(2,1)S(1)} copy-done((bf16[384,64,128]{2,1,0:T(8,128)(2,1)S(1)}, bf16[384,64,128]{2,1,0:T(8,128)(2,1)}, u32[]{:S(2)}) %copy-start.3) | copy-done | bytes 6291480
  191.5 3.6 %shard_map.72 = (bf16[32,4096]{1,0:T(8,128)(2,1)S(1)}, bf16[32,4096]{1,0:T(8,128)(2,1)S(1)}, bf16[32,4096]{1,0:T(8,128)(2,1)S(1)}, bf16[32,4096]{1,0:T(8,128)(2,1)S(1)}) custom-call(s32[1225]{0:T(1024)S(1)} %concatenate.26.meta, bf16[32,4096]{1,0:T(8,128)(2,1)S(1)} %shard_map.70.refs_0_, bf16[32,4096]{1,0:T(8,128)(2,1)S(1)} %collective-permute-done.21.refs_1_, ...), custom_call_target="tpu_custom_call" | custom-call | flops 8000000000 | bytes 1 | tf_op jit(solution)/shard_map/pallas_call | solution.py:254
  199.9 5.8 %collective-permute-done.27 = bf16[32,4096]{1,0:T(8,128)(2,1)S(1)} collective-permute-done((bf16[32,4096]{1,0:T(8,128)(2,1)S(1)}, bf16[32,4096]{1,0:T(8,128)(2,1)S(1)}, u32[]{:S(2)}, u32[]{:S(2)}) %collective-permute-start.27) | collective-permute-done | bytes 262176 | tf_op jit(solution)/shard_map/ppermute | solution.py:326
  205.7 3.9 %collective-permute-done.29 = bf16[32,4096]{1,0:T(8,128)(2,1)S(1)} collective-permute-done((bf16[32,4096]{1,0:T(8,128)(2,1)S(1)}, bf16[32,4096]{1,0:T(8,128)(2,1)S(1)}, u32[]{:S(2)}, u32[]{:S(2)}) %collective-permute-start.29) | collective-permute-done | bytes 262176 | tf_op jit(solution)/shard_map/ppermute | solution.py:326
  (148 shorter events, 55.7 us)
Async XLA Ops:
  3.7 56.3 %all-to-all-start = ((bf16[32,4,4096]{2,0,1:T(8,128)(2,1)}), bf16[32,4,4096]{2,0,1:T(8,128)(2,1)S(1)}, u32[]{:S(2)}, u32[]{:S(2)}) async-start(bf16[32,4,4096]{2,0,1:T(8,128)(2,1)} %bitcast.20), calls=%async_computation | async-start | bytes 2097152 | tf_op jit(solution)/shard_map/all_to_all | solution.py:335
  10.8 20.4 %collective-permute-start = (bf16[24,64,128]{2,1,0:T(8,128)(2,1)}, bf16[24,64,128]{2,1,0:T(8,128)(2,1)}, u32[]{:S(2)}, u32[]{:S(2)}) collective-permute-start(bf16[24,64,128]{2,1,0:T(8,128)(2,1)} %constant_dynamic-slice_fusion.4), channel_id=1, source_target_pairs={{0,4},{2,6},{4,0},{6,2},{8,12},{10,14},{12,8},{14,10},{1,5},{3,7},... | collective-permute-start | bytes 1179656 | tf_op jit(solution)/shard_map/ppermute | solution.py:367
  31.1 7.5 %collective-permute-start.1 = (s32[3,384]{1,0:T(4,128)S(1)}, s32[3,384]{1,0:T(4,128)S(1)}, u32[]{:S(2)}, u32[]{:S(2)}) collective-permute-start(s32[3,384]{1,0:T(4,128)S(1)} %add_add_fusion), channel_id=1, source_target_pairs={{0,8},{2,10},{4,12},{6,14},{8,0},{10,2},{12,4},{14,6},{1,9},{3,11}... | collective-permute-start | bytes 13832 | tf_op jit(solution)/shard_map/ppermute | solution.py:381
  36.2 19.1 %collective-permute-start.2 = (bf16[24,64,128]{2,1,0:T(8,128)(2,1)}, bf16[24,64,128]{2,1,0:T(8,128)(2,1)}, u32[]{:S(2)}, u32[]{:S(2)}) collective-permute-start(bf16[24,64,128]{2,1,0:T(8,128)(2,1)} %dynamic-slice_select_fusion), channel_id=1, source_target_pairs={{0,8},{2,10},{4,12},{6,14},{8,0},{10,2},{12,4},{14,6},{1,9},{3,11}... | collective-permute-start | bytes 1179656 | tf_op jit(solution)/shard_map/ppermute | solution.py:369
  55.3 32.9 %collective-permute-start.7 = (bf16[24,64,128]{2,1,0:T(8,128)(2,1)}, bf16[24,64,128]{2,1,0:T(8,128)(2,1)}, u32[]{:S(2)}, u32[]{:S(2)}) collective-permute-start(bf16[24,64,128]{2,1,0:T(8,128)(2,1)} %get-tuple-element.38), channel_id=1, source_target_pairs={{0,8},{2,10},{4,12},{6,14},{8,0},{10,2},{12,4},{14,6},{1,9},{3,11}... | collective-permute-start | bytes 1179656 | tf_op jit(solution)/shard_map/ppermute | solution.py:373
  57.6 29.0 %collective-permute-start.4 = (bf16[24,64,128]{2,1,0:T(8,128)(2,1)}, bf16[24,64,128]{2,1,0:T(8,128)(2,1)}, u32[]{:S(2)}, u32[]{:S(2)}) collective-permute-start(bf16[24,64,128]{2,1,0:T(8,128)(2,1)} %collective-permute-done.2.refs_4_), channel_id=1, source_target_pairs={{0,4},{2,6},{4,0},{6,2},{8,12},{10,14},{12,8},{14,10},{1,5},{3,7},... | collective-permute-start | bytes 1179656 | tf_op jit(solution)/shard_map/ppermute | solution.py:375
  58.5 28.1 %collective-permute-start.5 = (bf16[24,64,128]{2,1,0:T(8,128)(2,1)}, bf16[24,64,128]{2,1,0:T(8,128)(2,1)}, u32[]{:S(2)}, u32[]{:S(2)}) collective-permute-start(bf16[24,64,128]{2,1,0:T(8,128)(2,1)} %collective-permute-done.2.refs_4_), channel_id=1, source_target_pairs={{0,16},{16,0},{1,17},{17,1},{2,18},{18,2},{3,19},{19,3},{4,20},{20... | collective-permute-start | bytes 1179656 | tf_op jit(solution)/shard_map/ppermute | solution.py:402
  61.0 58.1 %all-to-all-start.1 = ((bf16[32,4,4096]{2,0,1:T(8,128)(2,1)}), bf16[32,4,4096]{2,0,1:T(8,128)(2,1)S(1)}, u32[]{:S(2)}, u32[]{:S(2)}) async-start(bf16[32,4,4096]{2,0,1:T(8,128)(2,1)} %bitcast.27), calls=%async_computation.1 | async-start | bytes 2097152 | tf_op jit(solution)/shard_map/all_to_all | solution.py:335
  65.1 31.0 %collective-permute-start.3 = (bf16[24,64,128]{2,1,0:T(8,128)(2,1)}, bf16[24,64,128]{2,1,0:T(8,128)(2,1)S(1)}, u32[]{:S(2)}, u32[]{:S(2)}) collective-permute-start(bf16[24,64,128]{2,1,0:T(8,128)(2,1)} %get-tuple-element.36), channel_id=1, source_target_pairs={{0,8},{2,10},{4,12},{6,14},{8,0},{10,2},{12,4},{14,6},{1,9},{3,11}... | collective-permute-start | bytes 1179656 | tf_op jit(solution)/shard_map/ppermute | solution.py:374
  67.8 28.8 %collective-permute-start.12 = (bf16[24,64,128]{2,1,0:T(8,128)(2,1)}, bf16[24,64,128]{2,1,0:T(8,128)(2,1)}, u32[]{:S(2)}, u32[]{:S(2)}) collective-permute-start(bf16[24,64,128]{2,1,0:T(8,128)(2,1)} %collective-permute-done.2.refs_4_), channel_id=1, source_target_pairs={{0,1},{1,0},{2,3},{3,2},{4,5},{5,4},{6,7},{7,6},{8,9},{9,8},{10,11... | collective-permute-start | bytes 1179656 | tf_op jit(solution)/shard_map/ppermute | solution.py:405
  86.6 18.0 %collective-permute-start.6 = (bf16[24,64,128]{2,1,0:T(8,128)(2,1)}, bf16[24,64,128]{2,1,0:T(8,128)(2,1)}, u32[]{:S(2)}, u32[]{:S(2)}) collective-permute-start(bf16[24,64,128]{2,1,0:T(8,128)(2,1)} %collective-permute-done.4.refs_5_), channel_id=1, source_target_pairs={{0,16},{16,0},{1,17},{17,1},{2,18},{18,2},{3,19},{19,3},{4,20},{20... | collective-permute-start | bytes 1179656 | tf_op jit(solution)/shard_map/ppermute | solution.py:402
  88.1 16.5 %collective-permute-start.8 = (bf16[24,64,128]{2,1,0:T(8,128)(2,1)}, bf16[24,64,128]{2,1,0:T(8,128)(2,1)}, u32[]{:S(2)}, u32[]{:S(2)}) collective-permute-start(bf16[24,64,128]{2,1,0:T(8,128)(2,1)} %collective-permute-done.7.refs_0_), channel_id=1, source_target_pairs={{0,16},{16,0},{1,17},{17,1},{2,18},{18,2},{3,19},{19,3},{4,20},{20... | collective-permute-start | bytes 1179656 | tf_op jit(solution)/shard_map/ppermute | solution.py:402
  96.1 17.7 %collective-permute-start.10 = (bf16[24,64,128]{2,1,0:T(8,128)(2,1)}, bf16[24,64,128]{2,1,0:T(8,128)(2,1)S(1)}, u32[]{:S(2)}, u32[]{:S(2)}) collective-permute-start(bf16[24,64,128]{2,1,0:T(8,128)(2,1)} %collective-permute-done.7.refs_0_), channel_id=1, source_target_pairs={{0,1},{1,0},{2,3},{3,2},{4,5},{5,4},{6,7},{7,6},{8,9},{9,8},{10,11... | collective-permute-start | bytes 1179656 | tf_op jit(solution)/shard_map/ppermute | solution.py:405
  96.1 19.9 %collective-permute-start.13 = (bf16[24,64,128]{2,1,0:T(8,128)(2,1)}, bf16[24,64,128]{2,1,0:T(8,128)(2,1)S(1)}, u32[]{:S(2)}, u32[]{:S(2)}) collective-permute-start(bf16[24,64,128]{2,1,0:T(8,128)(2,1)} %collective-permute-done.4.refs_5_), channel_id=1, source_target_pairs={{0,1},{1,0},{2,3},{3,2},{4,5},{5,4},{6,7},{7,6},{8,9},{9,8},{10,11... | collective-permute-start | bytes 1179656 | tf_op jit(solution)/shard_map/ppermute | solution.py:405
  96.6 20.2 %collective-permute-start.14 = (bf16[24,64,128]{2,1,0:T(8,128)(2,1)}, bf16[24,64,128]{2,1,0:T(8,128)(2,1)S(1)}, u32[]{:S(2)}, u32[]{:S(2)}) collective-permute-start(bf16[24,64,128]{2,1,0:T(8,128)(2,1)} %collective-permute-done.5.refs_6_), channel_id=1, source_target_pairs={{0,1},{1,0},{2,3},{3,2},{4,5},{5,4},{6,7},{7,6},{8,9},{9,8},{10,11... | collective-permute-start | bytes 1179656 | tf_op jit(solution)/shard_map/ppermute | solution.py:405
  104.6 13.0 %collective-permute-start.11 = (bf16[24,64,128]{2,1,0:T(8,128)(2,1)}, bf16[24,64,128]{2,1,0:T(8,128)(2,1)S(1)}, u32[]{:S(2)}, u32[]{:S(2)}) collective-permute-start(bf16[24,64,128]{2,1,0:T(8,128)(2,1)} %collective-permute-done.8.refs_1_), channel_id=1, source_target_pairs={{0,1},{1,0},{2,3},{3,2},{4,5},{5,4},{6,7},{7,6},{8,9},{9,8},{10,11... | collective-permute-start | bytes 1179656 | tf_op jit(solution)/shard_map/ppermute | solution.py:405
  104.6 13.7 %collective-permute-start.15 = (bf16[24,64,128]{2,1,0:T(8,128)(2,1)}, bf16[24,64,128]{2,1,0:T(8,128)(2,1)S(1)}, u32[]{:S(2)}, u32[]{:S(2)}) collective-permute-start(bf16[24,64,128]{2,1,0:T(8,128)(2,1)} %collective-permute-done.6.refs_7_), channel_id=1, source_target_pairs={{0,1},{1,0},{2,3},{3,2},{4,5},{5,4},{6,7},{7,6},{8,9},{9,8},{10,11... | collective-permute-start | bytes 1179656 | tf_op jit(solution)/shard_map/ppermute | solution.py:405
  114.5 18.7 %collective-permute-start.9 = (bf16[24,64,128]{2,1,0:T(8,128)(2,1)S(1)}, bf16[24,64,128]{2,1,0:T(8,128)(2,1)}, u32[]{:S(2)}, u32[]{:S(2)}) collective-permute-start(bf16[24,64,128]{2,1,0:T(8,128)(2,1)S(1)} %collective-permute-done.3.refs_0_), channel_id=1, source_target_pairs={{0,16},{16,0},{1,17},{17,1},{2,18},{18,2},{3,19},{19,3},{4,20},{20... | collective-permute-start | bytes 1179656 | tf_op jit(solution)/shard_map/ppermute | solution.py:402
  133.3 2.2 %collective-permute-start.16 = (bf16[24,64,128]{2,1,0:T(8,128)(2,1)S(1)}, bf16[24,64,128]{2,1,0:T(8,128)(2,1)S(1)}, u32[]{:S(2)}, u32[]{:S(2)}) collective-permute-start(bf16[24,64,128]{2,1,0:T(8,128)(2,1)S(1)} %collective-permute-done.3.refs_0_), channel_id=1, source_target_pairs={{0,1},{1,0},{2,3},{3,2},{4,5},{5,4},{6,7},{7,6},{8,9},{9,8},{10,11... | collective-permute-start | bytes 1179656 | tf_op jit(solution)/shard_map/ppermute | solution.py:405
  133.3 2.5 %collective-permute-start.17 = (bf16[24,64,128]{2,1,0:T(8,128)(2,1)}, bf16[24,64,128]{2,1,0:T(8,128)(2,1)S(1)}, u32[]{:S(2)}, u32[]{:S(2)}) collective-permute-start(bf16[24,64,128]{2,1,0:T(8,128)(2,1)} %collective-permute-done.9.refs_1_), channel_id=1, source_target_pairs={{0,1},{1,0},{2,3},{3,2},{4,5},{5,4},{6,7},{7,6},{8,9},{9,8},{10,11... | collective-permute-start | bytes 1179656 | tf_op jit(solution)/shard_map/ppermute | solution.py:405
  139.9 8.4 %collective-permute-start.18 = (bf16[32,4096]{1,0:T(8,128)(2,1)S(1)}, bf16[32,4096]{1,0:T(8,128)(2,1)S(1)}, u32[]{:S(2)}, u32[]{:S(2)}) collective-permute-start(bf16[32,4096]{1,0:T(8,128)(2,1)S(1)} %get-tuple-element.50), channel_id=1, source_target_pairs={{0,2},{2,0},{4,6},{6,4},{8,10},{10,8},{12,14},{14,12},{1,3},{3,1},... | collective-permute-start | bytes 786440 | tf_op jit(solution)/shard_map/ppermute | solution.py:326
  140.8 10.1 %collective-permute-start.19 = (bf16[32,4096]{1,0:T(8,128)(2,1)S(1)}, bf16[32,4096]{1,0:T(8,128)(2,1)S(1)}, u32[]{:S(2)}, u32[]{:S(2)}) collective-permute-start(bf16[32,4096]{1,0:T(8,128)(2,1)S(1)} %get-tuple-element.51), channel_id=1, source_target_pairs={{0,4},{2,6},{4,0},{6,2},{8,12},{10,14},{12,8},{14,10},{1,5},{3,7},... | collective-permute-start | bytes 786440 | tf_op jit(solution)/shard_map/ppermute | solution.py:326
  143.9 13.3 %collective-permute-start.20 = (bf16[32,4096]{1,0:T(8,128)(2,1)S(1)}, bf16[32,4096]{1,0:T(8,128)(2,1)S(1)}, u32[]{:S(2)}, u32[]{:S(2)}) collective-permute-start(bf16[32,4096]{1,0:T(8,128)(2,1)S(1)} %get-tuple-element.52), channel_id=1, source_target_pairs={{0,6},{2,4},{4,2},{6,0},{8,14},{10,12},{12,10},{14,8},{1,7},{3,5},... | collective-permute-start | bytes 786440 | tf_op jit(solution)/shard_map/ppermute | solution.py:326
  158.1 8.4 %collective-permute-start.21 = (bf16[32,4096]{1,0:T(8,128)(2,1)S(1)}, bf16[32,4096]{1,0:T(8,128)(2,1)S(1)}, u32[]{:S(2)}, u32[]{:S(2)}) collective-permute-start(bf16[32,4096]{1,0:T(8,128)(2,1)S(1)} %shard_map.70.refs_0_), channel_id=1, source_target_pairs={{0,2},{2,0},{4,6},{6,4},{8,10},{10,8},{12,14},{14,12},{1,3},{3,1},... | collective-permute-start | bytes 786440 | tf_op jit(solution)/shard_map/ppermute | solution.py:326
  158.5 9.2 %collective-permute-start.22 = (bf16[32,4096]{1,0:T(8,128)(2,1)S(1)}, bf16[32,4096]{1,0:T(8,128)(2,1)S(1)}, u32[]{:S(2)}, u32[]{:S(2)}) collective-permute-start(bf16[32,4096]{1,0:T(8,128)(2,1)S(1)} %shard_map.70.refs_0_), channel_id=1, source_target_pairs={{0,4},{2,6},{4,0},{6,2},{8,12},{10,14},{12,8},{14,10},{1,5},{3,7},... | collective-permute-start | bytes 786440 | tf_op jit(solution)/shard_map/ppermute | solution.py:326
  160.3 12.2 %collective-permute-start.23 = (bf16[32,4096]{1,0:T(8,128)(2,1)S(1)}, bf16[32,4096]{1,0:T(8,128)(2,1)S(1)}, u32[]{:S(2)}, u32[]{:S(2)}) collective-permute-start(bf16[32,4096]{1,0:T(8,128)(2,1)S(1)} %shard_map.70.refs_0_), channel_id=1, source_target_pairs={{0,6},{2,4},{4,2},{6,0},{8,14},{10,12},{12,10},{14,8},{1,7},{3,5},... | collective-permute-start | bytes 786440 | tf_op jit(solution)/shard_map/ppermute | solution.py:326
  182.0 16.3 %collective-permute-start.24 = (bf16[32,4096]{1,0:T(8,128)(2,1)S(1)}, bf16[32,4096]{1,0:T(8,128)(2,1)S(1)}, u32[]{:S(2)}, u32[]{:S(2)}) collective-permute-start(bf16[32,4096]{1,0:T(8,128)(2,1)S(1)} %get-tuple-element.56), channel_id=1, source_target_pairs={{0,2},{2,0},{4,6},{6,4},{8,10},{10,8},{12,14},{14,12},{1,3},{3,1},... | collective-permute-start | bytes 786440 | tf_op jit(solution)/shard_map/ppermute | solution.py:326
  182.1 17.7 %collective-permute-start.25 = (bf16[32,4096]{1,0:T(8,128)(2,1)S(1)}, bf16[32,4096]{1,0:T(8,128)(2,1)S(1)}, u32[]{:S(2)}, u32[]{:S(2)}) collective-permute-start(bf16[32,4096]{1,0:T(8,128)(2,1)S(1)} %get-tuple-element.57), channel_id=1, source_target_pairs={{0,4},{2,6},{4,0},{6,2},{8,12},{10,14},{12,8},{14,10},{1,5},{3,7},... | collective-permute-start | bytes 786440 | tf_op jit(solution)/shard_map/ppermute | solution.py:326
  187.4 12.4 %collective-permute-start.26 = (bf16[32,4096]{1,0:T(8,128)(2,1)S(1)}, bf16[32,4096]{1,0:T(8,128)(2,1)S(1)}, u32[]{:S(2)}, u32[]{:S(2)}) collective-permute-start(bf16[32,4096]{1,0:T(8,128)(2,1)S(1)} %get-tuple-element.58), channel_id=1, source_target_pairs={{0,6},{2,4},{4,2},{6,0},{8,14},{10,12},{12,10},{14,8},{1,7},{3,5},... | collective-permute-start | bytes 786440 | tf_op jit(solution)/shard_map/ppermute | solution.py:326
  195.1 10.5 %collective-permute-start.27 = (bf16[32,4096]{1,0:T(8,128)(2,1)S(1)}, bf16[32,4096]{1,0:T(8,128)(2,1)S(1)}, u32[]{:S(2)}, u32[]{:S(2)}) collective-permute-start(bf16[32,4096]{1,0:T(8,128)(2,1)S(1)} %get-tuple-element.60), channel_id=1, source_target_pairs={{0,2},{2,0},{4,6},{6,4},{8,10},{10,8},{12,14},{14,12},{1,3},{3,1},... | collective-permute-start | bytes 786440 | tf_op jit(solution)/shard_map/ppermute | solution.py:326
  196.3 9.4 %collective-permute-start.28 = (bf16[32,4096]{1,0:T(8,128)(2,1)S(1)}, bf16[32,4096]{1,0:T(8,128)(2,1)S(1)}, u32[]{:S(2)}, u32[]{:S(2)}) collective-permute-start(bf16[32,4096]{1,0:T(8,128)(2,1)S(1)} %get-tuple-element.61), channel_id=1, source_target_pairs={{0,4},{2,6},{4,0},{6,2},{8,12},{10,14},{12,8},{14,10},{1,5},{3,7},... | collective-permute-start | bytes 786440 | tf_op jit(solution)/shard_map/ppermute | solution.py:326
  198.3 11.3 %collective-permute-start.29 = (bf16[32,4096]{1,0:T(8,128)(2,1)S(1)}, bf16[32,4096]{1,0:T(8,128)(2,1)S(1)}, u32[]{:S(2)}, u32[]{:S(2)}) collective-permute-start(bf16[32,4096]{1,0:T(8,128)(2,1)S(1)} %get-tuple-element.62), channel_id=1, source_target_pairs={{0,6},{2,4},{4,2},{6,0},{8,14},{10,12},{12,10},{14,8},{1,7},{3,5},... | collective-permute-start | bytes 786440 | tf_op jit(solution)/shard_map/ppermute | solution.py:326
  (27 other events, 126.7 us)
